TPU v7x, 128 devices: a whole 4x4x4 slice. The times are simulated.
128 devices in a mesh: group: 16 (over z, x), tp: 8 (over y, core).
Axes of the slice: x: 4, y: 4, z: 4, core: 2. Of those that a mesh axis runs over, the one named last changes fastest.
Arguments:
- attention_slot_outputs: bfloat16 [12288, 8192], P('group', 'tp'), may hold values from -6 to 6
- output_gradient_rows: bfloat16 [6144, 8192], P('group', 'tp'), may hold values from -6 to 6
- output_weight: bfloat16 [8192, 8192], P('tp'), may hold values from -0.0625 to 0.0625
- down_weight: bfloat16 [8192, 64], P('tp'), may hold values from -0.0625 to 0.0625
- up_weight: bfloat16 [64, 8192], P(None, 'tp'), may hold values from -0.0625 to 0.0625
- assign: int32 [48], replicated, may hold values from 0 to 15, as said below
- counts: int32 [16], replicated, may hold values from 0 to 6, as said below
Outputs:
- attention_input_gradient: bfloat16 [12288, 8192], P('group', 'tp')
- down_weight_gradient: float32 [8192, 64], P('tp')
- up_weight_gradient: float32 [64, 8192], P(None, 'tp')
Inputs may be any that keep to these rules, and one draw needn't show every extreme that they name: `assign`: the 3 rows g * 3 to g * 3 + 2 go to 3 different groups. Some group receives 6 rows. counts[g] is at least the number of rows assigned to group g.
All inputs are finite; a program needn't handle non-finite values.
Results may differ from a plain program's by a relative error of at most 0.0034.
Values may be sent and summed in bfloat16 or wider, within the bound.
No kernel may reach another device: no remote copies, remote signals or barrier semaphores. Data moves between devices by JAX's collectives and lax.ppermute only.
A program may use at most 128 MiB of HBM per device.

v0:
```python
import math

import jax
import jax.numpy as jnp
from jax import lax
from jax.sharding import PartitionSpec as P

ROW_TOKENS = 128


adapter_scale = 2.0


def body(
    attention_slot_outputs,
    output_gradient_rows,
    output_weight,
    down_weight,
    up_weight,
    assign,
    counts,
):
    groups = counts.shape[0]
    rows_here = output_gradient_rows.shape[0] // ROW_TOKENS
    slot_cap = attention_slot_outputs.shape[0] // ROW_TOKENS
    width_here = output_gradient_rows.shape[1]
    own_group = lax.axis_index("group")
    group_ids = jnp.arange(groups, dtype=jnp.int32)
    onehot = (assign[:, None] == group_ids[None, :]).astype(jnp.int32)
    before = jnp.cumsum(onehot, axis=0) - onehot
    order_in = jnp.sum(before * onehot, axis=1)
    free_slots = jnp.sum(onehot * counts[None, :], axis=1)
    position = slot_cap - free_slots + order_in
    source_group = jnp.arange(assign.shape[0], dtype=jnp.int32) // rows_here
    own_dest = lax.dynamic_slice_in_dim(assign, own_group * rows_here, rows_here)
    send_match = (own_dest[:, None] == group_ids[None, :]).astype(jnp.int32)
    send_has = jnp.sum(send_match, axis=0) > 0
    send_index = jnp.sum(send_match * jnp.arange(rows_here, dtype=jnp.int32)[:, None], axis=0)
    slot_ids = jnp.arange(slot_cap, dtype=jnp.int32)
    slot_match = ((assign == own_group)[:, None] & (position[:, None] == slot_ids[None, :])).astype(
        jnp.int32
    )
    slot_has = jnp.sum(slot_match, axis=0) > 0
    slot_source = jnp.sum(slot_match * source_group[:, None], axis=0)
    scale_factor = adapter_scale / math.sqrt(assign.shape[0] * ROW_TOKENS)

    def outer_sum(left, right):
        return scale_factor * lax.dot_general(
            left, right, (((0,), (0,)), ((), ())), preferred_element_type=jnp.float32
        )

    selected_rows = jnp.take(
        output_gradient_rows.reshape(rows_here, ROW_TOKENS, width_here), send_index, axis=0
    )
    received = lax.all_to_all(
        jnp.where(send_has[:, None, None], selected_rows, jnp.zeros_like(selected_rows)),
        "group",
        split_axis=0,
        concat_axis=0,
        tiled=True,
    )
    selected_rows = jnp.take(received, slot_source, axis=0)
    selected_rows = jnp.where(slot_has[:, None, None], selected_rows, jnp.zeros_like(selected_rows))
    slot_gradient = selected_rows.reshape(slot_cap * ROW_TOKENS, received.shape[2])
    projected_portion = jnp.dot(
        attention_slot_outputs, down_weight, preferred_element_type=jnp.float32
    )
    low_total, projected_total = lax.psum(
        (
            lax.dot_general(
                slot_gradient,
                up_weight,
                (((1,), (1,)), ((), ())),
                preferred_element_type=jnp.float32,
            ),
            projected_portion,
        ),
        "tp",
    )
    lowrank_gradient = low_total.astype(jnp.bfloat16)
    projected_gradient = projected_total.astype(jnp.bfloat16)
    base = lax.dot_general(
        lax.all_gather(slot_gradient, "tp", axis=1, tiled=True),
        output_weight,
        (((1,), (1,)), ((), ())),
        preferred_element_type=jnp.float32,
    )
    attention_input_gradient = (
        base
        + adapter_scale
        * lax.dot_general(
            lowrank_gradient,
            down_weight,
            (((1,), (1,)), ((), ())),
            preferred_element_type=jnp.float32,
        )
    ).astype(jnp.bfloat16)
    down_contribution = outer_sum(attention_slot_outputs, lowrank_gradient)
    up_contribution = outer_sum(projected_gradient, slot_gradient)
    down_weight_gradient, up_weight_gradient = lax.psum(
        (down_contribution, up_contribution), "group"
    )
    return (attention_input_gradient, down_weight_gradient, up_weight_gradient)


def solution(mesh):
    in_specs = (
        P("group", "tp"),
        P("group", "tp"),
        P("tp", None),
        P("tp", None),
        P(None, "tp"),
        P(),
        P(),
    )
    out_specs = (P("group", "tp"), P("tp", None), P(None, "tp"))
    return jax.shard_map(body, mesh=mesh, in_specs=in_specs, out_specs=out_specs, check_vma=False)
```

profile of v0, /device:TPU:0, one launch (start us, length us, event | category | flops | bytes accessed | tf_op | source)
XLA Modules:
  0.0 236.6 jit_solution(9064255125940493259)
XLA Ops:
  8.0 0.0 copy-start
  8.0 0.8 dynamic_slice.3
  8.9 0.1 convert_reduce_fusion.1
  9.0 3.9 %gather_fusion = bf16[16,128,1024]{2,1,0:T(8,128)(2,1)} fusion(bf16[3,128,1024]{2,1,0:T(8,128)(2,1)} %bitcast.31, s32[1024]{0:T(1024)S(1)} %pad_clamp_fusion.1), kind=kCustom, calls=%fused_computation | custom fusion | bytes 8388672 | tf_op jit(solution)/shard_map/jit(_take)/gather | solution.py:52
  12.9 4.7 %select_select_fusion = bf16[16,128,1024]{2,1,0:T(8,128)(2,1)} fusion(bf16[16,128,1024]{2,1,0:T(8,128)(2,1)} %gather_fusion, pred[16]{0:T(512)(128)(4,1)S(1)} %get-tuple-element.13, pred[16]{0:T(512)(128)(4,1)S(1)} %get-tuple-element.14), kind=kLoop, calls=%fused_computation.2 | loop fusion | flops 4194304 | bytes 8388640 | tf_op jit(solution)/shard_map/jit(_where)/select_n | solution.py:56
  17.6 8.1 %all-to-all-start = ((bf16[16,128,1024]{2,1,0:T(8,128)(2,1)}), bf16[16,128,1024]{2,1,0:T(8,128)(2,1)}, u32[]{:S(2)}, u32[]{:S(2)}) async-start(bf16[16,128,1024]{2,1,0:T(8,128)(2,1)} %select_select_fusion), calls=%async_computation | async-start | bytes 8388608 | tf_op jit(solution)/shard_map/all_to_all | solution.py:55
  25.7 0.0 all-gather.2.cloned.1.call-start
  25.8 0.0 copy-done.4
  25.8 0.1 fusion.6
  25.9 0.1 reduce_window_sum.11
  26.0 0.0 copy-done.5
  26.0 0.2 select_reduce_fusion.1
  26.2 0.1 convert_reduce_fusion
  26.4 0.1 broadcast_bitcast_fusion
  26.4 0.1 broadcast_bitcast_fusion.1
  26.5 62.5 %all-to-all-done = bf16[16,128,1024]{2,1,0:T(8,128)(2,1)} async-done(((bf16[16,128,1024]{2,1,0:T(8,128)(2,1)}), bf16[16,128,1024]{2,1,0:T(8,128)(2,1)}, u32[]{:S(2)}, u32[]{:S(2)}) %all-to-all-start) | async-done | bytes 4194336 | tf_op jit(solution)/shard_map/all_to_all | solution.py:55
  89.0 2.8 %gather_fusion.1 = bf16[6,128,1024]{2,1,0:T(8,128)(2,1)S(1)} fusion(bf16[16,128,1024]{2,1,0:T(8,128)(2,1)} %all-to-all-done, s32[1024]{0:T(1024)S(1)} %pad_clamp_fusion), kind=kCustom, calls=%fused_computation.1 | custom fusion | bytes 3145752 | tf_op jit(solution)/shard_map/jit(_take)/gather | solution.py:62
  91.8 1.5 fusion
  93.3 0.0 all-gather.2.cloned.1.call-update
  93.3 0.0 all-reduce.5.cloned.1.call-start
  93.4 1.6 fusion.11
  95.0 2.2 fusion.10
  97.2 41.2 %all-reduce.6 = (bf16[768,64]{0,1:T(8,128)(2,1)}, bf16[768,64]{1,0:T(8,128)(2,1)}) all-reduce(f32[768,64]{0,1:T(8,128)} %fusion.10, f32[768,64]{1,0:T(8,128)S(1)} %fusion.11), channel_id=1, replica_groups=mesh['group'=16,'tp'=8] {'tp'}, use_global_device_ids=true, to_apply=%region_7.8 | all-reduce | flops 98304 | bytes 589824 | tf_op jit(solution)/shard_map/psum | solution.py:68
  138.4 2.1 fusion.1
  140.5 2.0 convolution_multiply_fusion
  142.5 2.3 fusion.12
  144.8 0.0 all-reduce.5.cloned.1.call-update
  144.8 19.8 %all-gather.2.cloned.1.call-done = bf16[768,8192]{1,0:T(8,128)(2,1)} async-done(((bf16[768,1024]{1,0:T(8,128)(2,1)}), bf16[768,8192]{1,0:T(8,128)(2,1)}) %all-gather.2.cloned.1.call-update) | async-done | bytes 12582928 | tf_op jit(solution)/shard_map/all_gather | solution.py:83
  164.6 21.7 %add_convert_fusion = bf16[768,1024]{1,0:T(8,128)(2,1)} fusion(f32[768,1024]{1,0:T(8,128)} %fusion.12, bf16[768,8192]{1,0:T(8,128)(2,1)} %all-gather.2.cloned.1.call-done, bf16[1024,8192]{1,0:T(8,128)(2,1)} %param.9), kind=kOutput, calls=%fused_computation.3 | convolution fusion | flops 12887261184 | bytes 34078720 | tf_op jit(solution)/shard_map/dot_general | solution.py:82
  186.3 39.5 %all-reduce.5.cloned.1.call-done = (f32[1024,64]{0,1:T(8,128)}, f32[64,1024]{1,0:T(8,128)}) async-done(((f32[1024,64]{0,1:T(8,128)}, f32[64,1024]{1,0:T(8,128)}), (f32[1024,64]{0,1:T(8,128)}, f32[64,1024]{1,0:T(8,128)})) %all-reduce.5.cloned.1.call-update) | async-done | bytes 524304 | tf_op jit(solution)/shard_map/psum | solution.py:100
  225.8 1.7 copy.16
  227.5 1.7 copy.17
  (18 shorter events, 0.1 us)
Async XLA Ops:
  8.0 85.4 %copy-start = (bf16[768,1024]{1,0:T(8,128)(2,1)S(1)}, bf16[768,1024]{1,0:T(8,128)(2,1)}, u32[]{:S(2)}) copy-start(bf16[768,1024]{1,0:T(8,128)(2,1)} %param.7) | copy-start | bytes 4718596
  17.6 8.2 %copy-start.4 = (s32[48]{0:T(128)S(1)}, s32[48]{0:T(128)}, u32[]{:S(2)}) copy-start(s32[48]{0:T(128)} %param.12) | copy-start | bytes 580
  17.6 8.4 %copy-start.5 = (s32[16]{0:T(128)S(1)}, s32[16]{0:T(128)}, u32[]{:S(2)}) copy-start(s32[16]{0:T(128)} %param.13) | copy-start | bytes 196
  17.6 71.4 %all-to-all-start = ((bf16[16,128,1024]{2,1,0:T(8,128)(2,1)}), bf16[16,128,1024]{2,1,0:T(8,128)(2,1)}, u32[]{:S(2)}, u32[]{:S(2)}) async-start(bf16[16,128,1024]{2,1,0:T(8,128)(2,1)} %select_select_fusion), calls=%async_computation | async-start | bytes 8388608 | tf_op jit(solution)/shard_map/all_to_all | solution.py:55
  25.7 138.8 %all-gather.2.cloned.1.call-start = ((), (), s32[]{:S(2)}) async-start(), calls=%async_computation.1 | async-start | bytes 14155776 | tf_op jit(solution)/shard_map/all_gather | solution.py:83
  93.3 1.7 copy-start.1
  93.3 132.5 %all-reduce.5.cloned.1.call-start = ((), (), s32[]{:S(2)}) async-start(), calls=%async_computation.2 | async-start | bytes 1048576 | tf_op jit(solution)/shard_map/psum | solution.py:100
  138.4 4.1 %copy-start.2 = (bf16[1024,64]{0,1:T(8,128)(2,1)S(1)}, bf16[1024,64]{0,1:T(8,128)(2,1)}, u32[]{:S(2)}) copy-start(bf16[1024,64]{0,1:T(8,128)(2,1)} %param.10) | copy-start | bytes 393220
  138.4 4.1 %copy-start.3 = (bf16[768,64]{0,1:T(8,128)(2,1)S(1)}, bf16[768,64]{0,1:T(8,128)(2,1)}, u32[]{:S(2)}) copy-start(bf16[768,64]{0,1:T(8,128)(2,1)} %get-tuple-element.11) | copy-start | bytes 294916
Sparse Core Ops, SparseCore 0:
  93.5 71.0 all-gather.1
Sparse Core Ops, SparseCore 1:
  144.9 80.9 all-reduce.4
where the time goes:
time: 237 us
  waiting for transfers between devices  122 us (51%)
  blocking collectives  41.2 us (17%)
  matrix products  31.8 us (13%)
  between operations  15.6 us (7%)
  local copies, waits for them, and re-layouts  11.1 us (5%)
  starting transfers between devices  8.23 us (3%)
  other arithmetic  6.81 us (3%)
    all_to_all x1, waiting for transfers between devices, body(): lax.all_to_all(jnp.where(send_has[:, None, None], selected_rows, jnp.zero...  62.5 us
    psum x1, blocking collectives, body(): lax.psum((lax.dot_general(slot_gradient, up_weight, (((1,), (1,)), ((), (...  41.2 us
    psum x1, waiting for transfers between devices, body(): lax.psum((down_contribution, up_contribution), 'group')  39.5 us
    dot_general x1, matrix products, body(): lax.dot_general(lax.all_gather(slot_gradient, 'tp', axis=1, tiled=True),...  21.7 us
    all_gather x1, waiting for transfers between devices, body(): lax.all_gather(slot_gradient, 'tp', axis=1, tiled=True)  19.8 us
    all_to_all x1, starting transfers between devices, body(): lax.all_to_all(jnp.where(send_has[:, None, None], selected_rows, jnp.zero...  8.14 us
  transfers between devices with their start and end apart: 3, of which 3 were waited for; matrix products, arithmetic and copies ran while one was open for 14% of the time, Pallas kernels for 0%

commit v1 on v0

v1 whole, which is shorter than its diff:
```python
import math

import jax
import jax.numpy as jnp
from jax import lax
from jax.sharding import PartitionSpec as P

ROW_TOKENS = 128


adapter_scale = 2.0


def body(
    attention_slot_outputs,
    output_gradient_rows,
    output_weight,
    down_weight,
    up_weight,
    assign,
    counts,
):
    groups = counts.shape[0]
    rows = assign.shape[0]
    rows_here = output_gradient_rows.shape[0] // ROW_TOKENS
    slot_cap = attention_slot_outputs.shape[0] // ROW_TOKENS
    width_here = output_gradient_rows.shape[1]
    rank = up_weight.shape[0]
    tp = lax.axis_size("tp")
    piece = ROW_TOKENS // groups
    own_group = lax.axis_index("group")
    group_ids = jnp.arange(groups, dtype=jnp.int32)
    onehot = (assign[:, None] == group_ids[None, :]).astype(jnp.int32)
    before = jnp.cumsum(onehot, axis=0) - onehot
    order_in = jnp.sum(before * onehot, axis=1)
    free_slots = jnp.sum(onehot * counts[None, :], axis=1)
    position = slot_cap - free_slots + order_in
    own_dest = lax.dynamic_slice_in_dim(assign, own_group * rows_here, rows_here)
    own_position = lax.dynamic_slice_in_dim(position, own_group * rows_here, rows_here)
    scale_factor = adapter_scale / math.sqrt(rows * ROW_TOKENS)

    spread = lax.all_to_all(
        output_gradient_rows.reshape(rows_here, groups, piece, width_here).transpose(1, 0, 2, 3),
        "group",
        split_axis=0,
        concat_axis=0,
        tiled=True,
    ).reshape(rows * piece, width_here)

    low_part = lax.dot_general(
        up_weight, output_gradient_rows, (((1,), (1,)), ((), ())),
        preferred_element_type=jnp.float32,
    )
    projected_part = lax.dot_general(
        down_weight, attention_slot_outputs, (((0,), (1,)), ((), ())),
        preferred_element_type=jnp.float32,
    )
    parts = jnp.concatenate([low_part, projected_part], axis=1)
    tokens_both = parts.shape[1]
    parts = lax.all_to_all(
        parts.reshape(tp, rank // tp, tokens_both), "tp", split_axis=0, concat_axis=0, tiled=True
    )
    sums = jnp.sum(parts, axis=0).astype(jnp.bfloat16)
    sums = lax.all_to_all(
        jnp.broadcast_to(sums[None], (tp, rank // tp, tokens_both)),
        "tp", split_axis=0, concat_axis=0, tiled=True,
    ).reshape(rank, tokens_both)
    low = sums[:, : rows_here * ROW_TOKENS].reshape(rank, rows_here, ROW_TOKENS)
    projected = sums[:, rows_here * ROW_TOKENS :].reshape(rank, slot_cap, ROW_TOKENS)

    low_send = jnp.zeros((groups, rank, ROW_TOKENS), jnp.bfloat16)
    for r in range(rows_here):
        hit = own_dest[r] == group_ids
        low_send = jnp.where(hit[:, None, None], low[:, r][None], low_send)
    row_position = position.reshape(groups, rows_here)
    hit_row = assign.reshape(groups, rows_here) == own_group
    wanted = jnp.sum(jnp.where(hit_row, row_position, 0), axis=1)
    projected_send = jnp.zeros((groups, rank, ROW_TOKENS), jnp.bfloat16)
    for s in range(slot_cap):
        hit = wanted == s
        projected_send = jnp.where(hit[:, None, None], projected[:, s][None], projected_send)
    crossed = lax.all_to_all(
        jnp.concatenate([low_send, projected_send], axis=1),
        "group", split_axis=0, concat_axis=0, tiled=True,
    )
    slot_ids = jnp.arange(slot_cap, dtype=jnp.int32)
    slot_match = (hit_row[:, :, None] & (row_position[:, :, None] == slot_ids)).any(axis=1)
    slot_has = slot_match.any(axis=0)
    slot_source = jnp.sum(slot_match * group_ids[:, None], axis=0)
    low_slot = jnp.concatenate(
        [
            jnp.where(
                slot_has[s],
                lax.dynamic_index_in_dim(crossed, slot_source[s], 0, keepdims=False)[:rank],
                jnp.zeros((rank, ROW_TOKENS), jnp.bfloat16),
            )
            for s in range(slot_cap)
        ],
        axis=1,
    )
    projected_row = jnp.concatenate(
        [
            lax.dynamic_index_in_dim(crossed, own_dest[r], 0, keepdims=False)[rank:]
            for r in range(rows_here)
        ],
        axis=1,
    )
    down_part = jnp.dot(low_slot, attention_slot_outputs, preferred_element_type=jnp.float32)
    up_part = jnp.dot(projected_row, output_gradient_rows, preferred_element_type=jnp.float32)
    grads = (scale_factor * jnp.concatenate([down_part, up_part], axis=0)).astype(jnp.bfloat16)
    share = 2 * rank // groups
    grads = lax.all_to_all(
        grads.reshape(groups, share, width_here), "group", split_axis=0, concat_axis=0, tiled=True
    )
    grads = jnp.sum(grads.astype(jnp.float32), axis=0)
    grads = lax.all_to_all(
        jnp.broadcast_to(grads[None], (groups, share, width_here)),
        "group", split_axis=0, concat_axis=0, tiled=True,
    ).reshape(2 * rank, width_here)
    down_weight_gradient = grads[:rank].T
    up_weight_gradient = grads[rank:]

    index = lax.axis_index("tp")
    chips = tp // 2
    y, core = index // 2, index % 2
    forward = [(2 * a + b, 2 * ((a + 1) % chips) + b) for a in range(chips) for b in range(2)]
    backward = [(2 * a + b, 2 * ((a - 1) % chips) + b) for a in range(chips) for b in range(2)]
    swap = [(i, i ^ 1) for i in range(tp)]
    half = spread.shape[0] // 2

    from_left = lax.ppermute(spread, "tp", forward)
    from_right = lax.ppermute(spread, "tp", backward)
    far = jnp.concatenate(
        [
            lax.ppermute(from_left[:half], "tp", forward),
            lax.ppermute(from_right[half:], "tp", backward),
        ],
        axis=0,
    )

    def term(block, owner_y, owner_core):
        columns = lax.dynamic_slice_in_dim(
            output_weight, (owner_y * 2 + owner_core) * width_here, width_here, axis=1
        )
        columns_up = lax.dynamic_slice_in_dim(
            up_all, owner_y * 2 + owner_core, 1, axis=0
        )[0]
        return (
            lax.dot_general(
                block, columns, (((1,), (1,)), ((), ())), preferred_element_type=jnp.float32
            ),
            lax.dot_general(
                block, columns_up, (((1,), (1,)), ((), ())), preferred_element_type=jnp.float32
            ),
        )

    up_all = lax.all_gather(up_weight, "tp", axis=0)
    base, low_own = 0.0, 0.0
    for block, step in ((spread, 0), (from_left, chips - 1), (from_right, 1), (far, 2)):
        owner = lax.rem(y + step, chips)
        for part, owner_core in ((block, core), (lax.ppermute(block, "tp", swap), 1 - core)):
            a, b = term(part, owner, owner_core)
            base, low_own = base + a, low_own + b
    row_input = (
        base
        + adapter_scale
        * lax.dot_general(
            low_own.astype(jnp.bfloat16), down_weight, (((1,), (1,)), ((), ())),
            preferred_element_type=jnp.float32,
        )
    ).astype(jnp.bfloat16)

    all_match = (assign[None, :] == group_ids[:, None])[:, None, :] & (
        position[None, None, :] == slot_ids[None, :, None]
    )
    all_match = all_match.reshape(groups * slot_cap, rows)
    all_has = all_match.any(axis=1)
    all_source = jnp.sum(all_match * jnp.arange(rows, dtype=jnp.int32)[None, :], axis=1)
    placed = jnp.take(row_input.reshape(rows, piece, width_here), all_source, axis=0)
    placed = jnp.where(all_has[:, None, None], placed, jnp.zeros_like(placed))
    arrived = lax.all_to_all(
        placed.reshape(groups, slot_cap, piece, width_here),
        "group", split_axis=0, concat_axis=0, tiled=True,
    )
    attention_input_gradient = arrived.transpose(1, 0, 2, 3).reshape(
        slot_cap * ROW_TOKENS, width_here
    )
    return (attention_input_gradient, down_weight_gradient, up_weight_gradient)


def solution(mesh):
    in_specs = (
        P("group", "tp"),
        P("group", "tp"),
        P("tp", None),
        P("tp", None),
        P(None, "tp"),
        P(),
        P(),
    )
    out_specs = (P("group", "tp"), P("tp", None), P(None, "tp"))
    return jax.shard_map(body, mesh=mesh, in_specs=in_specs, out_specs=out_specs, check_vma=False)
```

time: 237 us -> 215 us (0.907); the launches traced: 237 us -> 212 us
  waiting for transfers between devices: 122 us -> 52.6 us
  blocking collectives: 41.2 us -> 0 us
  starting transfers between devices: 8.23 us -> 45.6 us
  matrix products: 31.8 us -> 48.5 us
  between operations: 15.6 us -> 31.2 us
  other arithmetic: 6.81 us -> 16.7 us
  local copies, waits for them, and re-layouts: 11.1 us -> 17.6 us
    psum x1 -> x0, blocking collectives: 41.2 us -> none  [body(): lax.psum((lax.dot_general(slot_gradient, up_weight, (((1,), (1,)), ((), (...]
    psum x1 -> x0, waiting for transfers between devices: 39.5 us -> none  [body(): lax.psum((down_contribution, up_contribution), 'group')]
    all_to_all x1 -> x7, starting transfers between devices: 8.14 us -> 38.4 us  [the longest x1 7.72 us: body(): lax.all_to_all(output_gradient_rows.reshape(rows_here, groups, piece, wid...]
    all_gather x1, waiting for transfers between devices: 19.8 us -> 0.01 us  [body(): up_all = lax.all_gather(up_weight, 'tp', axis=0)]
    dot_general x6 -> x20, matrix products: 31.8 us -> 48.5 us  [the longest x8 33.8 us: term(): lax.dot_general(block, columns, (((1,), (1,)), ((), ())), preferred_eleme...]
    all_to_all x1 -> x7, waiting for transfers between devices: 62.5 us -> 51.9 us  [the longest x1 24.6 us: body(): lax.all_to_all(placed.reshape(groups, slot_cap, piece, width_here), 'grou...]
    slice x0 -> x11, local copies, waits for them, and re-layouts: none -> 7.42 us  [the longest x1 1.87 us: body(): up_weight_gradient = grads[rank:]]
    ppermute x0 -> x8, starting transfers between devices: none -> 7.25 us  [the longest x1 3.06 us: body(): lax.ppermute(from_right[half:], 'tp', backward)]
  transfers between devices with their start and end apart: 3 -> 16, of which waited for: 3 -> 5; matrix products, arithmetic and copies ran while one was open for 14% -> 38% of each run, Pallas kernels for 0% -> 0%
where the time goes in v1:
time: 215 us; the launch traced here: 212 us
  waiting for transfers between devices  52.6 us (24%)
  matrix products  48.5 us (23%)
  starting transfers between devices  45.6 us (21%)
  between operations  31.2 us (15%)
  local copies, waits for them, and re-layouts  17.6 us (8%)
  other arithmetic  16.7 us (8%)
    dot_general x8, matrix products, term(): lax.dot_general(block, columns, (((1,), (1,)), ((), ())), preferred_eleme...  33.8 us
    all_to_all x1, waiting for transfers between devices, body(): lax.all_to_all(placed.reshape(groups, slot_cap, piece, width_here), 'grou...  24.6 us
    all_to_all x1, waiting for transfers between devices, body(): lax.all_to_all(output_gradient_rows.reshape(rows_here, groups, piece, wid...  12.6 us
    dot_general x7, matrix products, term(): lax.dot_general(block, columns_up, (((1,), (1,)), ((), ())), preferred_el...  7.93 us
    all_to_all x1, starting transfers between devices, body(): lax.all_to_all(output_gradient_rows.reshape(rows_here, groups, piece, wid...  7.72 us
    all_to_all x1, starting transfers between devices, body(): lax.all_to_all(placed.reshape(groups, slot_cap, piece, width_here), 'grou...  7.14 us
    all_to_all x1, starting transfers between devices, body(): lax.all_to_all(grads.reshape(groups, share, width_here), 'group', split_a...  7.09 us
    unnamed x5, other arithmetic  6.74 us
  transfers between devices with their start and end apart: 16, of which 5 were waited for; matrix products, arithmetic and copies ran while one was open for 38% of the time, Pallas kernels for 0%

profile of v1, /device:TPU:0, one launch (start us, length us, event | category | flops | bytes accessed | tf_op | source)
XLA Modules:
  0.0 212.2 jit_solution(9710822973359543942)
XLA Ops:
  7.9 1.6 fusion.101
  9.5 1.6 fusion.102
  11.9 4.6 %all-to-all-start.2 = ((f32[8,8,1152]{2,1,0:T(8,128)}), f32[8,8,1152]{2,1,0:T(8,128)S(1)}, u32[]{:S(2)}, u32[]{:S(2)}) async-start(f32[8,8,1152]{2,1,0:T(8,128)} %maximum_bitcast_fusion), calls=%async_computation.2 | async-start | bytes 589824 | tf_op jit(solution)/shard_map/all_to_all | solution.py:60
  19.7 4.6 %all-to-all-done.2 = f32[8,8,1152]{2,1,0:T(8,128)S(1)} async-done(((f32[8,8,1152]{2,1,0:T(8,128)}), f32[8,8,1152]{2,1,0:T(8,128)S(1)}, u32[]{:S(2)}, u32[]{:S(2)}) %all-to-all-start.2) | async-done | bytes 294944 | tf_op jit(solution)/shard_map/all_to_all | solution.py:60
  25.0 3.4 %all-to-all-start.3 = ((bf16[8,8,1152]{2,1,0:T(8,128)(2,1)}), bf16[8,8,1152]{2,1,0:T(8,128)(2,1)S(1)}, u32[]{:S(2)}, u32[]{:S(2)}) async-start(bf16[8,8,1152]{2,1,0:T(8,128)(2,1)} %broadcast_in_dim.178), calls=%async_computation.3 | async-start | bytes 294912 | tf_op jit(solution)/shard_map/all_to_all | solution.py:64
  30.2 4.6 %all-to-all-done.3 = bf16[8,8,1152]{2,1,0:T(8,128)(2,1)S(1)} async-done(((bf16[8,8,1152]{2,1,0:T(8,128)(2,1)}), bf16[8,8,1152]{2,1,0:T(8,128)(2,1)S(1)}, u32[]{:S(2)}, u32[]{:S(2)}) %all-to-all-start.3) | async-done | bytes 147488 | tf_op jit(solution)/shard_map/all_to_all | solution.py:64
  34.8 7.7 %all-to-all-start = ((bf16[16,3,8,1024]{3,2,1,0:T(8,128)(2,1)}), bf16[16,3,8,1024]{3,2,1,0:T(8,128)(2,1)}, u32[]{:S(2)}, u32[]{:S(2)}) async-start(bf16[16,3,8,1024]{3,2,1,0:T(8,128)(2,1)} %copy.22), calls=%async_computation | async-start | bytes 1572864 | tf_op jit(solution)/shard_map/all_to_all | solution.py:42
  44.2 12.6 %all-to-all-done = bf16[16,3,8,1024]{3,2,1,0:T(8,128)(2,1)} async-done(((bf16[16,3,8,1024]{3,2,1,0:T(8,128)(2,1)}), bf16[16,3,8,1024]{3,2,1,0:T(8,128)(2,1)}, u32[]{:S(2)}, u32[]{:S(2)}) %all-to-all-start) | async-done | bytes 786464 | tf_op jit(solution)/shard_map/all_to_all | solution.py:42
  56.8 4.2 %all-to-all-start.4 = ((bf16[16,128,128]{2,1,0:T(8,128)(2,1)}), bf16[16,128,128]{2,1,0:T(8,128)(2,1)}, u32[]{:S(2)}, u32[]{:S(2)}) async-start(bf16[16,128,128]{2,1,0:T(8,128)(2,1)} %pad_maximum_fusion), calls=%async_computation.4 | async-start | bytes 1048576 | tf_op jit(solution)/shard_map/all_to_all | solution.py:82
  80.9 1.9 collective-permute-start.3
  93.0 7.1 %all-to-all-start.5 = ((bf16[16,8,1024]{2,1,0:T(8,128)(2,1)}), bf16[16,8,1024]{2,1,0:T(8,128)(2,1)S(1)}, u32[]{:S(2)}, u32[]{:S(2)}) async-start(bf16[16,8,1024]{2,1,0:T(8,128)(2,1)} %fusion.31), calls=%async_computation.5 | async-start | bytes 524288 | tf_op jit(solution)/shard_map/all_to_all | solution.py:112
  100.1 4.0 %fusion.14 = f32[1024,384]{0,1:T(8,128)} fusion(bf16[384,1024]{1,0:T(8,128)(2,1)} %bitcast.2, bf16[1024,8192]{1,0:T(8,128)(2,1)} %param.9, s32[]{:T(128)S(6)} %select_n.208), kind=kOutput, calls=%fused_computation.15 | convolution fusion | flops 805306368 | bytes 4456452 | tf_op jit(solution)/shard_map/dot_general | solution.py:149
  104.1 5.4 %all-to-all-done.5 = bf16[16,8,1024]{2,1,0:T(8,128)(2,1)S(1)} async-done(((bf16[16,8,1024]{2,1,0:T(8,128)(2,1)}), bf16[16,8,1024]{2,1,0:T(8,128)(2,1)S(1)}, u32[]{:S(2)}, u32[]{:S(2)}) %all-to-all-start.5) | async-done | bytes 262176 | tf_op jit(solution)/shard_map/all_to_all | solution.py:112
  110.4 4.2 %all-to-all-start.6 = ((f32[16,8,1024]{2,1,0:T(8,128)}), f32[16,8,1024]{2,1,0:T(8,128)}, u32[]{:S(2)}, u32[]{:S(2)}) async-start(f32[16,8,1024]{2,1,0:T(8,128)} %broadcast_in_dim.206), calls=%async_computation.6 | async-start | bytes 1048576 | tf_op jit(solution)/shard_map/all_to_all | solution.py:116
  114.7 1.8 slice.187
  117.4 3.1 %collective-permute-start.6 = (bf16[192,1024]{1,0:T(8,128)(2,1)}, bf16[192,1024]{1,0:T(8,128)(2,1)}, u32[]{:S(2)}, u32[]{:S(2)}) collective-permute-start(bf16[192,1024]{1,0:T(8,128)(2,1)} %slice.188), channel_id=1, source_target_pairs={{0,6},{1,7},{2,0},{3,1},{4,2},{5,3},{6,4},{7,5},{8,14},{9,15},{10,... | collective-permute-start | bytes 1179656 | tf_op jit(solution)/shard_map/ppermute | solution.py:136
  121.0 3.7 %fusion.6 = f32[1024,384]{0,1:T(8,128)} fusion(bf16[384,1024]{1,0:T(8,128)(2,1)S(1)} %collective-permute-done.3, bf16[1024,8192]{1,0:T(8,128)(2,1)} %param.9, s32[]{:T(128)S(6)} %select_n.212), kind=kOutput, calls=%fused_computation.7 | convolution fusion | flops 805306368 | bytes 4456452 | tf_op jit(solution)/shard_map/dot_general | solution.py:149
  124.7 3.9 %fusion.10 = f32[1024,384]{0,1:T(8,128)} fusion(bf16[384,1024]{1,0:T(8,128)(2,1)} %collective-permute-done.1, bf16[1024,8192]{1,0:T(8,128)(2,1)} %param.9, s32[]{:T(128)S(6)} %select_n.210), kind=kOutput, calls=%fused_computation.11 | convolution fusion | flops 805306368 | bytes 4456452 | tf_op jit(solution)/shard_map/dot_general | solution.py:149
  128.7 4.0 %fusion.12 = f32[1024,384]{0,1:T(8,128)} fusion(bf16[384,1024]{1,0:T(8,128)(2,1)} %collective-permute-done, bf16[1024,8192]{1,0:T(8,128)(2,1)} %param.9, s32[]{:T(128)S(6)} %select_n.209), kind=kOutput, calls=%fused_computation.13 | convolution fusion | flops 805306368 | bytes 4456452 | tf_op jit(solution)/shard_map/dot_general | solution.py:149
  132.7 1.6 fusion.43
  134.3 1.6 convolution_add_fusion.3
  140.1 3.8 %fusion.2 = f32[384,1024]{1,0:T(8,128)} fusion(bf16[384,1024]{1,0:T(8,128)(2,1)S(1)} %constant_dynamic-update-slice_fusion, bf16[1024,8192]{1,0:T(8,128)(2,1)} %param.9, s32[]{:T(128)S(6)} %select_n.214), kind=kOutput, calls=%fused_computation.3 | convolution fusion | flops 805306368 | bytes 4456452 | tf_op jit(solution)/shard_map/dot_general | solution.py:149
  144.3 4.0 %fusion.8 = f32[1024,384]{0,1:T(8,128)} fusion(bf16[384,1024]{1,0:T(8,128)(2,1)} %collective-permute-done.2, bf16[1024,8192]{1,0:T(8,128)(2,1)} %param.9, s32[]{:T(128)S(6)} %select_n.211), kind=kOutput, calls=%fused_computation.9 | convolution fusion | flops 805306368 | bytes 4456452 | tf_op jit(solution)/shard_map/dot_general | solution.py:149
  150.8 3.8 %fusion = f32[384,1024]{1,0:T(8,128)} fusion(bf16[384,1024]{1,0:T(8,128)(2,1)S(1)} %collective-permute-done.7, bf16[1024,8192]{1,0:T(8,128)(2,1)} %param.9, s32[]{:T(128)S(6)} %select_n.215), kind=kOutput, calls=%fused_computation.1 | convolution fusion | flops 805306368 | bytes 4456452 | tf_op jit(solution)/shard_map/dot_general | solution.py:149
  154.6 3.0 %fusion.29 = f32[384,1024]{1,0:T(8,128)} fusion(bf16[1024,64]{0,1:T(8,128)(2,1)S(1)} %copy-done.3, f32[384,64]{0,1:T(8,128)} %fusion.32, f32[384,64]{0,1:T(8,128)S(1)} %fusion.34, f32[64,384]{1,0:T(8,128)S(1)} %fusion.27, bf16[384,1024]{1,0:T(8,128)(2,1)S(1)} %collective-permute-done.4, bf16[8,64,1024]{2,1,0:T(8,128)(2,1)} %bitcast.162, s32[]{:T(128)S(6)} %select_n.221), kind=kOutput, calls=%fused_computation.32 | convolution fusion | flops 100761600 | bytes 2916356 | tf_op jit(solution)/shard_map/dot_general | solution.py:167
  157.6 6.6 %fusion.21 = bf16[48,8,1024]{2,1,0:T(8,128)(2,1)S(1)} fusion(f32[384,1024]{1,0:T(8,128)} %fusion.29, f32[384,1024]{1,0:T(8,128)} %fusion, f32[384,1024]{1,0:T(8,128)} %fusion.2, bf16[384,1024]{1,0:T(8,128)(2,1)S(1)} %collective-permute-done.4, bf16[1024,8192]{1,0:T(8,128)(2,1)} %param.9, s32[]{:T(128)S(6)} %select_n.213, f32[1024,384]{0,1:T(8,128)} %fusion.6, ...), kind=kOutput, calls=%fused_computation.22 | convolution fusion | flops 809238528 | bytes 16252932 | tf_op jit(solution)/shard_map/dot_general | solution.py:149
  164.2 1.9 gather_fusion
  166.1 2.8 %select_select_fusion = bf16[16,6,8,1024]{3,2,1,0:T(8,128)(2,1)} fusion(bf16[16,6,8,1024]{3,2,1,0:T(8,128)(2,1)} %bitcast.158, pred[16,6]{1,0:T(8,128)(4,1)S(1)} %copy.21, pred[16,6]{1,0:T(8,128)(4,1)S(1)} %copy.20), kind=kLoop, calls=%fused_computation.21 | loop fusion | flops 1572864 | bytes 3145920 | tf_op jit(solution)/shard_map/jit(_where)/select_n | solution.py:180
  169.0 7.1 %all-to-all-start.1 = ((bf16[16,6,8,1024]{3,2,1,0:T(8,128)(2,1)}), bf16[16,6,8,1024]{3,2,1,0:T(8,128)(2,1)}, u32[]{:S(2)}, u32[]{:S(2)}) async-start(bf16[16,6,8,1024]{3,2,1,0:T(8,128)(2,1)} %select_select_fusion), calls=%async_computation.1 | async-start | bytes 3145728 | tf_op jit(solution)/shard_map/all_to_all | solution.py:181
  176.1 1.9 slice_bitcast_fusion
  178.0 24.6 %all-to-all-done.1 = bf16[16,6,8,1024]{3,2,1,0:T(8,128)(2,1)} async-done(((bf16[16,6,8,1024]{3,2,1,0:T(8,128)(2,1)}), bf16[16,6,8,1024]{3,2,1,0:T(8,128)(2,1)}, u32[]{:S(2)}, u32[]{:S(2)}) %all-to-all-start.1) | async-done | bytes 1572896 | tf_op jit(solution)/shard_map/all_to_all | solution.py:181
  202.6 2.7 %copy.24 = bf16[16,6,8,1024]{3,2,0,1:T(8,128)(2,1)} copy(bf16[16,6,8,1024]{3,2,1,0:T(8,128)(2,1)} %all-to-all-done.1) | data formatting | bytes 3145728 | tf_op jit(solution)/shard_map/all_to_all | solution.py:181
  (99 shorter events, 31.6 us)
Async XLA Ops:
  7.2 2.3 %copy-start = (bf16[768,1024]{1,0:T(8,128)(2,1)S(1)}, bf16[768,1024]{1,0:T(8,128)(2,1)}, u32[]{:S(2)}) copy-start(bf16[768,1024]{1,0:T(8,128)(2,1)} %param.7) | copy-start | bytes 4718596
  7.2 125.5 %all-gather.3.cloned.1.call-start = ((), (), s32[]{:S(2)}) async-start(), calls=%async_computation.7 | async-start | bytes 1179648 | tf_op jit(solution)/shard_map/all_gather | solution.py:157
  9.5 6.9 %copy-start.4 = (s32[48]{0:T(128)S(1)}, s32[48]{0:T(128)}, u32[]{:S(2)}) copy-start(s32[48]{0:T(128)} %param.12) | copy-start | bytes 580
  9.5 7.1 %copy-start.5 = (s32[16]{0:T(128)S(1)}, s32[16]{0:T(128)}, u32[]{:S(2)}) copy-start(s32[16]{0:T(128)} %param.13) | copy-start | bytes 196
  9.5 19.5 %copy-start.1 = (bf16[384,1024]{1,0:T(8,128)(2,1)S(1)}, bf16[384,1024]{1,0:T(8,128)(2,1)}, u32[]{:S(2)}) copy-start(bf16[384,1024]{1,0:T(8,128)(2,1)} %param.8) | copy-start | bytes 2359300
  11.9 12.4 %all-to-all-start.2 = ((f32[8,8,1152]{2,1,0:T(8,128)}), f32[8,8,1152]{2,1,0:T(8,128)S(1)}, u32[]{:S(2)}, u32[]{:S(2)}) async-start(f32[8,8,1152]{2,1,0:T(8,128)} %maximum_bitcast_fusion), calls=%async_computation.2 | async-start | bytes 589824 | tf_op jit(solution)/shard_map/all_to_all | solution.py:60
  25.0 9.8 %all-to-all-start.3 = ((bf16[8,8,1152]{2,1,0:T(8,128)(2,1)}), bf16[8,8,1152]{2,1,0:T(8,128)(2,1)S(1)}, u32[]{:S(2)}, u32[]{:S(2)}) async-start(bf16[8,8,1152]{2,1,0:T(8,128)(2,1)} %broadcast_in_dim.178), calls=%async_computation.3 | async-start | bytes 294912 | tf_op jit(solution)/shard_map/all_to_all | solution.py:64
  34.8 22.0 %all-to-all-start = ((bf16[16,3,8,1024]{3,2,1,0:T(8,128)(2,1)}), bf16[16,3,8,1024]{3,2,1,0:T(8,128)(2,1)}, u32[]{:S(2)}, u32[]{:S(2)}) async-start(bf16[16,3,8,1024]{3,2,1,0:T(8,128)(2,1)} %copy.22), calls=%async_computation | async-start | bytes 1572864 | tf_op jit(solution)/shard_map/all_to_all | solution.py:42
  56.8 25.9 %all-to-all-start.4 = ((bf16[16,128,128]{2,1,0:T(8,128)(2,1)}), bf16[16,128,128]{2,1,0:T(8,128)(2,1)}, u32[]{:S(2)}, u32[]{:S(2)}) async-start(bf16[16,128,128]{2,1,0:T(8,128)(2,1)} %pad_maximum_fusion), calls=%async_computation.4 | async-start | bytes 1048576 | tf_op jit(solution)/shard_map/all_to_all | solution.py:82
  79.5 35.2 %collective-permute-start.1 = (bf16[384,1024]{1,0:T(8,128)(2,1)}, bf16[384,1024]{1,0:T(8,128)(2,1)}, u32[]{:S(2)}, u32[]{:S(2)}) collective-permute-start(bf16[384,1024]{1,0:T(8,128)(2,1)} %bitcast.2), channel_id=1, source_target_pairs={{0,2},{1,3},{2,4},{3,5},{4,6},{5,7},{6,0},{7,1},{8,10},{9,11},{10,... | collective-permute-start | bytes 2359304 | tf_op jit(solution)/shard_map/ppermute | solution.py:131
  80.9 35.7 %collective-permute-start.3 = (bf16[384,1024]{1,0:T(8,128)(2,1)}, bf16[384,1024]{1,0:T(8,128)(2,1)S(1)}, u32[]{:S(2)}, u32[]{:S(2)}) collective-permute-start(bf16[384,1024]{1,0:T(8,128)(2,1)} %bitcast.2), channel_id=1, source_target_pairs={{0,6},{1,7},{2,0},{3,1},{4,2},{5,3},{6,4},{7,5},{8,14},{9,15},{10,... | collective-permute-start | bytes 2359304 | tf_op jit(solution)/shard_map/ppermute | solution.py:132
  82.7 46.0 %collective-permute-start = (bf16[384,1024]{1,0:T(8,128)(2,1)}, bf16[384,1024]{1,0:T(8,128)(2,1)}, u32[]{:S(2)}, u32[]{:S(2)}) collective-permute-start(bf16[384,1024]{1,0:T(8,128)(2,1)} %bitcast.2), channel_id=1, source_target_pairs={{0,1},{1,0},{2,3},{3,2},{4,5},{5,4},{6,7},{7,6},{8,9},{9,8},{10,11... | collective-permute-start | bytes 2359304 | tf_op jit(solution)/shard_map/ppermute | solution.py:161
  93.0 16.4 %all-to-all-start.5 = ((bf16[16,8,1024]{2,1,0:T(8,128)(2,1)}), bf16[16,8,1024]{2,1,0:T(8,128)(2,1)S(1)}, u32[]{:S(2)}, u32[]{:S(2)}) async-start(bf16[16,8,1024]{2,1,0:T(8,128)(2,1)} %fusion.31), calls=%async_computation.5 | async-start | bytes 524288 | tf_op jit(solution)/shard_map/all_to_all | solution.py:112
  110.4 58.6 %all-to-all-start.6 = ((f32[16,8,1024]{2,1,0:T(8,128)}), f32[16,8,1024]{2,1,0:T(8,128)}, u32[]{:S(2)}, u32[]{:S(2)}) async-start(f32[16,8,1024]{2,1,0:T(8,128)} %broadcast_in_dim.206), calls=%async_computation.6 | async-start | bytes 1048576 | tf_op jit(solution)/shard_map/all_to_all | solution.py:116
  116.4 21.3 %collective-permute-start.5 = (bf16[192,1024]{1,0:T(8,128)(2,1)}, bf16[192,1024]{1,0:T(8,128)(2,1)}, u32[]{:S(2)}, u32[]{:S(2)}) collective-permute-start(bf16[192,1024]{1,0:T(8,128)(2,1)} %slice.187), channel_id=1, source_target_pairs={{0,2},{1,3},{2,4},{3,5},{4,6},{5,7},{6,0},{7,1},{8,10},{9,11},{10,... | collective-permute-start | bytes 1179656 | tf_op jit(solution)/shard_map/ppermute | solution.py:135
  117.4 21.4 %collective-permute-start.6 = (bf16[192,1024]{1,0:T(8,128)(2,1)}, bf16[192,1024]{1,0:T(8,128)(2,1)}, u32[]{:S(2)}, u32[]{:S(2)}) collective-permute-start(bf16[192,1024]{1,0:T(8,128)(2,1)} %slice.188), channel_id=1, source_target_pairs={{0,6},{1,7},{2,0},{3,1},{4,2},{5,3},{6,4},{7,5},{8,14},{9,15},{10,... | collective-permute-start | bytes 1179656 | tf_op jit(solution)/shard_map/ppermute | solution.py:136
  120.5 23.8 %collective-permute-start.2 = (bf16[384,1024]{1,0:T(8,128)(2,1)}, bf16[384,1024]{1,0:T(8,128)(2,1)}, u32[]{:S(2)}, u32[]{:S(2)}) collective-permute-start(bf16[384,1024]{1,0:T(8,128)(2,1)} %collective-permute-done.1), channel_id=1, source_target_pairs={{0,1},{1,0},{2,3},{3,2},{4,5},{5,4},{6,7},{7,6},{8,9},{9,8},{10,11... | collective-permute-start | bytes 2359304 | tf_op jit(solution)/shard_map/ppermute | solution.py:161
  120.5 34.1 %collective-permute-start.4 = (bf16[384,1024]{1,0:T(8,128)(2,1)S(1)}, bf16[384,1024]{1,0:T(8,128)(2,1)S(1)}, u32[]{:S(2)}, u32[]{:S(2)}) collective-permute-start(bf16[384,1024]{1,0:T(8,128)(2,1)S(1)} %collective-permute-done.3), channel_id=1, source_target_pairs={{0,1},{1,0},{2,3},{3,2},{4,5},{5,4},{6,7},{7,6},{8,9},{9,8},{10,11... | collective-permute-start | bytes 2359304 | tf_op jit(solution)/shard_map/ppermute | solution.py:161
  132.7 3.2 %copy-start.2 = (bf16[512,1024]{1,0:T(8,128)(2,1)S(1)}, bf16[512,1024]{1,0:T(8,128)(2,1)}, u32[]{:S(2)}) copy-start(bf16[512,1024]{1,0:T(8,128)(2,1)} %all-gather.3.cloned.1.call-done) | copy-start | bytes 3145732
  139.9 10.0 %collective-permute-start.7 = (bf16[384,1024]{1,0:T(8,128)(2,1)S(1)}, bf16[384,1024]{1,0:T(8,128)(2,1)S(1)}, u32[]{:S(2)}, u32[]{:S(2)}) collective-permute-start(bf16[384,1024]{1,0:T(8,128)(2,1)S(1)} %constant_dynamic-update-slice_fusion), channel_id=1, source_target_pairs={{0,1},{1,0},{2,3},{3,2},{4,5},{5,4},{6,7},{7,6},{8,9},{9,8},{10,11... | collective-permute-start | bytes 2359304 | tf_op jit(solution)/shard_map/ppermute | solution.py:161
  150.8 3.8 %copy-start.3 = (bf16[1024,64]{0,1:T(8,128)(2,1)S(1)}, bf16[1024,64]{0,1:T(8,128)(2,1)}, u32[]{:S(2)}) copy-start(bf16[1024,64]{0,1:T(8,128)(2,1)} %param.10) | copy-start | bytes 393220
  169.0 33.6 %all-to-all-start.1 = ((bf16[16,6,8,1024]{3,2,1,0:T(8,128)(2,1)}), bf16[16,6,8,1024]{3,2,1,0:T(8,128)(2,1)}, u32[]{:S(2)}, u32[]{:S(2)}) async-start(bf16[16,6,8,1024]{3,2,1,0:T(8,128)(2,1)} %select_select_fusion), calls=%async_computation.1 | async-start | bytes 3145728 | tf_op jit(solution)/shard_map/all_to_all | solution.py:181
Sparse Core Ops, SparseCore 0:
  9.7 26.6 all-gather.2

commit v2 on v1

v2 whole, which is shorter than its diff:
```python
import functools
import math

import jax
import jax.numpy as jnp
from jax import lax
from jax.experimental import pallas as pl
from jax.experimental.pallas import tpu as pltpu
from jax.sharding import PartitionSpec as P

ROW_TOKENS = 128
LANES = 128


adapter_scale = 2.0

CONTRACT_MINOR = (((1,), (1,)), ((), ()))


def dot_minor(left, right):
    return lax.dot_general(left, right, CONTRACT_MINOR, preferred_element_type=jnp.float32)


def early_kernel(count, owner, *refs):
    blocks, (weight, up, base, low) = refs[:count], refs[count:]
    block_id, tile = pl.program_id(0), pl.program_id(1)
    width = weight.shape[0]
    columns = pl.ds(pl.multiple_of(tile * width, width), width)
    for i in range(count):

        @pl.when(block_id == i)
        def _():
            value = dot_minor(blocks[i][...], weight[...])
            if i == 0:
                base[:, columns] = value
            else:
                base[:, columns] += value

            @pl.when(tile == 0)
            def _():
                value_low = dot_minor(blocks[i][...], up[0])
                if i == 0:
                    low[...] = value_low
                else:
                    low[...] += value_low


def early_products(owner, blocks, output_weight, up_all):
    count = len(blocks)
    tokens, width = blocks[0].shape
    out_width = output_weight.shape[0]
    rank = up_all.shape[1]
    tiles = 2
    whole = pl.BlockSpec((tokens, width), lambda k, n, owner: (0, 0))
    return pl.pallas_call(
        functools.partial(early_kernel, count),
        grid_spec=pltpu.PrefetchScalarGridSpec(
            num_scalar_prefetch=1,
            grid=(count, tiles),
            in_specs=[whole] * count
            + [
                pl.BlockSpec((out_width // tiles, width), lambda k, n, owner: (n, owner[k])),
                pl.BlockSpec((1, rank, width), lambda k, n, owner: (owner[k], 0, 0)),
            ],
            out_specs=[
                pl.BlockSpec((tokens, out_width), lambda k, n, owner: (0, 0)),
                pl.BlockSpec((tokens, rank), lambda k, n, owner: (0, 0)),
            ],
        ),
        out_shape=[
            jax.ShapeDtypeStruct((tokens, out_width), jnp.float32),
            jax.ShapeDtypeStruct((tokens, rank), jnp.float32),
        ],
        compiler_params=pltpu.CompilerParams(vmem_limit_bytes=40 * 2**20),
        cost_estimate=pl.CostEstimate(
            flops=2 * count * tokens * width * out_width,
            bytes_accessed=2 * count * width * (tokens + out_width) + 8 * tokens * out_width,
            transcendentals=0,
        ),
        name="early_products",
    )(owner, *blocks, output_weight, up_all)


def last_kernel(
    owner, dest, place, far_a, far_b, other_a, other_b, weight_far, weight_other,
    up_far, up_other, base, low, down, out, low_rounded,
):
    half = far_a.shape[0]
    rows = dest.shape[0]
    piece = 2 * half // rows

    @pl.when(pl.program_id(0) == 0)
    def _():
        for start, far, other in ((0, far_a, other_a), (half, far_b, other_b)):
            part = pl.ds(start, half)
            total = low[part, :] + dot_minor(far[...], up_far[0]) + dot_minor(other[...], up_other[0])
            low_rounded[part, :] = total.astype(jnp.bfloat16)

    out[...] = jnp.zeros_like(out)
    for start, far, other in ((0, far_a, other_a), (half, far_b, other_b)):
        part = pl.ds(start, half)
        total = base[part, :] + dot_minor(far[...], weight_far[...])
        total += dot_minor(other[...], weight_other[...])
        total += adapter_scale * dot_minor(low_rounded[part, :], down[...])
        for i in range(half // piece):
            row = start // piece + i
            mine = total[i * piece : (i + 1) * piece]
            folded = jnp.concatenate([mine[:, :LANES], mine[:, LANES:]], axis=0)
            out[dest[row], place[row]] = folded.astype(jnp.bfloat16)


def last_products(
    owner, dest, place, far, other, output_weight, up_all, base, low, down_weight, groups, slots
):
    half, width = far[0].shape
    tokens = 2 * half
    out_width = output_weight.shape[0]
    rank = up_all.shape[1]
    piece = tokens // dest.shape[0]
    tile = 2 * LANES
    whole = pl.BlockSpec((half, width), lambda n, *s: (0, 0))
    return pl.pallas_call(
        last_kernel,
        grid_spec=pltpu.PrefetchScalarGridSpec(
            num_scalar_prefetch=3,
            grid=(out_width // tile,),
            in_specs=[whole] * 4
            + [
                pl.BlockSpec((tile, width), lambda n, owner, *s: (n, owner[0])),
                pl.BlockSpec((tile, width), lambda n, owner, *s: (n, owner[1])),
                pl.BlockSpec((1, rank, width), lambda n, owner, *s: (owner[0], 0, 0)),
                pl.BlockSpec((1, rank, width), lambda n, owner, *s: (owner[1], 0, 0)),
                pl.BlockSpec((tokens, tile), lambda n, *s: (0, n)),
                pl.BlockSpec((tokens, rank), lambda n, *s: (0, 0)),
                pl.BlockSpec((tile, rank), lambda n, *s: (n, 0)),
            ],
            out_specs=pl.BlockSpec(
                (groups, slots + 1, 2 * piece, LANES), lambda n, *s: (0, 0, 0, n)
            ),
            scratch_shapes=[pltpu.VMEM((tokens, rank), jnp.bfloat16)],
        ),
        out_shape=jax.ShapeDtypeStruct(
            (groups, slots + 1, 2 * piece, out_width // 2), jnp.bfloat16
        ),
        compiler_params=pltpu.CompilerParams(vmem_limit_bytes=40 * 2**20),
        cost_estimate=pl.CostEstimate(
            flops=4 * tokens * width * out_width,
            bytes_accessed=4 * width * (tokens + out_width) + 8 * tokens * out_width,
            transcendentals=0,
        ),
        name="last_products",
    )(
        owner, dest, place, *far, *other, output_weight, output_weight, up_all, up_all, base, low,
        down_weight,
    )


def unfold_kernel(arrived, out):
    groups, _, folded, _ = arrived.shape
    piece = folded // 2
    for pair in range(groups // 2):
        halves = []
        for j in (2 * pair, 2 * pair + 1):
            value = arrived[j, 0].astype(jnp.float32)
            pieces = []
            for n in range(value.shape[1] // LANES):
                lanes = slice(n * LANES, (n + 1) * LANES)
                pieces += [value[:piece, lanes], value[piece:, lanes]]
            halves.append(jnp.concatenate(pieces, axis=1))
        out[pl.ds(pair * folded, folded), :] = jnp.concatenate(halves, axis=0).astype(out.dtype)


def unfold(arrived, slots):
    groups, _, folded, half_width = arrived.shape
    return pl.pallas_call(
        unfold_kernel,
        grid=(slots,),
        in_specs=[pl.BlockSpec((groups, 1, folded, half_width), lambda s: (0, s, 0, 0))],
        out_specs=pl.BlockSpec((groups * folded // 2, 2 * half_width), lambda s: (s, 0)),
        out_shape=jax.ShapeDtypeStruct(
            (slots * groups * folded // 2, 2 * half_width), jnp.bfloat16
        ),
        compiler_params=pltpu.CompilerParams(vmem_limit_bytes=16 * 2**20),
        name="unfold",
    )(arrived)


def body(
    attention_slot_outputs,
    output_gradient_rows,
    output_weight,
    down_weight,
    up_weight,
    assign,
    counts,
):
    groups = counts.shape[0]
    rows = assign.shape[0]
    rows_here = output_gradient_rows.shape[0] // ROW_TOKENS
    slot_cap = attention_slot_outputs.shape[0] // ROW_TOKENS
    width_here = output_gradient_rows.shape[1]
    rank = up_weight.shape[0]
    tp = lax.axis_size("tp")
    piece = ROW_TOKENS // groups
    own_group = lax.axis_index("group")
    group_ids = jnp.arange(groups, dtype=jnp.int32)
    onehot = (assign[:, None] == group_ids[None, :]).astype(jnp.int32)
    before = jnp.cumsum(onehot, axis=0) - onehot
    order_in = jnp.sum(before * onehot, axis=1)
    free_slots = jnp.sum(onehot * counts[None, :], axis=1)
    position = slot_cap - free_slots + order_in
    own_dest = lax.dynamic_slice_in_dim(assign, own_group * rows_here, rows_here)
    scale_factor = adapter_scale / math.sqrt(rows * ROW_TOKENS)

    spread = lax.all_to_all(
        output_gradient_rows.reshape(rows_here, groups, piece, width_here).transpose(1, 0, 2, 3),
        "group",
        split_axis=0,
        concat_axis=0,
        tiled=True,
    ).reshape(rows * piece, width_here)

    up_all = lax.all_gather(up_weight, "tp", axis=0)
    low_part = dot_minor(up_weight, output_gradient_rows)
    projected_part = lax.dot_general(
        down_weight, attention_slot_outputs, (((0,), (1,)), ((), ())),
        preferred_element_type=jnp.float32,
    )
    parts = lax.all_gather(jnp.concatenate([low_part, projected_part], axis=1), "tp", axis=0)
    sums = jnp.sum(parts, axis=0).astype(jnp.bfloat16)
    low = sums[:, : rows_here * ROW_TOKENS].reshape(rank, rows_here, ROW_TOKENS)
    projected = sums[:, rows_here * ROW_TOKENS :].reshape(rank, slot_cap, ROW_TOKENS)

    low_send = jnp.zeros((groups, rank, ROW_TOKENS), jnp.bfloat16)
    for r in range(rows_here):
        hit = own_dest[r] == group_ids
        low_send = jnp.where(hit[:, None, None], low[:, r][None], low_send)
    row_position = position.reshape(groups, rows_here)
    hit_row = assign.reshape(groups, rows_here) == own_group
    wanted = jnp.sum(jnp.where(hit_row, row_position, 0), axis=1)
    projected_send = jnp.zeros((groups, rank, ROW_TOKENS), jnp.bfloat16)
    for s in range(slot_cap):
        hit = wanted == s
        projected_send = jnp.where(hit[:, None, None], projected[:, s][None], projected_send)
    crossed = lax.all_to_all(
        jnp.concatenate([low_send, projected_send], axis=1),
        "group", split_axis=0, concat_axis=0, tiled=True,
    )
    slot_ids = jnp.arange(slot_cap, dtype=jnp.int32)
    slot_match = (hit_row[:, :, None] & (row_position[:, :, None] == slot_ids)).any(axis=1)
    slot_has = slot_match.any(axis=0)
    slot_source = jnp.sum(slot_match * group_ids[:, None], axis=0)
    low_slot = jnp.concatenate(
        [
            jnp.where(
                slot_has[s],
                lax.dynamic_index_in_dim(crossed, slot_source[s], 0, keepdims=False)[:rank],
                jnp.zeros((rank, ROW_TOKENS), jnp.bfloat16),
            )
            for s in range(slot_cap)
        ],
        axis=1,
    )
    projected_row = jnp.concatenate(
        [
            lax.dynamic_index_in_dim(crossed, own_dest[r], 0, keepdims=False)[rank:]
            for r in range(rows_here)
        ],
        axis=1,
    )
    down_part = jnp.dot(low_slot, attention_slot_outputs, preferred_element_type=jnp.float32)
    up_part = jnp.dot(projected_row, output_gradient_rows, preferred_element_type=jnp.float32)
    share = 2 * rank // groups
    grads = lax.all_to_all(
        jnp.concatenate([down_part, up_part], axis=0).reshape(groups, share, width_here),
        "group", split_axis=0, concat_axis=0, tiled=True,
    )
    grads = (scale_factor * jnp.sum(grads, axis=0)).astype(jnp.bfloat16)

    index = lax.axis_index("tp")
    chips = tp // 2
    y, core = index // 2, index % 2
    forward = [(2 * a + b, 2 * ((a + 1) % chips) + b) for a in range(chips) for b in range(2)]
    backward = [(2 * a + b, 2 * ((a - 1) % chips) + b) for a in range(chips) for b in range(2)]
    swap = [(i, i ^ 1) for i in range(tp)]
    half = spread.shape[0] // 2

    from_left = lax.ppermute(spread, "tp", forward)
    from_right = lax.ppermute(spread, "tp", backward)
    far = [
        lax.ppermute(from_left[:half], "tp", forward),
        lax.ppermute(from_right[half:], "tp", backward),
    ]
    blocks, owner = [], []
    for block, step in ((spread, 0), (from_left, chips - 1), (from_right, 1)):
        blocks += [block, lax.ppermute(block, "tp", swap)]
        pair = 2 * lax.rem(y + step, chips)
        owner += [pair + core, pair + 1 - core]
    base, low_own = early_products(jnp.stack(owner), blocks, output_weight, up_all)
    pair = 2 * lax.rem(y + 2, chips)
    placed = last_products(
        jnp.stack([pair + core, pair + 1 - core]),
        assign,
        position,
        far,
        [lax.ppermute(part, "tp", swap) for part in far],
        output_weight,
        up_all,
        base,
        low_own,
        down_weight,
        groups,
        slot_cap,
    )

    folded = (2 * piece, width_here // 2)
    placed = placed.at[:, slot_cap].set(jnp.broadcast_to(grads.reshape(folded), (groups,) + folded))
    arrived = lax.all_to_all(placed, "group", split_axis=0, concat_axis=0, tiled=True)
    attention_input_gradient = unfold(arrived, slot_cap)
    grads = arrived[:, slot_cap].reshape(2 * rank, width_here).astype(jnp.float32)
    return (attention_input_gradient, grads[:rank].T, grads[rank:])


def solution(mesh):
    in_specs = (
        P("group", "tp"),
        P("group", "tp"),
        P("tp", None),
        P("tp", None),
        P(None, "tp"),
        P(),
        P(),
    )
    out_specs = (P("group", "tp"), P("tp", None), P(None, "tp"))
    return jax.shard_map(body, mesh=mesh, in_specs=in_specs, out_specs=out_specs, check_vma=False)
```

time: 215 us -> 173 us (0.80)
  matrix products: 48.5 us -> 3.64 us
  waiting for transfers between devices: 52.6 us -> 10.3 us
  blocking collectives: 0 us -> 32.8 us
  Pallas kernels: 0 us -> 25.6 us
  starting transfers between devices: 45.6 us -> 31.7 us
  other arithmetic: 16.7 us -> 20.1 us
    dot_general x17 -> x1, matrix products: 46.3 us -> 0.36 us  [dot_minor(): lax.dot_general(left, right, CONTRACT_MINOR, preferred_element_type=jnp.f...]
    all_to_all x5 -> x1, waiting for transfers between devices: 39.3 us -> 0.01 us  [body(): lax.all_to_all(jnp.concatenate([down_part, up_part], axis=0).reshape(grou...]
    all_to_all x0 -> x1, blocking collectives: none -> 32.8 us  [body(): lax.all_to_all(placed, 'group', split_axis=0, concat_axis=0, tiled=True)]
    pallas_call x0 -> x3, Pallas kernels: none -> 25.6 us  [the longest x1 15.5 us: early_products(): pl.pallas_call(functools.partial(early_kernel, count), grid_spec=pltpu.Pr...]
    all_to_all x5 -> x1, starting transfers between devices: 26.4 us -> 7.18 us  [body(): lax.all_to_all(jnp.concatenate([down_part, up_part], axis=0).reshape(grou...]
    all_to_all x1, waiting for transfers between devices: 12.6 us -> 7.55 us  [body(): lax.all_to_all(output_gradient_rows.reshape(rows_here, groups, piece, wid...]
    all_to_all x1, starting transfers between devices: 4.23 us -> 8.86 us  [body(): lax.all_to_all(jnp.concatenate([low_send, projected_send], axis=1), 'grou...]
    select_n x2 -> x0, other arithmetic: 2.84 us -> none  [the longest x1 2.84 us: body(): placed = jnp.where(all_has[:, None, None], placed, jnp.zeros_like(placed))]
  transfers between devices with their start and end apart: 16 -> 14, of which waited for: 5 -> 3; matrix products, arithmetic and copies ran while one was open for 38% -> 17% of each run, Pallas kernels for 0% -> 14%
where the time goes in v2:
time: 173 us; the launch traced here: 172 us
  blocking collectives  32.8 us (19%)
  starting transfers between devices  31.7 us (18%)
  between operations  31.6 us (18%)
  Pallas kernels  25.6 us (15%)
  other arithmetic  20.1 us (12%)
  local copies, waits for them, and re-layouts  16.1 us (9%)
  waiting for transfers between devices  10.3 us (6%)
  matrix products  3.64 us (2%)
    all_to_all x1, blocking collectives, body(): lax.all_to_all(placed, 'group', split_axis=0, concat_axis=0, tiled=True)  32.8 us
    pallas_call x1, Pallas kernels, early_products(): pl.pallas_call(functools.partial(early_kernel, count), grid_spec=pltpu.Pr...  15.5 us
    all_to_all x1, starting transfers between devices, body(): lax.all_to_all(jnp.concatenate([low_send, projected_send], axis=1), 'grou...  8.86 us
    all_to_all x1, starting transfers between devices, body(): lax.all_to_all(output_gradient_rows.reshape(rows_here, groups, piece, wid...  7.96 us
    pallas_call x1, Pallas kernels, last_products(): pl.pallas_call(last_kernel, grid_spec=pltpu.PrefetchScalarGridSpec(num_sc...  7.8 us
    all_to_all x1, waiting for transfers between devices, body(): lax.all_to_all(output_gradient_rows.reshape(rows_here, groups, piece, wid...  7.55 us
    all_to_all x1, starting transfers between devices, body(): lax.all_to_all(jnp.concatenate([down_part, up_part], axis=0).reshape(grou...  7.18 us
    unnamed x5, other arithmetic  6.79 us
  transfers between devices with their start and end apart: 14, of which 3 were waited for; matrix products, arithmetic and copies ran while one was open for 17% of the time, Pallas kernels for 14%

profile of v2, /device:TPU:0, one launch (start us, length us, event | category | flops | bytes accessed | tf_op | source)
XLA Modules:
  0.0 171.7 jit_solution(4034069824796464242)
XLA Ops:
  7.2 1.3 copy-done
  8.6 1.5 fusion.30
  11.3 0.9 copy.39
  12.2 8.0 %all-to-all-start = ((bf16[16,3,8,1024]{3,2,1,0:T(8,128)(2,1)}), bf16[16,3,8,1024]{3,2,1,0:T(8,128)(2,1)S(1)}, u32[]{:S(2)}, u32[]{:S(2)}) async-start(bf16[16,3,8,1024]{3,2,1,0:T(8,128)(2,1)} %bitcast.91), calls=%async_computation | async-start | bytes 1572864 | tf_op jit(solution)/shard_map/all_to_all | solution.py:215
  23.5 1.2 iota_compare_fusion.4
  24.7 1.8 %iota_compare_fusion.2 = (pred[16]{0:T(512)(128)(4,1)}, pred[16]{0:T(512)(128)(4,1)}) fusion(s32[]{:T(128)} %bitcast.16, s32[]{:T(128)} %bitcast.15), kind=kLoop, calls=%fused_computation.56 | loop fusion | flops 32 | bytes 40 | tf_op jit(solution)/shard_map/eq | solution.py:236
  27.1 7.5 %all-to-all-done = bf16[16,3,8,1024]{3,2,1,0:T(8,128)(2,1)S(1)} async-done(((bf16[16,3,8,1024]{3,2,1,0:T(8,128)(2,1)}), bf16[16,3,8,1024]{3,2,1,0:T(8,128)(2,1)S(1)}, u32[]{:S(2)}, u32[]{:S(2)}) %all-to-all-start) | async-done | bytes 786464 | tf_op jit(solution)/shard_map/all_to_all | solution.py:215
  34.7 1.6 collective-permute-start
  36.2 1.7 collective-permute-start.2
  37.9 1.9 %all-gather.7.cloned.1.call-done = f32[512,1152]{1,0:T(8,128)} async-done(((f32[64,1152]{1,0:T(8,128)}), f32[512,1152]{1,0:T(8,128)}) %all-gather.7.cloned.1.call-update) | async-done | bytes 2359312 | tf_op jit(solution)/shard_map/all_gather | solution.py:229
  39.8 1.8 %reduce_sum.56 = bf16[64,1152]{1,0:T(8,128)(2,1)S(1)} reduce(f32[8,64,1152]{2,1,0:T(8,128)} %bitcast.101, f32[]{:T(128)} %constant.115.clone.1), dimensions={0}, to_apply=%region_4.5 | reduce | flops 516096 | bytes 2506756 | tf_op jit(solution)/shard_map/reduce_sum | solution.py:230
  44.6 8.9 %all-to-all-start.1 = ((bf16[16,128,128]{2,1,0:T(8,128)(2,1)}), bf16[16,128,128]{2,1,0:T(8,128)(2,1)}, u32[]{:S(2)}, u32[]{:S(2)}) async-start(bf16[16,128,128]{2,1,0:T(8,128)(2,1)} %pad_maximum_fusion), calls=%async_computation.1 | async-start | bytes 1048576 | tf_op jit(solution)/shard_map/all_to_all | solution.py:245
  55.1 1.8 %collective-permute-start.1 = (bf16[192,1024]{1,0:T(8,128)(2,1)}, bf16[192,1024]{1,0:T(8,128)(2,1)}, u32[]{:S(2)}, u32[]{:S(2)}) collective-permute-start(bf16[192,1024]{1,0:T(8,128)(2,1)} %slice.214), channel_id=1, source_target_pairs={{0,2},{1,3},{2,4},{3,5},{4,6},{5,7},{6,0},{7,1},{8,10},{9,11},{10,... | collective-permute-start | bytes 1179656 | tf_op jit(solution)/shard_map/ppermute | solution.py:291
  56.9 1.8 %slice.215 = bf16[192,1024]{1,0:T(8,128)(2,1)} slice(bf16[384,1024]{1,0:T(8,128)(2,1)} %collective-permute-done.2.refs_4_), slice={[192:384], [0:1024]} | slice | bytes 786432 | tf_op jit(solution)/shard_map/slice | solution.py:292
  58.7 1.4 collective-permute-start.3
  80.2 1.4 fusion.18
  81.6 1.3 fusion.16
  82.9 1.4 fusion.14
  84.2 1.4 fusion.12
  85.6 1.4 fusion.10
  87.0 1.4 fusion.8
  89.1 1.4 fusion
  91.7 7.2 %all-to-all-start.2 = ((f32[16,8,1024]{2,1,0:T(8,128)}), f32[16,8,1024]{2,1,0:T(8,128)}, u32[]{:S(2)}, u32[]{:S(2)}) async-start(f32[16,8,1024]{2,1,0:T(8,128)} %maximum_bitcast_fusion), calls=%async_computation.2 | async-start | bytes 1048576 | tf_op jit(solution)/shard_map/all_to_all | solution.py:274
  99.0 1.2 copy-done.1
  100.2 15.5 %early_products.1 = (f32[384,1024]{1,0:T(8,128)S(1)}, f32[384,64]{1,0:T(8,128)S(1)}) custom-call(s32[6]{0:T(128)S(1)} %stack.39.owner, bf16[384,1024]{1,0:T(8,128)(2,1)S(1)} %bitcast.99, bf16[384,1024]{1,0:T(8,128)(2,1)} %collective-permute-done.6.refs_1_, bf16[384,1024]{1,0:T(8,128)(2,1)S(1)} %collective-permute-done.refs_2_, ...), custom_call_target="tpu_custom_call" | custom-call | flops 4831838208 | bytes 20447232 | tf_op jit(solution)/shard_map/early_products/pallas_call | solution.py:55
  115.7 7.8 %last_products.1 = bf16[16,7,16,512]{3,2,1,0:T(8,128)(2,1)} custom-call(s32[2]{0:T(128)S(1)} %pad_add_fusion.owner, s32[48]{0:T(128)S(1)} %copy-done.3, s32[48]{0:T(128)S(1)} %subtract_add_fusion.place, bf16[192,1024]{1,0:T(8,128)(2,1)} %collective-permute-done.1.far_a, bf16[192,1024]{1,0:T(8,128)(2,1)} %collective-permute-done.3.far_b, ...), custom_call_target="tpu_custom_call" | custom-call | flops 1610612736 | bytes 8912896 | tf_op jit(solution)/shard_map/last_products/pallas_call | solution.py:122
  123.5 1.1 reduce_sum.59
  125.4 32.8 %all_to_all.20.arrived = bf16[16,7,16,512]{3,2,1,0:T(8,128)(2,1)S(1)} all-to-all(bf16[16,7,16,512]{3,2,1,0:T(8,128)(2,1)} %broadcast_dynamic-update-slice_fusion), channel_id=1, replica_groups=mesh['group'=16,'tp'=8] {'group'}, dimensions={0} | all-to-all | bytes 3670016 | tf_op jit(solution)/shard_map/all_to_all | solution.py:318
  158.2 0.8 fusion.23
  159.0 1.7 %slice.211 = f32[64,1024]{1,0:T(8,128)} reshape(f32[8,1,16,512]{3,2,1,0:T(8,128)} %get-tuple-element.24) | data formatting | bytes 524288 | tf_op jit(solution)/shard_map/slice | solution.py:321
  160.8 1.7 %slice.213 = f32[64,1024]{1,0:T(8,128)} reshape(f32[8,1,16,512]{3,2,1,0:T(8,128)} %get-tuple-element.23) | data formatting | bytes 524288 | tf_op jit(solution)/shard_map/slice | solution.py:321
  162.5 2.3 %unfold.1 = bf16[768,1024]{1,0:T(8,128)(2,1)} custom-call(bf16[16,7,16,512]{3,2,1,0:T(8,128)(2,1)S(1)} %all_to_all.20.arrived), custom_call_target="tpu_custom_call" | custom-call | tf_op jit(solution)/shard_map/unfold/pallas_call | solution.py:175
  (81 shorter events, 15.3 us)
Async XLA Ops:
  7.2 1.4 copy-start
  7.2 2.9 %copy-start.4 = (bf16[384,1024]{1,0:T(8,128)(2,1)S(1)}, bf16[384,1024]{1,0:T(8,128)(2,1)}, u32[]{:S(2)}) copy-start(bf16[384,1024]{1,0:T(8,128)(2,1)} %param.10) | copy-start | bytes 2359300
  7.2 2.9 %copy-start.5 = (bf16[64,1024]{1,0:T(8,128)(2,1)S(1)}, bf16[64,1024]{1,0:T(8,128)(2,1)}, u32[]{:S(2)}) copy-start(bf16[64,1024]{1,0:T(8,128)(2,1)} %param.13) | copy-start | bytes 393220
  7.2 32.6 %all-gather.7.cloned.1.call-start = ((), (), s32[]{:S(2)}) async-start(), calls=%async_computation.5 | async-start | bytes 2654208 | tf_op jit(solution)/shard_map/all_gather | solution.py:229
  11.2 9.7 %copy-start.3 = (s32[48]{0:T(128)S(1)}, s32[48]{0:T(128)}, u32[]{:S(2)}) copy-start(s32[48]{0:T(128)} %dest.1) | copy-start | bytes 580
  11.2 9.8 %copy-start.8 = (s32[16]{0:T(128)S(1)}, s32[16]{0:T(128)}, u32[]{:S(2)}) copy-start(s32[16]{0:T(128)} %param.15) | copy-start | bytes 196
  12.2 22.5 %all-to-all-start = ((bf16[16,3,8,1024]{3,2,1,0:T(8,128)(2,1)}), bf16[16,3,8,1024]{3,2,1,0:T(8,128)(2,1)S(1)}, u32[]{:S(2)}, u32[]{:S(2)}) async-start(bf16[16,3,8,1024]{3,2,1,0:T(8,128)(2,1)} %bitcast.91), calls=%async_computation | async-start | bytes 1572864 | tf_op jit(solution)/shard_map/all_to_all | solution.py:215
  20.2 78.8 %all-gather.5.cloned.1.call-start = ((), (), s32[]{:S(2)}) async-start(), calls=%async_computation.4 | async-start | bytes 1179648 | tf_op jit(solution)/shard_map/all_gather | solution.py:223
  34.7 19.7 %collective-permute-start = (bf16[384,1024]{1,0:T(8,128)(2,1)S(1)}, bf16[384,1024]{1,0:T(8,128)(2,1)S(1)}, u32[]{:S(2)}, u32[]{:S(2)}) collective-permute-start(bf16[384,1024]{1,0:T(8,128)(2,1)S(1)} %bitcast.96), channel_id=1, source_target_pairs={{0,2},{1,3},{2,4},{3,5},{4,6},{5,7},{6,0},{7,1},{8,10},{9,11},{10,... | collective-permute-start | bytes 2359304 | tf_op jit(solution)/shard_map/ppermute | solution.py:288
  36.2 20.7 %collective-permute-start.2 = (bf16[384,1024]{1,0:T(8,128)(2,1)S(1)}, bf16[384,1024]{1,0:T(8,128)(2,1)}, u32[]{:S(2)}, u32[]{:S(2)}) collective-permute-start(bf16[384,1024]{1,0:T(8,128)(2,1)S(1)} %bitcast.97), channel_id=1, source_target_pairs={{0,6},{1,7},{2,0},{3,1},{4,2},{5,3},{6,4},{7,5},{8,14},{9,15},{10,... | collective-permute-start | bytes 2359304 | tf_op jit(solution)/shard_map/ppermute | solution.py:289
  42.1 11.4 %copy-start.7 = (s32[16,3]{0,1:T(4,128)S(1)}, s32[16,3]{0,1:T(4,128)}, u32[]{:S(2)}) copy-start(s32[16,3]{0,1:T(4,128)} %copy.19) | copy-start | bytes 580
  44.6 27.8 %copy-start.6 = (bf16[1024,64]{0,1:T(8,128)(2,1)S(1)}, bf16[1024,64]{0,1:T(8,128)(2,1)}, u32[]{:S(2)}) copy-start(bf16[1024,64]{0,1:T(8,128)(2,1)} %param.12) | copy-start | bytes 393220
  44.6 35.6 %all-to-all-start.1 = ((bf16[16,128,128]{2,1,0:T(8,128)(2,1)}), bf16[16,128,128]{2,1,0:T(8,128)(2,1)}, u32[]{:S(2)}, u32[]{:S(2)}) async-start(bf16[16,128,128]{2,1,0:T(8,128)(2,1)} %pad_maximum_fusion), calls=%async_computation.1 | async-start | bytes 1048576 | tf_op jit(solution)/shard_map/all_to_all | solution.py:245
  55.1 24.5 %collective-permute-start.1 = (bf16[192,1024]{1,0:T(8,128)(2,1)}, bf16[192,1024]{1,0:T(8,128)(2,1)}, u32[]{:S(2)}, u32[]{:S(2)}) collective-permute-start(bf16[192,1024]{1,0:T(8,128)(2,1)} %slice.214), channel_id=1, source_target_pairs={{0,2},{1,3},{2,4},{3,5},{4,6},{5,7},{6,0},{7,1},{8,10},{9,11},{10,... | collective-permute-start | bytes 1179656 | tf_op jit(solution)/shard_map/ppermute | solution.py:291
  58.7 21.4 %collective-permute-start.3 = (bf16[192,1024]{1,0:T(8,128)(2,1)}, bf16[192,1024]{1,0:T(8,128)(2,1)}, u32[]{:S(2)}, u32[]{:S(2)}) collective-permute-start(bf16[192,1024]{1,0:T(8,128)(2,1)} %slice.215), channel_id=1, source_target_pairs={{0,6},{1,7},{2,0},{3,1},{4,2},{5,3},{6,4},{7,5},{8,14},{9,15},{10,... | collective-permute-start | bytes 1179656 | tf_op jit(solution)/shard_map/ppermute | solution.py:292
  79.0 19.9 %collective-permute-start.6 = (bf16[384,1024]{1,0:T(8,128)(2,1)S(1)}, bf16[384,1024]{1,0:T(8,128)(2,1)}, u32[]{:S(2)}, u32[]{:S(2)}) collective-permute-start(bf16[384,1024]{1,0:T(8,128)(2,1)S(1)} %bitcast.98), channel_id=1, source_target_pairs={{0,1},{1,0},{2,3},{3,2},{4,5},{5,4},{6,7},{7,6},{8,9},{9,8},{10,11... | collective-permute-start | bytes 2359304 | tf_op jit(solution)/shard_map/ppermute | solution.py:296
  79.0 19.9 %collective-permute-start.7 = (bf16[384,1024]{1,0:T(8,128)(2,1)S(1)}, bf16[384,1024]{1,0:T(8,128)(2,1)}, u32[]{:S(2)}, u32[]{:S(2)}) collective-permute-start(bf16[384,1024]{1,0:T(8,128)(2,1)S(1)} %collective-permute-done.refs_2_), channel_id=1, source_target_pairs={{0,1},{1,0},{2,3},{3,2},{4,5},{5,4},{6,7},{7,6},{8,9},{9,8},{10,11... | collective-permute-start | bytes 2359304 | tf_op jit(solution)/shard_map/ppermute | solution.py:296
  79.6 19.4 %collective-permute-start.8 = (bf16[384,1024]{1,0:T(8,128)(2,1)}, bf16[384,1024]{1,0:T(8,128)(2,1)}, u32[]{:S(2)}, u32[]{:S(2)}) collective-permute-start(bf16[384,1024]{1,0:T(8,128)(2,1)} %collective-permute-done.2.refs_4_), channel_id=1, source_target_pairs={{0,1},{1,0},{2,3},{3,2},{4,5},{5,4},{6,7},{7,6},{8,9},{9,8},{10,11... | collective-permute-start | bytes 2359304 | tf_op jit(solution)/shard_map/ppermute | solution.py:296
  79.6 36.1 %collective-permute-start.4 = (bf16[192,1024]{1,0:T(8,128)(2,1)}, bf16[192,1024]{1,0:T(8,128)(2,1)}, u32[]{:S(2)}, u32[]{:S(2)}) collective-permute-start(bf16[192,1024]{1,0:T(8,128)(2,1)} %collective-permute-done.1.far_a), channel_id=1, source_target_pairs={{0,1},{1,0},{2,3},{3,2},{4,5},{5,4},{6,7},{7,6},{8,9},{9,8},{10,11... | collective-permute-start | bytes 1179656 | tf_op jit(solution)/shard_map/ppermute | solution.py:306
  80.1 35.6 %collective-permute-start.5 = (bf16[192,1024]{1,0:T(8,128)(2,1)}, bf16[192,1024]{1,0:T(8,128)(2,1)}, u32[]{:S(2)}, u32[]{:S(2)}) collective-permute-start(bf16[192,1024]{1,0:T(8,128)(2,1)} %collective-permute-done.3.far_b), channel_id=1, source_target_pairs={{0,1},{1,0},{2,3},{3,2},{4,5},{5,4},{6,7},{7,6},{8,9},{9,8},{10,11... | collective-permute-start | bytes 1179656 | tf_op jit(solution)/shard_map/ppermute | solution.py:306
  91.7 31.8 %all-to-all-start.2 = ((f32[16,8,1024]{2,1,0:T(8,128)}), f32[16,8,1024]{2,1,0:T(8,128)}, u32[]{:S(2)}, u32[]{:S(2)}) async-start(f32[16,8,1024]{2,1,0:T(8,128)} %maximum_bitcast_fusion), calls=%async_computation.2 | async-start | bytes 1048576 | tf_op jit(solution)/shard_map/all_to_all | solution.py:274
  99.0 1.2 copy-start.1
  100.2 15.5 %copy-start.2 = (bf16[512,1024]{1,0:T(8,128)(2,1)S(1)}, bf16[512,1024]{1,0:T(8,128)(2,1)}, u32[]{:S(2)}) copy-start(bf16[512,1024]{1,0:T(8,128)(2,1)} %all-gather.5.cloned.1.call-done) | copy-start | bytes 3145732
Sparse Core Ops, SparseCore 0:
  11.4 28.4 all-gather.6
  41.5 26.7 all-gather.4

commit v3 on v0

v3 whole, which is shorter than its diff:
```python
import functools
import math

import jax
import jax.numpy as jnp
from jax import lax
from jax.experimental import pallas as pl
from jax.experimental.pallas import tpu as pltpu
from jax.sharding import PartitionSpec as P

ROW_TOKENS = 128
LANES = 128


adapter_scale = 2.0

HBM = pl.BlockSpec(memory_space=pl.ANY)
VMEM = pl.BlockSpec(memory_space=pltpu.VMEM)
SMEM = pl.BlockSpec(memory_space=pltpu.SMEM)


def dot_minor(left, right):
    return lax.dot_general(
        left, right, (((1,), (1,)), ((), ())), preferred_element_type=jnp.float32
    )


def block_kernel(sizes, ahead, first, owner, *refs):
    refs = list(refs)
    count, loads = len(sizes), owner.shape[0] - len(sizes)
    parts = [[refs.pop(0) for _ in range(size)] for size in sizes]
    weight, up = refs.pop(0), refs.pop(0)
    if not first:
        base_in, low_in = refs.pop(0), refs.pop(0)
    base, low = refs.pop(0), refs.pop(0)
    if loads:
        later_w, later_u = refs.pop(0), refs.pop(0)
    x, w, u, x_sem, w_sem, u_sem = refs
    width = x.shape[2]
    copies = []
    for k in range(count):
        each, start = [], 0
        for i, part in enumerate(parts[k]):
            rows = pl.ds(start, part.shape[0])
            each.append(pltpu.make_async_copy(part, x.at[k, rows], x_sem.at[k, i]))
            start += part.shape[0]
        columns = pl.ds(pl.multiple_of(owner[k] * width, width), width)
        each.append(pltpu.make_async_copy(weight.at[:, columns], w.at[k], w_sem.at[k]))
        each.append(pltpu.make_async_copy(up.at[owner[k]], u.at[k], u_sem.at[k]))
        copies.append(each)
    for k in range(loads):
        columns = pl.ds(pl.multiple_of(owner[count + k] * width, width), width)
        lanes = pl.ds(k * width, width)
        copies.append([
            pltpu.make_async_copy(weight.at[:, columns], later_w.at[:, lanes], w_sem.at[count + k]),
            pltpu.make_async_copy(up.at[owner[count + k]], later_u.at[:, lanes], u_sem.at[count + k]),
        ])
    for k in range(ahead):
        for copy in copies[k]:
            copy.start()
    for k in range(count):
        for copy in copies[k]:
            copy.wait()
        if k + ahead < len(copies):
            for copy in copies[k + ahead]:
                copy.start()
        value, value_low = dot_minor(x[k], w[k]), dot_minor(x[k], u[k])
        if k > 0:
            base[...] += value
            low[...] += value_low
        elif first:
            base[...] = value
            low[...] = value_low
        else:
            base[...] = base_in[...] + value
            low[...] = low_in[...] + value_low
    for k in range(count, count + loads):
        if k + ahead < len(copies) and k >= count:
            for copy in copies[k + ahead]:
                copy.start()
        for copy in copies[k]:
            copy.wait()


def block_products(owner, blocks, output_weight, up_all, base=None, low=None, name="block_products"):
    count = len(blocks)
    loads = owner.shape[0] - count
    tokens = sum(part.shape[0] for part in blocks[0])
    width = blocks[0][0].shape[1]
    out_width = output_weight.shape[0]
    rank = up_all.shape[1]
    first = base is None
    out_shape = [
        jax.ShapeDtypeStruct((tokens, out_width), jnp.float32),
        jax.ShapeDtypeStruct((tokens, rank), jnp.float32),
    ]
    if loads:
        out_shape += [
            jax.ShapeDtypeStruct((out_width, loads * width), jnp.bfloat16),
            jax.ShapeDtypeStruct((rank, loads * width), jnp.bfloat16),
        ]
    parts = [part for block in blocks for part in block]
    return pl.pallas_call(
        functools.partial(block_kernel, [len(block) for block in blocks], 2, first),
        in_specs=[SMEM] + [HBM] * (len(parts) + 2) + ([] if first else [VMEM] * 2),
        out_specs=[VMEM] * len(out_shape),
        out_shape=out_shape,
        scratch_shapes=[
            pltpu.VMEM((count, tokens, width), jnp.bfloat16),
            pltpu.VMEM((count, out_width, width), jnp.bfloat16),
            pltpu.VMEM((count, rank, width), jnp.bfloat16),
            pltpu.SemaphoreType.DMA((count, 2)),
            pltpu.SemaphoreType.DMA((count + loads,)),
            pltpu.SemaphoreType.DMA((count + loads,)),
        ],
        compiler_params=pltpu.CompilerParams(vmem_limit_bytes=30 * 2**20),
        cost_estimate=pl.CostEstimate(
            flops=2 * count * tokens * width * out_width,
            bytes_accessed=2 * width * (count * tokens + (count + loads) * out_width),
            transcendentals=0,
        ),
        name=name,
    )(owner, *parts, output_weight, up_all, *([] if first else [base, low]))


def last_kernel(
    dest, place, far_a, far_b, other_a, other_b, w, u, base, low, down, out, x, low_rounded, x_sem
):
    half, width = far_a.shape
    rows = dest.shape[0]
    piece = 2 * half // rows
    tile = 2 * LANES
    copies = []
    for i, part in enumerate((far_a, far_b, other_a, other_b)):
        lanes = pl.ds((i // 2) * width, width)
        rows_of = pl.ds((i % 2) * half, half)
        copies.append(pltpu.make_async_copy(part, x.at[rows_of, lanes], x_sem.at[i]))
    for copy in copies:
        copy.start()
    out[...] = jnp.zeros_like(out)
    for copy in copies:
        copy.wait()
    low_rounded[...] = (low[...] + dot_minor(x[...], u[...])).astype(jnp.bfloat16)
    for n in range(w.shape[0] // tile):
        span = slice(n * tile, (n + 1) * tile)
        total = base[:, span] + dot_minor(x[...], w[span])
        total += adapter_scale * dot_minor(low_rounded[...], down[span])
        for row in range(rows):
            mine = total[row * piece : (row + 1) * piece]
            folded = jnp.concatenate([mine[:, :LANES], mine[:, LANES:]], axis=0)
            out[dest[row], place[row], :, n * LANES : (n + 1) * LANES] = folded.astype(jnp.bfloat16)


def last_products(dest, place, far, other, w, u, base, low, down_weight, groups, slots):
    half, width = far[0].shape
    tokens = 2 * half
    out_width, rank = down_weight.shape
    piece = tokens // dest.shape[0]
    return pl.pallas_call(
        last_kernel,
        in_specs=[SMEM] * 2 + [HBM] * 4 + [VMEM] * 5,
        out_specs=VMEM,
        scratch_shapes=[
            pltpu.VMEM((tokens, 2 * width), jnp.bfloat16),
            pltpu.VMEM((tokens, rank), jnp.bfloat16),
            pltpu.SemaphoreType.DMA((4,)),
        ],
        out_shape=jax.ShapeDtypeStruct(
            (groups, slots + 1, 2 * piece, out_width // 2), jnp.bfloat16
        ),
        compiler_params=pltpu.CompilerParams(vmem_limit_bytes=20 * 2**20),
        cost_estimate=pl.CostEstimate(
            flops=4 * tokens * width * out_width,
            bytes_accessed=4 * width * (tokens + out_width) + 8 * tokens * out_width,
            transcendentals=0,
        ),
        name="last_products",
    )(dest, place, *far, *other, w, u, base, low, down_weight)


def gradient_kernel(source, has, dest, crossed, attention, gradient, out, low, projected):
    rank = crossed.shape[2]
    for s in range(source.shape[0]):
        value = crossed[source[s], 0].astype(jnp.float32) * has[s].astype(jnp.float32)
        low[:, s * ROW_TOKENS : (s + 1) * ROW_TOKENS] = value.astype(jnp.bfloat16)
    for r in range(dest.shape[0]):
        projected[:, r * ROW_TOKENS : (r + 1) * ROW_TOKENS] = crossed[dest[r], 1]
    out[:rank] = jnp.dot(low[...], attention[...], preferred_element_type=jnp.float32)
    out[rank:] = jnp.dot(projected[...], gradient[...], preferred_element_type=jnp.float32)


def gradient_products(source, has, dest, crossed, attention, gradient):
    rank = crossed.shape[2]
    slot_tokens, width = attention.shape
    row_tokens = gradient.shape[0]
    return pl.pallas_call(
        gradient_kernel,
        in_specs=[SMEM] * 3 + [VMEM] * 3,
        out_specs=VMEM,
        out_shape=jax.ShapeDtypeStruct((2 * rank, width), jnp.float32),
        scratch_shapes=[
            pltpu.VMEM((rank, slot_tokens), jnp.bfloat16),
            pltpu.VMEM((rank, row_tokens), jnp.bfloat16),
        ],
        compiler_params=pltpu.CompilerParams(vmem_limit_bytes=16 * 2**20),
        cost_estimate=pl.CostEstimate(
            flops=2 * rank * width * (slot_tokens + row_tokens),
            bytes_accessed=2 * width * (slot_tokens + row_tokens),
            transcendentals=0,
        ),
        name="gradient_products",
    )(source, has, dest, crossed, attention, gradient)


def unfold_kernel(slots, arrived, out, down_gradient, up_gradient):
    groups, _, folded, half_width = arrived.shape
    piece = folded // 2
    step = pl.program_id(0)

    @pl.when(step < slots)
    def _():
        for pair in range(groups // 2):
            halves = []
            for j in (2 * pair, 2 * pair + 1):
                value = arrived[j, 0].astype(jnp.float32)
                pieces = []
                for n in range(half_width // LANES):
                    lanes = slice(n * LANES, (n + 1) * LANES)
                    pieces += [value[:piece, lanes], value[piece:, lanes]]
                halves.append(jnp.concatenate(pieces, axis=1))
            out[pl.ds(pair * folded, folded), :] = jnp.concatenate(halves, axis=0).astype(out.dtype)

    @pl.when(step == slots)
    def _():
        values = []
        for j in range(groups):
            value = arrived[j, 0].astype(jnp.float32)
            values.append(jnp.concatenate([value[:piece], value[piece:]], axis=1))
        down_gradient[...] = jnp.concatenate(values[: groups // 2], axis=0).T
        up_gradient[...] = jnp.concatenate(values[groups // 2 :], axis=0)


def unfold(arrived, slots):
    groups, _, folded, half_width = arrived.shape
    piece, width = folded // 2, 2 * half_width
    rank = groups * piece // 2
    return pl.pallas_call(
        functools.partial(unfold_kernel, slots),
        grid=(slots + 1,),
        in_specs=[pl.BlockSpec((groups, 1, folded, half_width), lambda s: (0, s, 0, 0))],
        out_specs=[
            pl.BlockSpec((groups * piece, width), lambda s: (jnp.minimum(s, slots - 1), 0)),
            pl.BlockSpec((width, rank), lambda s: (0, 0)),
            pl.BlockSpec((rank, width), lambda s: (0, 0)),
        ],
        out_shape=[
            jax.ShapeDtypeStruct((slots * groups * piece, width), jnp.bfloat16),
            jax.ShapeDtypeStruct((width, rank), jnp.float32),
            jax.ShapeDtypeStruct((rank, width), jnp.float32),
        ],
        compiler_params=pltpu.CompilerParams(vmem_limit_bytes=16 * 2**20),
        name="unfold",
    )(arrived)


def body(
    attention_slot_outputs,
    output_gradient_rows,
    output_weight,
    down_weight,
    up_weight,
    assign,
    counts,
):
    groups = counts.shape[0]
    rows = assign.shape[0]
    rows_here = output_gradient_rows.shape[0] // ROW_TOKENS
    slot_cap = attention_slot_outputs.shape[0] // ROW_TOKENS
    width_here = output_gradient_rows.shape[1]
    rank = up_weight.shape[0]
    tp = lax.axis_size("tp")
    piece = ROW_TOKENS // groups
    own_group = lax.axis_index("group")
    group_ids = jnp.arange(groups, dtype=jnp.int32)
    onehot = (assign[:, None] == group_ids[None, :]).astype(jnp.int32)
    before = jnp.cumsum(onehot, axis=0) - onehot
    order_in = jnp.sum(before * onehot, axis=1)
    free_slots = jnp.sum(onehot * counts[None, :], axis=1)
    position = slot_cap - free_slots + order_in
    own_dest = lax.dynamic_slice_in_dim(assign, own_group * rows_here, rows_here)
    scale_factor = adapter_scale / math.sqrt(rows * ROW_TOKENS)

    index = lax.axis_index("tp")
    chips = tp // 2
    y, core = index // 2, index % 2

    def move(value, n):
        pairs = [(2 * a + b, 2 * ((a + n) % chips) + b) for a in range(chips) for b in range(2)]
        return lax.ppermute(value, "tp", pairs)

    def swap(value):
        return lax.ppermute(value, "tp", [(i, i ^ 1) for i in range(tp)])

    spread = lax.all_to_all(
        output_gradient_rows.reshape(rows_here, groups, piece, width_here).transpose(1, 0, 2, 3),
        "group",
        split_axis=0,
        concat_axis=0,
        tiled=True,
    ).reshape(rows * piece, width_here)

    up_all = lax.all_gather(up_weight, "tp", axis=0)
    low_part = dot_minor(up_weight, output_gradient_rows)
    projected_part = lax.dot_general(
        down_weight, attention_slot_outputs, (((0,), (1,)), ((), ())),
        preferred_element_type=jnp.float32,
    )
    parts = jnp.concatenate([low_part, projected_part], axis=1)
    parts = parts + swap(parts)
    share = lax.dynamic_slice_in_dim(parts, core * (rank // 2), rank // 2, axis=0)
    share = share + move(share, 1) + move(share, -1) + move(share, 2)
    share = share.astype(jnp.bfloat16)
    other = swap(share)
    sums = jnp.where(
        core == 0, jnp.concatenate([share, other]), jnp.concatenate([other, share])
    ).reshape(rank, rows_here + slot_cap, ROW_TOKENS)

    row_position = position.reshape(groups, rows_here)
    hit_row = assign.reshape(groups, rows_here) == own_group
    low_pick = jnp.sum(
        jnp.where(own_dest[None, :] == group_ids[:, None], jnp.arange(1, rows_here + 1), 0), axis=1
    )
    projected_pick = jnp.sum(jnp.where(hit_row, rows_here + 1 + row_position, 0), axis=1)
    pick = jnp.stack([low_pick, projected_pick], axis=1)[:, :, None, None]
    send = jnp.zeros((groups, 2, rank, ROW_TOKENS), jnp.bfloat16)
    for i in range(rows_here + slot_cap):
        send = jnp.where(pick == i + 1, sums[:, i][None, None], send)
    crossed = lax.all_to_all(send, "group", split_axis=0, concat_axis=0, tiled=True)
    slot_ids = jnp.arange(slot_cap, dtype=jnp.int32)
    slot_match = (hit_row[:, :, None] & (row_position[:, :, None] == slot_ids)).any(axis=1)
    slot_has = slot_match.any(axis=0).astype(jnp.int32)
    slot_source = jnp.sum(slot_match * group_ids[:, None], axis=0)

    half = spread.shape[0] // 2
    top, bottom = lax.optimization_barrier((spread[:half], spread[half:]))
    left_top, right_bottom = move(top, 1), move(bottom, -1)
    left_bottom, right_top = move(bottom, 1), move(top, -1)
    far = [move(left_top, 1), move(right_bottom, -1)]

    def owners(*steps):
        pairs = [2 * lax.rem(y + step, chips) for step in steps]
        return jnp.stack([owner for pair in pairs for owner in (pair + core, pair + 1 - core)])

    base, low_own = block_products(
        owners(0), [(spread,), (swap(spread),)], output_weight, up_all, name="own_products"
    )
    left, right = (left_top, left_bottom), (right_top, right_bottom)
    base, low_own, far_weight, far_up = block_products(
        owners(chips - 1, 1, 2),
        [left, tuple(swap(part) for part in left), right, tuple(swap(part) for part in right)],
        output_weight,
        up_all,
        base,
        low_own,
        name="side_products",
    )
    crossed, _ = lax.optimization_barrier((crossed, base))
    grads = gradient_products(
        slot_source, slot_has, own_dest, crossed, attention_slot_outputs, output_gradient_rows
    )
    share_rows = 2 * rank // groups
    grads = lax.all_to_all(
        grads.reshape(groups, share_rows, width_here), "group", split_axis=0, concat_axis=0,
        tiled=True,
    )
    grads = (scale_factor * jnp.sum(grads, axis=0)).astype(jnp.bfloat16)
    placed = last_products(
        assign, position, far, [swap(part) for part in far], far_weight, far_up, base, low_own,
        down_weight, groups, slot_cap,
    )

    folded = (2 * piece, width_here // 2)
    grads = jnp.concatenate([grads[:, : folded[1]], grads[:, folded[1] :]], axis=0)
    placed = placed.at[:, slot_cap].set(jnp.broadcast_to(grads, (groups,) + folded))
    arrived = lax.all_to_all(placed, "group", split_axis=0, concat_axis=0, tiled=True)
    return tuple(unfold(arrived, slot_cap))


def solution(mesh):
    in_specs = (
        P("group", "tp"),
        P("group", "tp"),
        P("tp", None),
        P("tp", None),
        P(None, "tp"),
        P(),
        P(),
    )
    out_specs = (P("group", "tp"), P("tp", None), P(None, "tp"))
    return jax.shard_map(body, mesh=mesh, in_specs=in_specs, out_specs=out_specs, check_vma=False)
```

time: 237 us -> 171 us (0.72)
  waiting for transfers between devices: 122 us -> 21.3 us
  matrix products: 31.8 us -> 3.65 us
  starting transfers between devices: 8.23 us -> 35.1 us
  local copies, waits for them, and re-layouts: 11.1 us -> 34.4 us
  Pallas kernels: 0 us -> 22.9 us
  blocking collectives: 41.2 us -> 32.5 us
    all_to_all x1 -> x3, waiting for transfers between devices: 62.5 us -> 0.01 us  [the longest x1 0.01 us: body(): lax.all_to_all(output_gradient_rows.reshape(rows_here, groups, piece, wid...]
    psum x1 -> x0, blocking collectives: 41.2 us -> none  [body(): lax.psum((lax.dot_general(slot_gradient, up_weight, (((1,), (1,)), ((), (...]
    psum x1 -> x0, waiting for transfers between devices: 39.5 us -> none  [body(): lax.psum((down_contribution, up_contribution), 'group')]
    all_to_all x0 -> x1, blocking collectives: none -> 32.5 us  [body(): lax.all_to_all(placed, 'group', split_axis=0, concat_axis=0, tiled=True)]
    dot_general x6 -> x2, matrix products: 31.8 us -> 3.65 us  [the longest x1 2.08 us: body(): lax.dot_general(down_weight, attention_slot_outputs, (((0,), (1,)), ((),...]
    pallas_call x0 -> x5, Pallas kernels: none -> 22.9 us  [the longest x2 13.2 us: block_products(): pl.pallas_call(functools.partial(block_kernel, [len(block) for block in b...]
    unnamed x14 -> x70, local copies, waits for them, and re-layouts: 3.37 us -> 25.5 us
    ppermute x0 -> x18, waiting for transfers between devices: none -> 20.6 us  [the longest x9 20.1 us: move(): return lax.ppermute(value, 'tp', pairs)]
  transfers between devices with their start and end apart: 3 -> 22, of which waited for: 3 -> 6; matrix products, arithmetic and copies ran while one was open for 14% -> 10% of each run, Pallas kernels for 0% -> 12%
where the time goes in v3:
time: 171 us; the launch traced here: 170 us
  starting transfers between devices  35.1 us (21%)
  local copies, waits for them, and re-layouts  34.4 us (20%)
  blocking collectives  32.5 us (19%)
  Pallas kernels  22.9 us (13%)
  waiting for transfers between devices  21.3 us (12%)
  between operations  14.6 us (9%)
  other arithmetic  5.16 us (3%)
  matrix products  3.65 us (2%)
    all_to_all x1, blocking collectives, body(): lax.all_to_all(placed, 'group', split_axis=0, concat_axis=0, tiled=True)  32.5 us
    unnamed x70, local copies, waits for them, and re-layouts  25.5 us
    ppermute x9, waiting for transfers between devices, move(): return lax.ppermute(value, 'tp', pairs)  20.1 us
    pallas_call x2, Pallas kernels, block_products(): pl.pallas_call(functools.partial(block_kernel, [len(block) for block in b...  13.2 us
    ppermute x9, starting transfers between devices, move(): return lax.ppermute(value, 'tp', pairs)  11.5 us
    all_to_all x1, starting transfers between devices, body(): lax.all_to_all(output_gradient_rows.reshape(rows_here, groups, piece, wid...  7.96 us
    all_to_all x1, starting transfers between devices, body(): lax.all_to_all(grads.reshape(groups, share_rows, width_here), 'group', sp...  7.16 us
    all_to_all x1, starting transfers between devices, body(): lax.all_to_all(send, 'group', split_axis=0, concat_axis=0, tiled=True)  7 us
  transfers between devices with their start and end apart: 22, of which 6 were waited for; matrix products, arithmetic and copies ran while one was open for 10% of the time, Pallas kernels for 12%

profile of v3, /device:TPU:0, one launch (start us, length us, event | category | flops | bytes accessed | tf_op | source)
XLA Modules:
  0.0 169.6 jit_solution(12529214763700693555)
XLA Ops:
  7.9 1.6 fusion.9
  9.5 2.1 %fusion.10 = f32[64,768]{1,0:T(8,128)S(1)} fusion(bf16[1024,64]{0,1:T(8,128)(2,1)} %param.12, bf16[768,1024]{1,0:T(8,128)(2,1)} %attention.1), kind=kOutput, calls=%fused_computation.51 | convolution fusion | flops 100663296 | bytes 1900544 | tf_op jit(solution)/shard_map/dot_general | solution.py:314
  12.7 8.0 %all-to-all-start = ((bf16[16,3,8,1024]{3,2,1,0:T(8,128)(2,1)}), bf16[16,3,8,1024]{3,2,1,0:T(8,128)(2,1)S(1)}, u32[]{:S(2)}, u32[]{:S(2)}) async-start(bf16[16,3,8,1024]{3,2,1,0:T(8,128)(2,1)} %bitcast.40), calls=%async_computation | async-start | bytes 1572864 | tf_op jit(solution)/shard_map/all_to_all | solution.py:304
  21.6 1.6 collective-permute-start.14
  23.2 1.7 collective-permute-start.15
  24.9 2.0 %collective-permute-start.16 = (f32[32,1152]{1,0:T(8,128)S(1)}, f32[32,1152]{1,0:T(8,128)S(1)}, u32[]{:S(2)}, u32[]{:S(2)}) collective-permute-start(f32[32,1152]{1,0:T(8,128)S(1)} %fusion.1), channel_id=1, source_target_pairs={{0,4},{1,5},{2,6},{3,7},{4,0},{5,1},{6,2},{7,3},{8,12},{9,13},{10,... | collective-permute-start | bytes 442376 | tf_op jit(solution)/shard_map/ppermute | solution.py:299
  33.2 3.2 %collective-permute-done.16 = f32[32,1152]{1,0:T(8,128)S(1)} collective-permute-done((f32[32,1152]{1,0:T(8,128)S(1)}, f32[32,1152]{1,0:T(8,128)S(1)}, u32[]{:S(2)}, u32[]{:S(2)}) %collective-permute-start.16) | collective-permute-done | bytes 147488 | tf_op jit(solution)/shard_map/ppermute | solution.py:299
  39.1 1.1 collective-permute-start.2
  40.2 1.1 collective-permute-start
  41.3 2.2 %collective-permute-start.9 = (bf16[192,1024]{1,0:T(8,128)(2,1)S(1)}, bf16[192,1024]{1,0:T(8,128)(2,1)}, u32[]{:S(2)}, u32[]{:S(2)}) collective-permute-start(bf16[192,1024]{1,0:T(8,128)(2,1)S(1)} %bitcast.50), channel_id=1, source_target_pairs={{0,6},{1,7},{2,0},{3,1},{4,2},{5,3},{6,4},{7,5},{8,14},{9,15},{10,... | collective-permute-start | bytes 1179656 | tf_op jit(solution)/shard_map/ppermute | solution.py:299
  43.5 7.6 %collective-permute-done.2.refs_5_ = bf16[192,1024]{1,0:T(8,128)(2,1)S(1)} collective-permute-done((bf16[192,1024]{1,0:T(8,128)(2,1)S(1)}, bf16[192,1024]{1,0:T(8,128)(2,1)S(1)}, u32[]{:S(2)}, u32[]{:S(2)}) %collective-permute-start.2) | collective-permute-done | bytes 393248 | tf_op jit(solution)/shard_map/ppermute | solution.py:299
  51.2 2.3 %collective-permute-done.refs_0_ = bf16[192,1024]{1,0:T(8,128)(2,1)S(1)} collective-permute-done((bf16[192,1024]{1,0:T(8,128)(2,1)S(1)}, bf16[192,1024]{1,0:T(8,128)(2,1)S(1)}, u32[]{:S(2)}, u32[]{:S(2)}) %collective-permute-start) | collective-permute-done | bytes 393248 | tf_op jit(solution)/shard_map/ppermute | solution.py:299
  53.5 5.6 %collective-permute-done.9.refs_4_ = bf16[192,1024]{1,0:T(8,128)(2,1)} collective-permute-done((bf16[192,1024]{1,0:T(8,128)(2,1)S(1)}, bf16[192,1024]{1,0:T(8,128)(2,1)}, u32[]{:S(2)}, u32[]{:S(2)}) %collective-permute-start.9) | collective-permute-done | bytes 393248 | tf_op jit(solution)/shard_map/ppermute | solution.py:299
  59.7 1.4 collective-permute-done.6.refs_1_
  61.1 1.2 collective-permute-start.3
  63.6 1.9 %select_select_fusion = bf16[16,2,64,128]{3,2,1,0:T(8,128)(2,1)} fusion(pred[16,2]{1,0:T(8,128)(4,1)} %copy.62, pred[16,2]{1,0:T(8,128)(4,1)} %copy.61, pred[16,2]{1,0:T(8,128)(4,1)} %copy.60, pred[16,2]{1,0:T(8,128)(4,1)} %copy.59, pred[16,2]{1,0:T(8,128)(4,1)} %copy.58, pred[16,2]{1,0:T(8,128)(4,1)} %copy.57, pred[16,2]{1,0:T(8,128)(4,1)} %copy.56, ...), kind=kLoop, calls=%fused_computation.1 | loop fusion | flops 2359296 | bytes 672032 | tf_op jit(solution)/shard_map/jit(_where)/select_n | solution.py:337
  65.5 7.0 %all-to-all-start.1 = ((bf16[16,2,64,128]{3,2,1,0:T(8,128)(2,1)}), bf16[16,2,64,128]{3,2,1,0:T(8,128)(2,1)}, u32[]{:S(2)}, u32[]{:S(2)}) async-start(bf16[16,2,64,128]{3,2,1,0:T(8,128)(2,1)} %select_select_fusion), calls=%async_computation.1 | async-start | bytes 1048576 | tf_op jit(solution)/shard_map/all_to_all | solution.py:338
  72.6 1.1 convert_element_type.14.has
  73.7 5.8 %copy-done = bf16[1024,8192]{1,0:T(8,128)(2,1)S(1)} copy-done((bf16[1024,8192]{1,0:T(8,128)(2,1)S(1)}, bf16[1024,8192]{1,0:T(8,128)(2,1)}, u32[]{:S(2)}) %copy-start) | copy-done | bytes 16777240
  79.5 1.2 copy-done.3
  80.7 4.4 %own_products.1 = (f32[384,1024]{1,0:T(8,128)S(1)}, f32[384,64]{1,0:T(8,128)S(1)}) custom-call(s32[2]{0:T(128)S(1)} %pad_add_fusion.1.owner, bf16[384,1024]{1,0:T(8,128)(2,1)S(1)} %bitcast.43, bf16[384,1024]{1,0:T(8,128)(2,1)S(1)} %collective-permute-done.12.refs_1_, bf16[1024,8192]{1,0:T(8,128)(2,1)S(1)} %copy-done, bf16[8,64,1024]{2,1,0:T(8,128)(2,1)S(1)} %bitcast.45), custom_call_target="tpu_custom_call" | custom-call | flops 1610612736 | bytes 5767168 | tf_op jit(solution)/shard_map/own_products/pallas_call | solution.py:103
  87.8 8.8 %side_products.1 = (f32[384,1024]{1,0:T(8,128)S(1)}, f32[384,64]{1,0:T(8,128)S(1)}, bf16[1024,2048]{1,0:T(8,128)(2,1)S(1)}, bf16[64,2048]{1,0:T(8,128)(2,1)S(1)}) custom-call(s32[6]{0:T(128)S(1)} %stack.45.owner, bf16[192,1024]{1,0:T(8,128)(2,1)S(1)} %copy-done.15, bf16[192,1024]{1,0:T(8,128)(2,1)} %collective-permute-done.6.refs_1_, ...), custom_call_target="tpu_custom_call" | custom-call | flops 3221225472 | bytes 15728640 | tf_op jit(solution)/shard_map/side_products/pallas_call | solution.py:103
  96.6 2.0 %copy-done.4 = bf16[1024,2048]{1,0:T(8,128)(2,1)} copy-done((bf16[1024,2048]{1,0:T(8,128)(2,1)}, bf16[1024,2048]{1,0:T(8,128)(2,1)S(1)}, u32[]{:S(2)}) %copy-start.4) | copy-done | bytes 4194328
  98.6 1.1 copy-done.6
  102.3 2.4 %gradient_products.1 = f32[128,1024]{1,0:T(8,128)} custom-call(s32[6]{0:T(128)S(1)} %copy-done.25, s32[6]{0:T(128)S(1)} %copy-done.26, s32[3]{0:T(128)S(1)} %copy-done.24, bf16[16,2,64,128]{3,2,1,0:T(8,128)(2,1)} %all-to-all-done.1.crossed, bf16[768,1024]{1,0:T(8,128)(2,1)S(1)} %copy-done.2, bf16[384,1024]{1,0:T(8,128)(2,1)S(1)} %copy-done.1), custom_call_target="tpu_custom_call" | custom-call | flops 150994944 | bytes 2359296 | tf_op jit(solution)/shard_map/gradient_products/pallas_call | solution.py:196
  104.7 7.2 %all-to-all-start.2 = ((f32[16,8,1024]{2,1,0:T(8,128)}), f32[16,8,1024]{2,1,0:T(8,128)S(1)}, u32[]{:S(2)}, u32[]{:S(2)}) async-start(f32[16,8,1024]{2,1,0:T(8,128)} %bitcast.16), calls=%async_computation.2 | async-start | bytes 1048576 | tf_op jit(solution)/shard_map/all_to_all | solution.py:372
  111.9 1.1 copy.51.down
  114.5 2.2 %copy-done.5 = bf16[1024,2048]{1,0:T(8,128)(2,1)S(1)} copy-done((bf16[1024,2048]{1,0:T(8,128)(2,1)S(1)}, bf16[1024,2048]{1,0:T(8,128)(2,1)}, u32[]{:S(2)}) %copy-start.5) | copy-done | bytes 4194328
  116.7 1.4 copy-done.7
  121.9 4.1 %last_products.1 = bf16[16,7,16,512]{3,2,1,0:T(8,128)(2,1)S(1)} custom-call(s32[48]{0:T(128)S(1)} %copy-done.22, s32[48]{0:T(128)S(1)} %subtract_add_fusion.place, bf16[192,1024]{1,0:T(8,128)(2,1)S(1)} %collective-permute-done.1.far_a, bf16[192,1024]{1,0:T(8,128)(2,1)} %collective-permute-done.3.far_b, bf16[192,1024]{1,0:T(8,128)(2,1)S(1)} %copy-done.9, ...), custom_call_target="tpu_custom_call" | custom-call | flops 1610612736 | bytes 8912896 | tf_op jit(solution)/shard_map/last_products/pallas_call | solution.py:159
  126.1 32.5 %all_to_all.20.arrived = bf16[16,7,16,512]{3,2,1,0:T(8,128)(2,1)S(1)} all-to-all(bf16[16,7,16,512]{3,2,1,0:T(8,128)(2,1)S(1)} %broadcast_dynamic-update-slice_fusion), channel_id=1, replica_groups=mesh['group'=16,'tp'=8] {'group'}, dimensions={0} | all-to-all | bytes 3670016 | tf_op jit(solution)/shard_map/all_to_all | solution.py:385
  158.6 3.2 %unfold.1 = (bf16[768,1024]{1,0:T(8,128)(2,1)}, f32[1024,64]{1,0:T(8,128)S(1)}, f32[64,1024]{1,0:T(8,128)}) custom-call(bf16[16,7,16,512]{3,2,1,0:T(8,128)(2,1)S(1)} %all_to_all.20.arrived), custom_call_target="tpu_custom_call" | custom-call | tf_op jit(solution)/shard_map/unfold/pallas_call | solution.py:247
  (135 shorter events, 25.2 us)
Async XLA Ops:
  7.2 66.6 %all-gather.3.cloned.1.call-start = ((), (), s32[]{:S(2)}) async-start(), calls=%async_computation.4 | async-start | bytes 1179648 | tf_op jit(solution)/shard_map/all_gather | solution.py:312
  11.6 9.3 %copy-start.31 = (s32[16]{0:T(128)S(1)}, s32[16]{0:T(128)}, u32[]{:S(2)}) copy-start(s32[16]{0:T(128)} %param.15) | copy-start | bytes 196
  11.6 9.9 %collective-permute-start.13 = (f32[64,1152]{1,0:T(8,128)S(1)}, f32[64,1152]{1,0:T(8,128)S(1)}, u32[]{:S(2)}, u32[]{:S(2)}) collective-permute-start(f32[64,1152]{1,0:T(8,128)S(1)} %pad_maximum_fusion), channel_id=1, source_target_pairs={{0,1},{1,0},{2,3},{3,2},{4,5},{5,4},{6,7},{7,6},{8,9},{9,8},{10,11... | collective-permute-start | bytes 884744 | tf_op jit(solution)/shard_map/ppermute | solution.py:302
  12.7 26.1 %all-to-all-start = ((bf16[16,3,8,1024]{3,2,1,0:T(8,128)(2,1)}), bf16[16,3,8,1024]{3,2,1,0:T(8,128)(2,1)S(1)}, u32[]{:S(2)}, u32[]{:S(2)}) async-start(bf16[16,3,8,1024]{3,2,1,0:T(8,128)(2,1)} %bitcast.40), calls=%async_computation | async-start | bytes 1572864 | tf_op jit(solution)/shard_map/all_to_all | solution.py:304
  20.8 18.3 %copy-start.23 = (s32[3]{0:T(128)}, s32[3]{0:T(128)S(1)}, u32[]{:S(2)}) copy-start(s32[3]{0:T(128)S(1)} %dynamic_slice.6.dest) | copy-start | bytes 40
  21.6 11.6 %collective-permute-start.14 = (f32[32,1152]{1,0:T(8,128)S(1)}, f32[32,1152]{1,0:T(8,128)S(1)}, u32[]{:S(2)}, u32[]{:S(2)}) collective-permute-start(f32[32,1152]{1,0:T(8,128)S(1)} %fusion.1), channel_id=1, source_target_pairs={{0,2},{1,3},{2,4},{3,5},{4,6},{5,7},{6,0},{7,1},{8,10},{9,11},{10,... | collective-permute-start | bytes 442376 | tf_op jit(solution)/shard_map/ppermute | solution.py:299
  23.2 10.0 %collective-permute-start.15 = (f32[32,1152]{1,0:T(8,128)S(1)}, f32[32,1152]{1,0:T(8,128)S(1)}, u32[]{:S(2)}, u32[]{:S(2)}) collective-permute-start(f32[32,1152]{1,0:T(8,128)S(1)} %fusion.1), channel_id=1, source_target_pairs={{0,6},{1,7},{2,0},{3,1},{4,2},{5,3},{6,4},{7,5},{8,14},{9,15},{10,... | collective-permute-start | bytes 442376 | tf_op jit(solution)/shard_map/ppermute | solution.py:299
  24.9 11.5 %collective-permute-start.16 = (f32[32,1152]{1,0:T(8,128)S(1)}, f32[32,1152]{1,0:T(8,128)S(1)}, u32[]{:S(2)}, u32[]{:S(2)}) collective-permute-start(f32[32,1152]{1,0:T(8,128)S(1)} %fusion.1), channel_id=1, source_target_pairs={{0,4},{1,5},{2,6},{3,7},{4,0},{5,1},{6,2},{7,3},{8,12},{9,13},{10,... | collective-permute-start | bytes 442376 | tf_op jit(solution)/shard_map/ppermute | solution.py:299
  36.4 1.3 collective-permute-start.17
  38.8 12.3 %copy-start.29 = (bf16[64,1,128]{2,1,0:T(2,128)(2,1)S(1)}, bf16[64,1,128]{2,1,0:T(2,128)(2,1)}, u32[]{:S(2)}) copy-start(bf16[64,1,128]{2,1,0:T(2,128)(2,1)} %get-tuple-element.54) | copy-start | bytes 49156
  38.8 12.4 %copy-start.30 = (bf16[64,1,128]{2,1,0:T(2,128)(2,1)S(1)}, bf16[64,1,128]{2,1,0:T(2,128)(2,1)}, u32[]{:S(2)}) copy-start(bf16[64,1,128]{2,1,0:T(2,128)(2,1)} %get-tuple-element.55) | copy-start | bytes 49156
  38.8 12.4 %copy-start.27 = (bf16[64,1,128]{2,1,0:T(2,128)(2,1)S(1)}, bf16[64,1,128]{2,1,0:T(2,128)(2,1)}, u32[]{:S(2)}) copy-start(bf16[64,1,128]{2,1,0:T(2,128)(2,1)} %get-tuple-element.52) | copy-start | bytes 49156
  38.8 12.4 %copy-start.28 = (bf16[64,1,128]{2,1,0:T(2,128)(2,1)S(1)}, bf16[64,1,128]{2,1,0:T(2,128)(2,1)}, u32[]{:S(2)}) copy-start(bf16[64,1,128]{2,1,0:T(2,128)(2,1)} %get-tuple-element.53) | copy-start | bytes 49156
  38.8 24.3 %collective-permute-start.12 = (bf16[384,1024]{1,0:T(8,128)(2,1)S(1)}, bf16[384,1024]{1,0:T(8,128)(2,1)S(1)}, u32[]{:S(2)}, u32[]{:S(2)}) collective-permute-start(bf16[384,1024]{1,0:T(8,128)(2,1)S(1)} %bitcast.42), channel_id=1, source_target_pairs={{0,1},{1,0},{2,3},{3,2},{4,5},{5,4},{6,7},{7,6},{8,9},{9,8},{10,11... | collective-permute-start | bytes 2359304 | tf_op jit(solution)/shard_map/ppermute | solution.py:302
  39.1 12.0 %collective-permute-start.2 = (bf16[192,1024]{1,0:T(8,128)(2,1)S(1)}, bf16[192,1024]{1,0:T(8,128)(2,1)S(1)}, u32[]{:S(2)}, u32[]{:S(2)}) collective-permute-start(bf16[192,1024]{1,0:T(8,128)(2,1)S(1)} %bitcast.47), channel_id=1, source_target_pairs={{0,6},{1,7},{2,0},{3,1},{4,2},{5,3},{6,4},{7,5},{8,14},{9,15},{10,... | collective-permute-start | bytes 1179656 | tf_op jit(solution)/shard_map/ppermute | solution.py:299
  40.2 13.3 %collective-permute-start = (bf16[192,1024]{1,0:T(8,128)(2,1)S(1)}, bf16[192,1024]{1,0:T(8,128)(2,1)S(1)}, u32[]{:S(2)}, u32[]{:S(2)}) collective-permute-start(bf16[192,1024]{1,0:T(8,128)(2,1)S(1)} %bitcast.49), channel_id=1, source_target_pairs={{0,2},{1,3},{2,4},{3,5},{4,6},{5,7},{6,0},{7,1},{8,10},{9,11},{10,... | collective-permute-start | bytes 1179656 | tf_op jit(solution)/shard_map/ppermute | solution.py:299
  41.3 17.8 %collective-permute-start.9 = (bf16[192,1024]{1,0:T(8,128)(2,1)S(1)}, bf16[192,1024]{1,0:T(8,128)(2,1)}, u32[]{:S(2)}, u32[]{:S(2)}) collective-permute-start(bf16[192,1024]{1,0:T(8,128)(2,1)S(1)} %bitcast.50), channel_id=1, source_target_pairs={{0,6},{1,7},{2,0},{3,1},{4,2},{5,3},{6,4},{7,5},{8,14},{9,15},{10,... | collective-permute-start | bytes 1179656 | tf_op jit(solution)/shard_map/ppermute | solution.py:299
  43.5 17.6 %collective-permute-start.6 = (bf16[192,1024]{1,0:T(8,128)(2,1)S(1)}, bf16[192,1024]{1,0:T(8,128)(2,1)}, u32[]{:S(2)}, u32[]{:S(2)}) collective-permute-start(bf16[192,1024]{1,0:T(8,128)(2,1)S(1)} %bitcast.48), channel_id=1, source_target_pairs={{0,2},{1,3},{2,4},{3,5},{4,6},{5,7},{6,0},{7,1},{8,10},{9,11},{10,... | collective-permute-start | bytes 1179656 | tf_op jit(solution)/shard_map/ppermute | solution.py:299
  51.1 34.1 %copy-start.12 = (bf16[192,1024]{1,0:T(8,128)(2,1)}, bf16[192,1024]{1,0:T(8,128)(2,1)S(1)}, u32[]{:S(2)}) copy-start(bf16[192,1024]{1,0:T(8,128)(2,1)S(1)} %collective-permute-done.2.refs_5_) | copy-start | bytes 1179652
  51.1 11.2 %collective-permute-start.11 = (bf16[192,1024]{1,0:T(8,128)(2,1)S(1)}, bf16[192,1024]{1,0:T(8,128)(2,1)S(1)}, u32[]{:S(2)}, u32[]{:S(2)}) collective-permute-start(bf16[192,1024]{1,0:T(8,128)(2,1)S(1)} %collective-permute-done.2.refs_5_), channel_id=1, source_target_pairs={{0,1},{1,0},{2,3},{3,2},{4,5},{5,4},{6,7},{7,6},{8,9},{9,8},{10,11... | collective-permute-start | bytes 1179656 | tf_op jit(solution)/shard_map/ppermute | solution.py:302
  53.5 31.7 %copy-start.14 = (bf16[192,1024]{1,0:T(8,128)(2,1)}, bf16[192,1024]{1,0:T(8,128)(2,1)S(1)}, u32[]{:S(2)}) copy-start(bf16[192,1024]{1,0:T(8,128)(2,1)S(1)} %collective-permute-done.refs_0_) | copy-start | bytes 1179652
  53.5 32.3 %collective-permute-start.7 = (bf16[192,1024]{1,0:T(8,128)(2,1)S(1)}, bf16[192,1024]{1,0:T(8,128)(2,1)}, u32[]{:S(2)}, u32[]{:S(2)}) collective-permute-start(bf16[192,1024]{1,0:T(8,128)(2,1)S(1)} %collective-permute-done.refs_0_), channel_id=1, source_target_pairs={{0,1},{1,0},{2,3},{3,2},{4,5},{5,4},{6,7},{7,6},{8,9},{9,8},{10,11... | collective-permute-start | bytes 1179656 | tf_op jit(solution)/shard_map/ppermute | solution.py:302
  59.1 26.1 %collective-permute-start.1 = (bf16[192,1024]{1,0:T(8,128)(2,1)S(1)}, bf16[192,1024]{1,0:T(8,128)(2,1)S(1)}, u32[]{:S(2)}, u32[]{:S(2)}) collective-permute-start(bf16[192,1024]{1,0:T(8,128)(2,1)S(1)} %collective-permute-done.refs_0_), channel_id=1, source_target_pairs={{0,2},{1,3},{2,4},{3,5},{4,6},{5,7},{6,0},{7,1},{8,10},{9,11},{10,... | collective-permute-start | bytes 1179656 | tf_op jit(solution)/shard_map/ppermute | solution.py:299
  61.1 24.2 %collective-permute-start.3 = (bf16[192,1024]{1,0:T(8,128)(2,1)S(1)}, bf16[192,1024]{1,0:T(8,128)(2,1)}, u32[]{:S(2)}, u32[]{:S(2)}) collective-permute-start(bf16[192,1024]{1,0:T(8,128)(2,1)S(1)} %collective-permute-done.2.refs_5_), channel_id=1, source_target_pairs={{0,6},{1,7},{2,0},{3,1},{4,2},{5,3},{6,4},{7,5},{8,14},{9,15},{10,... | collective-permute-start | bytes 1179656 | tf_op jit(solution)/shard_map/ppermute | solution.py:299
  63.1 22.7 %collective-permute-start.10 = (bf16[192,1024]{1,0:T(8,128)(2,1)}, bf16[192,1024]{1,0:T(8,128)(2,1)}, u32[]{:S(2)}, u32[]{:S(2)}) collective-permute-start(bf16[192,1024]{1,0:T(8,128)(2,1)} %collective-permute-done.9.refs_4_), channel_id=1, source_target_pairs={{0,1},{1,0},{2,3},{3,2},{4,5},{5,4},{6,7},{7,6},{8,9},{9,8},{10,11... | collective-permute-start | bytes 1179656 | tf_op jit(solution)/shard_map/ppermute | solution.py:302
  63.1 22.7 %collective-permute-start.8 = (bf16[192,1024]{1,0:T(8,128)(2,1)}, bf16[192,1024]{1,0:T(8,128)(2,1)}, u32[]{:S(2)}, u32[]{:S(2)}) collective-permute-start(bf16[192,1024]{1,0:T(8,128)(2,1)} %collective-permute-done.6.refs_1_), channel_id=1, source_target_pairs={{0,1},{1,0},{2,3},{3,2},{4,5},{5,4},{6,7},{7,6},{8,9},{9,8},{10,11... | collective-permute-start | bytes 1179656 | tf_op jit(solution)/shard_map/ppermute | solution.py:302
  65.5 35.6 %all-to-all-start.1 = ((bf16[16,2,64,128]{3,2,1,0:T(8,128)(2,1)}), bf16[16,2,64,128]{3,2,1,0:T(8,128)(2,1)}, u32[]{:S(2)}, u32[]{:S(2)}) async-start(bf16[16,2,64,128]{3,2,1,0:T(8,128)(2,1)} %select_select_fusion), calls=%async_computation.1 | async-start | bytes 1048576 | tf_op jit(solution)/shard_map/all_to_all | solution.py:338
  85.2 27.7 %collective-permute-start.4 = (bf16[192,1024]{1,0:T(8,128)(2,1)S(1)}, bf16[192,1024]{1,0:T(8,128)(2,1)S(1)}, u32[]{:S(2)}, u32[]{:S(2)}) collective-permute-start(bf16[192,1024]{1,0:T(8,128)(2,1)S(1)} %collective-permute-done.1.far_a), channel_id=1, source_target_pairs={{0,1},{1,0},{2,3},{3,2},{4,5},{5,4},{6,7},{7,6},{8,9},{9,8},{10,11... | collective-permute-start | bytes 1179656 | tf_op jit(solution)/shard_map/ppermute | solution.py:302
  85.3 28.4 %collective-permute-start.5 = (bf16[192,1024]{1,0:T(8,128)(2,1)}, bf16[192,1024]{1,0:T(8,128)(2,1)S(1)}, u32[]{:S(2)}, u32[]{:S(2)}) collective-permute-start(bf16[192,1024]{1,0:T(8,128)(2,1)} %collective-permute-done.3.far_b), channel_id=1, source_target_pairs={{0,1},{1,0},{2,3},{3,2},{4,5},{5,4},{6,7},{7,6},{8,9},{9,8},{10,11... | collective-permute-start | bytes 1179656 | tf_op jit(solution)/shard_map/ppermute | solution.py:302
  87.8 13.3 %copy-start.2 = (bf16[768,1024]{1,0:T(8,128)(2,1)S(1)}, bf16[768,1024]{1,0:T(8,128)(2,1)}, u32[]{:S(2)}) copy-start(bf16[768,1024]{1,0:T(8,128)(2,1)} %attention.1) | copy-start | bytes 4718596
  87.8 13.3 %copy-start.24 = (s32[3]{0:T(128)S(1)}, s32[3]{0:T(128)}, u32[]{:S(2)}) copy-start(s32[3]{0:T(128)} %copy-done.23) | copy-start | bytes 40
  104.7 21.3 %all-to-all-start.2 = ((f32[16,8,1024]{2,1,0:T(8,128)}), f32[16,8,1024]{2,1,0:T(8,128)S(1)}, u32[]{:S(2)}, u32[]{:S(2)}) async-start(f32[16,8,1024]{2,1,0:T(8,128)} %bitcast.16), calls=%async_computation.2 | async-start | bytes 1048576 | tf_op jit(solution)/shard_map/all_to_all | solution.py:372
  (22 other events, 43.1 us)
Sparse Core Ops, SparseCore 0:
  9.7 28.5 all-gather.2

commit v4 on v3

v4 whole, which is shorter than its diff:
```python
import functools
import math

import jax
import jax.numpy as jnp
from jax import lax
from jax.experimental import pallas as pl
from jax.experimental.pallas import tpu as pltpu
from jax.sharding import PartitionSpec as P

ROW_TOKENS = 128
LANES = 128


adapter_scale = 2.0

HBM = pl.BlockSpec(memory_space=pltpu.HBM)
VMEM = pl.BlockSpec(memory_space=pltpu.VMEM)
SMEM = pl.BlockSpec(memory_space=pltpu.SMEM)


def dot_minor(left, right):
    return lax.dot_general(
        left, right, (((1,), (1,)), ((), ())), preferred_element_type=jnp.float32
    )


def block_kernel(table, first, index, *refs):
    refs = list(refs)
    count = len(table)
    blocks = [refs.pop(0) for _ in range(count)]
    weight, up = refs.pop(0), refs.pop(0)
    if not first:
        base_in, low_in = refs.pop(0), refs.pop(0)
    base, low, x, x_sem = refs
    width = x.shape[2]
    copies = [pltpu.make_async_copy(blocks[k], x.at[k], x_sem.at[k]) for k in range(count)]
    for copy in copies[:2]:
        copy.start()
    for k in range(count):
        copies[k].wait()
        if k + 2 < count:
            copies[k + 2].start()
        owner = index[table[k]]
        columns = pl.ds(pl.multiple_of(owner * width, width), width)
        value, value_low = dot_minor(x[k], weight[:, columns]), dot_minor(x[k], up[owner])
        if k > 0:
            base[...] += value
            low[...] += value_low
        elif first:
            base[...] = value
            low[...] = value_low
        else:
            base[...] = base_in[...] + value
            low[...] = low_in[...] + value_low


def block_products(index, table, blocks, output_weight, up_all, base=None, low=None, name=""):
    count = len(blocks)
    tokens, width = blocks[0].shape
    out_width = output_weight.shape[0]
    rank = up_all.shape[1]
    first = base is None
    return pl.pallas_call(
        functools.partial(block_kernel, table, first),
        in_specs=[SMEM] + [HBM] * count + [VMEM] * (2 if first else 4),
        out_specs=[VMEM] * 2,
        out_shape=[
            jax.ShapeDtypeStruct((tokens, out_width), jnp.float32),
            jax.ShapeDtypeStruct((tokens, rank), jnp.float32),
        ],
        scratch_shapes=[
            pltpu.VMEM((count, tokens, width), jnp.bfloat16),
            pltpu.SemaphoreType.DMA((count,)),
        ],
        compiler_params=pltpu.CompilerParams(vmem_limit_bytes=32 * 2**20),
        cost_estimate=pl.CostEstimate(
            flops=2 * count * tokens * width * out_width,
            bytes_accessed=2 * width * count * tokens,
            transcendentals=0,
        ),
        name=name,
    )(index, *blocks, output_weight, up_all, *([] if first else [base, low]))


def last_kernel(
    rows, table, index, far_a, far_b, other_a, other_b, weight, up, base, low, down, out, x,
    low_rounded, x_sem,
):
    half, width = far_a.shape
    piece = 2 * half // rows
    tile = 2 * LANES
    copies = []
    for i, part in enumerate((far_a, far_b, other_a, other_b)):
        rows_of = pl.ds((i % 2) * half, half)
        copies.append(pltpu.make_async_copy(part, x.at[i // 2, rows_of], x_sem.at[i]))
    for copy in copies:
        copy.start()
    out[...] = jnp.zeros_like(out)
    for copy in copies:
        copy.wait()
    owners = [index[i] for i in table]
    total = low[...]
    for k, owner in enumerate(owners):
        total += dot_minor(x[k], up[owner])
    low_rounded[...] = total.astype(jnp.bfloat16)
    for n in range(weight.shape[0] // tile):
        span = slice(n * tile, (n + 1) * tile)
        total = base[:, span]
        for k, owner in enumerate(owners):
            columns = pl.ds(pl.multiple_of(owner * width, width), width)
            total += dot_minor(x[k], weight[span, columns])
        total += adapter_scale * jnp.dot(
            low_rounded[...], down[:, span], preferred_element_type=jnp.float32
        )
        for row in range(rows):
            mine = total[row * piece : (row + 1) * piece]
            folded = jnp.concatenate([mine[:, :LANES], mine[:, LANES:]], axis=0)
            out[index[row], index[rows + row], :, n * LANES : (n + 1) * LANES] = folded.astype(
                jnp.bfloat16
            )


def last_products(rows, index, table, far, other, weight, up, base, low, down, groups, slots):
    half, width = far[0].shape
    tokens = 2 * half
    rank, out_width = down.shape
    piece = tokens // rows
    return pl.pallas_call(
        functools.partial(last_kernel, rows, table),
        in_specs=[SMEM] + [HBM] * 4 + [VMEM] * 5,
        out_specs=VMEM,
        scratch_shapes=[
            pltpu.VMEM((2, tokens, width), jnp.bfloat16),
            pltpu.VMEM((tokens, rank), jnp.bfloat16),
            pltpu.SemaphoreType.DMA((4,)),
        ],
        out_shape=jax.ShapeDtypeStruct(
            (groups, slots + 1, 2 * piece, out_width // 2), jnp.bfloat16
        ),
        compiler_params=pltpu.CompilerParams(vmem_limit_bytes=32 * 2**20),
        cost_estimate=pl.CostEstimate(
            flops=4 * tokens * width * out_width,
            bytes_accessed=4 * width * tokens + 8 * tokens * out_width,
            transcendentals=0,
        ),
        name="last_products",
    )(index, *far, *other, weight, up, base, low, down)


def send_kernel(groups, core_at, pick_at, index, share, other, out):
    half = share.shape[0]
    core = index[core_at]
    for group in range(groups):
        for kind in range(2):
            pick = index[pick_at + 2 * group + kind]
            lanes = pl.ds(pl.multiple_of(jnp.maximum(pick, 0) * ROW_TOKENS, ROW_TOKENS), ROW_TOKENS)
            keep = (pick >= 0).astype(jnp.float32)
            for owner, part in ((core, share), (1 - core, other)):
                value = part[:, lanes].astype(jnp.float32) * keep
                rows = pl.ds(pl.multiple_of(owner * half, half), half)
                out[group, kind, rows] = value.astype(jnp.bfloat16)


def rank_sums_to_send(index, core_at, pick_at, groups, share, other):
    rank = 2 * share.shape[0]
    return pl.pallas_call(
        functools.partial(send_kernel, groups, core_at, pick_at),
        in_specs=[SMEM, VMEM, VMEM],
        out_specs=VMEM,
        out_shape=jax.ShapeDtypeStruct((groups, 2, rank, ROW_TOKENS), jnp.bfloat16),
        compiler_params=pltpu.CompilerParams(vmem_limit_bytes=16 * 2**20),
        cost_estimate=pl.CostEstimate(
            flops=groups * rank * ROW_TOKENS, bytes_accessed=4 * groups * rank * ROW_TOKENS,
            transcendentals=0,
        ),
        name="rank_sums_to_send",
    )(index, share, other)


def gradient_kernel(
    source_at, dest_at, index, crossed, attention, gradient, out, low, projected, tokens, more, sem
):
    rank = crossed.shape[2]
    copies = [
        pltpu.make_async_copy(attention, tokens, sem.at[0]),
        pltpu.make_async_copy(gradient, more, sem.at[1]),
    ]
    for copy in copies:
        copy.start()
    for s in range(tokens.shape[0] // ROW_TOKENS):
        source = index[source_at + s]
        keep = (source >= 0).astype(jnp.float32)
        value = crossed[jnp.maximum(source, 0), 0].astype(jnp.float32) * keep
        low[:, s * ROW_TOKENS : (s + 1) * ROW_TOKENS] = value.astype(jnp.bfloat16)
    for r in range(more.shape[0] // ROW_TOKENS):
        projected[:, r * ROW_TOKENS : (r + 1) * ROW_TOKENS] = crossed[index[dest_at + r], 1]
    copies[0].wait()
    out[:rank] = jnp.dot(low[...], tokens[...], preferred_element_type=jnp.float32)
    copies[1].wait()
    out[rank:] = jnp.dot(projected[...], more[...], preferred_element_type=jnp.float32)


def gradient_products(index, source_at, dest_at, crossed, attention, gradient):
    rank = crossed.shape[2]
    slot_tokens, width = attention.shape
    row_tokens = gradient.shape[0]
    return pl.pallas_call(
        functools.partial(gradient_kernel, source_at, dest_at),
        in_specs=[SMEM, VMEM, HBM, HBM],
        out_specs=VMEM,
        out_shape=jax.ShapeDtypeStruct((2 * rank, width), jnp.float32),
        scratch_shapes=[
            pltpu.VMEM((rank, slot_tokens), jnp.bfloat16),
            pltpu.VMEM((rank, row_tokens), jnp.bfloat16),
            pltpu.VMEM(attention.shape, jnp.bfloat16),
            pltpu.VMEM(gradient.shape, jnp.bfloat16),
            pltpu.SemaphoreType.DMA((2,)),
        ],
        compiler_params=pltpu.CompilerParams(vmem_limit_bytes=16 * 2**20),
        cost_estimate=pl.CostEstimate(
            flops=2 * rank * width * (slot_tokens + row_tokens),
            bytes_accessed=2 * width * (slot_tokens + row_tokens),
            transcendentals=0,
        ),
        name="gradient_products",
    )(index, crossed, attention, gradient)


def unfold_kernel(slots, arrived, out, down_gradient, up_gradient):
    groups, _, folded, half_width = arrived.shape
    piece = folded // 2
    step = pl.program_id(0)

    @pl.when(step < slots)
    def _():
        for pair in range(groups // 2):
            halves = []
            for j in (2 * pair, 2 * pair + 1):
                value = arrived[j, 0].astype(jnp.float32)
                pieces = []
                for n in range(half_width // LANES):
                    lanes = slice(n * LANES, (n + 1) * LANES)
                    pieces += [value[:piece, lanes], value[piece:, lanes]]
                halves.append(jnp.concatenate(pieces, axis=1))
            out[pl.ds(pair * folded, folded), :] = jnp.concatenate(halves, axis=0).astype(out.dtype)

    @pl.when(step == slots)
    def _():
        values = []
        for j in range(groups):
            value = arrived[j, 0].astype(jnp.float32)
            values.append(jnp.concatenate([value[:piece], value[piece:]], axis=1))
        down_gradient[...] = jnp.concatenate(values[: groups // 2], axis=0)
        up_gradient[...] = jnp.concatenate(values[groups // 2 :], axis=0)


def unfold(arrived, slots):
    groups, _, folded, half_width = arrived.shape
    piece, width = folded // 2, 2 * half_width
    rank = groups * piece // 2
    return pl.pallas_call(
        functools.partial(unfold_kernel, slots),
        grid=(slots + 1,),
        in_specs=[pl.BlockSpec((groups, 1, folded, half_width), lambda s: (0, s, 0, 0))],
        out_specs=[
            pl.BlockSpec((groups * piece, width), lambda s: (jnp.minimum(s, slots - 1), 0)),
            pl.BlockSpec((rank, width), lambda s: (0, 0)),
            pl.BlockSpec((rank, width), lambda s: (0, 0)),
        ],
        out_shape=[
            jax.ShapeDtypeStruct((slots * groups * piece, width), jnp.bfloat16),
            jax.ShapeDtypeStruct((rank, width), jnp.float32),
            jax.ShapeDtypeStruct((rank, width), jnp.float32),
        ],
        compiler_params=pltpu.CompilerParams(vmem_limit_bytes=16 * 2**20),
        name="unfold",
    )(arrived)


def body(
    attention_slot_outputs,
    output_gradient_rows,
    output_weight,
    down_weight,
    up_weight,
    assign,
    counts,
):
    groups = counts.shape[0]
    rows = assign.shape[0]
    rows_here = output_gradient_rows.shape[0] // ROW_TOKENS
    slot_cap = attention_slot_outputs.shape[0] // ROW_TOKENS
    width_here = output_gradient_rows.shape[1]
    rank = up_weight.shape[0]
    tp = lax.axis_size("tp")
    piece = ROW_TOKENS // groups
    own_group = lax.axis_index("group")
    group_ids = jnp.arange(groups, dtype=jnp.int32)
    onehot = (assign[:, None] == group_ids[None, :]).astype(jnp.int32)
    before = jnp.cumsum(onehot, axis=0) - onehot
    order_in = jnp.sum(before * onehot, axis=1)
    free_slots = jnp.sum(onehot * counts[None, :], axis=1)
    position = slot_cap - free_slots + order_in
    own_dest = lax.dynamic_slice_in_dim(assign, own_group * rows_here, rows_here)
    scale_factor = adapter_scale / math.sqrt(rows * ROW_TOKENS)

    index = lax.axis_index("tp")
    chips = tp // 2
    y, core = index // 2, index % 2

    def move(value, n):
        pairs = [(2 * a + b, 2 * ((a + n) % chips) + b) for a in range(chips) for b in range(2)]
        return lax.ppermute(value, "tp", pairs)

    def swap(value):
        return lax.ppermute(value, "tp", [(i, i ^ 1) for i in range(tp)])

    spread = lax.all_to_all(
        output_gradient_rows.reshape(rows_here, groups, piece, width_here).transpose(1, 0, 2, 3),
        "group",
        split_axis=0,
        concat_axis=0,
        tiled=True,
    ).reshape(rows * piece, width_here)

    slot_ids = jnp.arange(slot_cap, dtype=jnp.int32)
    row_ids = jnp.arange(rows_here, dtype=jnp.int32)
    row_position = position.reshape(groups, rows_here)
    hit_row = assign.reshape(groups, rows_here) == own_group
    low_pick = jnp.max(jnp.where(own_dest[None, :] == group_ids[:, None], row_ids, -1), axis=1)
    projected_pick = jnp.max(jnp.where(hit_row, rows_here + row_position, -1), axis=1)
    slot_match = hit_row[:, :, None] & (row_position[:, :, None] == slot_ids)
    slot_source = jnp.max(jnp.where(slot_match, group_ids[:, None, None], -1), axis=(0, 1))
    owners = []
    for step in (0, chips - 1, 1, 2):
        pair = 2 * lax.rem(y + step, chips)
        owners += [pair + core, pair + 1 - core]
    pieces = [
        assign, position, jnp.stack([low_pick, projected_pick], axis=1).reshape(-1), slot_source,
        own_dest, jnp.stack(owners + [core]).astype(jnp.int32),
    ]
    at = [0]
    for part in pieces:
        at.append(at[-1] + part.shape[0])
    _, _, pick_at, source_at, dest_at, owner_at, end = at
    table = jnp.concatenate(pieces)

    up_all = lax.all_gather(up_weight, "tp", axis=0)
    low_part = dot_minor(up_weight, output_gradient_rows)
    projected_part = lax.dot_general(
        down_weight, attention_slot_outputs, (((0,), (1,)), ((), ())),
        preferred_element_type=jnp.float32,
    )
    parts = jnp.concatenate([low_part, projected_part], axis=1)
    parts = parts + swap(parts)
    share = lax.dynamic_slice_in_dim(parts, core * (rank // 2), rank // 2, axis=0)
    share = share + move(share, 1) + move(share, -1) + move(share, 2)
    share = share.astype(jnp.bfloat16)

    crossed = lax.all_to_all(
        rank_sums_to_send(table, end - 1, pick_at, groups, share, swap(share)),
        "group", split_axis=0, concat_axis=0, tiled=True,
    )

    half = spread.shape[0] // 2
    left, right = move(spread, 1), move(spread, -1)
    far = [move(left[:half], 1), move(right[half:], -1)]
    base, low_own = block_products(
        table, [owner_at, owner_at + 1], [spread, swap(spread)], output_weight, up_all,
        name="own_products",
    )
    swapped = [swap(left), swap(right)]
    crossed, _ = lax.optimization_barrier((crossed, (base, swapped)))
    base, low_own = block_products(
        table, [owner_at + i for i in range(2, 6)], [left, swapped[0], right, swapped[1]],
        output_weight, up_all, base, low_own, name="side_products",
    )
    grads = gradient_products(
        table, source_at, dest_at, crossed, attention_slot_outputs, output_gradient_rows
    )
    share_rows = 2 * rank // groups
    grads = lax.all_to_all(
        grads.reshape(groups, share_rows, width_here), "group", split_axis=0, concat_axis=0,
        tiled=True,
    )
    grads = (scale_factor * jnp.sum(grads, axis=0)).astype(jnp.bfloat16)
    placed = last_products(
        rows, table, [owner_at + 6, owner_at + 7], far, [swap(part) for part in far],
        output_weight, up_all, base, low_own, down_weight.T, groups, slot_cap,
    )

    folded = (2 * piece, width_here // 2)
    grads = jnp.concatenate([grads[:, : folded[1]], grads[:, folded[1] :]], axis=0)
    placed = placed.at[:, slot_cap].set(jnp.broadcast_to(grads, (groups,) + folded))
    arrived = lax.all_to_all(placed, "group", split_axis=0, concat_axis=0, tiled=True)
    attention_gradient, down_gradient, up_gradient = unfold(arrived, slot_cap)
    return attention_gradient, down_gradient.T, up_gradient


def solution(mesh):
    in_specs = (
        P("group", "tp"),
        P("group", "tp"),
        P("tp", None),
        P("tp", None),
        P(None, "tp"),
        P(),
        P(),
    )
    out_specs = (P("group", "tp"), P("tp", None), P(None, "tp"))
    return jax.shard_map(body, mesh=mesh, in_specs=in_specs, out_specs=out_specs, check_vma=False)
```

time: 171 us -> 169 us (0.988)
  local copies, waits for them, and re-layouts: 34.4 us -> 19.1 us
  waiting for transfers between devices: 21.3 us -> 33.6 us
  Pallas kernels: 22.9 us -> 30.8 us
  starting transfers between devices: 35.1 us -> 28.2 us
    unnamed x70 -> x28, local copies, waits for them, and re-layouts: 25.5 us -> 12.7 us
    all_to_all x1, waiting for transfers between devices: 0.01 us -> 9.22 us  [body(): lax.all_to_all(output_gradient_rows.reshape(rows_here, groups, piece, wid...]
    pallas_call x4 -> x5, Pallas kernels: 19.7 us -> 27.6 us  [the longest x2 15.4 us: block_products(): pl.pallas_call(functools.partial(block_kernel, table, first), in_specs=[S...]
    eq x9 -> x0, local copies, waits for them, and re-layouts: 5.49 us -> none  [body(): send = jnp.where(pick == i + 1, sums[:, i][None, None], send)]
    ppermute x9 -> x7, waiting for transfers between devices: 20.1 us -> 23.7 us  [move(): return lax.ppermute(value, 'tp', pairs)]
    all_to_all x1, starting transfers between devices: 7 us -> 4.24 us  [body(): lax.all_to_all(rank_sums_to_send(table, end - 1, pick_at, groups, share,...]
    slice x2, local copies, waits for them, and re-layouts: 0.91 us -> 3.53 us  [body(): far = [move(left[:half], 1), move(right[half:], -1)]]
    all_to_all x1, starting transfers between devices: 7.16 us -> 4.69 us  [body(): lax.all_to_all(grads.reshape(groups, share_rows, width_here), 'group', sp...]
  transfers between devices with their start and end apart: 22 -> 18, of which waited for: 6 -> 6; matrix products, arithmetic and copies ran while one was open for 10% -> 7% of each run, Pallas kernels for 12% -> 17%
where the time goes in v4:
time: 169 us; the launch traced here: 167 us
  waiting for transfers between devices  33.6 us (20%)
  blocking collectives  32.5 us (19%)
  Pallas kernels  30.8 us (18%)
  starting transfers between devices  28.2 us (17%)
  local copies, waits for them, and re-layouts  19.1 us (11%)
  between operations  14.3 us (8%)
  other arithmetic  6.16 us (4%)
  matrix products  2.5 us (1%)
    all_to_all x1, blocking collectives, body(): lax.all_to_all(placed, 'group', split_axis=0, concat_axis=0, tiled=True)  32.5 us
    ppermute x7, waiting for transfers between devices, move(): return lax.ppermute(value, 'tp', pairs)  23.7 us
    pallas_call x2, Pallas kernels, block_products(): pl.pallas_call(functools.partial(block_kernel, table, first), in_specs=[S...  15.4 us
    unnamed x28, local copies, waits for them, and re-layouts  12.7 us
    ppermute x7, starting transfers between devices, move(): return lax.ppermute(value, 'tp', pairs)  10.5 us
    pallas_call x1, Pallas kernels, last_products(): pl.pallas_call(functools.partial(last_kernel, rows, table), in_specs=[SME...  9.59 us
    all_to_all x1, waiting for transfers between devices, body(): lax.all_to_all(output_gradient_rows.reshape(rows_here, groups, piece, wid...  9.22 us
    all_to_all x1, starting transfers between devices, body(): lax.all_to_all(output_gradient_rows.reshape(rows_here, groups, piece, wid...  8.09 us
  transfers between devices with their start and end apart: 18, of which 6 were waited for; matrix products, arithmetic and copies ran while one was open for 7% of the time, Pallas kernels for 17%

profile of v4, /device:TPU:0, one launch (start us, length us, event | category | flops | bytes accessed | tf_op | source)
XLA Modules:
  0.0 167.3 jit_solution(1139920088377142991)
XLA Ops:
  7.2 2.2 %copy.19 = bf16[3,16,8,1024]{3,2,0,1:T(8,128)(2,1)} copy(bf16[3,16,8,1024]{3,2,1,0:T(8,128)(2,1)} %bitcast.27) | data formatting | bytes 1572864 | tf_op jit(solution)/shard_map/reshape | solution.py:320
  9.4 8.1 %all-to-all-start = ((bf16[16,3,8,1024]{3,2,1,0:T(8,128)(2,1)}), bf16[16,3,8,1024]{3,2,1,0:T(8,128)(2,1)S(1)}, u32[]{:S(2)}, u32[]{:S(2)}) async-start(bf16[16,3,8,1024]{3,2,1,0:T(8,128)(2,1)} %bitcast.34), calls=%async_computation | async-start | bytes 1572864 | tf_op jit(solution)/shard_map/all_to_all | solution.py:319
  18.9 1.9 %fusion.5 = f32[64,384]{1,0:T(8,128)} fusion(bf16[64,1024]{1,0:T(8,128)(2,1)} %param.13, bf16[384,1024]{1,0:T(8,128)(2,1)S(1)} %copy-done.3), kind=kOutput, calls=%fused_computation.24 | convolution fusion | flops 50331648 | bytes 1015808 | tf_op jit(solution)/shard_map/dot_general | solution.py:23
  20.8 1.6 pad_maximum_fusion
  22.8 9.2 %all-to-all-done = bf16[16,3,8,1024]{3,2,1,0:T(8,128)(2,1)S(1)} async-done(((bf16[16,3,8,1024]{3,2,1,0:T(8,128)(2,1)}), bf16[16,3,8,1024]{3,2,1,0:T(8,128)(2,1)S(1)}, u32[]{:S(2)}, u32[]{:S(2)}) %all-to-all-start) | async-done | bytes 786464 | tf_op jit(solution)/shard_map/all_to_all | solution.py:319
  32.0 1.6 collective-permute-start
  33.6 1.7 collective-permute-start.2
  35.6 1.6 fusion.1
  37.6 2.9 %collective-permute-start.11 = (f32[32,1152]{1,0:T(8,128)}, f32[32,1152]{1,0:T(8,128)}, u32[]{:S(2)}, u32[]{:S(2)}) collective-permute-start(f32[32,1152]{1,0:T(8,128)} %fusion.1), channel_id=1, source_target_pairs={{0,6},{1,7},{2,0},{3,1},{4,2},{5,3},{6,4},{7,5},{8,14},{9,15},{10,... | collective-permute-start | bytes 442376 | tf_op jit(solution)/shard_map/ppermute | solution.py:314
  41.5 16.8 %collective-permute-done.10 = f32[32,1152]{1,0:T(8,128)S(1)} collective-permute-done((f32[32,1152]{1,0:T(8,128)}, f32[32,1152]{1,0:T(8,128)S(1)}, u32[]{:S(2)}, u32[]{:S(2)}) %collective-permute-start.10) | collective-permute-done | bytes 147488 | tf_op jit(solution)/shard_map/ppermute | solution.py:314
  58.9 0.8 collective-permute-done.11
  59.8 3.0 %collective-permute-done.12 = f32[32,1152]{1,0:T(8,128)} collective-permute-done((f32[32,1152]{1,0:T(8,128)}, f32[32,1152]{1,0:T(8,128)}, u32[]{:S(2)}, u32[]{:S(2)}) %collective-permute-start.12) | collective-permute-done | bytes 147488 | tf_op jit(solution)/shard_map/ppermute | solution.py:314
  62.7 1.1 add_convert_fusion.share
  64.0 1.8 %slice.41 = bf16[192,1024]{1,0:T(8,128)(2,1)} slice(bf16[384,1024]{1,0:T(8,128)(2,1)} %collective-permute-done.refs_0_), slice={[0:192], [0:1024]} | slice | bytes 786432 | tf_op jit(solution)/shard_map/slice | solution.py:368
  66.5 1.8 %slice.42 = bf16[192,1024]{1,0:T(8,128)(2,1)} slice(bf16[384,1024]{1,0:T(8,128)(2,1)} %collective-permute-done.2.refs_2_), slice={[192:384], [0:1024]} | slice | bytes 786432 | tf_op jit(solution)/shard_map/slice | solution.py:368
  68.3 2.5 %collective-permute-start.3 = (bf16[192,1024]{1,0:T(8,128)(2,1)}, bf16[192,1024]{1,0:T(8,128)(2,1)}, u32[]{:S(2)}, u32[]{:S(2)}) collective-permute-start(bf16[192,1024]{1,0:T(8,128)(2,1)} %slice.42), channel_id=1, source_target_pairs={{0,6},{1,7},{2,0},{3,1},{4,2},{5,3},{6,4},{7,5},{8,14},{9,15},{10,... | collective-permute-start | bytes 1179656 | tf_op jit(solution)/shard_map/ppermute | solution.py:314
  72.6 4.2 %all-to-all-start.1 = ((bf16[16,2,64,128]{3,2,1,0:T(8,128)(2,1)}), bf16[16,2,64,128]{3,2,1,0:T(8,128)(2,1)}, u32[]{:S(2)}, u32[]{:S(2)}) async-start(bf16[16,2,64,128]{3,2,1,0:T(8,128)(2,1)} %copy-done.6), calls=%async_computation.1 | async-start | bytes 1048576 | tf_op jit(solution)/shard_map/all_to_all | solution.py:361
  76.8 2.0 %collective-permute-done.1.far_a = bf16[192,1024]{1,0:T(8,128)(2,1)} collective-permute-done((bf16[192,1024]{1,0:T(8,128)(2,1)}, bf16[192,1024]{1,0:T(8,128)(2,1)}, u32[]{:S(2)}, u32[]{:S(2)}) %collective-permute-start.1) | collective-permute-done | bytes 393248 | tf_op jit(solution)/shard_map/ppermute | solution.py:314
  78.9 1.0 collective-permute-done.3.far_b
  79.9 5.8 %copy-done = bf16[1024,8192]{1,0:T(8,128)(2,1)S(1)} copy-done((bf16[1024,8192]{1,0:T(8,128)(2,1)S(1)}, bf16[1024,8192]{1,0:T(8,128)(2,1)}, u32[]{:S(2)}) %copy-start) | copy-done | bytes 16777240
  85.7 1.2 copy-done.1
  86.9 3.4 %own_products.1 = (f32[384,1024]{1,0:T(8,128)S(1)}, f32[384,64]{1,0:T(8,128)S(1)}) custom-call(s32[146]{0:T(256)S(1)} %concatenate.11.index, bf16[384,1024]{1,0:T(8,128)(2,1)S(1)} %bitcast.31, bf16[384,1024]{1,0:T(8,128)(2,1)} %collective-permute-done.8.refs_1_, bf16[1024,8192]{1,0:T(8,128)(2,1)S(1)} %copy-done, bf16[8,64,1024]{2,1,0:T(8,128)(2,1)S(1)} %bitcast.24), custom_call_target="tpu_custom_call" | custom-call | flops 1610612736 | bytes 1572864 | tf_op jit(solution)/shard_map/own_products/pallas_call | solution.py:64
  90.4 1.1 copy-done.7
  92.2 2.0 %gradient_products.1 = f32[128,1024]{1,0:T(8,128)S(1)} custom-call(s32[146]{0:T(256)S(1)} %concatenate.11.index, bf16[16,2,64,128]{3,2,1,0:T(8,128)(2,1)} %all-to-all-done.1.crossed, bf16[768,1024]{1,0:T(8,128)(2,1)S(1)} %copy-done.4, bf16[384,1024]{1,0:T(8,128)(2,1)S(1)} %copy-done.3), custom_call_target="tpu_custom_call" | custom-call | flops 150994944 | bytes 2359296 | tf_op jit(solution)/shard_map/gradient_products/pallas_call | solution.py:208
  95.0 4.7 %all-to-all-start.2 = ((f32[16,8,1024]{2,1,0:T(8,128)}), f32[16,8,1024]{2,1,0:T(8,128)}, u32[]{:S(2)}, u32[]{:S(2)}) async-start(f32[16,8,1024]{2,1,0:T(8,128)} %bitcast.32), calls=%async_computation.2 | async-start | bytes 1048576 | tf_op jit(solution)/shard_map/all_to_all | solution.py:383
  99.7 1.4 copy-done.8
  101.1 0.9 copy-done.11
  102.0 11.9 %side_products.1 = (f32[384,1024]{1,0:T(8,128)S(1)}, f32[384,64]{1,0:T(8,128)S(1)}) custom-call(s32[146]{0:T(256)S(1)} %concatenate.11.index, bf16[384,1024]{1,0:T(8,128)(2,1)} %collective-permute-done.refs_0_, bf16[384,1024]{1,0:T(8,128)(2,1)} %collective-permute-done.6.refs_1_, bf16[384,1024]{1,0:T(8,128)(2,1)} %collective-permute-done.2.refs_2_, ...), custom_call_target="tpu_custom_call" | custom-call | flops 3221225472 | bytes 3145728 | tf_op jit(solution)/shard_map/side_products/pallas_call | solution.py:64
  114.0 9.6 %last_products.1 = bf16[16,7,16,512]{3,2,1,0:T(8,128)(2,1)S(1)} custom-call(s32[146]{0:T(256)S(1)} %concatenate.11.index, bf16[192,1024]{1,0:T(8,128)(2,1)} %collective-permute-done.1.far_a, bf16[192,1024]{1,0:T(8,128)(2,1)} %collective-permute-done.3.far_b, bf16[192,1024]{1,0:T(8,128)(2,1)} %collective-permute-done.4.other_a, ...), custom_call_target="tpu_custom_call" | custom-call | flops 1610612736 | bytes 4718592 | tf_op jit(solution)/shard_map/last_products/pallas_call | solution.py:129
  123.6 1.1 reduce_sum.29
  124.7 32.5 %all_to_all.20.arrived = bf16[16,7,16,512]{3,2,1,0:T(8,128)(2,1)S(1)} all-to-all(bf16[16,7,16,512]{3,2,1,0:T(8,128)(2,1)S(1)} %broadcast_dynamic-update-slice_fusion), channel_id=1, replica_groups=mesh['group'=16,'tp'=8] {'group'}, dimensions={0} | all-to-all | bytes 3670016 | tf_op jit(solution)/shard_map/all_to_all | solution.py:396
  157.2 3.2 %unfold.1 = (bf16[768,1024]{1,0:T(8,128)(2,1)}, f32[64,1024]{1,0:T(8,128)}, f32[64,1024]{1,0:T(8,128)}) custom-call(bf16[16,7,16,512]{3,2,1,0:T(8,128)(2,1)S(1)} %all_to_all.20.arrived), custom_call_target="tpu_custom_call" | custom-call | tf_op jit(solution)/shard_map/unfold/pallas_call | solution.py:262
  (70 shorter events, 8.3 us)
Async XLA Ops:
  7.2 11.1 %copy-start.4 = (bf16[768,1024]{1,0:T(8,128)(2,1)S(1)}, bf16[768,1024]{1,0:T(8,128)(2,1)}, u32[]{:S(2)}) copy-start(bf16[768,1024]{1,0:T(8,128)(2,1)} %attention.1) | copy-start | bytes 4718596
  7.2 11.1 %copy-start.9 = (bf16[1024,64]{0,1:T(8,128)(2,1)S(1)}, bf16[1024,64]{0,1:T(8,128)(2,1)}, u32[]{:S(2)}) copy-start(bf16[1024,64]{0,1:T(8,128)(2,1)} %param.12) | copy-start | bytes 393220
  9.4 9.5 %copy-start.3 = (bf16[384,1024]{1,0:T(8,128)(2,1)S(1)}, bf16[384,1024]{1,0:T(8,128)(2,1)}, u32[]{:S(2)}) copy-start(bf16[384,1024]{1,0:T(8,128)(2,1)} %gradient.1) | copy-start | bytes 2359300
  9.4 22.6 %all-to-all-start = ((bf16[16,3,8,1024]{3,2,1,0:T(8,128)(2,1)}), bf16[16,3,8,1024]{3,2,1,0:T(8,128)(2,1)S(1)}, u32[]{:S(2)}, u32[]{:S(2)}) async-start(bf16[16,3,8,1024]{3,2,1,0:T(8,128)(2,1)} %bitcast.34), calls=%async_computation | async-start | bytes 1572864 | tf_op jit(solution)/shard_map/all_to_all | solution.py:319
  17.5 62.4 %all-gather.3.cloned.1.call-start = ((), (), s32[]{:S(2)}) async-start(), calls=%async_computation.4 | async-start | bytes 1179648 | tf_op jit(solution)/shard_map/all_gather | solution.py:349
  18.2 4.2 %copy-start.12 = (s32[48]{0:T(128)S(1)}, s32[48]{0:T(128)}, u32[]{:S(2)}) copy-start(s32[48]{0:T(128)} %param.14) | copy-start | bytes 580
  18.2 4.3 %copy-start.13 = (s32[16]{0:T(128)S(1)}, s32[16]{0:T(128)}, u32[]{:S(2)}) copy-start(s32[16]{0:T(128)} %param.15) | copy-start | bytes 196
  22.4 13.2 %collective-permute-start.9 = (f32[64,1152]{1,0:T(8,128)}, f32[64,1152]{1,0:T(8,128)}, u32[]{:S(2)}, u32[]{:S(2)}) collective-permute-start(f32[64,1152]{1,0:T(8,128)} %pad_maximum_fusion), channel_id=1, source_target_pairs={{0,1},{1,0},{2,3},{3,2},{4,5},{5,4},{6,7},{7,6},{8,9},{9,8},{10,11... | collective-permute-start | bytes 884744 | tf_op jit(solution)/shard_map/ppermute | solution.py:317
  32.0 26.4 %collective-permute-start = (bf16[384,1024]{1,0:T(8,128)(2,1)S(1)}, bf16[384,1024]{1,0:T(8,128)(2,1)}, u32[]{:S(2)}, u32[]{:S(2)}) collective-permute-start(bf16[384,1024]{1,0:T(8,128)(2,1)S(1)} %bitcast.28), channel_id=1, source_target_pairs={{0,2},{1,3},{2,4},{3,5},{4,6},{5,7},{6,0},{7,1},{8,10},{9,11},{10,... | collective-permute-start | bytes 2359304 | tf_op jit(solution)/shard_map/ppermute | solution.py:314
  33.6 25.3 %collective-permute-start.2 = (bf16[384,1024]{1,0:T(8,128)(2,1)S(1)}, bf16[384,1024]{1,0:T(8,128)(2,1)}, u32[]{:S(2)}, u32[]{:S(2)}) collective-permute-start(bf16[384,1024]{1,0:T(8,128)(2,1)S(1)} %bitcast.29), channel_id=1, source_target_pairs={{0,6},{1,7},{2,0},{3,1},{4,2},{5,3},{6,4},{7,5},{8,14},{9,15},{10,... | collective-permute-start | bytes 2359304 | tf_op jit(solution)/shard_map/ppermute | solution.py:314
  37.2 21.1 %collective-permute-start.10 = (f32[32,1152]{1,0:T(8,128)}, f32[32,1152]{1,0:T(8,128)S(1)}, u32[]{:S(2)}, u32[]{:S(2)}) collective-permute-start(f32[32,1152]{1,0:T(8,128)} %fusion.1), channel_id=1, source_target_pairs={{0,2},{1,3},{2,4},{3,5},{4,6},{5,7},{6,0},{7,1},{8,10},{9,11},{10,... | collective-permute-start | bytes 442376 | tf_op jit(solution)/shard_map/ppermute | solution.py:314
  37.6 22.2 %collective-permute-start.11 = (f32[32,1152]{1,0:T(8,128)}, f32[32,1152]{1,0:T(8,128)}, u32[]{:S(2)}, u32[]{:S(2)}) collective-permute-start(f32[32,1152]{1,0:T(8,128)} %fusion.1), channel_id=1, source_target_pairs={{0,6},{1,7},{2,0},{3,1},{4,2},{5,3},{6,4},{7,5},{8,14},{9,15},{10,... | collective-permute-start | bytes 442376 | tf_op jit(solution)/shard_map/ppermute | solution.py:314
  40.5 22.3 %collective-permute-start.12 = (f32[32,1152]{1,0:T(8,128)}, f32[32,1152]{1,0:T(8,128)}, u32[]{:S(2)}, u32[]{:S(2)}) collective-permute-start(f32[32,1152]{1,0:T(8,128)} %fusion.1), channel_id=1, source_target_pairs={{0,4},{1,5},{2,6},{3,7},{4,0},{5,1},{6,2},{7,3},{8,12},{9,13},{10,... | collective-permute-start | bytes 442376 | tf_op jit(solution)/shard_map/ppermute | solution.py:314
  58.3 21.6 %collective-permute-start.8 = (bf16[384,1024]{1,0:T(8,128)(2,1)S(1)}, bf16[384,1024]{1,0:T(8,128)(2,1)}, u32[]{:S(2)}, u32[]{:S(2)}) collective-permute-start(bf16[384,1024]{1,0:T(8,128)(2,1)S(1)} %bitcast.30), channel_id=1, source_target_pairs={{0,1},{1,0},{2,3},{3,2},{4,5},{5,4},{6,7},{7,6},{8,9},{9,8},{10,11... | collective-permute-start | bytes 2359304 | tf_op jit(solution)/shard_map/ppermute | solution.py:317
  58.3 33.8 %collective-permute-start.6 = (bf16[384,1024]{1,0:T(8,128)(2,1)}, bf16[384,1024]{1,0:T(8,128)(2,1)}, u32[]{:S(2)}, u32[]{:S(2)}) collective-permute-start(bf16[384,1024]{1,0:T(8,128)(2,1)} %collective-permute-done.refs_0_), channel_id=1, source_target_pairs={{0,1},{1,0},{2,3},{3,2},{4,5},{5,4},{6,7},{7,6},{8,9},{9,8},{10,11... | collective-permute-start | bytes 2359304 | tf_op jit(solution)/shard_map/ppermute | solution.py:317
  58.8 33.3 %collective-permute-start.7 = (bf16[384,1024]{1,0:T(8,128)(2,1)}, bf16[384,1024]{1,0:T(8,128)(2,1)}, u32[]{:S(2)}, u32[]{:S(2)}) collective-permute-start(bf16[384,1024]{1,0:T(8,128)(2,1)} %collective-permute-done.2.refs_2_), channel_id=1, source_target_pairs={{0,1},{1,0},{2,3},{3,2},{4,5},{5,4},{6,7},{7,6},{8,9},{9,8},{10,11... | collective-permute-start | bytes 2359304 | tf_op jit(solution)/shard_map/ppermute | solution.py:317
  63.8 4.5 %collective-permute-start.13 = (bf16[32,1152]{1,0:T(8,128)(2,1)S(1)}, bf16[32,1152]{1,0:T(8,128)(2,1)S(1)}, u32[]{:S(2)}, u32[]{:S(2)}) collective-permute-start(bf16[32,1152]{1,0:T(8,128)(2,1)S(1)} %add_convert_fusion.share), channel_id=1, source_target_pairs={{0,1},{1,0},{2,3},{3,2},{4,5},{5,4},{6,7},{7,6},{8,9},{9,8},{10,11... | collective-permute-start | bytes 221192 | tf_op jit(solution)/shard_map/ppermute | solution.py:317
  65.8 13.0 %collective-permute-start.1 = (bf16[192,1024]{1,0:T(8,128)(2,1)}, bf16[192,1024]{1,0:T(8,128)(2,1)}, u32[]{:S(2)}, u32[]{:S(2)}) collective-permute-start(bf16[192,1024]{1,0:T(8,128)(2,1)} %slice.41), channel_id=1, source_target_pairs={{0,2},{1,3},{2,4},{3,5},{4,6},{5,7},{6,0},{7,1},{8,10},{9,11},{10,... | collective-permute-start | bytes 1179656 | tf_op jit(solution)/shard_map/ppermute | solution.py:314
  68.3 11.6 %collective-permute-start.3 = (bf16[192,1024]{1,0:T(8,128)(2,1)}, bf16[192,1024]{1,0:T(8,128)(2,1)}, u32[]{:S(2)}, u32[]{:S(2)}) collective-permute-start(bf16[192,1024]{1,0:T(8,128)(2,1)} %slice.42), channel_id=1, source_target_pairs={{0,6},{1,7},{2,0},{3,1},{4,2},{5,3},{6,4},{7,5},{8,14},{9,15},{10,... | collective-permute-start | bytes 1179656 | tf_op jit(solution)/shard_map/ppermute | solution.py:314
  71.8 0.8 copy-start.6
  72.6 19.6 %all-to-all-start.1 = ((bf16[16,2,64,128]{3,2,1,0:T(8,128)(2,1)}), bf16[16,2,64,128]{3,2,1,0:T(8,128)(2,1)}, u32[]{:S(2)}, u32[]{:S(2)}) async-start(bf16[16,2,64,128]{3,2,1,0:T(8,128)(2,1)} %copy-done.6), calls=%async_computation.1 | async-start | bytes 1048576 | tf_op jit(solution)/shard_map/all_to_all | solution.py:361
  78.9 35.1 %collective-permute-start.4 = (bf16[192,1024]{1,0:T(8,128)(2,1)}, bf16[192,1024]{1,0:T(8,128)(2,1)}, u32[]{:S(2)}, u32[]{:S(2)}) collective-permute-start(bf16[192,1024]{1,0:T(8,128)(2,1)} %collective-permute-done.1.far_a), channel_id=1, source_target_pairs={{0,1},{1,0},{2,3},{3,2},{4,5},{5,4},{6,7},{7,6},{8,9},{9,8},{10,11... | collective-permute-start | bytes 1179656 | tf_op jit(solution)/shard_map/ppermute | solution.py:317
  79.9 34.1 %collective-permute-start.5 = (bf16[192,1024]{1,0:T(8,128)(2,1)}, bf16[192,1024]{1,0:T(8,128)(2,1)}, u32[]{:S(2)}, u32[]{:S(2)}) collective-permute-start(bf16[192,1024]{1,0:T(8,128)(2,1)} %collective-permute-done.3.far_b), channel_id=1, source_target_pairs={{0,1},{1,0},{2,3},{3,2},{4,5},{5,4},{6,7},{7,6},{8,9},{9,8},{10,11... | collective-permute-start | bytes 1179656 | tf_op jit(solution)/shard_map/ppermute | solution.py:317
  79.9 5.8 %copy-start = (bf16[1024,8192]{1,0:T(8,128)(2,1)S(1)}, bf16[1024,8192]{1,0:T(8,128)(2,1)}, u32[]{:S(2)}) copy-start(bf16[1024,8192]{1,0:T(8,128)(2,1)} %weight.1) | copy-start | bytes 50331652
  85.7 1.2 copy-start.1
  90.4 1.1 copy-start.7
  91.5 0.7 copy-start.10
  92.2 7.5 %copy-start.2 = (bf16[512,1024]{1,0:T(8,128)(2,1)S(1)}, bf16[512,1024]{1,0:T(8,128)(2,1)}, u32[]{:S(2)}) copy-start(bf16[512,1024]{1,0:T(8,128)(2,1)} %all-gather.3.cloned.1.call-done) | copy-start | bytes 3145732
  94.2 0.8 copy-start.5
  95.0 28.6 %all-to-all-start.2 = ((f32[16,8,1024]{2,1,0:T(8,128)}), f32[16,8,1024]{2,1,0:T(8,128)}, u32[]{:S(2)}, u32[]{:S(2)}) async-start(f32[16,8,1024]{2,1,0:T(8,128)} %bitcast.32), calls=%async_computation.2 | async-start | bytes 1048576 | tf_op jit(solution)/shard_map/all_to_all | solution.py:383
  99.7 1.4 copy-start.8
  101.1 0.9 copy-start.11
Sparse Core Ops, SparseCore 0:
  20.0 26.6 all-gather.2

commit v5 on v4

--- a/solution.py
+++ b/solution.py
@@ -23,6 +23,58 @@
     return lax.dot_general(
         left, right, (((1,), (1,)), ((), ())), preferred_element_type=jnp.float32
     )
+
+
+def load_kernel(weight, out, sem):
+    count, _, width = out.shape
+    copies = [
+        pltpu.make_async_copy(weight.at[:, pl.ds(k * width, width)], out.at[k], sem.at[k])
+        for k in range(count)
+    ]
+    for copy in copies:
+        copy.start()
+    for copy in copies:
+        copy.wait()
+
+
+def load_columns(weight, count):
+    rows, width = weight.shape[0], weight.shape[1] // count
+    return pl.pallas_call(
+        load_kernel,
+        in_specs=[HBM],
+        out_specs=VMEM,
+        out_shape=jax.ShapeDtypeStruct((count, rows, width), weight.dtype),
+        scratch_shapes=[pltpu.SemaphoreType.DMA((count,))],
+        compiler_params=pltpu.CompilerParams(vmem_limit_bytes=20 * 2**20),
+        cost_estimate=pl.CostEstimate(
+            flops=0, bytes_accessed=4 * count * rows * width, transcendentals=0
+        ),
+        name="load_columns",
+    )(weight)
+
+
+def halves_kernel(left, right, top, bottom, sem):
+    half = top.shape[0]
+    copies = [
+        pltpu.make_async_copy(left.at[pl.ds(0, half)], top, sem.at[0]),
+        pltpu.make_async_copy(right.at[pl.ds(half, half)], bottom, sem.at[1]),
+    ]
+    for copy in copies:
+        copy.start()
+    for copy in copies:
+        copy.wait()
+
+
+def take_halves(left, right):
+    half = jax.ShapeDtypeStruct((left.shape[0] // 2, left.shape[1]), left.dtype)
+    return pl.pallas_call(
+        halves_kernel,
+        in_specs=[HBM] * 2,
+        out_specs=[HBM] * 2,
+        out_shape=[half] * 2,
+        scratch_shapes=[pltpu.SemaphoreType.DMA((2,))],
+        name="take_halves",
+    )(left, right)
 
 
 def block_kernel(table, first, index, *refs):
@@ -33,7 +85,6 @@
     if not first:
         base_in, low_in = refs.pop(0), refs.pop(0)
     base, low, x, x_sem = refs
-    width = x.shape[2]
     copies = [pltpu.make_async_copy(blocks[k], x.at[k], x_sem.at[k]) for k in range(count)]
     for copy in copies[:2]:
         copy.start()
@@ -42,8 +93,7 @@
         if k + 2 < count:
             copies[k + 2].start()
         owner = index[table[k]]
-        columns = pl.ds(pl.multiple_of(owner * width, width), width)
-        value, value_low = dot_minor(x[k], weight[:, columns]), dot_minor(x[k], up[owner])
+        value, value_low = dot_minor(x[k], weight[owner]), dot_minor(x[k], up[owner])
         if k > 0:
             base[...] += value
             low[...] += value_low
@@ -58,7 +108,7 @@
 def block_products(index, table, blocks, output_weight, up_all, base=None, low=None, name=""):
     count = len(blocks)
     tokens, width = blocks[0].shape
-    out_width = output_weight.shape[0]
+    out_width = output_weight.shape[1]
     rank = up_all.shape[1]
     first = base is None
     return pl.pallas_call(
@@ -87,7 +137,7 @@
     rows, table, index, far_a, far_b, other_a, other_b, weight, up, base, low, down, out, x,
     low_rounded, x_sem,
 ):
-    half, width = far_a.shape
+    half = far_a.shape[0]
     piece = 2 * half // rows
     tile = 2 * LANES
     copies = []
@@ -104,12 +154,11 @@
     for k, owner in enumerate(owners):
         total += dot_minor(x[k], up[owner])
     low_rounded[...] = total.astype(jnp.bfloat16)
-    for n in range(weight.shape[0] // tile):
+    for n in range(weight.shape[1] // tile):
         span = slice(n * tile, (n + 1) * tile)
         total = base[:, span]
         for k, owner in enumerate(owners):
-            columns = pl.ds(pl.multiple_of(owner * width, width), width)
-            total += dot_minor(x[k], weight[span, columns])
+            total += dot_minor(x[k], weight[owner, span])
         total += adapter_scale * jnp.dot(
             low_rounded[...], down[:, span], preferred_element_type=jnp.float32
         )
@@ -363,18 +412,20 @@
         "group", split_axis=0, concat_axis=0, tiled=True,
     )
 
-    half = spread.shape[0] // 2
+    weight = load_columns(output_weight, tp)
+    spread, _ = lax.optimization_barrier((spread, share))
     left, right = move(spread, 1), move(spread, -1)
-    far = [move(left[:half], 1), move(right[half:], -1)]
+    left_top, right_bottom = take_halves(left, right)
+    far = [move(left_top, 1), move(right_bottom, -1)]
     base, low_own = block_products(
-        table, [owner_at, owner_at + 1], [spread, swap(spread)], output_weight, up_all,
+        table, [owner_at, owner_at + 1], [spread, swap(spread)], weight, up_all,
         name="own_products",
     )
     swapped = [swap(left), swap(right)]
     crossed, _ = lax.optimization_barrier((crossed, (base, swapped)))
     base, low_own = block_products(
         table, [owner_at + i for i in range(2, 6)], [left, swapped[0], right, swapped[1]],
-        output_weight, up_all, base, low_own, name="side_products",
+        weight, up_all, base, low_own, name="side_products",
     )
     grads = gradient_products(
         table, source_at, dest_at, crossed, attention_slot_outputs, output_gradient_rows
@@ -387,7 +438,7 @@
     grads = (scale_factor * jnp.sum(grads, axis=0)).astype(jnp.bfloat16)
     placed = last_products(
         rows, table, [owner_at + 6, owner_at + 7], far, [swap(part) for part in far],
-        output_weight, up_all, base, low_own, down_weight.T, groups, slot_cap,
+        weight, up_all, base, low_own, down_weight.T, groups, slot_cap,
     )
 
     folded = (2 * piece, width_here // 2)

time: 169 us -> 200 us (1.18)
  Pallas kernels: 30.8 us -> 59.9 us
  local copies, waits for them, and re-layouts: 19.1 us -> 27.1 us
  other arithmetic: 6.16 us -> 0.85 us
  starting transfers between devices: 28.2 us -> 32.5 us
  waiting for transfers between devices: 33.6 us -> 29.6 us
    pallas_call x0 -> x2, Pallas kernels: none -> 28.2 us  [the longest x1 24.9 us: take_halves(): pl.pallas_call(halves_kernel, in_specs=[HBM] * 2, out_specs=[HBM] * 2, ou...]
    unnamed x28 -> x36, local copies, waits for them, and re-layouts: 12.7 us -> 25.5 us
    all_to_all x1, waiting for transfers between devices: 9.22 us -> 3.22 us  [body(): lax.all_to_all(output_gradient_rows.reshape(rows_here, groups, piece, wid...]
    slice x2 -> x0, local copies, waits for them, and re-layouts: 3.53 us -> none  [body(): far = [move(left[:half], 1), move(right[half:], -1)]]
    ppermute x7, waiting for transfers between devices: 23.7 us -> 26.3 us  [move(): return lax.ppermute(value, 'tp', pairs)]
    all_to_all x1, starting transfers between devices: 4.69 us -> 7.1 us  [body(): lax.all_to_all(grads.reshape(groups, share_rows, width_here), 'group', sp...]
  transfers between devices with their start and end apart: 18 -> 18, of which waited for: 6 -> 5; matrix products, arithmetic and copies ran while one was open for 7% -> 1% of each run, Pallas kernels for 17% -> 28%
where the time goes in v5:
time: 200 us; the launch traced here: 199 us
  Pallas kernels  59.9 us (30%)
  starting transfers between devices  32.5 us (16%)
  blocking collectives  32.3 us (16%)
  waiting for transfers between devices  29.6 us (15%)
  local copies, waits for them, and re-layouts  27.1 us (14%)
  between operations  14.4 us (7%)
  matrix products  2.5 us (1%)
    all_to_all x1, blocking collectives, body(): lax.all_to_all(placed, 'group', split_axis=0, concat_axis=0, tiled=True)  32.3 us
    ppermute x7, waiting for transfers between devices, move(): return lax.ppermute(value, 'tp', pairs)  26.3 us
    unnamed x36, local copies, waits for them, and re-layouts  25.5 us
    pallas_call x1, Pallas kernels, take_halves(): pl.pallas_call(halves_kernel, in_specs=[HBM] * 2, out_specs=[HBM] * 2, ou...  24.9 us
    pallas_call x2, Pallas kernels, block_products(): pl.pallas_call(functools.partial(block_kernel, table, first), in_specs=[S...  15.5 us
    ppermute x7, starting transfers between devices, move(): return lax.ppermute(value, 'tp', pairs)  11.8 us
    pallas_call x1, Pallas kernels, last_products(): pl.pallas_call(functools.partial(last_kernel, rows, table), in_specs=[SME...  9.6 us
    all_to_all x1, starting transfers between devices, body(): lax.all_to_all(output_gradient_rows.reshape(rows_here, groups, piece, wid...  8.09 us
  transfers between devices with their start and end apart: 18, of which 5 were waited for; matrix products, arithmetic and copies ran while one was open for 1% of the time, Pallas kernels for 28%

profile of v5, /device:TPU:0, one launch (start us, length us, event | category | flops | bytes accessed | tf_op | source)
XLA Modules:
  0.0 199.1 jit_solution(12809161693748115117)
XLA Ops:
  7.2 2.1 %fusion.6 = f32[64,768]{1,0:T(8,128)S(1)} fusion(bf16[1024,64]{0,1:T(8,128)(2,1)} %param.12, bf16[768,1024]{1,0:T(8,128)(2,1)} %attention.1), kind=kOutput, calls=%fused_computation.25 | convolution fusion | flops 100663296 | bytes 1900544 | tf_op jit(solution)/shard_map/dot_general | solution.py:400
  10.8 8.1 %all-to-all-start = ((bf16[16,3,8,1024]{3,2,1,0:T(8,128)(2,1)}), bf16[16,3,8,1024]{3,2,1,0:T(8,128)(2,1)S(1)}, u32[]{:S(2)}, u32[]{:S(2)}) async-start(bf16[16,3,8,1024]{3,2,1,0:T(8,128)(2,1)} %bitcast.23), calls=%async_computation | async-start | bytes 1572864 | tf_op jit(solution)/shard_map/all_to_all | solution.py:368
  19.0 1.6 collective-permute-start.1
  20.6 1.7 collective-permute-start.2
  22.3 2.0 collective-permute-start.3
  24.3 2.0 %collective-permute-done.1 = f32[32,1152]{1,0:T(8,128)S(1)} collective-permute-done((f32[32,1152]{1,0:T(8,128)S(1)}, f32[32,1152]{1,0:T(8,128)S(1)}, u32[]{:S(2)}, u32[]{:S(2)}) %collective-permute-start.1) | collective-permute-done | bytes 147488 | tf_op jit(solution)/shard_map/ppermute | solution.py:363
  26.3 2.5 %collective-permute-done.2 = f32[32,1152]{1,0:T(8,128)S(1)} collective-permute-done((f32[32,1152]{1,0:T(8,128)S(1)}, f32[32,1152]{1,0:T(8,128)S(1)}, u32[]{:S(2)}, u32[]{:S(2)}) %collective-permute-start.2) | collective-permute-done | bytes 147488 | tf_op jit(solution)/shard_map/ppermute | solution.py:363
  28.8 1.8 collective-permute-done.3
  30.7 3.2 %all-to-all-done = bf16[16,3,8,1024]{3,2,1,0:T(8,128)(2,1)S(1)} async-done(((bf16[16,3,8,1024]{3,2,1,0:T(8,128)(2,1)}), bf16[16,3,8,1024]{3,2,1,0:T(8,128)(2,1)S(1)}, u32[]{:S(2)}, u32[]{:S(2)}) %all-to-all-start) | async-done | bytes 786464 | tf_op jit(solution)/shard_map/all_to_all | solution.py:368
  33.9 1.6 collective-permute-start.4
  35.5 1.7 collective-permute-start.5
  38.1 19.9 %collective-permute-done.4.left.refs_0_ = bf16[384,1024]{1,0:T(8,128)(2,1)} collective-permute-done((bf16[384,1024]{1,0:T(8,128)(2,1)S(1)}, bf16[384,1024]{1,0:T(8,128)(2,1)}, u32[]{:S(2)}, u32[]{:S(2)}) %collective-permute-start.4) | collective-permute-done | bytes 786464 | tf_op jit(solution)/shard_map/ppermute | solution.py:363
  58.9 24.9 %take_halves.1 = (bf16[192,1024]{1,0:T(8,128)(2,1)}, bf16[192,1024]{1,0:T(8,128)(2,1)}) custom-call(bf16[384,1024]{1,0:T(8,128)(2,1)} %collective-permute-done.4.left.refs_0_, bf16[384,1024]{1,0:T(8,128)(2,1)} %collective-permute-done.5.right.refs_2_), custom_call_target="tpu_custom_call" | custom-call | tf_op jit(solution)/shard_map/take_halves/pallas_call | solution.py:70
  83.8 1.3 collective-permute-start.6
  85.1 2.0 %collective-permute-start.7 = (bf16[192,1024]{1,0:T(8,128)(2,1)}, bf16[192,1024]{1,0:T(8,128)(2,1)}, u32[]{:S(2)}, u32[]{:S(2)}) collective-permute-start(bf16[192,1024]{1,0:T(8,128)(2,1)} %get-tuple-element.28), channel_id=1, source_target_pairs={{0,6},{1,7},{2,0},{3,1},{4,2},{5,3},{6,4},{7,5},{8,14},{9,15},{10,... | collective-permute-start | bytes 1179656 | tf_op jit(solution)/shard_map/ppermute | solution.py:363
  87.4 1.5 rank_sums_to_send.1
  88.9 4.2 %all-to-all-start.1 = ((bf16[16,2,64,128]{3,2,1,0:T(8,128)(2,1)}), bf16[16,2,64,128]{3,2,1,0:T(8,128)(2,1)}, u32[]{:S(2)}, u32[]{:S(2)}) async-start(bf16[16,2,64,128]{3,2,1,0:T(8,128)(2,1)} %rank_sums_to_send.1), calls=%async_computation.1 | async-start | bytes 1048576 | tf_op jit(solution)/shard_map/all_to_all | solution.py:410
  93.1 5.8 %copy-done.2 = bf16[1024,8192]{1,0:T(8,128)(2,1)S(1)} copy-done((bf16[1024,8192]{1,0:T(8,128)(2,1)S(1)}, bf16[1024,8192]{1,0:T(8,128)(2,1)}, u32[]{:S(2)}) %copy-start.2) | copy-done | bytes 16777240
  98.9 3.3 %load_columns.1.refs_2_.refs_4_.weight = bf16[8,1024,1024]{2,1,0:T(8,128)(2,1)S(1)} custom-call(bf16[1024,8192]{1,0:T(8,128)(2,1)S(1)} %copy-done.2), custom_call_target="tpu_custom_call" | custom-call | bytes 33554432 | tf_op jit(solution)/shard_map/load_columns/pallas_call | solution.py:42
  102.2 5.7 %copy-done = bf16[8,1024,1024]{2,1,0:T(8,128)(2,1)} copy-done((bf16[8,1024,1024]{2,1,0:T(8,128)(2,1)}, bf16[8,1024,1024]{2,1,0:T(8,128)(2,1)S(1)}, u32[]{:S(2)}) %copy-start) | copy-done | bytes 16777240
  109.3 5.8 %copy-done.1 = bf16[8,1024,1024]{2,1,0:T(8,128)(2,1)S(1)} copy-done((bf16[8,1024,1024]{2,1,0:T(8,128)(2,1)S(1)}, bf16[8,1024,1024]{2,1,0:T(8,128)(2,1)}, u32[]{:S(2)}) %copy-start.1) | copy-done | bytes 16777240
  115.1 1.2 copy-done.3
  116.3 1.1 copy-done.11
  117.4 3.5 %own_products.1 = (f32[384,1024]{1,0:T(8,128)S(1)}, f32[384,64]{1,0:T(8,128)S(1)}) custom-call(s32[146]{0:T(256)S(1)} %concatenate.11.index, bf16[384,1024]{1,0:T(8,128)(2,1)S(1)} %bitcast.31, bf16[384,1024]{1,0:T(8,128)(2,1)S(1)} %copy-done.11, bf16[8,1024,1024]{2,1,0:T(8,128)(2,1)S(1)} %copy-done.1, bf16[8,64,1024]{2,1,0:T(8,128)(2,1)S(1)} %bitcast.24), custom_call_target="tpu_custom_call" | custom-call | flops 1610612736 | bytes 1572864 | tf_op jit(solution)/shard_map/own_products/pallas_call | solution.py:114
  121.0 1.1 copy-done.8
  122.8 2.0 %gradient_products.1 = f32[128,1024]{1,0:T(8,128)S(1)} custom-call(s32[146]{0:T(256)S(1)} %concatenate.11.index, bf16[16,2,64,128]{3,2,1,0:T(8,128)(2,1)} %all-to-all-done.1.crossed, bf16[768,1024]{1,0:T(8,128)(2,1)S(1)} %copy-done.6, bf16[384,1024]{1,0:T(8,128)(2,1)S(1)} %copy-done.5), custom_call_target="tpu_custom_call" | custom-call | flops 150994944 | bytes 2359296 | tf_op jit(solution)/shard_map/gradient_products/pallas_call | solution.py:257
  125.6 7.1 %all-to-all-start.2 = ((f32[16,8,1024]{2,1,0:T(8,128)}), f32[16,8,1024]{2,1,0:T(8,128)S(1)}, u32[]{:S(2)}, u32[]{:S(2)}) async-start(f32[16,8,1024]{2,1,0:T(8,128)} %bitcast.32), calls=%async_computation.2 | async-start | bytes 1048576 | tf_op jit(solution)/shard_map/all_to_all | solution.py:434
  132.7 1.4 copy-done.9
  135.1 12.0 %side_products.1 = (f32[384,1024]{1,0:T(8,128)S(1)}, f32[384,64]{1,0:T(8,128)S(1)}) custom-call(s32[146]{0:T(256)S(1)} %concatenate.11.index, bf16[384,1024]{1,0:T(8,128)(2,1)} %collective-permute-done.4.left.refs_0_, bf16[384,1024]{1,0:T(8,128)(2,1)} %collective-permute-done.10.refs_1_, bf16[384,1024]{1,0:T(8,128)(2,1)} %collective-permute-done.5.right.refs_2_, ...), custom_call_target="tpu_custom_call" | custom-call | flops 3221225472 | bytes 3145728 | tf_op jit(solution)/shard_map/side_products/pallas_call | solution.py:114
  147.1 9.6 %last_products.1 = bf16[16,7,16,512]{3,2,1,0:T(8,128)(2,1)S(1)} custom-call(s32[146]{0:T(256)S(1)} %concatenate.11.index, bf16[192,1024]{1,0:T(8,128)(2,1)} %collective-permute-done.6.far_a, bf16[192,1024]{1,0:T(8,128)(2,1)} %collective-permute-done.7.far_b, bf16[192,1024]{1,0:T(8,128)(2,1)} %collective-permute-done.8.other_a, ...), custom_call_target="tpu_custom_call" | custom-call | flops 1610612736 | bytes 4718592 | tf_op jit(solution)/shard_map/last_products/pallas_call | solution.py:178
  156.8 32.3 %all_to_all.20.arrived = bf16[16,7,16,512]{3,2,1,0:T(8,128)(2,1)S(1)} all-to-all(bf16[16,7,16,512]{3,2,1,0:T(8,128)(2,1)S(1)} %broadcast_dynamic-update-slice_fusion), channel_id=1, replica_groups=mesh['group'=16,'tp'=8] {'group'}, dimensions={0} | all-to-all | bytes 3670016 | tf_op jit(solution)/shard_map/all_to_all | solution.py:447
  189.1 3.2 %unfold.1 = (bf16[768,1024]{1,0:T(8,128)(2,1)}, f32[64,1024]{1,0:T(8,128)}, f32[64,1024]{1,0:T(8,128)}) custom-call(bf16[16,7,16,512]{3,2,1,0:T(8,128)(2,1)S(1)} %all_to_all.20.arrived), custom_call_target="tpu_custom_call" | custom-call | tf_op jit(solution)/shard_map/unfold/pallas_call | solution.py:311
  (78 shorter events, 7.5 us)
Async XLA Ops:
  7.2 2.2 %copy-start.5 = (bf16[384,1024]{1,0:T(8,128)(2,1)S(1)}, bf16[384,1024]{1,0:T(8,128)(2,1)}, u32[]{:S(2)}) copy-start(bf16[384,1024]{1,0:T(8,128)(2,1)} %gradient.1) | copy-start | bytes 2359300
  7.2 2.2 %copy-start.15 = (bf16[64,1024]{1,0:T(8,128)(2,1)S(1)}, bf16[64,1024]{1,0:T(8,128)(2,1)}, u32[]{:S(2)}) copy-start(bf16[64,1024]{1,0:T(8,128)(2,1)} %param.13) | copy-start | bytes 393220
  9.7 9.2 %collective-permute-start = (f32[64,1152]{1,0:T(8,128)S(1)}, f32[64,1152]{1,0:T(8,128)S(1)}, u32[]{:S(2)}, u32[]{:S(2)}) collective-permute-start(f32[64,1152]{1,0:T(8,128)S(1)} %pad_maximum_fusion), channel_id=1, source_target_pairs={{0,1},{1,0},{2,3},{3,2},{4,5},{5,4},{6,7},{7,6},{8,9},{9,8},{10,11... | collective-permute-start | bytes 884744 | tf_op jit(solution)/shard_map/ppermute | solution.py:366
  10.8 26.4 %copy-start.16 = (s32[48]{0:T(128)S(1)}, s32[48]{0:T(128)}, u32[]{:S(2)}) copy-start(s32[48]{0:T(128)} %param.14) | copy-start | bytes 580
  10.8 26.6 %copy-start.17 = (s32[16]{0:T(128)S(1)}, s32[16]{0:T(128)}, u32[]{:S(2)}) copy-start(s32[16]{0:T(128)} %param.15) | copy-start | bytes 196
  10.8 23.1 %all-to-all-start = ((bf16[16,3,8,1024]{3,2,1,0:T(8,128)(2,1)}), bf16[16,3,8,1024]{3,2,1,0:T(8,128)(2,1)S(1)}, u32[]{:S(2)}, u32[]{:S(2)}) async-start(bf16[16,3,8,1024]{3,2,1,0:T(8,128)(2,1)} %bitcast.23), calls=%async_computation | async-start | bytes 1572864 | tf_op jit(solution)/shard_map/all_to_all | solution.py:368
  18.9 90.4 %all-gather.3.cloned.1.call-start = ((), (), s32[]{:S(2)}) async-start(), calls=%async_computation.4 | async-start | bytes 1179648 | tf_op jit(solution)/shard_map/all_gather | solution.py:398
  19.0 7.3 %collective-permute-start.1 = (f32[32,1152]{1,0:T(8,128)S(1)}, f32[32,1152]{1,0:T(8,128)S(1)}, u32[]{:S(2)}, u32[]{:S(2)}) collective-permute-start(f32[32,1152]{1,0:T(8,128)S(1)} %fusion.1), channel_id=1, source_target_pairs={{0,2},{1,3},{2,4},{3,5},{4,6},{5,7},{6,0},{7,1},{8,10},{9,11},{10,... | collective-permute-start | bytes 442376 | tf_op jit(solution)/shard_map/ppermute | solution.py:363
  20.6 8.2 %collective-permute-start.2 = (f32[32,1152]{1,0:T(8,128)S(1)}, f32[32,1152]{1,0:T(8,128)S(1)}, u32[]{:S(2)}, u32[]{:S(2)}) collective-permute-start(f32[32,1152]{1,0:T(8,128)S(1)} %fusion.1), channel_id=1, source_target_pairs={{0,6},{1,7},{2,0},{3,1},{4,2},{5,3},{6,4},{7,5},{8,14},{9,15},{10,... | collective-permute-start | bytes 442376 | tf_op jit(solution)/shard_map/ppermute | solution.py:363
  22.3 8.3 %collective-permute-start.3 = (f32[32,1152]{1,0:T(8,128)S(1)}, f32[32,1152]{1,0:T(8,128)S(1)}, u32[]{:S(2)}, u32[]{:S(2)}) collective-permute-start(f32[32,1152]{1,0:T(8,128)S(1)} %fusion.1), channel_id=1, source_target_pairs={{0,4},{1,5},{2,6},{3,7},{4,0},{5,1},{6,2},{7,3},{8,12},{9,13},{10,... | collective-permute-start | bytes 442376 | tf_op jit(solution)/shard_map/ppermute | solution.py:363
  33.9 24.1 %collective-permute-start.4 = (bf16[384,1024]{1,0:T(8,128)(2,1)S(1)}, bf16[384,1024]{1,0:T(8,128)(2,1)}, u32[]{:S(2)}, u32[]{:S(2)}) collective-permute-start(bf16[384,1024]{1,0:T(8,128)(2,1)S(1)} %bitcast.28), channel_id=1, source_target_pairs={{0,2},{1,3},{2,4},{3,5},{4,6},{5,7},{6,0},{7,1},{8,10},{9,11},{10,... | collective-permute-start | bytes 2359304 | tf_op jit(solution)/shard_map/ppermute | solution.py:363
  35.5 22.5 %collective-permute-start.5 = (bf16[384,1024]{1,0:T(8,128)(2,1)S(1)}, bf16[384,1024]{1,0:T(8,128)(2,1)}, u32[]{:S(2)}, u32[]{:S(2)}) collective-permute-start(bf16[384,1024]{1,0:T(8,128)(2,1)S(1)} %bitcast.29), channel_id=1, source_target_pairs={{0,6},{1,7},{2,0},{3,1},{4,2},{5,3},{6,4},{7,5},{8,14},{9,15},{10,... | collective-permute-start | bytes 2359304 | tf_op jit(solution)/shard_map/ppermute | solution.py:363
  37.9 70.5 %collective-permute-start.12 = (bf16[384,1024]{1,0:T(8,128)(2,1)S(1)}, bf16[384,1024]{1,0:T(8,128)(2,1)S(1)}, u32[]{:S(2)}, u32[]{:S(2)}) collective-permute-start(bf16[384,1024]{1,0:T(8,128)(2,1)S(1)} %bitcast.30), channel_id=1, source_target_pairs={{0,1},{1,0},{2,3},{3,2},{4,5},{5,4},{6,7},{7,6},{8,9},{9,8},{10,11... | collective-permute-start | bytes 2359304 | tf_op jit(solution)/shard_map/ppermute | solution.py:366
  58.0 64.7 %collective-permute-start.10 = (bf16[384,1024]{1,0:T(8,128)(2,1)}, bf16[384,1024]{1,0:T(8,128)(2,1)}, u32[]{:S(2)}, u32[]{:S(2)}) collective-permute-start(bf16[384,1024]{1,0:T(8,128)(2,1)} %collective-permute-done.4.left.refs_0_), channel_id=1, source_target_pairs={{0,1},{1,0},{2,3},{3,2},{4,5},{5,4},{6,7},{7,6},{8,9},{9,8},{10,11... | collective-permute-start | bytes 2359304 | tf_op jit(solution)/shard_map/ppermute | solution.py:366
  58.0 64.7 %collective-permute-start.11 = (bf16[384,1024]{1,0:T(8,128)(2,1)}, bf16[384,1024]{1,0:T(8,128)(2,1)}, u32[]{:S(2)}, u32[]{:S(2)}) collective-permute-start(bf16[384,1024]{1,0:T(8,128)(2,1)} %collective-permute-done.5.right.refs_2_), channel_id=1, source_target_pairs={{0,1},{1,0},{2,3},{3,2},{4,5},{5,4},{6,7},{7,6},{8,9},{9,8},{10,11... | collective-permute-start | bytes 2359304 | tf_op jit(solution)/shard_map/ppermute | solution.py:366
  58.7 26.5 %collective-permute-start.13 = (bf16[32,1152]{1,0:T(8,128)(2,1)S(1)}, bf16[32,1152]{1,0:T(8,128)(2,1)S(1)}, u32[]{:S(2)}, u32[]{:S(2)}) collective-permute-start(bf16[32,1152]{1,0:T(8,128)(2,1)S(1)} %add_convert_fusion.share), channel_id=1, source_target_pairs={{0,1},{1,0},{2,3},{3,2},{4,5},{5,4},{6,7},{7,6},{8,9},{9,8},{10,11... | collective-permute-start | bytes 221192 | tf_op jit(solution)/shard_map/ppermute | solution.py:366
  83.8 24.1 %collective-permute-start.6 = (bf16[192,1024]{1,0:T(8,128)(2,1)}, bf16[192,1024]{1,0:T(8,128)(2,1)}, u32[]{:S(2)}, u32[]{:S(2)}) collective-permute-start(bf16[192,1024]{1,0:T(8,128)(2,1)} %get-tuple-element.27), channel_id=1, source_target_pairs={{0,2},{1,3},{2,4},{3,5},{4,6},{5,7},{6,0},{7,1},{8,10},{9,11},{10,... | collective-permute-start | bytes 1179656 | tf_op jit(solution)/shard_map/ppermute | solution.py:363
  85.1 22.8 %collective-permute-start.7 = (bf16[192,1024]{1,0:T(8,128)(2,1)}, bf16[192,1024]{1,0:T(8,128)(2,1)}, u32[]{:S(2)}, u32[]{:S(2)}) collective-permute-start(bf16[192,1024]{1,0:T(8,128)(2,1)} %get-tuple-element.28), channel_id=1, source_target_pairs={{0,6},{1,7},{2,0},{3,1},{4,2},{5,3},{6,4},{7,5},{8,14},{9,15},{10,... | collective-permute-start | bytes 1179656 | tf_op jit(solution)/shard_map/ppermute | solution.py:363
  88.9 33.9 %all-to-all-start.1 = ((bf16[16,2,64,128]{3,2,1,0:T(8,128)(2,1)}), bf16[16,2,64,128]{3,2,1,0:T(8,128)(2,1)}, u32[]{:S(2)}, u32[]{:S(2)}) async-start(bf16[16,2,64,128]{3,2,1,0:T(8,128)(2,1)} %rank_sums_to_send.1), calls=%async_computation.1 | async-start | bytes 1048576 | tf_op jit(solution)/shard_map/all_to_all | solution.py:410
  93.1 5.8 %copy-start.2 = (bf16[1024,8192]{1,0:T(8,128)(2,1)S(1)}, bf16[1024,8192]{1,0:T(8,128)(2,1)}, u32[]{:S(2)}) copy-start(bf16[1024,8192]{1,0:T(8,128)(2,1)} %weight.1) | copy-start | bytes 50331652
  102.2 5.7 %copy-start = (bf16[8,1024,1024]{2,1,0:T(8,128)(2,1)}, bf16[8,1024,1024]{2,1,0:T(8,128)(2,1)S(1)}, u32[]{:S(2)}) copy-start(bf16[8,1024,1024]{2,1,0:T(8,128)(2,1)S(1)} %load_columns.1.refs_2_.refs_4_.weight) | copy-start | bytes 50331652
  107.9 39.1 %collective-permute-start.8 = (bf16[192,1024]{1,0:T(8,128)(2,1)}, bf16[192,1024]{1,0:T(8,128)(2,1)}, u32[]{:S(2)}, u32[]{:S(2)}) collective-permute-start(bf16[192,1024]{1,0:T(8,128)(2,1)} %collective-permute-done.6.far_a), channel_id=1, source_target_pairs={{0,1},{1,0},{2,3},{3,2},{4,5},{5,4},{6,7},{7,6},{8,9},{9,8},{10,11... | collective-permute-start | bytes 1179656 | tf_op jit(solution)/shard_map/ppermute | solution.py:366
  107.9 39.1 %collective-permute-start.9 = (bf16[192,1024]{1,0:T(8,128)(2,1)}, bf16[192,1024]{1,0:T(8,128)(2,1)}, u32[]{:S(2)}, u32[]{:S(2)}) collective-permute-start(bf16[192,1024]{1,0:T(8,128)(2,1)} %collective-permute-done.7.far_b), channel_id=1, source_target_pairs={{0,1},{1,0},{2,3},{3,2},{4,5},{5,4},{6,7},{7,6},{8,9},{9,8},{10,11... | collective-permute-start | bytes 1179656 | tf_op jit(solution)/shard_map/ppermute | solution.py:366
  109.3 5.8 %copy-start.1 = (bf16[8,1024,1024]{2,1,0:T(8,128)(2,1)S(1)}, bf16[8,1024,1024]{2,1,0:T(8,128)(2,1)}, u32[]{:S(2)}) copy-start(bf16[8,1024,1024]{2,1,0:T(8,128)(2,1)} %copy-done) | copy-start | bytes 50331652
  115.1 1.2 copy-start.3
  116.3 1.1 copy-start.11
  117.4 5.3 %copy-start.6 = (bf16[768,1024]{1,0:T(8,128)(2,1)S(1)}, bf16[768,1024]{1,0:T(8,128)(2,1)}, u32[]{:S(2)}) copy-start(bf16[768,1024]{1,0:T(8,128)(2,1)} %attention.1) | copy-start | bytes 4718596
  120.9 1.1 copy-start.8
  122.8 9.9 %copy-start.4 = (bf16[512,1024]{1,0:T(8,128)(2,1)S(1)}, bf16[512,1024]{1,0:T(8,128)(2,1)}, u32[]{:S(2)}) copy-start(bf16[512,1024]{1,0:T(8,128)(2,1)} %all-gather.3.cloned.1.call-done) | copy-start | bytes 3145732
  125.6 31.1 %all-to-all-start.2 = ((f32[16,8,1024]{2,1,0:T(8,128)}), f32[16,8,1024]{2,1,0:T(8,128)S(1)}, u32[]{:S(2)}, u32[]{:S(2)}) async-start(f32[16,8,1024]{2,1,0:T(8,128)} %bitcast.32), calls=%async_computation.2 | async-start | bytes 1048576 | tf_op jit(solution)/shard_map/all_to_all | solution.py:434
  132.7 1.4 copy-start.9
  135.1 12.0 %copy-start.12 = (bf16[1024,64]{0,1:T(8,128)(2,1)S(1)}, bf16[1024,64]{0,1:T(8,128)(2,1)}, u32[]{:S(2)}) copy-start(bf16[1024,64]{0,1:T(8,128)(2,1)} %param.12) | copy-start | bytes 393220
  (4 other events, 3.3 us)
Sparse Core Ops, SparseCore 0:
  24.4 25.2 all-gather.2

commit v6 on v4

--- a/solution.py
+++ b/solution.py
@@ -10,6 +10,7 @@
 
 ROW_TOKENS = 128
 LANES = 128
+VMEM_LIMIT = 56 * 2**20
 
 
 adapter_scale = 2.0
@@ -23,6 +24,29 @@
     return lax.dot_general(
         left, right, (((1,), (1,)), ((), ())), preferred_element_type=jnp.float32
     )
+
+
+def halves_kernel(left, right, top, bottom):
+    top[...] = left[...]
+    bottom[...] = right[...]
+
+
+def take_halves(left, right):
+    tokens, width = left.shape
+    half, lanes = tokens // 2, width // 2
+    shape = jax.ShapeDtypeStruct((half, width), left.dtype)
+    return pl.pallas_call(
+        halves_kernel,
+        grid=(width // lanes,),
+        in_specs=[
+            pl.BlockSpec((half, lanes), lambda i: (0, i)),
+            pl.BlockSpec((half, lanes), lambda i: (1, i)),
+        ],
+        out_specs=[pl.BlockSpec((half, lanes), lambda i: (0, i))] * 2,
+        out_shape=[shape] * 2,
+        compiler_params=pltpu.CompilerParams(vmem_limit_bytes=VMEM_LIMIT),
+        name="take_halves",
+    )(left, right)
 
 
 def block_kernel(table, first, index, *refs):
@@ -32,84 +56,127 @@
     weight, up = refs.pop(0), refs.pop(0)
     if not first:
         base_in, low_in = refs.pop(0), refs.pop(0)
-    base, low, x, x_sem = refs
+    base, low, x, w, u, x_sem, w_sem, u_sem = refs[:8]
     width = x.shape[2]
-    copies = [pltpu.make_async_copy(blocks[k], x.at[k], x_sem.at[k]) for k in range(count)]
-    for copy in copies[:2]:
-        copy.start()
+    copies = []
     for k in range(count):
-        copies[k].wait()
-        if k + 2 < count:
-            copies[k + 2].start()
         owner = index[table[k]]
         columns = pl.ds(pl.multiple_of(owner * width, width), width)
-        value, value_low = dot_minor(x[k], weight[:, columns]), dot_minor(x[k], up[owner])
-        if k > 0:
-            base[...] += value
-            low[...] += value_low
-        elif first:
+        copies.append([
+            pltpu.make_async_copy(blocks[k], x.at[k], x_sem.at[k]),
+            pltpu.make_async_copy(weight.at[:, columns], w.at[k], w_sem.at[k]),
+            pltpu.make_async_copy(up.at[owner], u.at[k], u_sem.at[k]),
+        ])
+    if not first:
+        base_was, low_was, was_sem = refs[8:]
+        copies.append([
+            pltpu.make_async_copy(base_in, base_was, was_sem.at[0]),
+            pltpu.make_async_copy(low_in, low_was, was_sem.at[1]),
+        ])
+    for each in copies[:2]:
+        for copy in each:
+            copy.start()
+    for k in range(count):
+        for copy in copies[k]:
+            copy.wait()
+        if k + 2 < len(copies):
+            for copy in copies[k + 2]:
+                copy.start()
+        value, value_low = dot_minor(x[k], w[k]), dot_minor(x[k], u[k])
+        if k == 0:
             base[...] = value
             low[...] = value_low
         else:
-            base[...] = base_in[...] + value
-            low[...] = low_in[...] + value_low
-
-
-def block_products(index, table, blocks, output_weight, up_all, base=None, low=None, name=""):
+            base[...] += value
+            low[...] += value_low
+    if not first:
+        for copy in copies[count]:
+            copy.wait()
+        base[...] += base_was[...]
+        low[...] += low_was[...]
+
+
+def block_products(index, table, blocks, weight, up_all, base=None, low=None, name=""):
     count = len(blocks)
     tokens, width = blocks[0].shape
-    out_width = output_weight.shape[0]
+    out_width = weight.shape[0]
     rank = up_all.shape[1]
     first = base is None
+    out_shape = [
+        jax.ShapeDtypeStruct((tokens, out_width), jnp.float32),
+        jax.ShapeDtypeStruct((tokens, rank), jnp.float32),
+    ]
+    scratch = [
+        pltpu.VMEM((count, tokens, width), jnp.bfloat16),
+        pltpu.VMEM((count, out_width, width), jnp.bfloat16),
+        pltpu.VMEM((count, rank, width), jnp.bfloat16),
+        pltpu.SemaphoreType.DMA((count,)),
+        pltpu.SemaphoreType.DMA((count,)),
+        pltpu.SemaphoreType.DMA((count,)),
+    ]
+    if not first:
+        scratch += [pltpu.VMEM(part.shape, part.dtype) for part in out_shape]
+        scratch += [pltpu.SemaphoreType.DMA((2,))]
     return pl.pallas_call(
         functools.partial(block_kernel, table, first),
-        in_specs=[SMEM] + [HBM] * count + [VMEM] * (2 if first else 4),
+        in_specs=[SMEM] + [HBM] * (count + (2 if first else 4)),
         out_specs=[VMEM] * 2,
-        out_shape=[
-            jax.ShapeDtypeStruct((tokens, out_width), jnp.float32),
-            jax.ShapeDtypeStruct((tokens, rank), jnp.float32),
-        ],
-        scratch_shapes=[
-            pltpu.VMEM((count, tokens, width), jnp.bfloat16),
-            pltpu.SemaphoreType.DMA((count,)),
-        ],
-        compiler_params=pltpu.CompilerParams(vmem_limit_bytes=32 * 2**20),
+        out_shape=out_shape,
+        scratch_shapes=scratch,
+        compiler_params=pltpu.CompilerParams(vmem_limit_bytes=VMEM_LIMIT),
         cost_estimate=pl.CostEstimate(
             flops=2 * count * tokens * width * out_width,
-            bytes_accessed=2 * width * count * tokens,
+            bytes_accessed=2 * width * count * (tokens + out_width),
             transcendentals=0,
         ),
         name=name,
-    )(index, *blocks, output_weight, up_all, *([] if first else [base, low]))
+    )(index, *blocks, weight, up_all, *([] if first else [base, low]))
 
 
 def last_kernel(
-    rows, table, index, far_a, far_b, other_a, other_b, weight, up, base, low, down, out, x,
-    low_rounded, x_sem,
+    rows, table, index, far_a, far_b, other_a, other_b, weight, up, base_in, low_in, down, out, x,
+    w, u, base, low, low_rounded, x_sem, w_sem, u_sem, was_sem,
 ):
     half, width = far_a.shape
     piece = 2 * half // rows
     tile = 2 * LANES
+    tiles = w.shape[0] // tile
     copies = []
     for i, part in enumerate((far_a, far_b, other_a, other_b)):
-        rows_of = pl.ds((i % 2) * half, half)
-        copies.append(pltpu.make_async_copy(part, x.at[i // 2, rows_of], x_sem.at[i]))
+        rows_of, lanes = pl.ds((i % 2) * half, half), pl.ds((i // 2) * width, width)
+        copies.append(pltpu.make_async_copy(part, x.at[rows_of, lanes], x_sem.at[i]))
+    for k in range(2):
+        lanes = pl.ds(k * width, width)
+        copies.append(pltpu.make_async_copy(up.at[index[table[k]]], u.at[:, lanes], u_sem.at[k]))
+    copies.append(pltpu.make_async_copy(low_in, low, was_sem.at[tiles]))
     for copy in copies:
         copy.start()
+    tile_copies = []
+    for n in range(tiles):
+        span = pl.ds(n * tile, tile)
+        each = [pltpu.make_async_copy(base_in.at[:, span], base.at[:, span], was_sem.at[n])]
+        for k in range(2):
+            columns = pl.ds(pl.multiple_of(index[table[k]] * width, width), width)
+            lanes = pl.ds(k * width, width)
+            each.append(
+                pltpu.make_async_copy(weight.at[span, columns], w.at[span, lanes], w_sem.at[n, k])
+            )
+        tile_copies.append(each)
+    for each in tile_copies[:2]:
+        for copy in each:
+            copy.start()
     out[...] = jnp.zeros_like(out)
     for copy in copies:
         copy.wait()
-    owners = [index[i] for i in table]
-    total = low[...]
-    for k, owner in enumerate(owners):
-        total += dot_minor(x[k], up[owner])
-    low_rounded[...] = total.astype(jnp.bfloat16)
-    for n in range(weight.shape[0] // tile):
+    low_rounded[...] = (low[...] + dot_minor(x[...], u[...])).astype(jnp.bfloat16)
+    for n in range(tiles):
         span = slice(n * tile, (n + 1) * tile)
-        total = base[:, span]
-        for k, owner in enumerate(owners):
-            columns = pl.ds(pl.multiple_of(owner * width, width), width)
-            total += dot_minor(x[k], weight[span, columns])
+        for copy in tile_copies[n]:
+            copy.wait()
+        if n + 2 < tiles:
+            for copy in tile_copies[n + 2]:
+                copy.start()
+        total = base[:, span] + dot_minor(x[...], w[span])
         total += adapter_scale * jnp.dot(
             low_rounded[...], down[:, span], preferred_element_type=jnp.float32
         )
@@ -126,19 +193,27 @@
     tokens = 2 * half
     rank, out_width = down.shape
     piece = tokens // rows
+    tiles = out_width // (2 * LANES)
     return pl.pallas_call(
         functools.partial(last_kernel, rows, table),
-        in_specs=[SMEM] + [HBM] * 4 + [VMEM] * 5,
+        in_specs=[SMEM] + [HBM] * 8 + [VMEM],
         out_specs=VMEM,
         scratch_shapes=[
-            pltpu.VMEM((2, tokens, width), jnp.bfloat16),
+            pltpu.VMEM((tokens, 2 * width), jnp.bfloat16),
+            pltpu.VMEM((out_width, 2 * width), jnp.bfloat16),
+            pltpu.VMEM((rank, 2 * width), jnp.bfloat16),
+            pltpu.VMEM((tokens, out_width), jnp.float32),
+            pltpu.VMEM((tokens, rank), jnp.float32),
             pltpu.VMEM((tokens, rank), jnp.bfloat16),
             pltpu.SemaphoreType.DMA((4,)),
+            pltpu.SemaphoreType.DMA((tiles, 2)),
+            pltpu.SemaphoreType.DMA((2,)),
+            pltpu.SemaphoreType.DMA((tiles + 1,)),
         ],
         out_shape=jax.ShapeDtypeStruct(
             (groups, slots + 1, 2 * piece, out_width // 2), jnp.bfloat16
         ),
-        compiler_params=pltpu.CompilerParams(vmem_limit_bytes=32 * 2**20),
+        compiler_params=pltpu.CompilerParams(vmem_limit_bytes=VMEM_LIMIT),
         cost_estimate=pl.CostEstimate(
             flops=4 * tokens * width * out_width,
             bytes_accessed=4 * width * tokens + 8 * tokens * out_width,
@@ -169,7 +244,7 @@
         in_specs=[SMEM, VMEM, VMEM],
         out_specs=VMEM,
         out_shape=jax.ShapeDtypeStruct((groups, 2, rank, ROW_TOKENS), jnp.bfloat16),
-        compiler_params=pltpu.CompilerParams(vmem_limit_bytes=16 * 2**20),
+        compiler_params=pltpu.CompilerParams(vmem_limit_bytes=VMEM_LIMIT),
         cost_estimate=pl.CostEstimate(
             flops=groups * rank * ROW_TOKENS, bytes_accessed=4 * groups * rank * ROW_TOKENS,
             transcendentals=0,
@@ -217,7 +292,7 @@
             pltpu.VMEM(gradient.shape, jnp.bfloat16),
             pltpu.SemaphoreType.DMA((2,)),
         ],
-        compiler_params=pltpu.CompilerParams(vmem_limit_bytes=16 * 2**20),
+        compiler_params=pltpu.CompilerParams(vmem_limit_bytes=VMEM_LIMIT),
         cost_estimate=pl.CostEstimate(
             flops=2 * rank * width * (slot_tokens + row_tokens),
             bytes_accessed=2 * width * (slot_tokens + row_tokens),
@@ -273,7 +348,7 @@
             jax.ShapeDtypeStruct((rank, width), jnp.float32),
             jax.ShapeDtypeStruct((rank, width), jnp.float32),
         ],
-        compiler_params=pltpu.CompilerParams(vmem_limit_bytes=16 * 2**20),
+        compiler_params=pltpu.CompilerParams(vmem_limit_bytes=VMEM_LIMIT),
         name="unfold",
     )(arrived)
 
@@ -363,17 +438,17 @@
         "group", split_axis=0, concat_axis=0, tiled=True,
     )
 
-    half = spread.shape[0] // 2
+    spread, _ = lax.optimization_barrier((spread, share))
     left, right = move(spread, 1), move(spread, -1)
-    far = [move(left[:half], 1), move(right[half:], -1)]
     base, low_own = block_products(
         table, [owner_at, owner_at + 1], [spread, swap(spread)], output_weight, up_all,
         name="own_products",
     )
-    swapped = [swap(left), swap(right)]
-    crossed, _ = lax.optimization_barrier((crossed, (base, swapped)))
+    left, right, _ = lax.optimization_barrier((left, right, (crossed, base)))
+    left_top, right_bottom = take_halves(left, right)
+    far = [move(left_top, 1), move(right_bottom, -1)]
     base, low_own = block_products(
-        table, [owner_at + i for i in range(2, 6)], [left, swapped[0], right, swapped[1]],
+        table, [owner_at + i for i in range(2, 6)], [left, swap(left), right, swap(right)],
         output_weight, up_all, base, low_own, name="side_products",
     )
     grads = gradient_products(

time: 169 us -> 159 us (0.941)
  blocking collectives: 32.5 us -> 50.8 us
  local copies, waits for them, and re-layouts: 19.1 us -> 5.38 us
  waiting for transfers between devices: 33.6 us -> 20 us
  Pallas kernels: 30.8 us -> 37.5 us
  other arithmetic: 6.16 us -> 0.83 us
  starting transfers between devices: 28.2 us -> 25.2 us
    all_to_all x0 -> x1, blocking collectives: none -> 18.3 us  [body(): lax.all_to_all(rank_sums_to_send(table, end - 1, pick_at, groups, share,...]
    unnamed x28 -> x26, local copies, waits for them, and re-layouts: 12.7 us -> 2.43 us
    all_to_all x1, waiting for transfers between devices: 9.22 us -> 0.01 us  [body(): lax.all_to_all(output_gradient_rows.reshape(rows_here, groups, piece, wid...]
    ppermute x7, waiting for transfers between devices: 23.7 us -> 15.8 us  [move(): return lax.ppermute(value, 'tp', pairs)]
    all_to_all x1 -> x0, starting transfers between devices: 4.24 us -> none  [body(): lax.all_to_all(rank_sums_to_send(table, end - 1, pick_at, groups, share,...]
    slice x2 -> x0, local copies, waits for them, and re-layouts: 3.53 us -> none  [body(): far = [move(left[:half], 1), move(right[half:], -1)]]
    all_to_all x1, waiting for transfers between devices: 0.01 us -> 3.45 us  [body(): lax.all_to_all(grads.reshape(groups, share_rows, width_here), 'group', sp...]
    pallas_call x1, Pallas kernels: 3.18 us -> 5.26 us  [unfold(): pl.pallas_call(functools.partial(unfold_kernel, slots), grid=(slots + 1,)...]
  transfers between devices with their start and end apart: 18 -> 17, of which waited for: 6 -> 4; matrix products, arithmetic and copies ran while one was open for 7% -> 4% of each run, Pallas kernels for 17% -> 15%
where the time goes in v6:
time: 159 us; the launch traced here: 158 us
  blocking collectives  50.8 us (32%)
  Pallas kernels  37.5 us (24%)
  starting transfers between devices  25.2 us (16%)
  waiting for transfers between devices  20 us (13%)
  between operations  14.4 us (9%)
  local copies, waits for them, and re-layouts  5.38 us (3%)
  matrix products  3.71 us (2%)
    all_to_all x1, blocking collectives, body(): lax.all_to_all(placed, 'group', split_axis=0, concat_axis=0, tiled=True)  32.5 us
    all_to_all x1, blocking collectives, body(): lax.all_to_all(rank_sums_to_send(table, end - 1, pick_at, groups, share,...  18.3 us
    ppermute x7, waiting for transfers between devices, move(): return lax.ppermute(value, 'tp', pairs)  15.8 us
    pallas_call x2, Pallas kernels, block_products(): pl.pallas_call(functools.partial(block_kernel, table, first), in_specs=[S...  15.5 us
    ppermute x7, starting transfers between devices, move(): return lax.ppermute(value, 'tp', pairs)  11.8 us
    pallas_call x1, Pallas kernels, last_products(): pl.pallas_call(functools.partial(last_kernel, rows, table), in_specs=[SME...  8.96 us
    all_to_all x1, starting transfers between devices, body(): lax.all_to_all(output_gradient_rows.reshape(rows_here, groups, piece, wid...  7.96 us
    pallas_call x1, Pallas kernels, unfold(): pl.pallas_call(functools.partial(unfold_kernel, slots), grid=(slots + 1,)...  5.26 us
  transfers between devices with their start and end apart: 17, of which 4 were waited for; matrix products, arithmetic and copies ran while one was open for 4% of the time, Pallas kernels for 15%

profile of v6, /device:TPU:0, one launch (start us, length us, event | category | flops | bytes accessed | tf_op | source)
XLA Modules:
  0.0 157.8 jit_solution(10891439531911510816)
XLA Ops:
  7.2 0.7 all-gather.3.cloned.1.call-update
  7.9 1.6 %fusion.5 = f32[64,384]{1,0:T(8,128)S(1)} fusion(bf16[64,1024]{1,0:T(8,128)(2,1)} %param.13, bf16[384,1024]{1,0:T(8,128)(2,1)} %gradient.1), kind=kOutput, calls=%fused_computation.24 | convolution fusion | flops 50331648 | bytes 1015808 | tf_op jit(solution)/shard_map/dot_general | solution.py:24
  9.5 2.1 %fusion.6 = f32[64,768]{1,0:T(8,128)S(1)} fusion(bf16[1024,64]{0,1:T(8,128)(2,1)} %param.12, bf16[768,1024]{1,0:T(8,128)(2,1)} %attention.1), kind=kOutput, calls=%fused_computation.25 | convolution fusion | flops 100663296 | bytes 1900544 | tf_op jit(solution)/shard_map/dot_general | solution.py:426
  11.8 0.9 copy.19
  12.7 8.0 %all-to-all-start = ((bf16[16,3,8,1024]{3,2,1,0:T(8,128)(2,1)}), bf16[16,3,8,1024]{3,2,1,0:T(8,128)(2,1)S(1)}, u32[]{:S(2)}, u32[]{:S(2)}) async-start(bf16[16,3,8,1024]{3,2,1,0:T(8,128)(2,1)} %bitcast.23), calls=%async_computation | async-start | bytes 1572864 | tf_op jit(solution)/shard_map/all_to_all | solution.py:394
  21.5 1.6 %collective-permute-start.1 = (f32[32,1152]{1,0:T(8,128)S(1)}, f32[32,1152]{1,0:T(8,128)S(1)}, u32[]{:S(2)}, u32[]{:S(2)}) collective-permute-start(f32[32,1152]{1,0:T(8,128)S(1)} %fusion.1), channel_id=1, source_target_pairs={{0,2},{1,3},{2,4},{3,5},{4,6},{5,7},{6,0},{7,1},{8,10},{9,11},{10,... | collective-permute-start | bytes 442376 | tf_op jit(solution)/shard_map/ppermute | solution.py:389
  23.1 1.7 %collective-permute-start.2 = (f32[32,1152]{1,0:T(8,128)S(1)}, f32[32,1152]{1,0:T(8,128)S(1)}, u32[]{:S(2)}, u32[]{:S(2)}) collective-permute-start(f32[32,1152]{1,0:T(8,128)S(1)} %fusion.1), channel_id=1, source_target_pairs={{0,6},{1,7},{2,0},{3,1},{4,2},{5,3},{6,4},{7,5},{8,14},{9,15},{10,... | collective-permute-start | bytes 442376 | tf_op jit(solution)/shard_map/ppermute | solution.py:389
  24.8 2.0 %collective-permute-start.3 = (f32[32,1152]{1,0:T(8,128)S(1)}, f32[32,1152]{1,0:T(8,128)S(1)}, u32[]{:S(2)}, u32[]{:S(2)}) collective-permute-start(f32[32,1152]{1,0:T(8,128)S(1)} %fusion.1), channel_id=1, source_target_pairs={{0,4},{1,5},{2,6},{3,7},{4,0},{5,1},{6,2},{7,3},{8,12},{9,13},{10,... | collective-permute-start | bytes 442376 | tf_op jit(solution)/shard_map/ppermute | solution.py:389
  27.1 4.5 %collective-permute-done.1 = f32[32,1152]{1,0:T(8,128)S(1)} collective-permute-done((f32[32,1152]{1,0:T(8,128)S(1)}, f32[32,1152]{1,0:T(8,128)S(1)}, u32[]{:S(2)}, u32[]{:S(2)}) %collective-permute-start.1) | collective-permute-done | bytes 147488 | tf_op jit(solution)/shard_map/ppermute | solution.py:389
  31.6 4.7 %collective-permute-done.3 = f32[32,1152]{1,0:T(8,128)S(1)} collective-permute-done((f32[32,1152]{1,0:T(8,128)S(1)}, f32[32,1152]{1,0:T(8,128)S(1)}, u32[]{:S(2)}, u32[]{:S(2)}) %collective-permute-start.3) | collective-permute-done | bytes 147488 | tf_op jit(solution)/shard_map/ppermute | solution.py:389
  36.6 0.6 collective-permute-start.6
  37.1 0.8 collective-permute-start.4
  37.9 2.4 %collective-permute-start.5 = (bf16[384,1024]{1,0:T(8,128)(2,1)S(1)}, bf16[384,1024]{1,0:T(8,128)(2,1)S(1)}, u32[]{:S(2)}, u32[]{:S(2)}) collective-permute-start(bf16[384,1024]{1,0:T(8,128)(2,1)S(1)} %bitcast.30), channel_id=1, source_target_pairs={{0,6},{1,7},{2,0},{3,1},{4,2},{5,3},{6,4},{7,5},{8,14},{9,15},{10,... | collective-permute-start | bytes 2359304 | tf_op jit(solution)/shard_map/ppermute | solution.py:389
  40.6 0.7 concatenate.11.index
  41.2 0.6 copy-done.10
  41.9 1.8 %rank_sums_to_send.1 = bf16[16,2,64,128]{3,2,1,0:T(8,128)(2,1)} custom-call(s32[146]{0:T(256)} %concatenate.11.index, bf16[32,1152]{1,0:T(8,128)(2,1)} %copy-done.9, bf16[32,1152]{1,0:T(8,128)(2,1)} %copy-done.10), custom_call_target="tpu_custom_call" | custom-call | flops 131072 | bytes 524288 | tf_op jit(solution)/shard_map/rank_sums_to_send/pallas_call | solution.py:242
  43.7 18.3 %all_to_all.20.crossed = bf16[16,2,64,128]{3,2,1,0:T(8,128)(2,1)} all-to-all(bf16[16,2,64,128]{3,2,1,0:T(8,128)(2,1)} %rank_sums_to_send.1), channel_id=1, replica_groups=mesh['group'=16,'tp'=8] {'group'}, dimensions={0} | all-to-all | bytes 1048576 | tf_op jit(solution)/shard_map/all_to_all | solution.py:436
  62.1 3.9 %gradient_products.1 = f32[128,1024]{1,0:T(8,128)} custom-call(s32[146]{0:T(256)} %concatenate.11.index, bf16[16,2,64,128]{3,2,1,0:T(8,128)(2,1)} %all_to_all.20.crossed, bf16[768,1024]{1,0:T(8,128)(2,1)} %attention.1, bf16[384,1024]{1,0:T(8,128)(2,1)} %gradient.1), custom_call_target="tpu_custom_call" | custom-call | flops 150994944 | bytes 2359296 | tf_op jit(solution)/shard_map/gradient_products/pallas_call | solution.py:283
  66.0 3.6 %all-to-all-start.2 = ((f32[16,8,1024]{2,1,0:T(8,128)}), f32[16,8,1024]{2,1,0:T(8,128)S(1)}, u32[]{:S(2)}, u32[]{:S(2)}) async-start(f32[16,8,1024]{2,1,0:T(8,128)} %bitcast.32), calls=%async_computation.2 | async-start | bytes 1048576 | tf_op jit(solution)/shard_map/all_to_all | solution.py:458
  69.6 6.2 %own_products.1 = (f32[384,1024]{1,0:T(8,128)}, f32[384,64]{1,0:T(8,128)}) custom-call(s32[146]{0:T(256)} %concatenate.11.index, bf16[384,1024]{1,0:T(8,128)(2,1)} %bitcast.31, bf16[384,1024]{1,0:T(8,128)(2,1)} %collective-permute-done.7.refs_1_, bf16[1024,8192]{1,0:T(8,128)(2,1)} %weight.1, bf16[8,64,1024]{2,1,0:T(8,128)(2,1)} %bitcast.24), custom_call_target="tpu_custom_call" | custom-call | flops 1610612736 | bytes 5767168 | tf_op jit(solution)/shard_map/own_products/pallas_call | solution.py:120
  76.5 3.4 %all-to-all-done.2 = f32[16,8,1024]{2,1,0:T(8,128)S(1)} async-done(((f32[16,8,1024]{2,1,0:T(8,128)}), f32[16,8,1024]{2,1,0:T(8,128)S(1)}, u32[]{:S(2)}, u32[]{:S(2)}) %all-to-all-start.2) | async-done | bytes 524320 | tf_op jit(solution)/shard_map/all_to_all | solution.py:458
  80.0 2.1 %take_halves.1 = (bf16[192,1024]{1,0:T(8,128)(2,1)}, bf16[192,1024]{1,0:T(8,128)(2,1)}) custom-call(bf16[384,1024]{1,0:T(8,128)(2,1)} %copy-done.2, bf16[384,1024]{1,0:T(8,128)(2,1)} %copy-done.3), custom_call_target="tpu_custom_call" | custom-call | tf_op jit(solution)/shard_map/take_halves/pallas_call | solution.py:38
  82.0 3.2 %collective-permute-start.9 = (bf16[192,1024]{1,0:T(8,128)(2,1)}, bf16[192,1024]{1,0:T(8,128)(2,1)S(1)}, u32[]{:S(2)}, u32[]{:S(2)}) collective-permute-start(bf16[192,1024]{1,0:T(8,128)(2,1)} %get-tuple-element.32), channel_id=1, source_target_pairs={{0,6},{1,7},{2,0},{3,1},{4,2},{5,3},{6,4},{7,5},{8,14},{9,15},{10,... | collective-permute-start | bytes 1179656 | tf_op jit(solution)/shard_map/ppermute | solution.py:389
  85.3 6.6 %collective-permute-done.8.far_a = bf16[192,1024]{1,0:T(8,128)(2,1)S(1)} collective-permute-done((bf16[192,1024]{1,0:T(8,128)(2,1)}, bf16[192,1024]{1,0:T(8,128)(2,1)S(1)}, u32[]{:S(2)}, u32[]{:S(2)}) %collective-permute-start.8) | collective-permute-done | bytes 393248 | tf_op jit(solution)/shard_map/ppermute | solution.py:389
  91.9 0.5 collective-permute-start.11
  92.4 0.9 copy-done.4
  93.4 9.3 %side_products.1 = (f32[384,1024]{1,0:T(8,128)}, f32[384,64]{1,0:T(8,128)}) custom-call(s32[146]{0:T(256)} %concatenate.11.index, bf16[384,1024]{1,0:T(8,128)(2,1)} %copy-done.2, bf16[384,1024]{1,0:T(8,128)(2,1)} %copy-done.4, bf16[384,1024]{1,0:T(8,128)(2,1)} %copy-done.3, bf16[384,1024]{1,0:T(8,128)(2,1)} %collective-permute-done.13.refs_3_, ...), custom_call_target="tpu_custom_call" | custom-call | flops 3221225472 | bytes 11534336 | tf_op jit(solution)/shard_map/side_products/pallas_call | solution.py:120
  102.7 0.7 copy-done.7
  103.5 9.0 %last_products.1 = bf16[16,7,16,512]{3,2,1,0:T(8,128)(2,1)} custom-call(s32[146]{0:T(256)} %concatenate.11.index, bf16[192,1024]{1,0:T(8,128)(2,1)} %copy-done.5, bf16[192,1024]{1,0:T(8,128)(2,1)} %copy-done.6, bf16[192,1024]{1,0:T(8,128)(2,1)} %copy-done.7, bf16[192,1024]{1,0:T(8,128)(2,1)} %copy-done.8, bf16[1024,8192]{1,0:T(8,128)(2,1)} %weight.1, ...), custom_call_target="tpu_custom_call" | custom-call | flops 1610612736 | bytes 4718592 | tf_op jit(solution)/shard_map/last_products/pallas_call | solution.py:197
  112.5 0.7 broadcast_dynamic-update-slice_fusion
  113.2 32.5 %all_to_all.21.arrived = bf16[16,7,16,512]{3,2,1,0:T(8,128)(2,1)} all-to-all(bf16[16,7,16,512]{3,2,1,0:T(8,128)(2,1)} %broadcast_dynamic-update-slice_fusion), channel_id=1, replica_groups=mesh['group'=16,'tp'=8] {'group'}, dimensions={0} | all-to-all | bytes 3670016 | tf_op jit(solution)/shard_map/all_to_all | solution.py:471
  145.7 5.3 %unfold.1 = (bf16[768,1024]{1,0:T(8,128)(2,1)}, f32[64,1024]{1,0:T(8,128)}, f32[64,1024]{1,0:T(8,128)}) custom-call(bf16[16,7,16,512]{3,2,1,0:T(8,128)(2,1)} %all_to_all.21.arrived), custom_call_target="tpu_custom_call" | custom-call | tf_op jit(solution)/shard_map/unfold/pallas_call | solution.py:337
  (66 shorter events, 2.5 us)
Async XLA Ops:
  7.2 62.4 %all-gather.3.cloned.1.call-start = ((), (), s32[]{:S(2)}) async-start(), calls=%async_computation.4 | async-start | bytes 1179648 | tf_op jit(solution)/shard_map/all_gather | solution.py:424
  7.9 3.9 %copy-start = (bf16[384,1024]{1,0:T(8,128)(2,1)S(1)}, bf16[384,1024]{1,0:T(8,128)(2,1)}, u32[]{:S(2)}) copy-start(bf16[384,1024]{1,0:T(8,128)(2,1)} %gradient.1) | copy-start | bytes 2359300
  11.7 9.8 %collective-permute-start = (f32[64,1152]{1,0:T(8,128)S(1)}, f32[64,1152]{1,0:T(8,128)S(1)}, u32[]{:S(2)}, u32[]{:S(2)}) collective-permute-start(f32[64,1152]{1,0:T(8,128)S(1)} %pad_maximum_fusion), channel_id=1, source_target_pairs={{0,1},{1,0},{2,3},{3,2},{4,5},{5,4},{6,7},{7,6},{8,9},{9,8},{10,11... | collective-permute-start | bytes 884744 | tf_op jit(solution)/shard_map/ppermute | solution.py:392
  11.8 8.9 %copy-start.11 = (s32[48]{0:T(128)S(1)}, s32[48]{0:T(128)}, u32[]{:S(2)}) copy-start(s32[48]{0:T(128)} %param.14) | copy-start | bytes 580
  11.8 9.1 %copy-start.12 = (s32[16]{0:T(128)S(1)}, s32[16]{0:T(128)}, u32[]{:S(2)}) copy-start(s32[16]{0:T(128)} %param.15) | copy-start | bytes 196
  12.7 23.6 %all-to-all-start = ((bf16[16,3,8,1024]{3,2,1,0:T(8,128)(2,1)}), bf16[16,3,8,1024]{3,2,1,0:T(8,128)(2,1)S(1)}, u32[]{:S(2)}, u32[]{:S(2)}) async-start(bf16[16,3,8,1024]{3,2,1,0:T(8,128)(2,1)} %bitcast.23), calls=%async_computation | async-start | bytes 1572864 | tf_op jit(solution)/shard_map/all_to_all | solution.py:394
  21.5 10.2 %collective-permute-start.1 = (f32[32,1152]{1,0:T(8,128)S(1)}, f32[32,1152]{1,0:T(8,128)S(1)}, u32[]{:S(2)}, u32[]{:S(2)}) collective-permute-start(f32[32,1152]{1,0:T(8,128)S(1)} %fusion.1), channel_id=1, source_target_pairs={{0,2},{1,3},{2,4},{3,5},{4,6},{5,7},{6,0},{7,1},{8,10},{9,11},{10,... | collective-permute-start | bytes 442376 | tf_op jit(solution)/shard_map/ppermute | solution.py:389
  23.1 8.5 %collective-permute-start.2 = (f32[32,1152]{1,0:T(8,128)S(1)}, f32[32,1152]{1,0:T(8,128)S(1)}, u32[]{:S(2)}, u32[]{:S(2)}) collective-permute-start(f32[32,1152]{1,0:T(8,128)S(1)} %fusion.1), channel_id=1, source_target_pairs={{0,6},{1,7},{2,0},{3,1},{4,2},{5,3},{6,4},{7,5},{8,14},{9,15},{10,... | collective-permute-start | bytes 442376 | tf_op jit(solution)/shard_map/ppermute | solution.py:389
  24.8 11.5 %collective-permute-start.3 = (f32[32,1152]{1,0:T(8,128)S(1)}, f32[32,1152]{1,0:T(8,128)S(1)}, u32[]{:S(2)}, u32[]{:S(2)}) collective-permute-start(f32[32,1152]{1,0:T(8,128)S(1)} %fusion.1), channel_id=1, source_target_pairs={{0,4},{1,5},{2,6},{3,7},{4,0},{5,1},{6,2},{7,3},{8,12},{9,13},{10,... | collective-permute-start | bytes 442376 | tf_op jit(solution)/shard_map/ppermute | solution.py:389
  36.3 4.9 %copy-start.9 = (bf16[32,1152]{1,0:T(8,128)(2,1)}, bf16[32,1152]{1,0:T(8,128)(2,1)S(1)}, u32[]{:S(2)}) copy-start(bf16[32,1152]{1,0:T(8,128)(2,1)S(1)} %add_convert_fusion.share) | copy-start | bytes 221188
  36.3 29.6 %copy-start.1 = (bf16[16,3,8,1024]{3,2,1,0:T(8,128)(2,1)}, bf16[16,3,8,1024]{3,2,1,0:T(8,128)(2,1)S(1)}, u32[]{:S(2)}) copy-start(bf16[16,3,8,1024]{3,2,1,0:T(8,128)(2,1)S(1)} %all-to-all-done) | copy-start | bytes 2359300
  36.4 33.2 %collective-permute-start.7 = (bf16[384,1024]{1,0:T(8,128)(2,1)S(1)}, bf16[384,1024]{1,0:T(8,128)(2,1)}, u32[]{:S(2)}, u32[]{:S(2)}) collective-permute-start(bf16[384,1024]{1,0:T(8,128)(2,1)S(1)} %bitcast.28), channel_id=1, source_target_pairs={{0,1},{1,0},{2,3},{3,2},{4,5},{5,4},{6,7},{7,6},{8,9},{9,8},{10,11... | collective-permute-start | bytes 2359304 | tf_op jit(solution)/shard_map/ppermute | solution.py:392
  36.6 4.7 %collective-permute-start.6 = (bf16[32,1152]{1,0:T(8,128)(2,1)S(1)}, bf16[32,1152]{1,0:T(8,128)(2,1)S(1)}, u32[]{:S(2)}, u32[]{:S(2)}) collective-permute-start(bf16[32,1152]{1,0:T(8,128)(2,1)S(1)} %add_convert_fusion.share), channel_id=1, source_target_pairs={{0,1},{1,0},{2,3},{3,2},{4,5},{5,4},{6,7},{7,6},{8,9},{9,8},{10,11... | collective-permute-start | bytes 221192 | tf_op jit(solution)/shard_map/ppermute | solution.py:392
  37.1 38.7 %collective-permute-start.4 = (bf16[384,1024]{1,0:T(8,128)(2,1)S(1)}, bf16[384,1024]{1,0:T(8,128)(2,1)S(1)}, u32[]{:S(2)}, u32[]{:S(2)}) collective-permute-start(bf16[384,1024]{1,0:T(8,128)(2,1)S(1)} %bitcast.29), channel_id=1, source_target_pairs={{0,2},{1,3},{2,4},{3,5},{4,6},{5,7},{6,0},{7,1},{8,10},{9,11},{10,... | collective-permute-start | bytes 2359304 | tf_op jit(solution)/shard_map/ppermute | solution.py:389
  37.9 37.9 %collective-permute-start.5 = (bf16[384,1024]{1,0:T(8,128)(2,1)S(1)}, bf16[384,1024]{1,0:T(8,128)(2,1)S(1)}, u32[]{:S(2)}, u32[]{:S(2)}) collective-permute-start(bf16[384,1024]{1,0:T(8,128)(2,1)S(1)} %bitcast.30), channel_id=1, source_target_pairs={{0,6},{1,7},{2,0},{3,1},{4,2},{5,3},{6,4},{7,5},{8,14},{9,15},{10,... | collective-permute-start | bytes 2359304 | tf_op jit(solution)/shard_map/ppermute | solution.py:389
  41.2 0.6 copy-start.10
  66.0 13.9 %all-to-all-start.2 = ((f32[16,8,1024]{2,1,0:T(8,128)}), f32[16,8,1024]{2,1,0:T(8,128)S(1)}, u32[]{:S(2)}, u32[]{:S(2)}) async-start(f32[16,8,1024]{2,1,0:T(8,128)} %bitcast.32), calls=%async_computation.2 | async-start | bytes 1048576 | tf_op jit(solution)/shard_map/all_to_all | solution.py:458
  75.9 4.1 %copy-start.2 = (bf16[384,1024]{1,0:T(8,128)(2,1)}, bf16[384,1024]{1,0:T(8,128)(2,1)S(1)}, u32[]{:S(2)}) copy-start(bf16[384,1024]{1,0:T(8,128)(2,1)S(1)} %collective-permute-done.4.left.refs_0_) | copy-start | bytes 2359300
  75.9 4.1 %copy-start.3 = (bf16[384,1024]{1,0:T(8,128)(2,1)}, bf16[384,1024]{1,0:T(8,128)(2,1)S(1)}, u32[]{:S(2)}) copy-start(bf16[384,1024]{1,0:T(8,128)(2,1)S(1)} %collective-permute-done.5.right.refs_2_) | copy-start | bytes 2359300
  75.9 16.5 %collective-permute-start.12 = (bf16[384,1024]{1,0:T(8,128)(2,1)S(1)}, bf16[384,1024]{1,0:T(8,128)(2,1)S(1)}, u32[]{:S(2)}, u32[]{:S(2)}) collective-permute-start(bf16[384,1024]{1,0:T(8,128)(2,1)S(1)} %collective-permute-done.4.left.refs_0_), channel_id=1, source_target_pairs={{0,1},{1,0},{2,3},{3,2},{4,5},{5,4},{6,7},{7,6},{8,9},{9,8},{10,11... | collective-permute-start | bytes 2359304 | tf_op jit(solution)/shard_map/ppermute | solution.py:392
  76.0 16.5 %collective-permute-start.13 = (bf16[384,1024]{1,0:T(8,128)(2,1)S(1)}, bf16[384,1024]{1,0:T(8,128)(2,1)}, u32[]{:S(2)}, u32[]{:S(2)}) collective-permute-start(bf16[384,1024]{1,0:T(8,128)(2,1)S(1)} %collective-permute-done.5.right.refs_2_), channel_id=1, source_target_pairs={{0,1},{1,0},{2,3},{3,2},{4,5},{5,4},{6,7},{7,6},{8,9},{9,8},{10,11... | collective-permute-start | bytes 2359304 | tf_op jit(solution)/shard_map/ppermute | solution.py:392
  82.0 9.9 %collective-permute-start.8 = (bf16[192,1024]{1,0:T(8,128)(2,1)}, bf16[192,1024]{1,0:T(8,128)(2,1)S(1)}, u32[]{:S(2)}, u32[]{:S(2)}) collective-permute-start(bf16[192,1024]{1,0:T(8,128)(2,1)} %get-tuple-element.31), channel_id=1, source_target_pairs={{0,2},{1,3},{2,4},{3,5},{4,6},{5,7},{6,0},{7,1},{8,10},{9,11},{10,... | collective-permute-start | bytes 1179656 | tf_op jit(solution)/shard_map/ppermute | solution.py:389
  82.0 9.9 %collective-permute-start.9 = (bf16[192,1024]{1,0:T(8,128)(2,1)}, bf16[192,1024]{1,0:T(8,128)(2,1)S(1)}, u32[]{:S(2)}, u32[]{:S(2)}) collective-permute-start(bf16[192,1024]{1,0:T(8,128)(2,1)} %get-tuple-element.32), channel_id=1, source_target_pairs={{0,6},{1,7},{2,0},{3,1},{4,2},{5,3},{6,4},{7,5},{8,14},{9,15},{10,... | collective-permute-start | bytes 1179656 | tf_op jit(solution)/shard_map/ppermute | solution.py:389
  91.9 10.7 %copy-start.5 = (bf16[192,1024]{1,0:T(8,128)(2,1)}, bf16[192,1024]{1,0:T(8,128)(2,1)S(1)}, u32[]{:S(2)}) copy-start(bf16[192,1024]{1,0:T(8,128)(2,1)S(1)} %collective-permute-done.8.far_a) | copy-start | bytes 1179652
  91.9 10.7 %collective-permute-start.10 = (bf16[192,1024]{1,0:T(8,128)(2,1)S(1)}, bf16[192,1024]{1,0:T(8,128)(2,1)S(1)}, u32[]{:S(2)}, u32[]{:S(2)}) collective-permute-start(bf16[192,1024]{1,0:T(8,128)(2,1)S(1)} %collective-permute-done.8.far_a), channel_id=1, source_target_pairs={{0,1},{1,0},{2,3},{3,2},{4,5},{5,4},{6,7},{7,6},{8,9},{9,8},{10,11... | collective-permute-start | bytes 1179656 | tf_op jit(solution)/shard_map/ppermute | solution.py:392
  91.9 10.7 %copy-start.6 = (bf16[192,1024]{1,0:T(8,128)(2,1)}, bf16[192,1024]{1,0:T(8,128)(2,1)S(1)}, u32[]{:S(2)}) copy-start(bf16[192,1024]{1,0:T(8,128)(2,1)S(1)} %collective-permute-done.9.far_b) | copy-start | bytes 1179652
  91.9 10.7 %collective-permute-start.11 = (bf16[192,1024]{1,0:T(8,128)(2,1)S(1)}, bf16[192,1024]{1,0:T(8,128)(2,1)S(1)}, u32[]{:S(2)}, u32[]{:S(2)}) collective-permute-start(bf16[192,1024]{1,0:T(8,128)(2,1)S(1)} %collective-permute-done.9.far_b), channel_id=1, source_target_pairs={{0,1},{1,0},{2,3},{3,2},{4,5},{5,4},{6,7},{7,6},{8,9},{9,8},{10,11... | collective-permute-start | bytes 1179656 | tf_op jit(solution)/shard_map/ppermute | solution.py:392
  92.4 0.9 copy-start.4
  102.7 0.7 copy-start.7
  102.7 0.8 copy-start.8
Sparse Core Ops, SparseCore 0:
  9.7 29.0 all-gather.2

commit v7 on v6

v7 whole, which is shorter than its diff:
```python
import functools
import math

import jax
import jax.numpy as jnp
from jax import lax
from jax.experimental import pallas as pl
from jax.experimental.pallas import tpu as pltpu
from jax.sharding import PartitionSpec as P

ROW_TOKENS = 128
LANES = 128
VMEM_LIMIT = 44 * 2**20
BASE_ROOM = 16
SMALL_LIMIT = 18 * 2**20


adapter_scale = 2.0

ANY = pl.BlockSpec(memory_space=pl.ANY)
HBM = pl.BlockSpec(memory_space=pltpu.HBM)
VMEM = pl.BlockSpec(memory_space=pltpu.VMEM)
SMEM = pl.BlockSpec(memory_space=pltpu.SMEM)


def dot_minor(left, right):
    return lax.dot_general(
        left, right, (((1,), (1,)), ((), ())), preferred_element_type=jnp.float32
    )


def halves_kernel(left, right, token, token_too, top, bottom, left_out, right_out, buffer, sem):
    half = top.shape[0]
    parts = ((left.at[pl.ds(0, half)], top), (right.at[pl.ds(half, half)], bottom))
    loads = [
        pltpu.make_async_copy(part, buffer.at[i], sem.at[i]) for i, (part, _) in enumerate(parts)
    ]
    stores = [
        pltpu.make_async_copy(buffer.at[i], out, sem.at[2 + i]) for i, (_, out) in enumerate(parts)
    ]
    for load in loads:
        load.start()
    for load, store in zip(loads, stores):
        load.wait()
        store.start()
    for store in stores:
        store.wait()


def take_halves(left, right, *tokens):
    half = jax.ShapeDtypeStruct((left.shape[0] // 2, left.shape[1]), left.dtype)
    return pl.pallas_call(
        halves_kernel,
        in_specs=[ANY] * 4,
        out_specs=[HBM] * 2 + [ANY] * 2,
        out_shape=[half] * 2 + [jax.ShapeDtypeStruct(left.shape, left.dtype)] * 2,
        input_output_aliases={0: 2, 1: 3},
        scratch_shapes=[
            pltpu.VMEM((2,) + half.shape, half.dtype),
            pltpu.SemaphoreType.DMA((4,)),
        ],
        compiler_params=pltpu.CompilerParams(vmem_limit_bytes=SMALL_LIMIT),
        cost_estimate=pl.CostEstimate(
            flops=0, bytes_accessed=8 * left.shape[0] * left.shape[1], transcendentals=0
        ),
        name="take_halves",
    )(left, right, *tokens)


def block_kernel(table, first, index, *refs):
    refs = list(refs)
    count = len(table)
    blocks = [refs.pop(0) for _ in range(count)]
    weight, up, _ = refs.pop(0), refs.pop(0), refs.pop(0)
    if not first:
        sums_in = refs.pop(0)
    sums_out, done, x, w, u, sums, sums_was, x_sem, w_sem, u_sem, sem = refs
    tokens, width = x.shape[1:]
    out_width, rank = w.shape[1], u.shape[1]
    done[...] = jnp.zeros_like(done)
    copies = []
    for k, place in enumerate(table):
        owner = index[place]
        columns = pl.ds(pl.multiple_of(owner * width, width), width)
        copies.append([
            pltpu.make_async_copy(blocks[k], x.at[k], x_sem.at[k]),
            pltpu.make_async_copy(weight.at[:, columns], w.at[k % 3], w_sem.at[k]),
            pltpu.make_async_copy(up.at[owner], u.at[k], u_sem.at[k]),
        ])
    if not first:
        copies.append([pltpu.make_async_copy(sums_in.at[pl.ds(0, tokens)], sums_was, sem.at[0])])
    for each in copies[:2]:
        for copy in each:
            copy.start()
    for k in range(count):
        for copy in copies[k]:
            copy.wait()
        if k + 2 < len(copies):
            for copy in copies[k + 2]:
                copy.start()
        value, value_low = dot_minor(x[k], w[k % 3]), dot_minor(x[k], u[k])
        if k > 0:
            sums[:, :out_width] += value
            sums[:, out_width : out_width + rank] += value_low
        else:
            sums[:, :out_width] = value
            sums[:, out_width : out_width + rank] = value_low
    if not first:
        copies[count][0].wait()
        sums[...] += sums_was[...]
    store = pltpu.make_async_copy(sums, sums_out.at[pl.ds(0, tokens)], sem.at[1])
    store.start()
    store.wait()


def block_products(index, table, blocks, weight, up_all, token, sums=None, name=""):
    count = len(blocks)
    tokens, width = blocks[0].shape
    out_width = weight.shape[0]
    rank = up_all.shape[1]
    first = sums is None
    return pl.pallas_call(
        functools.partial(block_kernel, table, first),
        in_specs=[SMEM] + [ANY] * (count + (3 if first else 4)),
        out_specs=[HBM, VMEM],
        out_shape=[
            jax.ShapeDtypeStruct((BASE_ROOM * tokens, out_width + LANES), jnp.float32),
            jax.ShapeDtypeStruct((8, LANES), jnp.float32),
        ],
        scratch_shapes=[
            pltpu.VMEM((count, tokens, width), jnp.bfloat16),
            pltpu.VMEM((3, out_width, width), jnp.bfloat16),
            pltpu.VMEM((count, rank, width), jnp.bfloat16),
            pltpu.VMEM((tokens, out_width + LANES), jnp.float32),
            pltpu.VMEM((tokens, out_width + LANES), jnp.float32),
            pltpu.SemaphoreType.DMA((count,)),
            pltpu.SemaphoreType.DMA((count,)),
            pltpu.SemaphoreType.DMA((count,)),
            pltpu.SemaphoreType.DMA((2,)),
        ],
        compiler_params=pltpu.CompilerParams(vmem_limit_bytes=VMEM_LIMIT),
        cost_estimate=pl.CostEstimate(
            flops=2 * count * tokens * width * out_width,
            bytes_accessed=2 * width * count * (tokens + out_width),
            transcendentals=0,
        ),
        name=name,
    )(index, *blocks, weight, up_all, token, *([] if first else [sums]))


def last_kernel(
    rows, scale, table, index, far_a, far_b, other_a, other_b, grads_in, weight, up, sums_in, down,
    out, x, w, u, sums, grads, low_rounded, x_sem, w_sem, u_sem, sem,
):
    half, width = far_a.shape
    out_width, rank = w.shape[0], u.shape[0]
    tokens = 2 * half
    piece = tokens // rows
    tile = 2 * LANES
    tiles = out_width // tile

    def load_sums(columns, semaphore):
        return pltpu.make_async_copy(
            sums_in.at[pl.ds(0, tokens), columns], sums.at[:, columns], semaphore
        )

    copies = []
    for i, part in enumerate((far_a, far_b, other_a, other_b)):
        rows_of, lanes = pl.ds((i % 2) * half, half), pl.ds((i // 2) * width, width)
        copies.append(pltpu.make_async_copy(part, x.at[rows_of, lanes], x_sem.at[i]))
    for k in range(2):
        lanes = pl.ds(k * width, width)
        copies.append(pltpu.make_async_copy(up.at[index[table[k]]], u.at[:, lanes], u_sem.at[k]))
    copies.append(load_sums(pl.ds(out_width, LANES), sem.at[tiles]))
    tile_copies = []
    for n in range(tiles):
        span = pl.ds(n * tile, tile)
        each = []
        for k in range(2):
            columns = pl.ds(pl.multiple_of(index[table[k]] * width, width), width)
            lanes = pl.ds(k * width, width)
            each.append(
                pltpu.make_async_copy(weight.at[span, columns], w.at[span, lanes], w_sem.at[n, k])
            )
        each.append(load_sums(span, sem.at[n]))
        tile_copies.append(each)
    load_grads = pltpu.make_async_copy(grads_in, grads, sem.at[tiles + 1])
    for each in [copies] + tile_copies + [[load_grads]]:
        for copy in each:
            copy.start()
    out[...] = jnp.zeros_like(out)
    for copy in copies:
        copy.wait()
    total = sums[:, out_width : out_width + rank] + dot_minor(x[...], u[...])
    low_rounded[...] = total.astype(jnp.bfloat16)
    for n in range(tiles):
        span = slice(n * tile, (n + 1) * tile)
        for copy in tile_copies[n]:
            copy.wait()
        total = sums[:, span] + dot_minor(x[...], w[span])
        total += adapter_scale * jnp.dot(
            low_rounded[...], down[:, span], preferred_element_type=jnp.float32
        )
        for row in range(rows):
            mine = total[row * piece : (row + 1) * piece]
            folded = jnp.concatenate([mine[:, :LANES], mine[:, LANES:]], axis=0)
            out[index[row], index[rows + row], :, n * LANES : (n + 1) * LANES] = folded.astype(
                jnp.bfloat16
            )
    load_grads.wait()
    total = scale * jnp.sum(grads[...], axis=0)
    folded = jnp.concatenate([total[:, : width // 2], total[:, width // 2 :]], axis=0)
    folded = folded.astype(jnp.bfloat16)
    for group in range(out.shape[0]):
        out[group, out.shape[1] - 1] = folded


def last_products(
    rows, scale, index, table, far, other, grads, weight, up, sums, down, groups, slots
):
    half, width = far[0].shape
    tokens = 2 * half
    rank, out_width = down.shape
    piece = tokens // rows
    tiles = out_width // (2 * LANES)
    return pl.pallas_call(
        functools.partial(last_kernel, rows, scale, table),
        in_specs=[SMEM] + [ANY] * 8 + [VMEM],
        out_specs=VMEM,
        scratch_shapes=[
            pltpu.VMEM((tokens, 2 * width), jnp.bfloat16),
            pltpu.VMEM((out_width, 2 * width), jnp.bfloat16),
            pltpu.VMEM((rank, 2 * width), jnp.bfloat16),
            pltpu.VMEM((tokens, out_width + LANES), jnp.float32),
            pltpu.VMEM(grads.shape, grads.dtype),
            pltpu.VMEM((tokens, rank), jnp.bfloat16),
            pltpu.SemaphoreType.DMA((4,)),
            pltpu.SemaphoreType.DMA((tiles, 2)),
            pltpu.SemaphoreType.DMA((2,)),
            pltpu.SemaphoreType.DMA((tiles + 2,)),
        ],
        out_shape=jax.ShapeDtypeStruct(
            (groups, slots + 1, 2 * piece, out_width // 2), jnp.bfloat16
        ),
        compiler_params=pltpu.CompilerParams(vmem_limit_bytes=VMEM_LIMIT),
        cost_estimate=pl.CostEstimate(
            flops=4 * tokens * width * out_width,
            bytes_accessed=4 * width * tokens + 8 * tokens * out_width,
            transcendentals=0,
        ),
        name="last_products",
    )(index, *far, *other, grads, weight, up, sums, down)


def send_kernel(groups, pick_at, index, share, out):
    for group in range(groups):
        for kind in range(2):
            pick = index[pick_at + 2 * group + kind]
            lanes = pl.ds(pl.multiple_of(jnp.maximum(pick, 0) * ROW_TOKENS, ROW_TOKENS), ROW_TOKENS)
            keep = (pick >= 0).astype(jnp.float32)
            out[group, kind] = (share[:, lanes] * keep).astype(jnp.bfloat16)


def rank_sums_to_send(index, pick_at, groups, share):
    half = share.shape[0]
    return pl.pallas_call(
        functools.partial(send_kernel, groups, pick_at),
        in_specs=[SMEM, VMEM],
        out_specs=VMEM,
        out_shape=jax.ShapeDtypeStruct((groups, 2, half, ROW_TOKENS), jnp.bfloat16),
        compiler_params=pltpu.CompilerParams(vmem_limit_bytes=SMALL_LIMIT),
        cost_estimate=pl.CostEstimate(
            flops=2 * groups * half * ROW_TOKENS, bytes_accessed=8 * groups * half * ROW_TOKENS,
            transcendentals=0,
        ),
        name="rank_sums_to_send",
    )(index, share)


def gradient_kernel(
    core_at, source_at, dest_at, index, crossed, crossed_other, token, attention, gradient, out,
    low, projected, tokens, more, sem,
):
    half = crossed.shape[2]
    rank = 2 * half
    core = index[core_at]
    halves = [
        (pl.ds(pl.multiple_of(owner * half, half), half), part)
        for owner, part in ((core, crossed), (1 - core, crossed_other))
    ]
    copies = [
        pltpu.make_async_copy(attention, tokens, sem.at[0]),
        pltpu.make_async_copy(gradient, more, sem.at[1]),
    ]
    for copy in copies:
        copy.start()
    for s in range(tokens.shape[0] // ROW_TOKENS):
        source = index[source_at + s]
        keep = (source >= 0).astype(jnp.float32)
        for ranks, part in halves:
            value = part[jnp.maximum(source, 0), 0].astype(jnp.float32) * keep
            low[ranks, s * ROW_TOKENS : (s + 1) * ROW_TOKENS] = value.astype(jnp.bfloat16)
    for r in range(more.shape[0] // ROW_TOKENS):
        for ranks, part in halves:
            projected[ranks, r * ROW_TOKENS : (r + 1) * ROW_TOKENS] = part[index[dest_at + r], 1]
    copies[0].wait()
    out[:rank] = jnp.dot(low[...], tokens[...], preferred_element_type=jnp.float32)
    copies[1].wait()
    out[rank:] = jnp.dot(projected[...], more[...], preferred_element_type=jnp.float32)


def gradient_products(
    index, core_at, source_at, dest_at, crossed, other, token, attention, gradient
):
    rank = 2 * crossed.shape[2]
    slot_tokens, width = attention.shape
    row_tokens = gradient.shape[0]
    return pl.pallas_call(
        functools.partial(gradient_kernel, core_at, source_at, dest_at),
        in_specs=[SMEM, VMEM, VMEM, ANY, ANY, ANY],
        out_specs=VMEM,
        out_shape=jax.ShapeDtypeStruct((2 * rank, width), jnp.float32),
        scratch_shapes=[
            pltpu.VMEM((rank, slot_tokens), jnp.bfloat16),
            pltpu.VMEM((rank, row_tokens), jnp.bfloat16),
            pltpu.VMEM(attention.shape, jnp.bfloat16),
            pltpu.VMEM(gradient.shape, jnp.bfloat16),
            pltpu.SemaphoreType.DMA((2,)),
        ],
        compiler_params=pltpu.CompilerParams(vmem_limit_bytes=SMALL_LIMIT),
        cost_estimate=pl.CostEstimate(
            flops=2 * rank * width * (slot_tokens + row_tokens),
            bytes_accessed=2 * width * (slot_tokens + row_tokens),
            transcendentals=0,
        ),
        name="gradient_products",
    )(index, crossed, other, token, attention, gradient)


def unfold_kernel(slots, arrived, out, down_gradient, up_gradient):
    groups, _, folded, half_width = arrived.shape
    piece = folded // 2
    step = pl.program_id(0)

    @pl.when(step < slots)
    def _():
        for pair in range(groups // 2):
            halves = []
            for j in (2 * pair, 2 * pair + 1):
                value = arrived[j, 0].astype(jnp.float32)
                pieces = []
                for n in range(half_width // LANES):
                    lanes = slice(n * LANES, (n + 1) * LANES)
                    pieces += [value[:piece, lanes], value[piece:, lanes]]
                halves.append(jnp.concatenate(pieces, axis=1))
            out[pl.ds(pair * folded, folded), :] = jnp.concatenate(halves, axis=0).astype(out.dtype)

    @pl.when(step == slots)
    def _():
        values = []
        for j in range(groups):
            value = arrived[j, 0].astype(jnp.float32)
            values.append(jnp.concatenate([value[:piece], value[piece:]], axis=1))
        down_gradient[...] = jnp.concatenate(values[: groups // 2], axis=0)
        up_gradient[...] = jnp.concatenate(values[groups // 2 :], axis=0)


def unfold(arrived, slots):
    groups, _, folded, half_width = arrived.shape
    piece, width = folded // 2, 2 * half_width
    rank = groups * piece // 2
    return pl.pallas_call(
        functools.partial(unfold_kernel, slots),
        grid=(slots + 1,),
        in_specs=[pl.BlockSpec((groups, 1, folded, half_width), lambda s: (0, s, 0, 0))],
        out_specs=[
            pl.BlockSpec((groups * piece, width), lambda s: (jnp.minimum(s, slots - 1), 0)),
            pl.BlockSpec((rank, width), lambda s: (0, 0)),
            pl.BlockSpec((rank, width), lambda s: (0, 0)),
        ],
        out_shape=[
            jax.ShapeDtypeStruct((slots * groups * piece, width), jnp.bfloat16),
            jax.ShapeDtypeStruct((rank, width), jnp.float32),
            jax.ShapeDtypeStruct((rank, width), jnp.float32),
        ],
        compiler_params=pltpu.CompilerParams(vmem_limit_bytes=SMALL_LIMIT),
        name="unfold",
    )(arrived)


def body(
    attention_slot_outputs,
    output_gradient_rows,
    output_weight,
    down_weight,
    up_weight,
    assign,
    counts,
):
    groups = counts.shape[0]
    rows = assign.shape[0]
    rows_here = output_gradient_rows.shape[0] // ROW_TOKENS
    slot_cap = attention_slot_outputs.shape[0] // ROW_TOKENS
    width_here = output_gradient_rows.shape[1]
    rank = up_weight.shape[0]
    tp = lax.axis_size("tp")
    piece = ROW_TOKENS // groups
    own_group = lax.axis_index("group")
    group_ids = jnp.arange(groups, dtype=jnp.int32)
    onehot = (assign[:, None] == group_ids[None, :]).astype(jnp.int32)
    before = jnp.cumsum(onehot, axis=0) - onehot
    order_in = jnp.sum(before * onehot, axis=1)
    free_slots = jnp.sum(onehot * counts[None, :], axis=1)
    position = slot_cap - free_slots + order_in
    own_dest = lax.dynamic_slice_in_dim(assign, own_group * rows_here, rows_here)
    scale_factor = adapter_scale / math.sqrt(rows * ROW_TOKENS)

    index = lax.axis_index("tp")
    chips = tp // 2
    y, core = index // 2, index % 2

    def move(value, n):
        pairs = [(2 * a + b, 2 * ((a + n) % chips) + b) for a in range(chips) for b in range(2)]
        return lax.ppermute(value, "tp", pairs)

    def swap(value):
        return lax.ppermute(value, "tp", [(i, i ^ 1) for i in range(tp)])

    pieces_out = output_gradient_rows.reshape(rows_here, groups, piece, width_here)
    pieces_out = pieces_out.transpose(1, 0, 2, 3)
    pieces_out, up_weight, down_weight_first = lax.optimization_barrier(
        (pieces_out, up_weight, down_weight)
    )
    spread = lax.all_to_all(
        pieces_out,
        "group",
        split_axis=0,
        concat_axis=0,
        tiled=True,
    ).reshape(rows * piece, width_here)

    slot_ids = jnp.arange(slot_cap, dtype=jnp.int32)
    row_ids = jnp.arange(rows_here, dtype=jnp.int32)
    row_position = position.reshape(groups, rows_here)
    hit_row = assign.reshape(groups, rows_here) == own_group
    low_pick = jnp.max(jnp.where(own_dest[None, :] == group_ids[:, None], row_ids, -1), axis=1)
    projected_pick = jnp.max(jnp.where(hit_row, rows_here + row_position, -1), axis=1)
    slot_match = hit_row[:, :, None] & (row_position[:, :, None] == slot_ids)
    slot_source = jnp.max(jnp.where(slot_match, group_ids[:, None, None], -1), axis=(0, 1))
    owners = []
    for step in (0, chips - 1, 1, 2):
        pair = 2 * lax.rem(y + step, chips)
        owners += [pair + core, pair + 1 - core]
    pieces = [
        assign, position, jnp.stack([low_pick, projected_pick], axis=1).reshape(-1), slot_source,
        own_dest, jnp.stack(owners + [core]).astype(jnp.int32),
    ]
    at = [0]
    for part in pieces:
        at.append(at[-1] + part.shape[0])
    _, _, pick_at, source_at, dest_at, owner_at, end = at
    table = jnp.concatenate(pieces)

    up_all = lax.all_gather(up_weight, "tp", axis=0)
    low_part = dot_minor(up_weight, output_gradient_rows)
    projected_part = lax.dot_general(
        down_weight_first, attention_slot_outputs, (((0,), (1,)), ((), ())),
        preferred_element_type=jnp.float32,
    )
    parts = jnp.concatenate([low_part, projected_part], axis=1)
    parts = parts + swap(parts)
    share = lax.dynamic_slice_in_dim(parts, core * (rank // 2), rank // 2, axis=0)
    share = share + move(share, 1) + move(share, -1) + move(share, 2)

    send = rank_sums_to_send(table, pick_at, groups, share)
    crossed = lax.all_to_all(send, "group", split_axis=0, concat_axis=0, tiled=True)

    spread, _ = lax.optimization_barrier((spread, share))
    left, right = move(spread, 1), move(spread, -1)
    other = swap(spread)
    sums, done = block_products(
        table, [owner_at, owner_at + 1], [spread, other], output_weight, up_all, send,
        name="own_products",
    )
    crossed_other = swap(crossed)
    left_top, right_bottom, left, right = take_halves(left, right, crossed, done)
    far = [move(left_top, 1), move(right_bottom, -1)]
    partial_grads = gradient_products(
        table, end - 1, source_at, dest_at, crossed, crossed_other, left_top, attention_slot_outputs,
        output_gradient_rows,
    )
    share_rows = 2 * rank // groups
    grads = lax.all_to_all(
        partial_grads.reshape(groups, share_rows, width_here), "group", split_axis=0, concat_axis=0,
        tiled=True,
    )
    sums, _ = block_products(
        table, [owner_at + i for i in range(2, 6)], [left, swap(left), right, swap(right)],
        output_weight, up_all, partial_grads, sums, name="side_products",
    )
    placed = last_products(
        rows, scale_factor, table, [owner_at + 6, owner_at + 7], far, [swap(part) for part in far],
        grads, output_weight, up_all, sums, down_weight.T, groups, slot_cap,
    )

    arrived = lax.all_to_all(placed, "group", split_axis=0, concat_axis=0, tiled=True)
    attention_gradient, down_gradient, up_gradient = unfold(arrived, slot_cap)
    return attention_gradient, down_gradient.T, up_gradient


def solution(mesh):
    in_specs = (
        P("group", "tp"),
        P("group", "tp"),
        P("tp", None),
        P("tp", None),
        P(None, "tp"),
        P(),
        P(),
    )
    out_specs = (P("group", "tp"), P("tp", None), P(None, "tp"))
    return jax.shard_map(body, mesh=mesh, in_specs=in_specs, out_specs=out_specs, check_vma=False)
```

time: 159 us -> 136 us (0.86)
  blocking collectives: 50.8 us -> 32.5 us
  starting transfers between devices: 25.2 us -> 32.8 us
  waiting for transfers between devices: 20 us -> 13.8 us
  Pallas kernels: 37.5 us -> 31.7 us
    all_to_all x1 -> x0, blocking collectives: 18.3 us -> none  [body(): lax.all_to_all(rank_sums_to_send(table, end - 1, pick_at, groups, share,...]
    all_to_all x2 -> x3, starting transfers between devices: 11.5 us -> 20.5 us  [the longest x1 7.97 us: body(): lax.all_to_all(pieces_out, 'group', split_axis=0, concat_axis=0, tiled=True)]
    ppermute x7, waiting for transfers between devices: 15.8 us -> 10.2 us  [move(): return lax.ppermute(value, 'tp', pairs)]
    pallas_call x4, Pallas kernels: 16.8 us -> 12 us  [the longest x1 7.24 us: last_products(): pl.pallas_call(functools.partial(last_kernel, rows, scale, table), in_spe...]
    pallas_call x1, Pallas kernels: 5.26 us -> 3.18 us  [unfold(): pl.pallas_call(functools.partial(unfold_kernel, slots), grid=(slots + 1,)...]
    ppermute x7, waiting for transfers between devices: 0.02 us -> 1.75 us  [swap(): return lax.ppermute(value, 'tp', [(i, i ^ 1) for i in range(tp)])]
    all_to_all x2 -> x3, waiting for transfers between devices: 3.45 us -> 1.84 us  [the longest x1 1.08 us: body(): lax.all_to_all(send, 'group', split_axis=0, concat_axis=0, tiled=True)]
    unnamed x26 -> x22, local copies, waits for them, and re-layouts: 2.43 us -> 4.03 us
  transfers between devices with their start and end apart: 17 -> 18, of which waited for: 4 -> 8; matrix products, arithmetic and copies ran while one was open for 4% -> 1% of each run, Pallas kernels for 15% -> 14%
where the time goes in v7:
time: 136 us; the launch traced here: 135 us
  starting transfers between devices  32.8 us (24%)
  blocking collectives  32.5 us (24%)
  Pallas kernels  31.7 us (23%)
  between operations  14.4 us (11%)
  waiting for transfers between devices  13.8 us (10%)
  local copies, waits for them, and re-layouts  6.9 us (5%)
  matrix products  2.16 us (2%)
    all_to_all x1, blocking collectives, body(): lax.all_to_all(placed, 'group', split_axis=0, concat_axis=0, tiled=True)  32.5 us
    pallas_call x2, Pallas kernels, block_products(): pl.pallas_call(functools.partial(block_kernel, table, first), in_specs=[S...  16.5 us
    ppermute x7, starting transfers between devices, move(): return lax.ppermute(value, 'tp', pairs)  11.5 us
    ppermute x7, waiting for transfers between devices, move(): return lax.ppermute(value, 'tp', pairs)  10.2 us
    all_to_all x1, starting transfers between devices, body(): lax.all_to_all(pieces_out, 'group', split_axis=0, concat_axis=0, tiled=True)  7.97 us
    pallas_call x1, Pallas kernels, last_products(): pl.pallas_call(functools.partial(last_kernel, rows, scale, table), in_spe...  7.24 us
    all_to_all x1, starting transfers between devices, body(): lax.all_to_all(send, 'group', split_axis=0, concat_axis=0, tiled=True)  6.34 us
    all_to_all x1, starting transfers between devices, body(): lax.all_to_all(partial_grads.reshape(groups, share_rows, width_here), 'gr...  6.2 us
  transfers between devices with their start and end apart: 18, of which 8 were waited for; matrix products, arithmetic and copies ran while one was open for 1% of the time, Pallas kernels for 14%

profile of v7, /device:TPU:0, one launch (start us, length us, event | category | flops | bytes accessed | tf_op | source)
XLA Modules:
  0.0 135.0 jit_solution(4523728205390417462)
XLA Ops:
  7.2 2.2 %copy.21 = bf16[3,16,8,1024]{3,2,0,1:T(8,128)(2,1)} copy(bf16[3,16,8,1024]{3,2,1,0:T(8,128)(2,1)} %bitcast.27) | data formatting | bytes 1572864 | tf_op jit(solution)/shard_map/reshape | solution.py:429
  9.4 1.6 %fusion.4 = f32[64,384]{1,0:T(8,128)S(1)} fusion(bf16[64,1024]{1,0:T(8,128)(2,1)} %param.11, bf16[384,1024]{1,0:T(8,128)(2,1)} %gradient.1), kind=kOutput, calls=%fused_computation.20 | convolution fusion | flops 50331648 | bytes 1015808 | tf_op jit(solution)/shard_map/dot_general | solution.py:27
  11.0 0.6 fusion.5
  11.8 8.0 %all-to-all-start = ((bf16[16,3,8,1024]{3,2,1,0:T(8,128)(2,1)}), bf16[16,3,8,1024]{3,2,1,0:T(8,128)(2,1)S(1)}, u32[]{:S(2)}, u32[]{:S(2)}) async-start(bf16[16,3,8,1024]{3,2,1,0:T(8,128)(2,1)} %bitcast.23), calls=%async_computation | async-start | bytes 1572864 | tf_op jit(solution)/shard_map/all_to_all | solution.py:434
  19.8 1.6 %collective-permute-start.1 = (f32[32,1152]{1,0:T(8,128)S(1)}, f32[32,1152]{1,0:T(8,128)S(1)}, u32[]{:S(2)}, u32[]{:S(2)}) collective-permute-start(f32[32,1152]{1,0:T(8,128)S(1)} %fusion.1), channel_id=1, source_target_pairs={{0,2},{1,3},{2,4},{3,5},{4,6},{5,7},{6,0},{7,1},{8,10},{9,11},{10,... | collective-permute-start | bytes 442376 | tf_op jit(solution)/shard_map/ppermute | solution.py:424
  21.5 1.7 %collective-permute-start.2 = (f32[32,1152]{1,0:T(8,128)S(1)}, f32[32,1152]{1,0:T(8,128)S(1)}, u32[]{:S(2)}, u32[]{:S(2)}) collective-permute-start(f32[32,1152]{1,0:T(8,128)S(1)} %fusion.1), channel_id=1, source_target_pairs={{0,6},{1,7},{2,0},{3,1},{4,2},{5,3},{6,4},{7,5},{8,14},{9,15},{10,... | collective-permute-start | bytes 442376 | tf_op jit(solution)/shard_map/ppermute | solution.py:424
  23.1 2.0 %collective-permute-start.3 = (f32[32,1152]{1,0:T(8,128)S(1)}, f32[32,1152]{1,0:T(8,128)S(1)}, u32[]{:S(2)}, u32[]{:S(2)}) collective-permute-start(f32[32,1152]{1,0:T(8,128)S(1)} %fusion.1), channel_id=1, source_target_pairs={{0,4},{1,5},{2,6},{3,7},{4,0},{5,1},{6,2},{7,3},{8,12},{9,13},{10,... | collective-permute-start | bytes 442376 | tf_op jit(solution)/shard_map/ppermute | solution.py:424
  25.5 1.7 %collective-permute-done.1 = f32[32,1152]{1,0:T(8,128)S(1)} collective-permute-done((f32[32,1152]{1,0:T(8,128)S(1)}, f32[32,1152]{1,0:T(8,128)S(1)}, u32[]{:S(2)}, u32[]{:S(2)}) %collective-permute-start.1) | collective-permute-done | bytes 147488 | tf_op jit(solution)/shard_map/ppermute | solution.py:424
  27.1 2.9 %collective-permute-done.2 = f32[32,1152]{1,0:T(8,128)S(1)} collective-permute-done((f32[32,1152]{1,0:T(8,128)S(1)}, f32[32,1152]{1,0:T(8,128)S(1)}, u32[]{:S(2)}, u32[]{:S(2)}) %collective-permute-start.2) | collective-permute-done | bytes 147488 | tf_op jit(solution)/shard_map/ppermute | solution.py:424
  30.0 4.0 %collective-permute-done.3 = f32[32,1152]{1,0:T(8,128)S(1)} collective-permute-done((f32[32,1152]{1,0:T(8,128)S(1)}, f32[32,1152]{1,0:T(8,128)S(1)}, u32[]{:S(2)}, u32[]{:S(2)}) %collective-permute-start.3) | collective-permute-done | bytes 147488 | tf_op jit(solution)/shard_map/ppermute | solution.py:424
  34.0 0.8 all-to-all-done
  34.8 1.6 %collective-permute-start.4 = (bf16[384,1024]{1,0:T(8,128)(2,1)S(1)}, bf16[384,1024]{1,0:T(8,128)(2,1)}, u32[]{:S(2)}, u32[]{:S(2)}) collective-permute-start(bf16[384,1024]{1,0:T(8,128)(2,1)S(1)} %bitcast.30), channel_id=1, source_target_pairs={{0,2},{1,3},{2,4},{3,5},{4,6},{5,7},{6,0},{7,1},{8,10},{9,11},{10,... | collective-permute-start | bytes 2359304 | tf_op jit(solution)/shard_map/ppermute | solution.py:424
  36.4 1.7 %collective-permute-start.5 = (bf16[384,1024]{1,0:T(8,128)(2,1)S(1)}, bf16[384,1024]{1,0:T(8,128)(2,1)}, u32[]{:S(2)}, u32[]{:S(2)}) collective-permute-start(bf16[384,1024]{1,0:T(8,128)(2,1)S(1)} %bitcast.31), channel_id=1, source_target_pairs={{0,6},{1,7},{2,0},{3,1},{4,2},{5,3},{6,4},{7,5},{8,14},{9,15},{10,... | collective-permute-start | bytes 2359304 | tf_op jit(solution)/shard_map/ppermute | solution.py:424
  39.1 1.4 %rank_sums_to_send.1.refs_4_ = bf16[16,2,32,128]{3,2,1,0:T(8,128)(2,1)} custom-call(s32[146]{0:T(256)S(1)} %concatenate.6.index, f32[32,1152]{1,0:T(8,128)S(1)} %add_add_fusion.share), custom_call_target="tpu_custom_call" | custom-call | flops 131072 | bytes 524288 | tf_op jit(solution)/shard_map/rank_sums_to_send/pallas_call | solution.py:266
  40.5 6.3 %all-to-all-start.1 = ((bf16[16,2,32,128]{3,2,1,0:T(8,128)(2,1)}), bf16[16,2,32,128]{3,2,1,0:T(8,128)(2,1)S(1)}, u32[]{:S(2)}, u32[]{:S(2)}) async-start(bf16[16,2,32,128]{3,2,1,0:T(8,128)(2,1)} %rank_sums_to_send.1.refs_4_), calls=%async_computation.1 | async-start | bytes 524288 | tf_op jit(solution)/shard_map/all_to_all | solution.py:476
  46.9 1.2 copy-done
  48.1 6.4 %own_products.1 = (f32[6144,1152]{1,0:T(8,128)}, f32[8,128]{1,0:T(8,128)S(1)}) custom-call(s32[146]{0:T(256)S(1)} %concatenate.6.index, bf16[384,1024]{1,0:T(8,128)(2,1)S(1)} %bitcast.32, bf16[384,1024]{1,0:T(8,128)(2,1)S(1)} %collective-permute-done.6.refs_1_, bf16[1024,8192]{1,0:T(8,128)(2,1)} %weight.1, bf16[8,64,1024]{2,1,0:T(8,128)(2,1)S(1)} %bitcast.24, ...), custom_call_target="tpu_custom_call" | custom-call | flops 1610612736 | bytes 5767168 | tf_op jit(solution)/shard_map/own_products/pallas_call | solution.py:122
  54.5 1.1 all-to-all-done.1.token.crossed
  55.5 0.6 collective-permute-done.4.left
  56.1 2.0 %take_halves.1 = (bf16[192,1024]{1,0:T(8,128)(2,1)}, bf16[192,1024]{1,0:T(8,128)(2,1)}, bf16[384,1024]{1,0:T(8,128)(2,1)}, bf16[384,1024]{1,0:T(8,128)(2,1)}) custom-call(bf16[384,1024]{1,0:T(8,128)(2,1)} %collective-permute-done.4.left, bf16[384,1024]{1,0:T(8,128)(2,1)} %collective-permute-done.5.right, ...), custom_call_target="tpu_custom_call", output_to_operand_aliasing={{2}: (0, {}), {3}: (1, {})} | custom-call | bytes 3145728 | tf_op jit(solution)/shard_map/take_halves/pallas_call | solution.py:52
  58.7 2.9 %collective-permute-start.8 = (bf16[192,1024]{1,0:T(8,128)(2,1)}, bf16[192,1024]{1,0:T(8,128)(2,1)}, u32[]{:S(2)}, u32[]{:S(2)}) collective-permute-start(bf16[192,1024]{1,0:T(8,128)(2,1)} %get-tuple-element.23), channel_id=1, source_target_pairs={{0,6},{1,7},{2,0},{3,1},{4,2},{5,3},{6,4},{7,5},{8,14},{9,15},{10,... | collective-permute-start | bytes 1179656 | tf_op jit(solution)/shard_map/ppermute | solution.py:424
  61.7 1.7 %collective-permute-done.11.crossed_other = bf16[16,2,32,128]{3,2,1,0:T(8,128)(2,1)S(1)} collective-permute-done((bf16[16,2,32,128]{3,2,1,0:T(8,128)(2,1)}, bf16[16,2,32,128]{3,2,1,0:T(8,128)(2,1)S(1)}, u32[]{:S(2)}, u32[]{:S(2)}) %collective-permute-start.11) | collective-permute-done | bytes 262176 | tf_op jit(solution)/shard_map/ppermute | solution.py:427
  63.5 0.9 copy-done.7
  64.4 1.4 %gradient_products.1.refs_6_ = f32[128,1024]{1,0:T(8,128)S(1)} custom-call(s32[146]{0:T(256)S(1)} %concatenate.6.index, bf16[16,2,32,128]{3,2,1,0:T(8,128)(2,1)S(1)} %copy-done.7, bf16[16,2,32,128]{3,2,1,0:T(8,128)(2,1)S(1)} %collective-permute-done.11.crossed_other, bf16[192,1024]{1,0:T(8,128)(2,1)} %get-tuple-element.22.token, ...), custom_call_target="tpu_custom_call" | custom-call | flops 150994944 | bytes 2359296 | tf_op jit(solution)/shard_map/gradient_products/pallas_call | solution.py:318
  65.9 0.8 copy-done.4
  66.6 6.2 %all-to-all-start.2 = ((f32[16,8,1024]{2,1,0:T(8,128)}), f32[16,8,1024]{2,1,0:T(8,128)S(1)}, u32[]{:S(2)}, u32[]{:S(2)}) async-start(f32[16,8,1024]{2,1,0:T(8,128)} %bitcast.28), calls=%async_computation.2 | async-start | bytes 1048576 | tf_op jit(solution)/shard_map/all_to_all | solution.py:493
  73.0 1.1 collective-permute-done.7.far_a
  74.0 1.0 copy-done.5
  75.1 10.2 %side_products.1 = (f32[6144,1152]{1,0:T(8,128)}, f32[8,128]{1,0:T(8,128)}) custom-call(s32[146]{0:T(256)S(1)} %concatenate.6.index, bf16[384,1024]{1,0:T(8,128)(2,1)} %get-tuple-element.24.refs_0_, bf16[384,1024]{1,0:T(8,128)(2,1)} %collective-permute-done.12.refs_1_, bf16[384,1024]{1,0:T(8,128)(2,1)} %get-tuple-element.25.refs_2_, ...), custom_call_target="tpu_custom_call" | custom-call | flops 3221225472 | bytes 11534336 | tf_op jit(solution)/shard_map/side_products/pallas_call | solution.py:122
  85.3 7.2 %last_products.1 = bf16[16,7,16,512]{3,2,1,0:T(8,128)(2,1)S(1)} custom-call(s32[146]{0:T(256)S(1)} %concatenate.6.index, bf16[192,1024]{1,0:T(8,128)(2,1)} %collective-permute-done.7.far_a, bf16[192,1024]{1,0:T(8,128)(2,1)} %collective-permute-done.8.far_b, bf16[192,1024]{1,0:T(8,128)(2,1)} %collective-permute-done.9.other_a, ...), custom_call_target="tpu_custom_call" | custom-call | flops 1610612736 | bytes 4718592 | tf_op jit(solution)/shard_map/last_products/pallas_call | solution.py:226
  92.5 32.5 %all_to_all.20.arrived = bf16[16,7,16,512]{3,2,1,0:T(8,128)(2,1)S(1)} all-to-all(bf16[16,7,16,512]{3,2,1,0:T(8,128)(2,1)S(1)} %last_products.1), channel_id=1, replica_groups=mesh['group'=16,'tp'=8] {'group'}, dimensions={0} | all-to-all | bytes 3670016 | tf_op jit(solution)/shard_map/all_to_all | solution.py:506
  125.0 3.2 %unfold.1 = (bf16[768,1024]{1,0:T(8,128)(2,1)}, f32[64,1024]{1,0:T(8,128)}, f32[64,1024]{1,0:T(8,128)}) custom-call(bf16[16,7,16,512]{3,2,1,0:T(8,128)(2,1)S(1)} %all_to_all.20.arrived), custom_call_target="tpu_custom_call" | custom-call | tf_op jit(solution)/shard_map/unfold/pallas_call | solution.py:372
  (58 shorter events, 2.5 us)
Async XLA Ops:
  7.2 3.8 %copy-start.8 = (bf16[1024,64]{0,1:T(8,128)(2,1)S(1)}, bf16[1024,64]{0,1:T(8,128)(2,1)}, u32[]{:S(2)}) copy-start(bf16[1024,64]{0,1:T(8,128)(2,1)} %param.10) | copy-start | bytes 393220
  7.2 3.8 %copy-start.3 = (bf16[768,1024]{1,0:T(8,128)(2,1)S(1)}, bf16[768,1024]{1,0:T(8,128)(2,1)}, u32[]{:S(2)}) copy-start(bf16[768,1024]{1,0:T(8,128)(2,1)} %attention.1) | copy-start | bytes 4718596
  7.2 39.7 %all-gather.3.cloned.1.call-start = ((), (), s32[]{:S(2)}) async-start(), calls=%async_computation.4 | async-start | bytes 1179648 | tf_op jit(solution)/shard_map/all_gather | solution.py:464
  11.6 13.5 %copy-start.9 = (s32[48]{0:T(128)S(1)}, s32[48]{0:T(128)}, u32[]{:S(2)}) copy-start(s32[48]{0:T(128)} %param.12) | copy-start | bytes 580
  11.6 13.6 %copy-start.10 = (s32[16]{0:T(128)S(1)}, s32[16]{0:T(128)}, u32[]{:S(2)}) copy-start(s32[16]{0:T(128)} %param.13) | copy-start | bytes 196
  11.7 8.1 %collective-permute-start = (f32[64,1152]{1,0:T(8,128)S(1)}, f32[64,1152]{1,0:T(8,128)S(1)}, u32[]{:S(2)}, u32[]{:S(2)}) collective-permute-start(f32[64,1152]{1,0:T(8,128)S(1)} %pad_maximum_fusion), channel_id=1, source_target_pairs={{0,1},{1,0},{2,3},{3,2},{4,5},{5,4},{6,7},{7,6},{8,9},{9,8},{10,11... | collective-permute-start | bytes 884744 | tf_op jit(solution)/shard_map/ppermute | solution.py:427
  11.8 23.0 %all-to-all-start = ((bf16[16,3,8,1024]{3,2,1,0:T(8,128)(2,1)}), bf16[16,3,8,1024]{3,2,1,0:T(8,128)(2,1)S(1)}, u32[]{:S(2)}, u32[]{:S(2)}) async-start(bf16[16,3,8,1024]{3,2,1,0:T(8,128)(2,1)} %bitcast.23), calls=%async_computation | async-start | bytes 1572864 | tf_op jit(solution)/shard_map/all_to_all | solution.py:434
  19.8 7.3 %collective-permute-start.1 = (f32[32,1152]{1,0:T(8,128)S(1)}, f32[32,1152]{1,0:T(8,128)S(1)}, u32[]{:S(2)}, u32[]{:S(2)}) collective-permute-start(f32[32,1152]{1,0:T(8,128)S(1)} %fusion.1), channel_id=1, source_target_pairs={{0,2},{1,3},{2,4},{3,5},{4,6},{5,7},{6,0},{7,1},{8,10},{9,11},{10,... | collective-permute-start | bytes 442376 | tf_op jit(solution)/shard_map/ppermute | solution.py:424
  21.5 8.6 %collective-permute-start.2 = (f32[32,1152]{1,0:T(8,128)S(1)}, f32[32,1152]{1,0:T(8,128)S(1)}, u32[]{:S(2)}, u32[]{:S(2)}) collective-permute-start(f32[32,1152]{1,0:T(8,128)S(1)} %fusion.1), channel_id=1, source_target_pairs={{0,6},{1,7},{2,0},{3,1},{4,2},{5,3},{6,4},{7,5},{8,14},{9,15},{10,... | collective-permute-start | bytes 442376 | tf_op jit(solution)/shard_map/ppermute | solution.py:424
  23.1 10.9 %collective-permute-start.3 = (f32[32,1152]{1,0:T(8,128)S(1)}, f32[32,1152]{1,0:T(8,128)S(1)}, u32[]{:S(2)}, u32[]{:S(2)}) collective-permute-start(f32[32,1152]{1,0:T(8,128)S(1)} %fusion.1), channel_id=1, source_target_pairs={{0,4},{1,5},{2,6},{3,7},{4,0},{5,1},{6,2},{7,3},{8,12},{9,13},{10,... | collective-permute-start | bytes 442376 | tf_op jit(solution)/shard_map/ppermute | solution.py:424
  34.8 12.0 %collective-permute-start.6 = (bf16[384,1024]{1,0:T(8,128)(2,1)S(1)}, bf16[384,1024]{1,0:T(8,128)(2,1)S(1)}, u32[]{:S(2)}, u32[]{:S(2)}) collective-permute-start(bf16[384,1024]{1,0:T(8,128)(2,1)S(1)} %bitcast.29), channel_id=1, source_target_pairs={{0,1},{1,0},{2,3},{3,2},{4,5},{5,4},{6,7},{7,6},{8,9},{9,8},{10,11... | collective-permute-start | bytes 2359304 | tf_op jit(solution)/shard_map/ppermute | solution.py:427
  34.8 21.3 %collective-permute-start.4 = (bf16[384,1024]{1,0:T(8,128)(2,1)S(1)}, bf16[384,1024]{1,0:T(8,128)(2,1)}, u32[]{:S(2)}, u32[]{:S(2)}) collective-permute-start(bf16[384,1024]{1,0:T(8,128)(2,1)S(1)} %bitcast.30), channel_id=1, source_target_pairs={{0,2},{1,3},{2,4},{3,5},{4,6},{5,7},{6,0},{7,1},{8,10},{9,11},{10,... | collective-permute-start | bytes 2359304 | tf_op jit(solution)/shard_map/ppermute | solution.py:424
  36.4 19.8 %collective-permute-start.5 = (bf16[384,1024]{1,0:T(8,128)(2,1)S(1)}, bf16[384,1024]{1,0:T(8,128)(2,1)}, u32[]{:S(2)}, u32[]{:S(2)}) collective-permute-start(bf16[384,1024]{1,0:T(8,128)(2,1)S(1)} %bitcast.31), channel_id=1, source_target_pairs={{0,6},{1,7},{2,0},{3,1},{4,2},{5,3},{6,4},{7,5},{8,14},{9,15},{10,... | collective-permute-start | bytes 2359304 | tf_op jit(solution)/shard_map/ppermute | solution.py:424
  40.5 15.1 %all-to-all-start.1 = ((bf16[16,2,32,128]{3,2,1,0:T(8,128)(2,1)}), bf16[16,2,32,128]{3,2,1,0:T(8,128)(2,1)S(1)}, u32[]{:S(2)}, u32[]{:S(2)}) async-start(bf16[16,2,32,128]{3,2,1,0:T(8,128)(2,1)} %rank_sums_to_send.1.refs_4_), calls=%async_computation.1 | async-start | bytes 524288 | tf_op jit(solution)/shard_map/all_to_all | solution.py:476
  46.9 1.2 copy-start
  54.5 9.0 %copy-start.2 = (bf16[384,1024]{1,0:T(8,128)(2,1)S(1)}, bf16[384,1024]{1,0:T(8,128)(2,1)}, u32[]{:S(2)}) copy-start(bf16[384,1024]{1,0:T(8,128)(2,1)} %gradient.1) | copy-start | bytes 2359300
  55.5 6.1 %copy-start.6 = (bf16[16,2,32,128]{3,2,1,0:T(8,128)(2,1)}, bf16[16,2,32,128]{3,2,1,0:T(8,128)(2,1)S(1)}, u32[]{:S(2)}) copy-start(bf16[16,2,32,128]{3,2,1,0:T(8,128)(2,1)S(1)} %all-to-all-done.1.token.crossed) | copy-start | bytes 786436
  58.1 15.9 %collective-permute-start.12 = (bf16[384,1024]{1,0:T(8,128)(2,1)}, bf16[384,1024]{1,0:T(8,128)(2,1)}, u32[]{:S(2)}, u32[]{:S(2)}) collective-permute-start(bf16[384,1024]{1,0:T(8,128)(2,1)} %get-tuple-element.24.refs_0_), channel_id=1, source_target_pairs={{0,1},{1,0},{2,3},{3,2},{4,5},{5,4},{6,7},{7,6},{8,9},{9,8},{10,11... | collective-permute-start | bytes 2359304 | tf_op jit(solution)/shard_map/ppermute | solution.py:427
  58.2 15.8 %collective-permute-start.13 = (bf16[384,1024]{1,0:T(8,128)(2,1)}, bf16[384,1024]{1,0:T(8,128)(2,1)}, u32[]{:S(2)}, u32[]{:S(2)}) collective-permute-start(bf16[384,1024]{1,0:T(8,128)(2,1)} %get-tuple-element.25.refs_2_), channel_id=1, source_target_pairs={{0,1},{1,0},{2,3},{3,2},{4,5},{5,4},{6,7},{7,6},{8,9},{9,8},{10,11... | collective-permute-start | bytes 2359304 | tf_op jit(solution)/shard_map/ppermute | solution.py:427
  58.7 14.1 %collective-permute-start.8 = (bf16[192,1024]{1,0:T(8,128)(2,1)}, bf16[192,1024]{1,0:T(8,128)(2,1)}, u32[]{:S(2)}, u32[]{:S(2)}) collective-permute-start(bf16[192,1024]{1,0:T(8,128)(2,1)} %get-tuple-element.23), channel_id=1, source_target_pairs={{0,6},{1,7},{2,0},{3,1},{4,2},{5,3},{6,4},{7,5},{8,14},{9,15},{10,... | collective-permute-start | bytes 1179656 | tf_op jit(solution)/shard_map/ppermute | solution.py:424
  61.6 12.4 %copy-start.1 = (bf16[512,1024]{1,0:T(8,128)(2,1)S(1)}, bf16[512,1024]{1,0:T(8,128)(2,1)}, u32[]{:S(2)}) copy-start(bf16[512,1024]{1,0:T(8,128)(2,1)} %all-gather.3.cloned.1.call-done) | copy-start | bytes 3145732
  61.6 12.4 %collective-permute-start.7 = (bf16[192,1024]{1,0:T(8,128)(2,1)}, bf16[192,1024]{1,0:T(8,128)(2,1)}, u32[]{:S(2)}, u32[]{:S(2)}) collective-permute-start(bf16[192,1024]{1,0:T(8,128)(2,1)} %get-tuple-element.22.token), channel_id=1, source_target_pairs={{0,2},{1,3},{2,4},{3,5},{4,6},{5,7},{6,0},{7,1},{8,10},{9,11},{10,... | collective-permute-start | bytes 1179656 | tf_op jit(solution)/shard_map/ppermute | solution.py:424
  61.7 1.8 %collective-permute-start.11 = (bf16[16,2,32,128]{3,2,1,0:T(8,128)(2,1)}, bf16[16,2,32,128]{3,2,1,0:T(8,128)(2,1)S(1)}, u32[]{:S(2)}, u32[]{:S(2)}) collective-permute-start(bf16[16,2,32,128]{3,2,1,0:T(8,128)(2,1)} %copy-done.6), channel_id=1, source_target_pairs={{0,1},{1,0},{2,3},{3,2},{4,5},{5,4},{6,7},{7,6},{8,9},{9,8},{10,11... | collective-permute-start | bytes 786440 | tf_op jit(solution)/shard_map/ppermute | solution.py:427
  63.5 1.0 copy-start.7
  65.9 0.8 copy-start.4
  66.6 18.6 %all-to-all-start.2 = ((f32[16,8,1024]{2,1,0:T(8,128)}), f32[16,8,1024]{2,1,0:T(8,128)S(1)}, u32[]{:S(2)}, u32[]{:S(2)}) async-start(f32[16,8,1024]{2,1,0:T(8,128)} %bitcast.28), calls=%async_computation.2 | async-start | bytes 1048576 | tf_op jit(solution)/shard_map/all_to_all | solution.py:493
  72.9 12.4 %collective-permute-start.10 = (bf16[192,1024]{1,0:T(8,128)(2,1)}, bf16[192,1024]{1,0:T(8,128)(2,1)}, u32[]{:S(2)}, u32[]{:S(2)}) collective-permute-start(bf16[192,1024]{1,0:T(8,128)(2,1)} %collective-permute-done.8.far_b), channel_id=1, source_target_pairs={{0,1},{1,0},{2,3},{3,2},{4,5},{5,4},{6,7},{7,6},{8,9},{9,8},{10,11... | collective-permute-start | bytes 1179656 | tf_op jit(solution)/shard_map/ppermute | solution.py:427
  74.0 11.3 %collective-permute-start.9 = (bf16[192,1024]{1,0:T(8,128)(2,1)}, bf16[192,1024]{1,0:T(8,128)(2,1)}, u32[]{:S(2)}, u32[]{:S(2)}) collective-permute-start(bf16[192,1024]{1,0:T(8,128)(2,1)} %collective-permute-done.7.far_a), channel_id=1, source_target_pairs={{0,1},{1,0},{2,3},{3,2},{4,5},{5,4},{6,7},{7,6},{8,9},{9,8},{10,11... | collective-permute-start | bytes 1179656 | tf_op jit(solution)/shard_map/ppermute | solution.py:427
  74.0 1.0 copy-start.5
Sparse Core Ops, SparseCore 0:
  11.9 27.5 all-gather.2

commit v8 on v7

--- a/solution.py
+++ b/solution.py
@@ -71,12 +71,11 @@
     refs = list(refs)
     count = len(table)
     blocks = [refs.pop(0) for _ in range(count)]
-    weight, up, _ = refs.pop(0), refs.pop(0), refs.pop(0)
+    weight, _ = refs.pop(0), refs.pop(0)
     if not first:
         sums_in = refs.pop(0)
-    sums_out, done, x, w, u, sums, sums_was, x_sem, w_sem, u_sem, sem = refs
+    sums_out, done, x, w, sums, sums_was, x_sem, w_sem, sem = refs
     tokens, width = x.shape[1:]
-    out_width, rank = w.shape[1], u.shape[1]
     done[...] = jnp.zeros_like(done)
     copies = []
     for k, place in enumerate(table):
@@ -84,27 +83,24 @@
         columns = pl.ds(pl.multiple_of(owner * width, width), width)
         copies.append([
             pltpu.make_async_copy(blocks[k], x.at[k], x_sem.at[k]),
-            pltpu.make_async_copy(weight.at[:, columns], w.at[k % 3], w_sem.at[k]),
-            pltpu.make_async_copy(up.at[owner], u.at[k], u_sem.at[k]),
+            pltpu.make_async_copy(weight.at[:, columns], w.at[k % 4], w_sem.at[k]),
         ])
     if not first:
         copies.append([pltpu.make_async_copy(sums_in.at[pl.ds(0, tokens)], sums_was, sem.at[0])])
-    for each in copies[:2]:
+    for each in copies[:3]:
         for copy in each:
             copy.start()
     for k in range(count):
         for copy in copies[k]:
             copy.wait()
-        if k + 2 < len(copies):
-            for copy in copies[k + 2]:
+        if k + 3 < len(copies):
+            for copy in copies[k + 3]:
                 copy.start()
-        value, value_low = dot_minor(x[k], w[k % 3]), dot_minor(x[k], u[k])
+        value = dot_minor(x[k], w[k % 4])
         if k > 0:
-            sums[:, :out_width] += value
-            sums[:, out_width : out_width + rank] += value_low
+            sums[...] += value
         else:
-            sums[:, :out_width] = value
-            sums[:, out_width : out_width + rank] = value_low
+            sums[...] = value
     if not first:
         copies[count][0].wait()
         sums[...] += sums_was[...]
@@ -113,27 +109,24 @@
     store.wait()
 
 
-def block_products(index, table, blocks, weight, up_all, token, sums=None, name=""):
+def block_products(index, table, blocks, weight, token, sums=None, name=""):
     count = len(blocks)
     tokens, width = blocks[0].shape
     out_width = weight.shape[0]
-    rank = up_all.shape[1]
     first = sums is None
     return pl.pallas_call(
         functools.partial(block_kernel, table, first),
-        in_specs=[SMEM] + [ANY] * (count + (3 if first else 4)),
+        in_specs=[SMEM] + [ANY] * (count + (2 if first else 3)),
         out_specs=[HBM, VMEM],
         out_shape=[
-            jax.ShapeDtypeStruct((BASE_ROOM * tokens, out_width + LANES), jnp.float32),
+            jax.ShapeDtypeStruct((BASE_ROOM * tokens, out_width), jnp.float32),
             jax.ShapeDtypeStruct((8, LANES), jnp.float32),
         ],
         scratch_shapes=[
             pltpu.VMEM((count, tokens, width), jnp.bfloat16),
-            pltpu.VMEM((3, out_width, width), jnp.bfloat16),
-            pltpu.VMEM((count, rank, width), jnp.bfloat16),
-            pltpu.VMEM((tokens, out_width + LANES), jnp.float32),
-            pltpu.VMEM((tokens, out_width + LANES), jnp.float32),
-            pltpu.SemaphoreType.DMA((count,)),
+            pltpu.VMEM((4, out_width, width), jnp.bfloat16),
+            pltpu.VMEM((tokens, out_width), jnp.float32),
+            pltpu.VMEM((tokens, out_width), jnp.float32),
             pltpu.SemaphoreType.DMA((count,)),
             pltpu.SemaphoreType.DMA((count,)),
             pltpu.SemaphoreType.DMA((2,)),
@@ -145,19 +138,21 @@
             transcendentals=0,
         ),
         name=name,
-    )(index, *blocks, weight, up_all, token, *([] if first else [sums]))
+    )(index, *blocks, weight, token, *([] if first else [sums]))
 
 
 def last_kernel(
-    rows, scale, table, index, far_a, far_b, other_a, other_b, grads_in, weight, up, sums_in, down,
-    out, x, w, u, sums, grads, low_rounded, x_sem, w_sem, u_sem, sem,
+    rows, scale, table, core_at, index, far_a, far_b, other_a, other_b, grads_in, crossed,
+    crossed_other, weight, sums_in, down, out, x, w, sums, grads, pieces, low, low_rounded, x_sem,
+    w_sem, sem,
 ):
     half, width = far_a.shape
-    out_width, rank = w.shape[0], u.shape[0]
+    groups, ranks = pieces.shape[1:3]
     tokens = 2 * half
     piece = tokens // rows
     tile = 2 * LANES
-    tiles = out_width // tile
+    tiles = w.shape[0] // tile
+    core = index[core_at]
 
     def load_sums(columns, semaphore):
         return pltpu.make_async_copy(
@@ -168,10 +163,10 @@
     for i, part in enumerate((far_a, far_b, other_a, other_b)):
         rows_of, lanes = pl.ds((i % 2) * half, half), pl.ds((i // 2) * width, width)
         copies.append(pltpu.make_async_copy(part, x.at[rows_of, lanes], x_sem.at[i]))
-    for k in range(2):
-        lanes = pl.ds(k * width, width)
-        copies.append(pltpu.make_async_copy(up.at[index[table[k]]], u.at[:, lanes], u_sem.at[k]))
-    copies.append(load_sums(pl.ds(out_width, LANES), sem.at[tiles]))
+    low_copies = [
+        pltpu.make_async_copy(crossed.at[:, 2], pieces.at[core], sem.at[tiles]),
+        pltpu.make_async_copy(crossed_other.at[:, 2], pieces.at[1 - core], sem.at[tiles + 1]),
+    ]
     tile_copies = []
     for n in range(tiles):
         span = pl.ds(n * tile, tile)
@@ -184,15 +179,20 @@
             )
         each.append(load_sums(span, sem.at[n]))
         tile_copies.append(each)
-    load_grads = pltpu.make_async_copy(grads_in, grads, sem.at[tiles + 1])
-    for each in [copies] + tile_copies + [[load_grads]]:
+    load_grads = pltpu.make_async_copy(grads_in, grads, sem.at[tiles + 2])
+    for each in [low_copies, copies] + tile_copies + [[load_grads]]:
         for copy in each:
             copy.start()
     out[...] = jnp.zeros_like(out)
+    for copy in low_copies:
+        copy.wait()
+    share = tokens // groups
+    for group in range(groups):
+        both = jnp.concatenate([pieces[0, group], pieces[1, group]], axis=0).astype(jnp.float32)
+        low[group * share : (group + 1) * share] = both.T[:share]
+    low_rounded[...] = low[...].astype(jnp.bfloat16)
     for copy in copies:
         copy.wait()
-    total = sums[:, out_width : out_width + rank] + dot_minor(x[...], u[...])
-    low_rounded[...] = total.astype(jnp.bfloat16)
     for n in range(tiles):
         span = slice(n * tile, (n + 1) * tile)
         for copy in tile_copies[n]:
@@ -216,28 +216,29 @@
 
 
 def last_products(
-    rows, scale, index, table, far, other, grads, weight, up, sums, down, groups, slots
+    rows, scale, index, table, core_at, far, other, grads, crossed, weight, sums, down, slots
 ):
     half, width = far[0].shape
     tokens = 2 * half
     rank, out_width = down.shape
+    groups = crossed[0].shape[0]
     piece = tokens // rows
     tiles = out_width // (2 * LANES)
     return pl.pallas_call(
-        functools.partial(last_kernel, rows, scale, table),
-        in_specs=[SMEM] + [ANY] * 8 + [VMEM],
+        functools.partial(last_kernel, rows, scale, table, core_at),
+        in_specs=[SMEM] + [ANY] * 9 + [VMEM],
         out_specs=VMEM,
         scratch_shapes=[
             pltpu.VMEM((tokens, 2 * width), jnp.bfloat16),
             pltpu.VMEM((out_width, 2 * width), jnp.bfloat16),
-            pltpu.VMEM((rank, 2 * width), jnp.bfloat16),
-            pltpu.VMEM((tokens, out_width + LANES), jnp.float32),
+            pltpu.VMEM((tokens, out_width), jnp.float32),
             pltpu.VMEM(grads.shape, grads.dtype),
+            pltpu.VMEM((2, groups, rank // 2, LANES), jnp.bfloat16),
+            pltpu.VMEM((tokens, rank), jnp.float32),
             pltpu.VMEM((tokens, rank), jnp.bfloat16),
             pltpu.SemaphoreType.DMA((4,)),
             pltpu.SemaphoreType.DMA((tiles, 2)),
-            pltpu.SemaphoreType.DMA((2,)),
-            pltpu.SemaphoreType.DMA((tiles + 2,)),
+            pltpu.SemaphoreType.DMA((tiles + 3,)),
         ],
         out_shape=jax.ShapeDtypeStruct(
             (groups, slots + 1, 2 * piece, out_width // 2), jnp.bfloat16
@@ -249,25 +250,35 @@
             transcendentals=0,
         ),
         name="last_products",
-    )(index, *far, *other, grads, weight, up, sums, down)
-
-
-def send_kernel(groups, pick_at, index, share, out):
+    )(index, *far, *other, grads, *crossed, weight, sums, down)
+
+
+def send_kernel(groups, rows_here, pick_at, index, share, out):
+    piece = ROW_TOKENS // groups
+    lane = lax.broadcasted_iota(jnp.int32, (share.shape[0], ROW_TOKENS), 1)
     for group in range(groups):
         for kind in range(2):
             pick = index[pick_at + 2 * group + kind]
             lanes = pl.ds(pl.multiple_of(jnp.maximum(pick, 0) * ROW_TOKENS, ROW_TOKENS), ROW_TOKENS)
             keep = (pick >= 0).astype(jnp.float32)
             out[group, kind] = (share[:, lanes] * keep).astype(jnp.bfloat16)
-
-
-def rank_sums_to_send(index, pick_at, groups, share):
+        value = jnp.zeros(lane.shape, jnp.float32)
+        for r in range(rows_here):
+            shift = (r - group) * piece % ROW_TOKENS
+            row = share[:, r * ROW_TOKENS : (r + 1) * ROW_TOKENS]
+            if shift:
+                row = pltpu.roll(row, shift, 1)
+            value = jnp.where(lane // piece == r, row, value)
+        out[group, 2] = value.astype(jnp.bfloat16)
+
+
+def rank_sums_to_send(index, pick_at, groups, rows_here, share):
     half = share.shape[0]
     return pl.pallas_call(
-        functools.partial(send_kernel, groups, pick_at),
+        functools.partial(send_kernel, groups, rows_here, pick_at),
         in_specs=[SMEM, VMEM],
         out_specs=VMEM,
-        out_shape=jax.ShapeDtypeStruct((groups, 2, half, ROW_TOKENS), jnp.bfloat16),
+        out_shape=jax.ShapeDtypeStruct((groups, 3, half, ROW_TOKENS), jnp.bfloat16),
         compiler_params=pltpu.CompilerParams(vmem_limit_bytes=SMALL_LIMIT),
         cost_estimate=pl.CostEstimate(
             flops=2 * groups * half * ROW_TOKENS, bytes_accessed=8 * groups * half * ROW_TOKENS,
@@ -279,21 +290,27 @@
 
 def gradient_kernel(
     core_at, source_at, dest_at, index, crossed, crossed_other, token, attention, gradient, out,
-    low, projected, tokens, more, sem,
+    done, parts, low, projected, sums, tokens, more, sem,
 ):
     half = crossed.shape[2]
     rank = 2 * half
     core = index[core_at]
-    halves = [
-        (pl.ds(pl.multiple_of(owner * half, half), half), part)
-        for owner, part in ((core, crossed), (1 - core, crossed_other))
+    part_copies = [
+        pltpu.make_async_copy(part.at[:, pl.ds(0, 2)], parts.at[i], sem.at[3 + i])
+        for i, part in enumerate((crossed, crossed_other))
     ]
     copies = [
         pltpu.make_async_copy(attention, tokens, sem.at[0]),
         pltpu.make_async_copy(gradient, more, sem.at[1]),
     ]
-    for copy in copies:
+    for copy in part_copies + copies:
         copy.start()
+    for copy in part_copies:
+        copy.wait()
+    halves = [
+        (pl.ds(pl.multiple_of(owner * half, half), half), parts.at[i])
+        for i, owner in enumerate((core, 1 - core))
+    ]
     for s in range(tokens.shape[0] // ROW_TOKENS):
         source = index[source_at + s]
         keep = (source >= 0).astype(jnp.float32)
@@ -304,9 +321,13 @@
         for ranks, part in halves:
             projected[ranks, r * ROW_TOKENS : (r + 1) * ROW_TOKENS] = part[index[dest_at + r], 1]
     copies[0].wait()
-    out[:rank] = jnp.dot(low[...], tokens[...], preferred_element_type=jnp.float32)
+    sums[:rank] = jnp.dot(low[...], tokens[...], preferred_element_type=jnp.float32)
     copies[1].wait()
-    out[rank:] = jnp.dot(projected[...], more[...], preferred_element_type=jnp.float32)
+    sums[rank:] = jnp.dot(projected[...], more[...], preferred_element_type=jnp.float32)
+    done[...] = jnp.zeros_like(done)
+    store = pltpu.make_async_copy(sums, out, sem.at[2])
+    store.start()
+    store.wait()
 
 
 def gradient_products(
@@ -317,15 +338,20 @@
     row_tokens = gradient.shape[0]
     return pl.pallas_call(
         functools.partial(gradient_kernel, core_at, source_at, dest_at),
-        in_specs=[SMEM, VMEM, VMEM, ANY, ANY, ANY],
-        out_specs=VMEM,
-        out_shape=jax.ShapeDtypeStruct((2 * rank, width), jnp.float32),
+        in_specs=[SMEM] + [ANY] * 5,
+        out_specs=[HBM, VMEM],
+        out_shape=[
+            jax.ShapeDtypeStruct((2 * rank, width), jnp.float32),
+            jax.ShapeDtypeStruct((8, LANES), jnp.float32),
+        ],
         scratch_shapes=[
+            pltpu.VMEM((2, crossed.shape[0], 2) + crossed.shape[2:], jnp.bfloat16),
             pltpu.VMEM((rank, slot_tokens), jnp.bfloat16),
             pltpu.VMEM((rank, row_tokens), jnp.bfloat16),
+            pltpu.VMEM((2 * rank, width), jnp.float32),
             pltpu.VMEM(attention.shape, jnp.bfloat16),
             pltpu.VMEM(gradient.shape, jnp.bfloat16),
-            pltpu.SemaphoreType.DMA((2,)),
+            pltpu.SemaphoreType.DMA((5,)),
         ],
         compiler_params=pltpu.CompilerParams(vmem_limit_bytes=SMALL_LIMIT),
         cost_estimate=pl.CostEstimate(
@@ -337,29 +363,27 @@
     )(index, crossed, other, token, attention, gradient)
 
 
-def unfold_kernel(slots, arrived, out, down_gradient, up_gradient):
-    groups, _, folded, half_width = arrived.shape
+def unfold_kernel(arrived, gradients, out, down_gradient, up_gradient):
+    groups, slots, folded, half_width = arrived.shape
     piece = folded // 2
-    step = pl.program_id(0)
-
-    @pl.when(step < slots)
-    def _():
+    for slot in range(slots):
         for pair in range(groups // 2):
             halves = []
             for j in (2 * pair, 2 * pair + 1):
-                value = arrived[j, 0].astype(jnp.float32)
+                value = arrived[j, slot].astype(jnp.float32)
                 pieces = []
                 for n in range(half_width // LANES):
                     lanes = slice(n * LANES, (n + 1) * LANES)
                     pieces += [value[:piece, lanes], value[piece:, lanes]]
                 halves.append(jnp.concatenate(pieces, axis=1))
-            out[pl.ds(pair * folded, folded), :] = jnp.concatenate(halves, axis=0).astype(out.dtype)
-
-    @pl.when(step == slots)
+            rows = pl.ds(slot * groups * piece + pair * folded, folded)
+            out[rows, :] = jnp.concatenate(halves, axis=0).astype(out.dtype)
+
+    @pl.when(pl.program_id(0) == 0)
     def _():
         values = []
         for j in range(groups):
-            value = arrived[j, 0].astype(jnp.float32)
+            value = gradients[j, 0].astype(jnp.float32)
             values.append(jnp.concatenate([value[:piece], value[piece:]], axis=1))
         down_gradient[...] = jnp.concatenate(values[: groups // 2], axis=0)
         up_gradient[...] = jnp.concatenate(values[groups // 2 :], axis=0)
@@ -369,12 +393,16 @@
     groups, _, folded, half_width = arrived.shape
     piece, width = folded // 2, 2 * half_width
     rank = groups * piece // 2
+    step = slots // 2
     return pl.pallas_call(
-        functools.partial(unfold_kernel, slots),
-        grid=(slots + 1,),
-        in_specs=[pl.BlockSpec((groups, 1, folded, half_width), lambda s: (0, s, 0, 0))],
+        unfold_kernel,
+        grid=(slots // step,),
+        in_specs=[
+            pl.BlockSpec((groups, step, folded, half_width), lambda s: (0, s, 0, 0)),
+            pl.BlockSpec((groups, 1, folded, half_width), lambda s: (0, slots, 0, 0)),
+        ],
         out_specs=[
-            pl.BlockSpec((groups * piece, width), lambda s: (jnp.minimum(s, slots - 1), 0)),
+            pl.BlockSpec((step * groups * piece, width), lambda s: (s, 0)),
             pl.BlockSpec((rank, width), lambda s: (0, 0)),
             pl.BlockSpec((rank, width), lambda s: (0, 0)),
         ],
@@ -385,7 +413,7 @@
         ],
         compiler_params=pltpu.CompilerParams(vmem_limit_bytes=SMALL_LIMIT),
         name="unfold",
-    )(arrived)
+    )(arrived, arrived)
 
 
 def body(
@@ -461,7 +489,6 @@
     _, _, pick_at, source_at, dest_at, owner_at, end = at
     table = jnp.concatenate(pieces)
 
-    up_all = lax.all_gather(up_weight, "tp", axis=0)
     low_part = dot_minor(up_weight, output_gradient_rows)
     projected_part = lax.dot_general(
         down_weight_first, attention_slot_outputs, (((0,), (1,)), ((), ())),
@@ -472,20 +499,20 @@
     share = lax.dynamic_slice_in_dim(parts, core * (rank // 2), rank // 2, axis=0)
     share = share + move(share, 1) + move(share, -1) + move(share, 2)
 
-    send = rank_sums_to_send(table, pick_at, groups, share)
+    send = rank_sums_to_send(table, pick_at, groups, rows_here, share)
     crossed = lax.all_to_all(send, "group", split_axis=0, concat_axis=0, tiled=True)
 
     spread, _ = lax.optimization_barrier((spread, share))
     left, right = move(spread, 1), move(spread, -1)
     other = swap(spread)
     sums, done = block_products(
-        table, [owner_at, owner_at + 1], [spread, other], output_weight, up_all, send,
+        table, [owner_at, owner_at + 1], [spread, other], output_weight, send,
         name="own_products",
     )
     crossed_other = swap(crossed)
     left_top, right_bottom, left, right = take_halves(left, right, crossed, done)
     far = [move(left_top, 1), move(right_bottom, -1)]
-    partial_grads = gradient_products(
+    partial_grads, done = gradient_products(
         table, end - 1, source_at, dest_at, crossed, crossed_other, left_top, attention_slot_outputs,
         output_gradient_rows,
     )
@@ -496,11 +523,12 @@
     )
     sums, _ = block_products(
         table, [owner_at + i for i in range(2, 6)], [left, swap(left), right, swap(right)],
-        output_weight, up_all, partial_grads, sums, name="side_products",
+        output_weight, done, sums, name="side_products",
     )
     placed = last_products(
-        rows, scale_factor, table, [owner_at + 6, owner_at + 7], far, [swap(part) for part in far],
-        grads, output_weight, up_all, sums, down_weight.T, groups, slot_cap,
+        rows, scale_factor, table, [owner_at + 6, owner_at + 7], end - 1, far,
+        [swap(part) for part in far], grads, (crossed, crossed_other), output_weight, sums,
+        down_weight.T, slot_cap,
     )
 
     arrived = lax.all_to_all(placed, "group", split_axis=0, concat_axis=0, tiled=True)

time: 136 us -> 115 us (0.85)
  between operations: 14.4 us -> 1 us
  waiting for transfers between devices: 13.8 us -> 21.8 us
  Pallas kernels: 31.7 us -> 26.6 us
  starting transfers between devices: 32.8 us -> 28.5 us
  local copies, waits for them, and re-layouts: 6.9 us -> 3.73 us
  blocking collectives: 32.5 us -> 30.3 us
    ppermute x7, waiting for transfers between devices: 10.2 us -> 14.2 us  [move(): return lax.ppermute(value, 'tp', pairs)]
    all_to_all x1, waiting for transfers between devices: 1.08 us -> 4.82 us  [body(): lax.all_to_all(send, 'group', split_axis=0, concat_axis=0, tiled=True)]
    unnamed x22 -> x18, local copies, waits for them, and re-layouts: 4.03 us -> 0.84 us
    pallas_call x2, Pallas kernels: 16.5 us -> 13.5 us  [block_products(): pl.pallas_call(functools.partial(block_kernel, table, first), in_specs=[S...]
    all_to_all x1, blocking collectives: 32.5 us -> 30.3 us  [body(): lax.all_to_all(placed, 'group', split_axis=0, concat_axis=0, tiled=True)]
    all_to_all x1, starting transfers between devices: 6.2 us -> 4.05 us  [body(): lax.all_to_all(partial_grads.reshape(groups, share_rows, width_here), 'gr...]
    all_to_all x1, starting transfers between devices: 6.34 us -> 4.19 us  [body(): lax.all_to_all(send, 'group', split_axis=0, concat_axis=0, tiled=True)]
    pallas_call x3, Pallas kernels: 11.8 us -> 9.65 us  [the longest x1 6.61 us: last_products(): pl.pallas_call(functools.partial(last_kernel, rows, scale, table, core_at...]
  transfers between devices with their start and end apart: 18 -> 17, of which waited for: 8 -> 8; matrix products, arithmetic and copies ran while one was open for 1% -> 1% of each run, Pallas kernels for 14% -> 14%
where the time goes in v8:
time: 115 us
  blocking collectives  30.3 us (26%)
  starting transfers between devices  28.5 us (25%)
  Pallas kernels  26.6 us (23%)
  waiting for transfers between devices  21.8 us (19%)
  local copies, waits for them, and re-layouts  3.73 us (3%)
  matrix products  2.08 us (2%)
    all_to_all x1, blocking collectives, body(): lax.all_to_all(placed, 'group', split_axis=0, concat_axis=0, tiled=True)  30.3 us
    ppermute x7, waiting for transfers between devices, move(): return lax.ppermute(value, 'tp', pairs)  14.2 us
    pallas_call x2, Pallas kernels, block_products(): pl.pallas_call(functools.partial(block_kernel, table, first), in_specs=[S...  13.5 us
    ppermute x7, starting transfers between devices, move(): return lax.ppermute(value, 'tp', pairs)  11.5 us
    all_to_all x1, starting transfers between devices, body(): lax.all_to_all(pieces_out, 'group', split_axis=0, concat_axis=0, tiled=True)  7.97 us
    pallas_call x1, Pallas kernels, last_products(): pl.pallas_call(functools.partial(last_kernel, rows, scale, table, core_at...  6.61 us
    all_to_all x1, waiting for transfers between devices, body(): lax.all_to_all(send, 'group', split_axis=0, concat_axis=0, tiled=True)  4.82 us
    all_to_all x1, starting transfers between devices, body(): lax.all_to_all(send, 'group', split_axis=0, concat_axis=0, tiled=True)  4.19 us
  transfers between devices with their start and end apart: 17, of which 8 were waited for; matrix products, arithmetic and copies ran while one was open for 1% of the time, Pallas kernels for 14%

profile of v8, /device:TPU:0, one launch (start us, length us, event | category | flops | bytes accessed | tf_op | source)
XLA Modules:
  0.0 114.9 jit_solution(9795512505232720799)
XLA Ops:
  0.7 2.2 %copy.21 = bf16[3,16,8,1024]{3,2,0,1:T(8,128)(2,1)} copy(bf16[3,16,8,1024]{3,2,1,0:T(8,128)(2,1)} %bitcast.23) | data formatting | bytes 1572864 | tf_op jit(solution)/shard_map/reshape | solution.py:457
  2.9 1.5 %fusion.4 = f32[64,384]{1,0:T(8,128)S(1)} fusion(bf16[64,1024]{1,0:T(8,128)(2,1)S(1)} %copy-done, bf16[384,1024]{1,0:T(8,128)(2,1)} %gradient.1), kind=kOutput, calls=%fused_computation.20 | convolution fusion | flops 50331648 | bytes 1015808 | tf_op jit(solution)/shard_map/dot_general | solution.py:27
  4.4 0.6 fusion.5
  5.1 8.0 %all-to-all-start = ((bf16[16,3,8,1024]{3,2,1,0:T(8,128)(2,1)}), bf16[16,3,8,1024]{3,2,1,0:T(8,128)(2,1)S(1)}, u32[]{:S(2)}, u32[]{:S(2)}) async-start(bf16[16,3,8,1024]{3,2,1,0:T(8,128)(2,1)} %bitcast.22), calls=%async_computation | async-start | bytes 1572864 | tf_op jit(solution)/shard_map/all_to_all | solution.py:462
  13.4 0.2 select_reduce_fusion.1
  13.7 1.6 %collective-permute-start.1 = (f32[32,1152]{1,0:T(8,128)S(1)}, f32[32,1152]{1,0:T(8,128)S(1)}, u32[]{:S(2)}, u32[]{:S(2)}) collective-permute-start(f32[32,1152]{1,0:T(8,128)S(1)} %fusion.1), channel_id=1, source_target_pairs={{0,2},{1,3},{2,4},{3,5},{4,6},{5,7},{6,0},{7,1},{8,10},{9,11},{10,... | collective-permute-start | bytes 442376 | tf_op jit(solution)/shard_map/ppermute | solution.py:452
  15.3 1.7 %collective-permute-start.2 = (f32[32,1152]{1,0:T(8,128)S(1)}, f32[32,1152]{1,0:T(8,128)S(1)}, u32[]{:S(2)}, u32[]{:S(2)}) collective-permute-start(f32[32,1152]{1,0:T(8,128)S(1)} %fusion.1), channel_id=1, source_target_pairs={{0,6},{1,7},{2,0},{3,1},{4,2},{5,3},{6,4},{7,5},{8,14},{9,15},{10,... | collective-permute-start | bytes 442376 | tf_op jit(solution)/shard_map/ppermute | solution.py:452
  17.0 2.0 %collective-permute-start.3 = (f32[32,1152]{1,0:T(8,128)S(1)}, f32[32,1152]{1,0:T(8,128)S(1)}, u32[]{:S(2)}, u32[]{:S(2)}) collective-permute-start(f32[32,1152]{1,0:T(8,128)S(1)} %fusion.1), channel_id=1, source_target_pairs={{0,4},{1,5},{2,6},{3,7},{4,0},{5,1},{6,2},{7,3},{8,12},{9,13},{10,... | collective-permute-start | bytes 442376 | tf_op jit(solution)/shard_map/ppermute | solution.py:452
  19.0 1.9 %collective-permute-done.1 = f32[32,1152]{1,0:T(8,128)S(1)} collective-permute-done((f32[32,1152]{1,0:T(8,128)S(1)}, f32[32,1152]{1,0:T(8,128)S(1)}, u32[]{:S(2)}, u32[]{:S(2)}) %collective-permute-start.1) | collective-permute-done | bytes 147488 | tf_op jit(solution)/shard_map/ppermute | solution.py:452
  21.0 2.5 %collective-permute-done.2 = f32[32,1152]{1,0:T(8,128)S(1)} collective-permute-done((f32[32,1152]{1,0:T(8,128)S(1)}, f32[32,1152]{1,0:T(8,128)S(1)}, u32[]{:S(2)}, u32[]{:S(2)}) %collective-permute-start.2) | collective-permute-done | bytes 147488 | tf_op jit(solution)/shard_map/ppermute | solution.py:452
  23.5 1.8 %collective-permute-done.3 = f32[32,1152]{1,0:T(8,128)S(1)} collective-permute-done((f32[32,1152]{1,0:T(8,128)S(1)}, f32[32,1152]{1,0:T(8,128)S(1)}, u32[]{:S(2)}, u32[]{:S(2)}) %collective-permute-start.3) | collective-permute-done | bytes 147488 | tf_op jit(solution)/shard_map/ppermute | solution.py:452
  25.3 2.8 %all-to-all-done = bf16[16,3,8,1024]{3,2,1,0:T(8,128)(2,1)S(1)} async-done(((bf16[16,3,8,1024]{3,2,1,0:T(8,128)(2,1)}), bf16[16,3,8,1024]{3,2,1,0:T(8,128)(2,1)S(1)}, u32[]{:S(2)}, u32[]{:S(2)}) %all-to-all-start) | async-done | bytes 786464 | tf_op jit(solution)/shard_map/all_to_all | solution.py:462
  28.4 1.6 %collective-permute-start.4 = (bf16[384,1024]{1,0:T(8,128)(2,1)S(1)}, bf16[384,1024]{1,0:T(8,128)(2,1)}, u32[]{:S(2)}, u32[]{:S(2)}) collective-permute-start(bf16[384,1024]{1,0:T(8,128)(2,1)S(1)} %bitcast.25), channel_id=1, source_target_pairs={{0,2},{1,3},{2,4},{3,5},{4,6},{5,7},{6,0},{7,1},{8,10},{9,11},{10,... | collective-permute-start | bytes 2359304 | tf_op jit(solution)/shard_map/ppermute | solution.py:452
  30.0 1.7 %collective-permute-start.5 = (bf16[384,1024]{1,0:T(8,128)(2,1)S(1)}, bf16[384,1024]{1,0:T(8,128)(2,1)}, u32[]{:S(2)}, u32[]{:S(2)}) collective-permute-start(bf16[384,1024]{1,0:T(8,128)(2,1)S(1)} %bitcast.26), channel_id=1, source_target_pairs={{0,6},{1,7},{2,0},{3,1},{4,2},{5,3},{6,4},{7,5},{8,14},{9,15},{10,... | collective-permute-start | bytes 2359304 | tf_op jit(solution)/shard_map/ppermute | solution.py:452
  32.1 0.1 select_reduce_fusion.2
  32.3 1.5 %rank_sums_to_send.1.refs_3_ = bf16[16,3,32,128]{3,2,1,0:T(8,128)(2,1)} custom-call(s32[146]{0:T(256)S(1)} %concatenate.6.index, f32[32,1152]{1,0:T(8,128)S(1)} %add_add_fusion.share), custom_call_target="tpu_custom_call" | custom-call | flops 131072 | bytes 524288 | tf_op jit(solution)/shard_map/rank_sums_to_send/pallas_call | solution.py:277
  33.8 4.2 %all-to-all-start.1 = ((bf16[16,3,32,128]{3,2,1,0:T(8,128)(2,1)}), bf16[16,3,32,128]{3,2,1,0:T(8,128)(2,1)S(1)}, u32[]{:S(2)}, u32[]{:S(2)}) async-start(bf16[16,3,32,128]{3,2,1,0:T(8,128)(2,1)} %rank_sums_to_send.1.refs_3_), calls=%async_computation.1 | async-start | bytes 786432 | tf_op jit(solution)/shard_map/all_to_all | solution.py:503
  38.0 5.3 %own_products.1 = (f32[6144,1024]{1,0:T(8,128)}, f32[8,128]{1,0:T(8,128)S(1)}) custom-call(s32[146]{0:T(256)S(1)} %concatenate.6.index, bf16[384,1024]{1,0:T(8,128)(2,1)S(1)} %bitcast.27, bf16[384,1024]{1,0:T(8,128)(2,1)S(1)} %collective-permute-done.6.refs_1_, bf16[1024,8192]{1,0:T(8,128)(2,1)} %weight.1, bf16[16,3,32,128]{3,2,1,0:T(8,128)(2,1)} %rank_sums_to_send.1.refs_3_), custom_call_target="tpu_custom_call" | custom-call | flops 1610612736 | bytes 5767168 | tf_op jit(solution)/shard_map/own_products/pallas_call | solution.py:117
  43.3 4.8 %all-to-all-done.1.token.crossed = bf16[16,3,32,128]{3,2,1,0:T(8,128)(2,1)S(1)} async-done(((bf16[16,3,32,128]{3,2,1,0:T(8,128)(2,1)}), bf16[16,3,32,128]{3,2,1,0:T(8,128)(2,1)S(1)}, u32[]{:S(2)}, u32[]{:S(2)}) %all-to-all-start.1) | async-done | bytes 393248 | tf_op jit(solution)/shard_map/all_to_all | solution.py:503
  48.1 1.6 %collective-permute-done.4.left = bf16[384,1024]{1,0:T(8,128)(2,1)} collective-permute-done((bf16[384,1024]{1,0:T(8,128)(2,1)S(1)}, bf16[384,1024]{1,0:T(8,128)(2,1)}, u32[]{:S(2)}, u32[]{:S(2)}) %collective-permute-start.4) | collective-permute-done | bytes 786464 | tf_op jit(solution)/shard_map/ppermute | solution.py:452
  49.8 2.0 %take_halves.1 = (bf16[192,1024]{1,0:T(8,128)(2,1)}, bf16[192,1024]{1,0:T(8,128)(2,1)}, bf16[384,1024]{1,0:T(8,128)(2,1)}, bf16[384,1024]{1,0:T(8,128)(2,1)}) custom-call(bf16[384,1024]{1,0:T(8,128)(2,1)} %collective-permute-done.4.left, bf16[384,1024]{1,0:T(8,128)(2,1)} %collective-permute-done.5.right, ...), custom_call_target="tpu_custom_call", output_to_operand_aliasing={{2}: (0, {}), {3}: (1, {})} | custom-call | bytes 3145728 | tf_op jit(solution)/shard_map/take_halves/pallas_call | solution.py:52
  51.8 0.5 collective-permute-start.13
  52.4 3.0 %collective-permute-start.8 = (bf16[192,1024]{1,0:T(8,128)(2,1)}, bf16[192,1024]{1,0:T(8,128)(2,1)S(1)}, u32[]{:S(2)}, u32[]{:S(2)}) collective-permute-start(bf16[192,1024]{1,0:T(8,128)(2,1)} %get-tuple-element.25), channel_id=1, source_target_pairs={{0,6},{1,7},{2,0},{3,1},{4,2},{5,3},{6,4},{7,5},{8,14},{9,15},{10,... | collective-permute-start | bytes 1179656 | tf_op jit(solution)/shard_map/ppermute | solution.py:452
  55.4 1.5 %gradient_products.1 = (f32[128,1024]{1,0:T(8,128)S(1)}, f32[8,128]{1,0:T(8,128)S(1)}) custom-call(s32[146]{0:T(256)S(1)} %concatenate.6.index, bf16[16,3,32,128]{3,2,1,0:T(8,128)(2,1)S(1)} %all-to-all-done.1.token.crossed, bf16[16,3,32,128]{3,2,1,0:T(8,128)(2,1)S(1)} %collective-permute-done.11.crossed_other, bf16[192,1024]{1,0:T(8,128)(2,1)} %get-tuple-element.24.token, ...), custom_call_target="tpu_custom_call" | custom-call | flops 150994944 | bytes 2359296 | tf_op jit(solution)/shard_map/gradient_products/pallas_call | solution.py:339
  57.0 0.8 copy-done.6
  57.8 4.0 %all-to-all-start.2 = ((f32[16,8,1024]{2,1,0:T(8,128)}), f32[16,8,1024]{2,1,0:T(8,128)S(1)}, u32[]{:S(2)}, u32[]{:S(2)}) async-start(f32[16,8,1024]{2,1,0:T(8,128)} %bitcast.29), calls=%async_computation.2 | async-start | bytes 1048576 | tf_op jit(solution)/shard_map/all_to_all | solution.py:520
  61.8 2.9 %collective-permute-done.8.far_b = bf16[192,1024]{1,0:T(8,128)(2,1)S(1)} collective-permute-done((bf16[192,1024]{1,0:T(8,128)(2,1)}, bf16[192,1024]{1,0:T(8,128)(2,1)S(1)}, u32[]{:S(2)}, u32[]{:S(2)}) %collective-permute-start.8) | collective-permute-done | bytes 393248 | tf_op jit(solution)/shard_map/ppermute | solution.py:452
  64.7 3.4 %collective-permute-done.7.far_a = bf16[192,1024]{1,0:T(8,128)(2,1)} collective-permute-done((bf16[192,1024]{1,0:T(8,128)(2,1)}, bf16[192,1024]{1,0:T(8,128)(2,1)}, u32[]{:S(2)}, u32[]{:S(2)}) %collective-permute-start.7) | collective-permute-done | bytes 393248 | tf_op jit(solution)/shard_map/ppermute | solution.py:452
  68.2 8.1 %side_products.1 = (f32[6144,1024]{1,0:T(8,128)}, f32[8,128]{1,0:T(8,128)}) custom-call(s32[146]{0:T(256)S(1)} %concatenate.6.index, bf16[384,1024]{1,0:T(8,128)(2,1)} %get-tuple-element.27.refs_0_, bf16[384,1024]{1,0:T(8,128)(2,1)} %collective-permute-done.12.refs_1_, bf16[384,1024]{1,0:T(8,128)(2,1)} %get-tuple-element.28.refs_2_, ...), custom_call_target="tpu_custom_call" | custom-call | flops 3221225472 | bytes 11534336 | tf_op jit(solution)/shard_map/side_products/pallas_call | solution.py:117
  76.4 6.6 %last_products.1 = bf16[16,7,16,512]{3,2,1,0:T(8,128)(2,1)S(1)} custom-call(s32[146]{0:T(256)S(1)} %concatenate.6.index, bf16[192,1024]{1,0:T(8,128)(2,1)} %collective-permute-done.7.far_a, bf16[192,1024]{1,0:T(8,128)(2,1)S(1)} %collective-permute-done.8.far_b, bf16[192,1024]{1,0:T(8,128)(2,1)S(1)} %collective-permute-done.9.other_a, ...), custom_call_target="tpu_custom_call" | custom-call | flops 1610612736 | bytes 4718592 | tf_op jit(solution)/shard_map/last_products/pallas_call | solution.py:227
  83.0 30.3 %all_to_all.20.arrived.gradients = bf16[16,7,16,512]{3,2,1,0:T(8,128)(2,1)S(1)} all-to-all(bf16[16,7,16,512]{3,2,1,0:T(8,128)(2,1)S(1)} %last_products.1), channel_id=1, replica_groups=mesh['group'=16,'tp'=8] {'group'}, dimensions={0} | all-to-all | bytes 3670016 | tf_op jit(solution)/shard_map/all_to_all | solution.py:534
  113.3 1.6 %unfold.1 = (bf16[768,1024]{1,0:T(8,128)(2,1)}, f32[64,1024]{1,0:T(8,128)}, f32[64,1024]{1,0:T(8,128)}) custom-call(bf16[16,7,16,512]{3,2,1,0:T(8,128)(2,1)S(1)} %all_to_all.20.arrived.gradients, bf16[16,7,16,512]{3,2,1,0:T(8,128)(2,1)S(1)} %all_to_all.20.arrived.gradients), custom_call_target="tpu_custom_call" | custom-call | tf_op jit(solution)/shard_map/unfold/pallas_call | solution.py:397
  (51 shorter events, 1.6 us)
Async XLA Ops:
  0.6 2.2 %copy-start = (bf16[64,1024]{1,0:T(8,128)(2,1)S(1)}, bf16[64,1024]{1,0:T(8,128)(2,1)}, u32[]{:S(2)}) copy-start(bf16[64,1024]{1,0:T(8,128)(2,1)} %param.11) | copy-start | bytes 393220
  0.6 3.7 %copy-start.4 = (bf16[1024,64]{0,1:T(8,128)(2,1)S(1)}, bf16[1024,64]{0,1:T(8,128)(2,1)}, u32[]{:S(2)}) copy-start(bf16[1024,64]{0,1:T(8,128)(2,1)} %param.10) | copy-start | bytes 393220
  0.7 3.7 %copy-start.3 = (bf16[768,1024]{1,0:T(8,128)(2,1)S(1)}, bf16[768,1024]{1,0:T(8,128)(2,1)}, u32[]{:S(2)}) copy-start(bf16[768,1024]{1,0:T(8,128)(2,1)} %attention.1) | copy-start | bytes 4718596
  4.4 8.8 %copy-start.7 = (s32[48]{0:T(128)S(1)}, s32[48]{0:T(128)}, u32[]{:S(2)}) copy-start(s32[48]{0:T(128)} %param.12) | copy-start | bytes 580
  4.4 9.0 %copy-start.8 = (s32[16]{0:T(128)S(1)}, s32[16]{0:T(128)}, u32[]{:S(2)}) copy-start(s32[16]{0:T(128)} %param.13) | copy-start | bytes 196
  5.0 8.6 %collective-permute-start = (f32[64,1152]{1,0:T(8,128)S(1)}, f32[64,1152]{1,0:T(8,128)S(1)}, u32[]{:S(2)}, u32[]{:S(2)}) collective-permute-start(f32[64,1152]{1,0:T(8,128)S(1)} %pad_maximum_fusion), channel_id=1, source_target_pairs={{0,1},{1,0},{2,3},{3,2},{4,5},{5,4},{6,7},{7,6},{8,9},{9,8},{10,11... | collective-permute-start | bytes 884744 | tf_op jit(solution)/shard_map/ppermute | solution.py:455
  5.1 23.0 %all-to-all-start = ((bf16[16,3,8,1024]{3,2,1,0:T(8,128)(2,1)}), bf16[16,3,8,1024]{3,2,1,0:T(8,128)(2,1)S(1)}, u32[]{:S(2)}, u32[]{:S(2)}) async-start(bf16[16,3,8,1024]{3,2,1,0:T(8,128)(2,1)} %bitcast.22), calls=%async_computation | async-start | bytes 1572864 | tf_op jit(solution)/shard_map/all_to_all | solution.py:462
  13.7 7.3 %collective-permute-start.1 = (f32[32,1152]{1,0:T(8,128)S(1)}, f32[32,1152]{1,0:T(8,128)S(1)}, u32[]{:S(2)}, u32[]{:S(2)}) collective-permute-start(f32[32,1152]{1,0:T(8,128)S(1)} %fusion.1), channel_id=1, source_target_pairs={{0,2},{1,3},{2,4},{3,5},{4,6},{5,7},{6,0},{7,1},{8,10},{9,11},{10,... | collective-permute-start | bytes 442376 | tf_op jit(solution)/shard_map/ppermute | solution.py:452
  15.3 8.2 %collective-permute-start.2 = (f32[32,1152]{1,0:T(8,128)S(1)}, f32[32,1152]{1,0:T(8,128)S(1)}, u32[]{:S(2)}, u32[]{:S(2)}) collective-permute-start(f32[32,1152]{1,0:T(8,128)S(1)} %fusion.1), channel_id=1, source_target_pairs={{0,6},{1,7},{2,0},{3,1},{4,2},{5,3},{6,4},{7,5},{8,14},{9,15},{10,... | collective-permute-start | bytes 442376 | tf_op jit(solution)/shard_map/ppermute | solution.py:452
  17.0 8.3 %collective-permute-start.3 = (f32[32,1152]{1,0:T(8,128)S(1)}, f32[32,1152]{1,0:T(8,128)S(1)}, u32[]{:S(2)}, u32[]{:S(2)}) collective-permute-start(f32[32,1152]{1,0:T(8,128)S(1)} %fusion.1), channel_id=1, source_target_pairs={{0,4},{1,5},{2,6},{3,7},{4,0},{5,1},{6,2},{7,3},{8,12},{9,13},{10,... | collective-permute-start | bytes 442376 | tf_op jit(solution)/shard_map/ppermute | solution.py:452
  28.1 9.9 %collective-permute-start.6 = (bf16[384,1024]{1,0:T(8,128)(2,1)S(1)}, bf16[384,1024]{1,0:T(8,128)(2,1)S(1)}, u32[]{:S(2)}, u32[]{:S(2)}) collective-permute-start(bf16[384,1024]{1,0:T(8,128)(2,1)S(1)} %bitcast.24), channel_id=1, source_target_pairs={{0,1},{1,0},{2,3},{3,2},{4,5},{5,4},{6,7},{7,6},{8,9},{9,8},{10,11... | collective-permute-start | bytes 2359304 | tf_op jit(solution)/shard_map/ppermute | solution.py:455
  28.4 21.3 %collective-permute-start.4 = (bf16[384,1024]{1,0:T(8,128)(2,1)S(1)}, bf16[384,1024]{1,0:T(8,128)(2,1)}, u32[]{:S(2)}, u32[]{:S(2)}) collective-permute-start(bf16[384,1024]{1,0:T(8,128)(2,1)S(1)} %bitcast.25), channel_id=1, source_target_pairs={{0,2},{1,3},{2,4},{3,5},{4,6},{5,7},{6,0},{7,1},{8,10},{9,11},{10,... | collective-permute-start | bytes 2359304 | tf_op jit(solution)/shard_map/ppermute | solution.py:452
  30.0 19.8 %collective-permute-start.5 = (bf16[384,1024]{1,0:T(8,128)(2,1)S(1)}, bf16[384,1024]{1,0:T(8,128)(2,1)}, u32[]{:S(2)}, u32[]{:S(2)}) collective-permute-start(bf16[384,1024]{1,0:T(8,128)(2,1)S(1)} %bitcast.26), channel_id=1, source_target_pairs={{0,6},{1,7},{2,0},{3,1},{4,2},{5,3},{6,4},{7,5},{8,14},{9,15},{10,... | collective-permute-start | bytes 2359304 | tf_op jit(solution)/shard_map/ppermute | solution.py:452
  33.8 14.4 %all-to-all-start.1 = ((bf16[16,3,32,128]{3,2,1,0:T(8,128)(2,1)}), bf16[16,3,32,128]{3,2,1,0:T(8,128)(2,1)S(1)}, u32[]{:S(2)}, u32[]{:S(2)}) async-start(bf16[16,3,32,128]{3,2,1,0:T(8,128)(2,1)} %rank_sums_to_send.1.refs_3_), calls=%async_computation.1 | async-start | bytes 786432 | tf_op jit(solution)/shard_map/all_to_all | solution.py:503
  43.3 12.1 %copy-start.2 = (bf16[384,1024]{1,0:T(8,128)(2,1)S(1)}, bf16[384,1024]{1,0:T(8,128)(2,1)}, u32[]{:S(2)}) copy-start(bf16[384,1024]{1,0:T(8,128)(2,1)} %gradient.1) | copy-start | bytes 2359300
  51.8 16.4 %collective-permute-start.12 = (bf16[384,1024]{1,0:T(8,128)(2,1)}, bf16[384,1024]{1,0:T(8,128)(2,1)}, u32[]{:S(2)}, u32[]{:S(2)}) collective-permute-start(bf16[384,1024]{1,0:T(8,128)(2,1)} %get-tuple-element.27.refs_0_), channel_id=1, source_target_pairs={{0,1},{1,0},{2,3},{3,2},{4,5},{5,4},{6,7},{7,6},{8,9},{9,8},{10,11... | collective-permute-start | bytes 2359304 | tf_op jit(solution)/shard_map/ppermute | solution.py:455
  51.8 16.3 %collective-permute-start.13 = (bf16[384,1024]{1,0:T(8,128)(2,1)}, bf16[384,1024]{1,0:T(8,128)(2,1)}, u32[]{:S(2)}, u32[]{:S(2)}) collective-permute-start(bf16[384,1024]{1,0:T(8,128)(2,1)} %get-tuple-element.28.refs_2_), channel_id=1, source_target_pairs={{0,1},{1,0},{2,3},{3,2},{4,5},{5,4},{6,7},{7,6},{8,9},{9,8},{10,11... | collective-permute-start | bytes 2359304 | tf_op jit(solution)/shard_map/ppermute | solution.py:455
  52.3 3.1 %collective-permute-start.11 = (bf16[16,3,32,128]{3,2,1,0:T(8,128)(2,1)S(1)}, bf16[16,3,32,128]{3,2,1,0:T(8,128)(2,1)S(1)}, u32[]{:S(2)}, u32[]{:S(2)}) collective-permute-start(bf16[16,3,32,128]{3,2,1,0:T(8,128)(2,1)S(1)} %all-to-all-done.1.token.crossed), channel_id=1, source_target_pairs={{0,1},{1,0},{2,3},{3,2},{4,5},{5,4},{6,7},{7,6},{8,9},{9,8},{10,11... | collective-permute-start | bytes 1179656 | tf_op jit(solution)/shard_map/ppermute | solution.py:455
  52.4 12.3 %collective-permute-start.8 = (bf16[192,1024]{1,0:T(8,128)(2,1)}, bf16[192,1024]{1,0:T(8,128)(2,1)S(1)}, u32[]{:S(2)}, u32[]{:S(2)}) collective-permute-start(bf16[192,1024]{1,0:T(8,128)(2,1)} %get-tuple-element.25), channel_id=1, source_target_pairs={{0,6},{1,7},{2,0},{3,1},{4,2},{5,3},{6,4},{7,5},{8,14},{9,15},{10,... | collective-permute-start | bytes 1179656 | tf_op jit(solution)/shard_map/ppermute | solution.py:452
  55.4 12.7 %collective-permute-start.7 = (bf16[192,1024]{1,0:T(8,128)(2,1)}, bf16[192,1024]{1,0:T(8,128)(2,1)}, u32[]{:S(2)}, u32[]{:S(2)}) collective-permute-start(bf16[192,1024]{1,0:T(8,128)(2,1)} %get-tuple-element.24.token), channel_id=1, source_target_pairs={{0,2},{1,3},{2,4},{3,5},{4,6},{5,7},{6,0},{7,1},{8,10},{9,11},{10,... | collective-permute-start | bytes 1179656 | tf_op jit(solution)/shard_map/ppermute | solution.py:452
  57.0 0.8 copy-start.6
  57.8 18.5 %all-to-all-start.2 = ((f32[16,8,1024]{2,1,0:T(8,128)}), f32[16,8,1024]{2,1,0:T(8,128)S(1)}, u32[]{:S(2)}, u32[]{:S(2)}) async-start(f32[16,8,1024]{2,1,0:T(8,128)} %bitcast.29), calls=%async_computation.2 | async-start | bytes 1048576 | tf_op jit(solution)/shard_map/all_to_all | solution.py:520
  64.7 11.6 %collective-permute-start.10 = (bf16[192,1024]{1,0:T(8,128)(2,1)S(1)}, bf16[192,1024]{1,0:T(8,128)(2,1)S(1)}, u32[]{:S(2)}, u32[]{:S(2)}) collective-permute-start(bf16[192,1024]{1,0:T(8,128)(2,1)S(1)} %collective-permute-done.8.far_b), channel_id=1, source_target_pairs={{0,1},{1,0},{2,3},{3,2},{4,5},{5,4},{6,7},{7,6},{8,9},{9,8},{10,11... | collective-permute-start | bytes 1179656 | tf_op jit(solution)/shard_map/ppermute | solution.py:455
  68.1 8.2 %collective-permute-start.9 = (bf16[192,1024]{1,0:T(8,128)(2,1)}, bf16[192,1024]{1,0:T(8,128)(2,1)S(1)}, u32[]{:S(2)}, u32[]{:S(2)}) collective-permute-start(bf16[192,1024]{1,0:T(8,128)(2,1)} %collective-permute-done.7.far_a), channel_id=1, source_target_pairs={{0,1},{1,0},{2,3},{3,2},{4,5},{5,4},{6,7},{7,6},{8,9},{9,8},{10,11... | collective-permute-start | bytes 1179656 | tf_op jit(solution)/shard_map/ppermute | solution.py:455
  68.1 8.2 %copy-start.5 = (bf16[1024,64]{0,1:T(8,128)(2,1)S(1)}, bf16[1024,64]{0,1:T(8,128)(2,1)}, u32[]{:S(2)}) copy-start(bf16[1024,64]{0,1:T(8,128)(2,1)} %param.10) | copy-start | bytes 393220
  83.0 31.9 %copy-start.1 = (bf16[64,1024]{1,0:T(8,128)(2,1)S(1)}, bf16[64,1024]{1,0:T(8,128)(2,1)}, u32[]{:S(2)}) copy-start(bf16[64,1024]{1,0:T(8,128)(2,1)} %param.11) | copy-start | bytes 393220

commit v9 on v8

--- a/solution.py
+++ b/solution.py
@@ -29,7 +29,25 @@
     )
 
 
-def halves_kernel(left, right, token, token_too, top, bottom, left_out, right_out, buffer, sem):
+def after_kernel(*refs):
+    pass
+
+
+def after(values, token):
+    count = len(values)
+    return pl.pallas_call(
+        after_kernel,
+        in_specs=[ANY] * (count + 1),
+        out_specs=[ANY] * count,
+        out_shape=[jax.ShapeDtypeStruct(value.shape, value.dtype) for value in values],
+        input_output_aliases={i: i for i in range(count)},
+        compiler_params=pltpu.CompilerParams(vmem_limit_bytes=2**20),
+        name="after",
+    )(*values, token)
+
+
+def halves_kernel(left, right, grads, token, top, bottom, *refs):
+    buffer, sem = refs[3:]
     half = top.shape[0]
     parts = ((left.at[pl.ds(0, half)], top), (right.at[pl.ds(half, half)], bottom))
     loads = [
@@ -47,14 +65,15 @@
         store.wait()
 
 
-def take_halves(left, right, *tokens):
+def take_halves(left, right, grads, token):
     half = jax.ShapeDtypeStruct((left.shape[0] // 2, left.shape[1]), left.dtype)
     return pl.pallas_call(
         halves_kernel,
         in_specs=[ANY] * 4,
-        out_specs=[HBM] * 2 + [ANY] * 2,
-        out_shape=[half] * 2 + [jax.ShapeDtypeStruct(left.shape, left.dtype)] * 2,
-        input_output_aliases={0: 2, 1: 3},
+        out_specs=[HBM] * 2 + [ANY] * 3,
+        out_shape=[half] * 2
+        + [jax.ShapeDtypeStruct(part.shape, part.dtype) for part in (left, right, grads)],
+        input_output_aliases={0: 2, 1: 3, 2: 4},
         scratch_shapes=[
             pltpu.VMEM((2,) + half.shape, half.dtype),
             pltpu.SemaphoreType.DMA((4,)),
@@ -64,7 +83,7 @@
             flops=0, bytes_accessed=8 * left.shape[0] * left.shape[1], transcendentals=0
         ),
         name="take_halves",
-    )(left, right, *tokens)
+    )(left, right, grads, token)
 
 
 def block_kernel(table, first, index, *refs):
@@ -509,22 +528,26 @@
         table, [owner_at, owner_at + 1], [spread, other], output_weight, send,
         name="own_products",
     )
+    (crossed,) = after([crossed], done)
     crossed_other = swap(crossed)
-    left_top, right_bottom, left, right = take_halves(left, right, crossed, done)
+    partial_grads, done = gradient_products(
+        table, end - 1, source_at, dest_at, crossed, crossed_other, done, attention_slot_outputs,
+        output_gradient_rows,
+    )
+    left_top, right_bottom, left, right, partial_grads = take_halves(
+        left, right, partial_grads, done
+    )
     far = [move(left_top, 1), move(right_bottom, -1)]
-    partial_grads, done = gradient_products(
-        table, end - 1, source_at, dest_at, crossed, crossed_other, left_top, attention_slot_outputs,
-        output_gradient_rows,
-    )
     share_rows = 2 * rank // groups
     grads = lax.all_to_all(
         partial_grads.reshape(groups, share_rows, width_here), "group", split_axis=0, concat_axis=0,
         tiled=True,
     )
-    sums, _ = block_products(
+    sums, done = block_products(
         table, [owner_at + i for i in range(2, 6)], [left, swap(left), right, swap(right)],
         output_weight, done, sums, name="side_products",
     )
+    far = after(far, done)
     placed = last_products(
         rows, scale_factor, table, [owner_at + 6, owner_at + 7], end - 1, far,
         [swap(part) for part in far], grads, (crossed, crossed_other), output_weight, sums,

time: 115 us -> 114 us (level)
  waiting for transfers between devices: 21.8 us -> 20.2 us
  blocking collectives: 30.3 us -> 31.5 us
    ppermute x7, waiting for transfers between devices: 14.2 us -> 8.73 us  [move(): return lax.ppermute(value, 'tp', pairs)]
    all_to_all x1, waiting for transfers between devices: 0.01 us -> 3.24 us  [body(): lax.all_to_all(partial_grads.reshape(groups, share_rows, width_here), 'gr...]
    ppermute x7, waiting for transfers between devices: 0.02 us -> 1.74 us  [swap(): return lax.ppermute(value, 'tp', [(i, i ^ 1) for i in range(tp)])]
    all_to_all x1, blocking collectives: 30.3 us -> 31.5 us  [body(): lax.all_to_all(placed, 'group', split_axis=0, concat_axis=0, tiled=True)]
  transfers between devices with their start and end apart: 17 -> 17, of which waited for: 8 -> 7; matrix products, arithmetic and copies ran while one was open for 1% -> 1% of each run, Pallas kernels for 14% -> 14%
where the time goes in v9:
time: 114 us; the launch traced here: 113 us
  blocking collectives  31.5 us (28%)
  starting transfers between devices  28.7 us (25%)
  Pallas kernels  25.9 us (23%)
  waiting for transfers between devices  20.2 us (18%)
  local copies, waits for them, and re-layouts  2.95 us (3%)
  matrix products  2.09 us (2%)
    all_to_all x1, blocking collectives, body(): lax.all_to_all(placed, 'group', split_axis=0, concat_axis=0, tiled=True)  31.5 us
    pallas_call x2, Pallas kernels, block_products(): pl.pallas_call(functools.partial(block_kernel, table, first), in_specs=[S...  12.9 us
    ppermute x7, starting transfers between devices, move(): return lax.ppermute(value, 'tp', pairs)  11.6 us
    ppermute x7, waiting for transfers between devices, move(): return lax.ppermute(value, 'tp', pairs)  8.73 us
    all_to_all x1, starting transfers between devices, body(): lax.all_to_all(pieces_out, 'group', split_axis=0, concat_axis=0, tiled=True)  7.97 us
    pallas_call x1, Pallas kernels, last_products(): pl.pallas_call(functools.partial(last_kernel, rows, scale, table, core_at...  6.6 us
    all_to_all x1, waiting for transfers between devices, body(): lax.all_to_all(send, 'group', split_axis=0, concat_axis=0, tiled=True)  4.82 us
    all_to_all x1, starting transfers between devices, body(): lax.all_to_all(send, 'group', split_axis=0, concat_axis=0, tiled=True)  4.28 us
  transfers between devices with their start and end apart: 17, of which 7 were waited for; matrix products, arithmetic and copies ran while one was open for 1% of the time, Pallas kernels for 14%

profile of v9, /device:TPU:0, one launch (start us, length us, event | category | flops | bytes accessed | tf_op | source)
XLA Modules:
  0.0 113.1 jit_solution(10746752771815737281)
XLA Ops:
  0.7 2.2 %copy.25 = bf16[3,16,8,1024]{3,2,0,1:T(8,128)(2,1)} copy(bf16[3,16,8,1024]{3,2,1,0:T(8,128)(2,1)} %bitcast.23) | data formatting | bytes 1572864 | tf_op jit(solution)/shard_map/reshape | solution.py:476
  2.9 1.5 %fusion.4 = f32[64,384]{1,0:T(8,128)S(1)} fusion(bf16[64,1024]{1,0:T(8,128)(2,1)S(1)} %copy-done, bf16[384,1024]{1,0:T(8,128)(2,1)} %gradient.1), kind=kOutput, calls=%fused_computation.20 | convolution fusion | flops 50331648 | bytes 1015808 | tf_op jit(solution)/shard_map/dot_general | solution.py:27
  4.4 0.6 fusion.5
  5.1 8.0 %all-to-all-start = ((bf16[16,3,8,1024]{3,2,1,0:T(8,128)(2,1)}), bf16[16,3,8,1024]{3,2,1,0:T(8,128)(2,1)S(1)}, u32[]{:S(2)}, u32[]{:S(2)}) async-start(bf16[16,3,8,1024]{3,2,1,0:T(8,128)(2,1)} %bitcast.22), calls=%async_computation | async-start | bytes 1572864 | tf_op jit(solution)/shard_map/all_to_all | solution.py:481
  13.2 3.1 %collective-permute-start.2 = (f32[32,1152]{1,0:T(8,128)S(1)}, f32[32,1152]{1,0:T(8,128)S(1)}, u32[]{:S(2)}, u32[]{:S(2)}) collective-permute-start(f32[32,1152]{1,0:T(8,128)S(1)} %fusion.1), channel_id=1, source_target_pairs={{0,6},{1,7},{2,0},{3,1},{4,2},{5,3},{6,4},{7,5},{8,14},{9,15},{10,... | collective-permute-start | bytes 442376 | tf_op jit(solution)/shard_map/ppermute | solution.py:471
  16.3 2.2 %collective-permute-start.3 = (f32[32,1152]{1,0:T(8,128)S(1)}, f32[32,1152]{1,0:T(8,128)S(1)}, u32[]{:S(2)}, u32[]{:S(2)}) collective-permute-start(f32[32,1152]{1,0:T(8,128)S(1)} %fusion.1), channel_id=1, source_target_pairs={{0,4},{1,5},{2,6},{3,7},{4,0},{5,1},{6,2},{7,3},{8,12},{9,13},{10,... | collective-permute-start | bytes 442376 | tf_op jit(solution)/shard_map/ppermute | solution.py:471
  18.7 0.1 copy.21
  18.9 0.2 select_reduce_fusion.1
  19.1 0.8 collective-permute-done.2
  19.9 6.5 %collective-permute-done.1 = f32[32,1152]{1,0:T(8,128)S(1)} collective-permute-done((f32[32,1152]{1,0:T(8,128)S(1)}, f32[32,1152]{1,0:T(8,128)S(1)}, u32[]{:S(2)}, u32[]{:S(2)}) %collective-permute-start.1) | collective-permute-done | bytes 147488 | tf_op jit(solution)/shard_map/ppermute | solution.py:471
  26.4 1.7 %all-to-all-done = bf16[16,3,8,1024]{3,2,1,0:T(8,128)(2,1)S(1)} async-done(((bf16[16,3,8,1024]{3,2,1,0:T(8,128)(2,1)}), bf16[16,3,8,1024]{3,2,1,0:T(8,128)(2,1)S(1)}, u32[]{:S(2)}, u32[]{:S(2)}) %all-to-all-start) | async-done | bytes 786464 | tf_op jit(solution)/shard_map/all_to_all | solution.py:481
  28.3 0.1 select_reduce_fusion.4
  28.4 0.1 select_reduce_fusion.2
  28.5 0.1 select_reduce_fusion.3
  28.6 3.1 %collective-permute-start.5 = (bf16[384,1024]{1,0:T(8,128)(2,1)S(1)}, bf16[384,1024]{1,0:T(8,128)(2,1)}, u32[]{:S(2)}, u32[]{:S(2)}) collective-permute-start(bf16[384,1024]{1,0:T(8,128)(2,1)S(1)} %bitcast.25), channel_id=1, source_target_pairs={{0,6},{1,7},{2,0},{3,1},{4,2},{5,3},{6,4},{7,5},{8,14},{9,15},{10,... | collective-permute-start | bytes 2359304 | tf_op jit(solution)/shard_map/ppermute | solution.py:471
  32.1 1.5 %rank_sums_to_send.1.refs_3_ = bf16[16,3,32,128]{3,2,1,0:T(8,128)(2,1)} custom-call(s32[146]{0:T(256)S(1)} %concatenate.6.index, f32[32,1152]{1,0:T(8,128)S(1)} %add_add_fusion.share), custom_call_target="tpu_custom_call" | custom-call | flops 131072 | bytes 524288 | tf_op jit(solution)/shard_map/rank_sums_to_send/pallas_call | solution.py:296
  33.6 4.3 %all-to-all-start.1 = ((bf16[16,3,32,128]{3,2,1,0:T(8,128)(2,1)}), bf16[16,3,32,128]{3,2,1,0:T(8,128)(2,1)S(1)}, u32[]{:S(2)}, u32[]{:S(2)}) async-start(bf16[16,3,32,128]{3,2,1,0:T(8,128)(2,1)} %rank_sums_to_send.1.refs_3_), calls=%async_computation.1 | async-start | bytes 786432 | tf_op jit(solution)/shard_map/all_to_all | solution.py:522
  37.9 5.3 %own_products.1 = (f32[6144,1024]{1,0:T(8,128)}, f32[8,128]{1,0:T(8,128)S(1)}) custom-call(s32[146]{0:T(256)S(1)} %concatenate.6.index, bf16[384,1024]{1,0:T(8,128)(2,1)S(1)} %bitcast.27, bf16[384,1024]{1,0:T(8,128)(2,1)} %collective-permute-done.6.refs_1_, bf16[1024,8192]{1,0:T(8,128)(2,1)} %weight.1, bf16[16,3,32,128]{3,2,1,0:T(8,128)(2,1)} %rank_sums_to_send.1.refs_3_), custom_call_target="tpu_custom_call" | custom-call | flops 1610612736 | bytes 5767168 | tf_op jit(solution)/shard_map/own_products/pallas_call | solution.py:136
  43.2 4.8 %all-to-all-done.1.refs_0_ = bf16[16,3,32,128]{3,2,1,0:T(8,128)(2,1)S(1)} async-done(((bf16[16,3,32,128]{3,2,1,0:T(8,128)(2,1)}), bf16[16,3,32,128]{3,2,1,0:T(8,128)(2,1)S(1)}, u32[]{:S(2)}, u32[]{:S(2)}) %all-to-all-start.1) | async-done | bytes 393248 | tf_op jit(solution)/shard_map/all_to_all | solution.py:522
  48.0 1.7 %collective-permute-done.7.crossed_other = bf16[16,3,32,128]{3,2,1,0:T(8,128)(2,1)S(1)} collective-permute-done((bf16[16,3,32,128]{3,2,1,0:T(8,128)(2,1)S(1)}, bf16[16,3,32,128]{3,2,1,0:T(8,128)(2,1)S(1)}, u32[]{:S(2)}, u32[]{:S(2)}) %collective-permute-start.7) | collective-permute-done | bytes 393248 | tf_op jit(solution)/shard_map/ppermute | solution.py:474
  49.8 1.5 %gradient_products.1 = (f32[128,1024]{1,0:T(8,128)S(1)}, f32[8,128]{1,0:T(8,128)S(1)}) custom-call(s32[146]{0:T(256)S(1)} %concatenate.6.index, bf16[16,3,32,128]{3,2,1,0:T(8,128)(2,1)S(1)} %after.2.crossed, bf16[16,3,32,128]{3,2,1,0:T(8,128)(2,1)S(1)} %collective-permute-done.7.crossed_other, f32[8,128]{1,0:T(8,128)S(1)} %get-tuple-element.27.refs_1_.token, ...), custom_call_target="tpu_custom_call" | custom-call | flops 150994944 | bytes 2359296 | tf_op jit(solution)/shard_map/gradient_products/pallas_call | solution.py:358
  51.3 1.4 %collective-permute-done.4.left = bf16[384,1024]{1,0:T(8,128)(2,1)} collective-permute-done((bf16[384,1024]{1,0:T(8,128)(2,1)S(1)}, bf16[384,1024]{1,0:T(8,128)(2,1)}, u32[]{:S(2)}, u32[]{:S(2)}) %collective-permute-start.4) | collective-permute-done | bytes 786464 | tf_op jit(solution)/shard_map/ppermute | solution.py:471
  52.7 1.8 %take_halves.1 = (bf16[192,1024]{1,0:T(8,128)(2,1)}, bf16[192,1024]{1,0:T(8,128)(2,1)S(1)}, bf16[384,1024]{1,0:T(8,128)(2,1)}, bf16[384,1024]{1,0:T(8,128)(2,1)}, f32[128,1024]{1,0:T(8,128)S(1)}) custom-call(bf16[384,1024]{1,0:T(8,128)(2,1)} %collective-permute-done.4.left, ...), custom_call_target="tpu_custom_call", output_to_operand_aliasing={{2}: (0, {}), {3}: (1, {}), {4}: (2, {})} | custom-call | bytes 3145728 | tf_op jit(solution)/shard_map/take_halves/pallas_call | solution.py:70
  54.6 0.5 collective-permute-start.11
  55.1 3.2 %collective-permute-start.9 = (bf16[192,1024]{1,0:T(8,128)(2,1)S(1)}, bf16[192,1024]{1,0:T(8,128)(2,1)S(1)}, u32[]{:S(2)}, u32[]{:S(2)}) collective-permute-start(bf16[192,1024]{1,0:T(8,128)(2,1)S(1)} %get-tuple-element.31), channel_id=1, source_target_pairs={{0,6},{1,7},{2,0},{3,1},{4,2},{5,3},{6,4},{7,5},{8,14},{9,15},{10,... | collective-permute-start | bytes 1179656 | tf_op jit(solution)/shard_map/ppermute | solution.py:471
  58.4 3.6 %all-to-all-start.2 = ((f32[16,8,1024]{2,1,0:T(8,128)}), f32[16,8,1024]{2,1,0:T(8,128)S(1)}, u32[]{:S(2)}, u32[]{:S(2)}) async-start(f32[16,8,1024]{2,1,0:T(8,128)} %bitcast.28), calls=%async_computation.2 | async-start | bytes 1048576 | tf_op jit(solution)/shard_map/all_to_all | solution.py:542
  62.0 7.6 %side_products.1 = (f32[6144,1024]{1,0:T(8,128)}, f32[8,128]{1,0:T(8,128)S(1)}) custom-call(s32[146]{0:T(256)S(1)} %concatenate.6.index, bf16[384,1024]{1,0:T(8,128)(2,1)} %get-tuple-element.32.refs_0_, bf16[384,1024]{1,0:T(8,128)(2,1)S(1)} %collective-permute-done.10.refs_1_, bf16[384,1024]{1,0:T(8,128)(2,1)} %get-tuple-element.33.refs_2_, ...), custom_call_target="tpu_custom_call" | custom-call | flops 3221225472 | bytes 11534336 | tf_op jit(solution)/shard_map/side_products/pallas_call | solution.py:136
  69.7 0.5 collective-permute-start.13
  70.2 3.2 %all-to-all-done.2.grads_in = f32[16,8,1024]{2,1,0:T(8,128)S(1)} async-done(((f32[16,8,1024]{2,1,0:T(8,128)}), f32[16,8,1024]{2,1,0:T(8,128)S(1)}, u32[]{:S(2)}, u32[]{:S(2)}) %all-to-all-start.2) | async-done | bytes 524320 | tf_op jit(solution)/shard_map/all_to_all | solution.py:542
  73.4 6.6 %last_products.1 = bf16[16,7,16,512]{3,2,1,0:T(8,128)(2,1)S(1)} custom-call(s32[146]{0:T(256)S(1)} %concatenate.6.index, bf16[192,1024]{1,0:T(8,128)(2,1)S(1)} %get-tuple-element.36.far_a, bf16[192,1024]{1,0:T(8,128)(2,1)S(1)} %get-tuple-element.37.far_b, bf16[192,1024]{1,0:T(8,128)(2,1)S(1)} %collective-permute-done.12.other_a, ...), custom_call_target="tpu_custom_call" | custom-call | flops 1610612736 | bytes 4718592 | tf_op jit(solution)/shard_map/last_products/pallas_call | solution.py:246
  80.1 31.5 %all_to_all.20.arrived.gradients = bf16[16,7,16,512]{3,2,1,0:T(8,128)(2,1)S(1)} all-to-all(bf16[16,7,16,512]{3,2,1,0:T(8,128)(2,1)S(1)} %last_products.1), channel_id=1, replica_groups=mesh['group'=16,'tp'=8] {'group'}, dimensions={0} | all-to-all | bytes 3670016 | tf_op jit(solution)/shard_map/all_to_all | solution.py:557
  111.5 1.6 %unfold.1 = (bf16[768,1024]{1,0:T(8,128)(2,1)}, f32[64,1024]{1,0:T(8,128)}, f32[64,1024]{1,0:T(8,128)}) custom-call(bf16[16,7,16,512]{3,2,1,0:T(8,128)(2,1)S(1)} %all_to_all.20.arrived.gradients, bf16[16,7,16,512]{3,2,1,0:T(8,128)(2,1)S(1)} %all_to_all.20.arrived.gradients), custom_call_target="tpu_custom_call" | custom-call | tf_op jit(solution)/shard_map/unfold/pallas_call | solution.py:416
  (57 shorter events, 1.2 us)
Async XLA Ops:
  0.6 2.2 %copy-start = (bf16[64,1024]{1,0:T(8,128)(2,1)S(1)}, bf16[64,1024]{1,0:T(8,128)(2,1)}, u32[]{:S(2)}) copy-start(bf16[64,1024]{1,0:T(8,128)(2,1)} %param.11) | copy-start | bytes 393220
  0.6 3.7 %copy-start.7 = (bf16[1024,64]{0,1:T(8,128)(2,1)S(1)}, bf16[1024,64]{0,1:T(8,128)(2,1)}, u32[]{:S(2)}) copy-start(bf16[1024,64]{0,1:T(8,128)(2,1)} %param.10) | copy-start | bytes 393220
  0.7 3.7 %copy-start.3 = (bf16[768,1024]{1,0:T(8,128)(2,1)S(1)}, bf16[768,1024]{1,0:T(8,128)(2,1)}, u32[]{:S(2)}) copy-start(bf16[768,1024]{1,0:T(8,128)(2,1)} %attention.1) | copy-start | bytes 4718596
  4.4 8.7 %copy-start.9 = (s32[48]{0:T(128)S(1)}, s32[48]{0:T(128)}, u32[]{:S(2)}) copy-start(s32[48]{0:T(128)} %param.12) | copy-start | bytes 580
  5.0 13.9 %copy-start.10 = (s32[16]{0:T(128)S(1)}, s32[16]{0:T(128)}, u32[]{:S(2)}) copy-start(s32[16]{0:T(128)} %param.13) | copy-start | bytes 196
  5.0 8.2 %collective-permute-start = (f32[64,1152]{1,0:T(8,128)S(1)}, f32[64,1152]{1,0:T(8,128)S(1)}, u32[]{:S(2)}, u32[]{:S(2)}) collective-permute-start(f32[64,1152]{1,0:T(8,128)S(1)} %pad_maximum_fusion), channel_id=1, source_target_pairs={{0,1},{1,0},{2,3},{3,2},{4,5},{5,4},{6,7},{7,6},{8,9},{9,8},{10,11... | collective-permute-start | bytes 884744 | tf_op jit(solution)/shard_map/ppermute | solution.py:474
  5.1 23.0 %all-to-all-start = ((bf16[16,3,8,1024]{3,2,1,0:T(8,128)(2,1)}), bf16[16,3,8,1024]{3,2,1,0:T(8,128)(2,1)S(1)}, u32[]{:S(2)}, u32[]{:S(2)}) async-start(bf16[16,3,8,1024]{3,2,1,0:T(8,128)(2,1)} %bitcast.22), calls=%async_computation | async-start | bytes 1572864 | tf_op jit(solution)/shard_map/all_to_all | solution.py:481
  13.2 6.6 %collective-permute-start.2 = (f32[32,1152]{1,0:T(8,128)S(1)}, f32[32,1152]{1,0:T(8,128)S(1)}, u32[]{:S(2)}, u32[]{:S(2)}) collective-permute-start(f32[32,1152]{1,0:T(8,128)S(1)} %fusion.1), channel_id=1, source_target_pairs={{0,6},{1,7},{2,0},{3,1},{4,2},{5,3},{6,4},{7,5},{8,14},{9,15},{10,... | collective-permute-start | bytes 442376 | tf_op jit(solution)/shard_map/ppermute | solution.py:471
  16.3 10.0 %collective-permute-start.1 = (f32[32,1152]{1,0:T(8,128)S(1)}, f32[32,1152]{1,0:T(8,128)S(1)}, u32[]{:S(2)}, u32[]{:S(2)}) collective-permute-start(f32[32,1152]{1,0:T(8,128)S(1)} %fusion.1), channel_id=1, source_target_pairs={{0,2},{1,3},{2,4},{3,5},{4,6},{5,7},{6,0},{7,1},{8,10},{9,11},{10,... | collective-permute-start | bytes 442376 | tf_op jit(solution)/shard_map/ppermute | solution.py:471
  16.3 10.0 %collective-permute-start.3 = (f32[32,1152]{1,0:T(8,128)S(1)}, f32[32,1152]{1,0:T(8,128)S(1)}, u32[]{:S(2)}, u32[]{:S(2)}) collective-permute-start(f32[32,1152]{1,0:T(8,128)S(1)} %fusion.1), channel_id=1, source_target_pairs={{0,4},{1,5},{2,6},{3,7},{4,0},{5,1},{6,2},{7,3},{8,12},{9,13},{10,... | collective-permute-start | bytes 442376 | tf_op jit(solution)/shard_map/ppermute | solution.py:471
  28.1 9.8 %collective-permute-start.6 = (bf16[384,1024]{1,0:T(8,128)(2,1)S(1)}, bf16[384,1024]{1,0:T(8,128)(2,1)}, u32[]{:S(2)}, u32[]{:S(2)}) collective-permute-start(bf16[384,1024]{1,0:T(8,128)(2,1)S(1)} %bitcast.24), channel_id=1, source_target_pairs={{0,1},{1,0},{2,3},{3,2},{4,5},{5,4},{6,7},{7,6},{8,9},{9,8},{10,11... | collective-permute-start | bytes 2359304 | tf_op jit(solution)/shard_map/ppermute | solution.py:474
  28.6 22.6 %collective-permute-start.5 = (bf16[384,1024]{1,0:T(8,128)(2,1)S(1)}, bf16[384,1024]{1,0:T(8,128)(2,1)}, u32[]{:S(2)}, u32[]{:S(2)}) collective-permute-start(bf16[384,1024]{1,0:T(8,128)(2,1)S(1)} %bitcast.25), channel_id=1, source_target_pairs={{0,6},{1,7},{2,0},{3,1},{4,2},{5,3},{6,4},{7,5},{8,14},{9,15},{10,... | collective-permute-start | bytes 2359304 | tf_op jit(solution)/shard_map/ppermute | solution.py:471
  31.7 21.0 %collective-permute-start.4 = (bf16[384,1024]{1,0:T(8,128)(2,1)S(1)}, bf16[384,1024]{1,0:T(8,128)(2,1)}, u32[]{:S(2)}, u32[]{:S(2)}) collective-permute-start(bf16[384,1024]{1,0:T(8,128)(2,1)S(1)} %bitcast.26), channel_id=1, source_target_pairs={{0,2},{1,3},{2,4},{3,5},{4,6},{5,7},{6,0},{7,1},{8,10},{9,11},{10,... | collective-permute-start | bytes 2359304 | tf_op jit(solution)/shard_map/ppermute | solution.py:471
  33.6 14.5 %all-to-all-start.1 = ((bf16[16,3,32,128]{3,2,1,0:T(8,128)(2,1)}), bf16[16,3,32,128]{3,2,1,0:T(8,128)(2,1)S(1)}, u32[]{:S(2)}, u32[]{:S(2)}) async-start(bf16[16,3,32,128]{3,2,1,0:T(8,128)(2,1)} %rank_sums_to_send.1.refs_3_), calls=%async_computation.1 | async-start | bytes 786432 | tf_op jit(solution)/shard_map/all_to_all | solution.py:522
  37.9 11.9 %copy-start.2 = (bf16[384,1024]{1,0:T(8,128)(2,1)S(1)}, bf16[384,1024]{1,0:T(8,128)(2,1)}, u32[]{:S(2)}) copy-start(bf16[384,1024]{1,0:T(8,128)(2,1)} %gradient.1) | copy-start | bytes 2359300
  48.0 1.7 %collective-permute-start.7 = (bf16[16,3,32,128]{3,2,1,0:T(8,128)(2,1)S(1)}, bf16[16,3,32,128]{3,2,1,0:T(8,128)(2,1)S(1)}, u32[]{:S(2)}, u32[]{:S(2)}) collective-permute-start(bf16[16,3,32,128]{3,2,1,0:T(8,128)(2,1)S(1)} %after.2.crossed), channel_id=1, source_target_pairs={{0,1},{1,0},{2,3},{3,2},{4,5},{5,4},{6,7},{7,6},{8,9},{9,8},{10,11... | collective-permute-start | bytes 1179656 | tf_op jit(solution)/shard_map/ppermute | solution.py:474
  49.8 4.8 %copy-start.5 = (bf16[16,3,32,128]{3,2,1,0:T(8,128)(2,1)}, bf16[16,3,32,128]{3,2,1,0:T(8,128)(2,1)S(1)}, u32[]{:S(2)}) copy-start(bf16[16,3,32,128]{3,2,1,0:T(8,128)(2,1)S(1)} %collective-permute-done.7.crossed_other) | copy-start | bytes 1179652
  54.5 3.8 %copy-start.4 = (f32[128,1024]{1,0:T(8,128)}, f32[128,1024]{1,0:T(8,128)S(1)}, u32[]{:S(2)}) copy-start(f32[128,1024]{1,0:T(8,128)S(1)} %get-tuple-element.38) | copy-start | bytes 1572868
  54.5 7.4 %collective-permute-start.10 = (bf16[384,1024]{1,0:T(8,128)(2,1)}, bf16[384,1024]{1,0:T(8,128)(2,1)S(1)}, u32[]{:S(2)}, u32[]{:S(2)}) collective-permute-start(bf16[384,1024]{1,0:T(8,128)(2,1)} %get-tuple-element.32.refs_0_), channel_id=1, source_target_pairs={{0,1},{1,0},{2,3},{3,2},{4,5},{5,4},{6,7},{7,6},{8,9},{9,8},{10,11... | collective-permute-start | bytes 2359304 | tf_op jit(solution)/shard_map/ppermute | solution.py:474
  54.6 7.3 %collective-permute-start.11 = (bf16[384,1024]{1,0:T(8,128)(2,1)}, bf16[384,1024]{1,0:T(8,128)(2,1)}, u32[]{:S(2)}, u32[]{:S(2)}) collective-permute-start(bf16[384,1024]{1,0:T(8,128)(2,1)} %get-tuple-element.33.refs_2_), channel_id=1, source_target_pairs={{0,1},{1,0},{2,3},{3,2},{4,5},{5,4},{6,7},{7,6},{8,9},{9,8},{10,11... | collective-permute-start | bytes 2359304 | tf_op jit(solution)/shard_map/ppermute | solution.py:474
  55.1 14.4 %collective-permute-start.8 = (bf16[192,1024]{1,0:T(8,128)(2,1)}, bf16[192,1024]{1,0:T(8,128)(2,1)S(1)}, u32[]{:S(2)}, u32[]{:S(2)}) collective-permute-start(bf16[192,1024]{1,0:T(8,128)(2,1)} %get-tuple-element.30), channel_id=1, source_target_pairs={{0,2},{1,3},{2,4},{3,5},{4,6},{5,7},{6,0},{7,1},{8,10},{9,11},{10,... | collective-permute-start | bytes 1179656 | tf_op jit(solution)/shard_map/ppermute | solution.py:471
  55.1 14.4 %collective-permute-start.9 = (bf16[192,1024]{1,0:T(8,128)(2,1)S(1)}, bf16[192,1024]{1,0:T(8,128)(2,1)S(1)}, u32[]{:S(2)}, u32[]{:S(2)}) collective-permute-start(bf16[192,1024]{1,0:T(8,128)(2,1)S(1)} %get-tuple-element.31), channel_id=1, source_target_pairs={{0,6},{1,7},{2,0},{3,1},{4,2},{5,3},{6,4},{7,5},{8,14},{9,15},{10,... | collective-permute-start | bytes 1179656 | tf_op jit(solution)/shard_map/ppermute | solution.py:471
  58.4 15.1 %all-to-all-start.2 = ((f32[16,8,1024]{2,1,0:T(8,128)}), f32[16,8,1024]{2,1,0:T(8,128)S(1)}, u32[]{:S(2)}, u32[]{:S(2)}) async-start(f32[16,8,1024]{2,1,0:T(8,128)} %bitcast.28), calls=%async_computation.2 | async-start | bytes 1048576 | tf_op jit(solution)/shard_map/all_to_all | solution.py:542
  62.0 11.5 %copy-start.6 = (bf16[16,3,32,128]{3,2,1,0:T(8,128)(2,1)S(1)}, bf16[16,3,32,128]{3,2,1,0:T(8,128)(2,1)}, u32[]{:S(2)}) copy-start(bf16[16,3,32,128]{3,2,1,0:T(8,128)(2,1)} %copy-done.5) | copy-start | bytes 1179652
  62.0 11.5 %copy-start.8 = (bf16[1024,64]{0,1:T(8,128)(2,1)S(1)}, bf16[1024,64]{0,1:T(8,128)(2,1)}, u32[]{:S(2)}) copy-start(bf16[1024,64]{0,1:T(8,128)(2,1)} %param.10) | copy-start | bytes 393220
  69.6 3.8 %collective-permute-start.12 = (bf16[192,1024]{1,0:T(8,128)(2,1)S(1)}, bf16[192,1024]{1,0:T(8,128)(2,1)S(1)}, u32[]{:S(2)}, u32[]{:S(2)}) collective-permute-start(bf16[192,1024]{1,0:T(8,128)(2,1)S(1)} %get-tuple-element.36.far_a), channel_id=1, source_target_pairs={{0,1},{1,0},{2,3},{3,2},{4,5},{5,4},{6,7},{7,6},{8,9},{9,8},{10,11... | collective-permute-start | bytes 1179656 | tf_op jit(solution)/shard_map/ppermute | solution.py:474
  69.7 3.7 %collective-permute-start.13 = (bf16[192,1024]{1,0:T(8,128)(2,1)S(1)}, bf16[192,1024]{1,0:T(8,128)(2,1)S(1)}, u32[]{:S(2)}, u32[]{:S(2)}) collective-permute-start(bf16[192,1024]{1,0:T(8,128)(2,1)S(1)} %get-tuple-element.37.far_b), channel_id=1, source_target_pairs={{0,1},{1,0},{2,3},{3,2},{4,5},{5,4},{6,7},{7,6},{8,9},{9,8},{10,11... | collective-permute-start | bytes 1179656 | tf_op jit(solution)/shard_map/ppermute | solution.py:474
  80.1 33.1 %copy-start.1 = (bf16[64,1024]{1,0:T(8,128)(2,1)S(1)}, bf16[64,1024]{1,0:T(8,128)(2,1)}, u32[]{:S(2)}) copy-start(bf16[64,1024]{1,0:T(8,128)(2,1)} %param.11) | copy-start | bytes 393220

commit v10 on v9

--- a/solution.py
+++ b/solution.py
@@ -27,6 +27,53 @@
     return lax.dot_general(
         left, right, (((1,), (1,)), ((), ())), preferred_element_type=jnp.float32
     )
+
+
+def prepare_kernel(
+    groups, gradient, attention, up, down, pieces, parts, rows_in, slots_in, sem
+):
+    loads = [
+        pltpu.make_async_copy(gradient, rows_in, sem.at[0]),
+        pltpu.make_async_copy(attention, slots_in, sem.at[1]),
+    ]
+    for load in loads:
+        load.start()
+    tokens = rows_in.shape[0]
+    rows_here, piece = tokens // ROW_TOKENS, ROW_TOKENS // groups
+    loads[0].wait()
+    starts = [r * ROW_TOKENS + j * piece for j in range(groups) for r in range(rows_here)]
+    for pair in range(len(starts) // 2):
+        both = []
+        for start in starts[2 * pair : 2 * pair + 2]:
+            tile = start // (2 * piece) * 2 * piece
+            value = rows_in[tile : tile + 2 * piece, :].astype(jnp.float32)
+            both.append(value[start - tile : start - tile + piece])
+        pieces[2 * pair * piece : 2 * (pair + 1) * piece, :] = jnp.concatenate(
+            both, axis=0
+        ).astype(pieces.dtype)
+    parts[:, :tokens] = dot_minor(up[...], rows_in[...])
+    loads[1].wait()
+    parts[:, tokens:] = dot_minor(down[...], slots_in[...])
+
+
+def prepare(groups, gradient, attention, up, down):
+    rank = up.shape[0]
+    return pl.pallas_call(
+        functools.partial(prepare_kernel, groups),
+        in_specs=[ANY] * 2 + [VMEM] * 2,
+        out_specs=[VMEM] * 2,
+        out_shape=[
+            jax.ShapeDtypeStruct(gradient.shape, gradient.dtype),
+            jax.ShapeDtypeStruct((rank, gradient.shape[0] + attention.shape[0]), jnp.float32),
+        ],
+        scratch_shapes=[
+            pltpu.VMEM(gradient.shape, gradient.dtype),
+            pltpu.VMEM(attention.shape, attention.dtype),
+            pltpu.SemaphoreType.DMA((2,)),
+        ],
+        compiler_params=pltpu.CompilerParams(vmem_limit_bytes=56 * 2**20),
+        name="prepare",
+    )(gradient, attention, up, down)
 
 
 def after_kernel(*refs):
@@ -199,7 +246,7 @@
         each.append(load_sums(span, sem.at[n]))
         tile_copies.append(each)
     load_grads = pltpu.make_async_copy(grads_in, grads, sem.at[tiles + 2])
-    for each in [low_copies, copies] + tile_copies + [[load_grads]]:
+    for each in [low_copies, copies, tile_copies[0]]:
         for copy in each:
             copy.start()
     out[...] = jnp.zeros_like(out)
@@ -210,6 +257,9 @@
         both = jnp.concatenate([pieces[0, group], pieces[1, group]], axis=0).astype(jnp.float32)
         low[group * share : (group + 1) * share] = both.T[:share]
     low_rounded[...] = low[...].astype(jnp.bfloat16)
+    for each in tile_copies[1:] + [[load_grads]]:
+        for copy in each:
+            copy.start()
     for copy in copies:
         copy.wait()
     for n in range(tiles):
@@ -473,13 +523,11 @@
     def swap(value):
         return lax.ppermute(value, "tp", [(i, i ^ 1) for i in range(tp)])
 
-    pieces_out = output_gradient_rows.reshape(rows_here, groups, piece, width_here)
-    pieces_out = pieces_out.transpose(1, 0, 2, 3)
-    pieces_out, up_weight, down_weight_first = lax.optimization_barrier(
-        (pieces_out, up_weight, down_weight)
+    pieces_out, parts = prepare(
+        groups, output_gradient_rows, attention_slot_outputs, up_weight, down_weight.T
     )
     spread = lax.all_to_all(
-        pieces_out,
+        pieces_out.reshape(groups, rows_here, piece, width_here),
         "group",
         split_axis=0,
         concat_axis=0,
@@ -508,12 +556,6 @@
     _, _, pick_at, source_at, dest_at, owner_at, end = at
     table = jnp.concatenate(pieces)
 
-    low_part = dot_minor(up_weight, output_gradient_rows)
-    projected_part = lax.dot_general(
-        down_weight_first, attention_slot_outputs, (((0,), (1,)), ((), ())),
-        preferred_element_type=jnp.float32,
-    )
-    parts = jnp.concatenate([low_part, projected_part], axis=1)
     parts = parts + swap(parts)
     share = lax.dynamic_slice_in_dim(parts, core * (rank // 2), rank // 2, axis=0)
     share = share + move(share, 1) + move(share, -1) + move(share, 2)
@@ -521,7 +563,6 @@
     send = rank_sums_to_send(table, pick_at, groups, rows_here, share)
     crossed = lax.all_to_all(send, "group", split_axis=0, concat_axis=0, tiled=True)
 
-    spread, _ = lax.optimization_barrier((spread, share))
     left, right = move(spread, 1), move(spread, -1)
     other = swap(spread)
     sums, done = block_products(

time: 114 us -> 113 us (level)
  Pallas kernels: 25.9 us -> 29.8 us
  waiting for transfers between devices: 20.2 us -> 17.2 us
  matrix products: 2.09 us -> 0 us
    ppermute x7, waiting for transfers between devices: 8.73 us -> 1.88 us  [move(): return lax.ppermute(value, 'tp', pairs)]
    all_to_all x1, waiting for transfers between devices: 1.69 us -> 6.95 us  [body(): lax.all_to_all(pieces_out.reshape(groups, rows_here, piece, width_here),...]
    pallas_call x0 -> x1, Pallas kernels: none -> 4.02 us  [prepare(): pl.pallas_call(functools.partial(prepare_kernel, groups), in_specs=[ANY]...]
    unnamed x22, local copies, waits for them, and re-layouts: 0.07 us -> 2.83 us
    reshape x1 -> x0, local copies, waits for them, and re-layouts: 2.2 us -> none  [body(): output_gradient_rows.reshape(rows_here, groups, piece, width_here)]
    all_to_all x1, waiting for transfers between devices: 4.82 us -> 2.62 us  [body(): lax.all_to_all(send, 'group', split_axis=0, concat_axis=0, tiled=True)]
    dot_general x2 -> x0, matrix products: 2.09 us -> none  [the longest x1 1.49 us: dot_minor(): lax.dot_general(left, right, (((1,), (1,)), ((), ())), preferred_element_...]
  transfers between devices with their start and end apart: 17 -> 17, of which waited for: 7 -> 6; matrix products, arithmetic and copies ran while one was open for 1% -> 1% of each run, Pallas kernels for 14% -> 14%
where the time goes in v10:
time: 113 us; the launch traced here: 112 us
  blocking collectives  31.4 us (28%)
  Pallas kernels  29.8 us (26%)
  starting transfers between devices  28.8 us (25%)
  waiting for transfers between devices  17.2 us (15%)
  local copies, waits for them, and re-layouts  3.51 us (3%)
    all_to_all x1, blocking collectives, body(): lax.all_to_all(placed, 'group', split_axis=0, concat_axis=0, tiled=True)  31.4 us
    pallas_call x2, Pallas kernels, block_products(): pl.pallas_call(functools.partial(block_kernel, table, first), in_specs=[S...  12.9 us
    ppermute x7, starting transfers between devices, move(): return lax.ppermute(value, 'tp', pairs)  11.6 us
    all_to_all x1, starting transfers between devices, body(): lax.all_to_all(pieces_out.reshape(groups, rows_here, piece, width_here),...  8.11 us
    all_to_all x1, waiting for transfers between devices, body(): lax.all_to_all(pieces_out.reshape(groups, rows_here, piece, width_here),...  6.95 us
    pallas_call x1, Pallas kernels, last_products(): pl.pallas_call(functools.partial(last_kernel, rows, scale, table, core_at...  6.4 us
    all_to_all x1, starting transfers between devices, body(): lax.all_to_all(send, 'group', split_axis=0, concat_axis=0, tiled=True)  4.28 us
    pallas_call x1, Pallas kernels, prepare(): pl.pallas_call(functools.partial(prepare_kernel, groups), in_specs=[ANY]...  4.02 us
  transfers between devices with their start and end apart: 17, of which 6 were waited for; matrix products, arithmetic and copies ran while one was open for 1% of the time, Pallas kernels for 14%

profile of v10, /device:TPU:0, one launch (start us, length us, event | category | flops | bytes accessed | tf_op | source)
XLA Modules:
  0.0 112.5 jit_solution(16275948882895456989)
XLA Ops:
  0.7 4.0 %prepare.1 = (bf16[384,1024]{1,0:T(8,128)(2,1)}, f32[64,1152]{1,0:T(8,128)}) custom-call(bf16[384,1024]{1,0:T(8,128)(2,1)} %gradient.3, bf16[768,1024]{1,0:T(8,128)(2,1)} %attention.3, bf16[64,1024]{1,0:T(8,128)(2,1)} %up.1, bf16[64,1024]{1,0:T(8,128)(2,1)} %bitcast.21), custom_call_target="tpu_custom_call" | custom-call | tf_op jit(solution)/shard_map/prepare/pallas_call | solution.py:61
  4.7 8.1 %all-to-all-start = ((bf16[16,3,8,1024]{3,2,1,0:T(8,128)(2,1)}), bf16[16,3,8,1024]{3,2,1,0:T(8,128)(2,1)S(1)}, u32[]{:S(2)}, u32[]{:S(2)}) async-start(bf16[16,3,8,1024]{3,2,1,0:T(8,128)(2,1)} %bitcast.23), calls=%async_computation | async-start | bytes 1572864 | tf_op jit(solution)/shard_map/all_to_all | solution.py:529
  13.1 0.2 select_reduce_fusion.1
  13.5 0.1 select_reduce_fusion.4
  13.7 0.1 select_reduce_fusion.3
  13.8 0.9 collective-permute-done.2
  14.7 3.1 %collective-permute-start.4 = (f32[32,1152]{1,0:T(8,128)S(1)}, f32[32,1152]{1,0:T(8,128)S(1)}, u32[]{:S(2)}, u32[]{:S(2)}) collective-permute-start(f32[32,1152]{1,0:T(8,128)S(1)} %dynamic-slice_add_fusion), channel_id=1, source_target_pairs={{0,6},{1,7},{2,0},{3,1},{4,2},{5,3},{6,4},{7,5},{8,14},{9,15},{10,... | collective-permute-start | bytes 442376 | tf_op jit(solution)/shard_map/ppermute | solution.py:521
  17.8 2.2 %collective-permute-start.5 = (f32[32,1152]{1,0:T(8,128)S(1)}, f32[32,1152]{1,0:T(8,128)S(1)}, u32[]{:S(2)}, u32[]{:S(2)}) collective-permute-start(f32[32,1152]{1,0:T(8,128)S(1)} %dynamic-slice_add_fusion), channel_id=1, source_target_pairs={{0,4},{1,5},{2,6},{3,7},{4,0},{5,1},{6,2},{7,3},{8,12},{9,13},{10,... | collective-permute-start | bytes 442376 | tf_op jit(solution)/shard_map/ppermute | solution.py:521
  20.0 0.1 copy.19
  20.4 7.0 %all-to-all-done = bf16[16,3,8,1024]{3,2,1,0:T(8,128)(2,1)S(1)} async-done(((bf16[16,3,8,1024]{3,2,1,0:T(8,128)(2,1)}), bf16[16,3,8,1024]{3,2,1,0:T(8,128)(2,1)S(1)}, u32[]{:S(2)}, u32[]{:S(2)}) %all-to-all-start) | async-done | bytes 786464 | tf_op jit(solution)/shard_map/all_to_all | solution.py:529
  27.3 0.1 select_reduce_fusion.2
  27.5 3.1 %collective-permute-start.1 = (bf16[384,1024]{1,0:T(8,128)(2,1)S(1)}, bf16[384,1024]{1,0:T(8,128)(2,1)}, u32[]{:S(2)}, u32[]{:S(2)}) collective-permute-start(bf16[384,1024]{1,0:T(8,128)(2,1)S(1)} %bitcast.17), channel_id=1, source_target_pairs={{0,6},{1,7},{2,0},{3,1},{4,2},{5,3},{6,4},{7,5},{8,14},{9,15},{10,... | collective-permute-start | bytes 2359304 | tf_op jit(solution)/shard_map/ppermute | solution.py:521
  30.7 1.5 %rank_sums_to_send.1.refs_3_ = bf16[16,3,32,128]{3,2,1,0:T(8,128)(2,1)} custom-call(s32[146]{0:T(256)S(1)} %concatenate.3.index, f32[32,1152]{1,0:T(8,128)S(1)} %add_add_fusion.share), custom_call_target="tpu_custom_call" | custom-call | flops 131072 | bytes 524288 | tf_op jit(solution)/shard_map/rank_sums_to_send/pallas_call | solution.py:346
  32.2 4.3 %all-to-all-start.1 = ((bf16[16,3,32,128]{3,2,1,0:T(8,128)(2,1)}), bf16[16,3,32,128]{3,2,1,0:T(8,128)(2,1)S(1)}, u32[]{:S(2)}, u32[]{:S(2)}) async-start(bf16[16,3,32,128]{3,2,1,0:T(8,128)(2,1)} %rank_sums_to_send.1.refs_3_), calls=%async_computation.1 | async-start | bytes 786432 | tf_op jit(solution)/shard_map/all_to_all | solution.py:564
  36.5 0.9 copy-done.5
  37.4 1.1 %copy-done.6 = bf16[384,1024]{1,0:T(8,128)(2,1)S(1)} copy-done((bf16[384,1024]{1,0:T(8,128)(2,1)S(1)}, bf16[384,1024]{1,0:T(8,128)(2,1)}, u32[]{:S(2)}) %copy-start.6) | copy-done | bytes 786456
  38.5 5.3 %own_products.1 = (f32[6144,1024]{1,0:T(8,128)}, f32[8,128]{1,0:T(8,128)S(1)}) custom-call(s32[146]{0:T(256)S(1)} %concatenate.3.index, bf16[384,1024]{1,0:T(8,128)(2,1)S(1)} %bitcast.19, bf16[384,1024]{1,0:T(8,128)(2,1)S(1)} %copy-done.6, bf16[1024,8192]{1,0:T(8,128)(2,1)} %weight.1, bf16[16,3,32,128]{3,2,1,0:T(8,128)(2,1)} %rank_sums_to_send.1.refs_3_), custom_call_target="tpu_custom_call" | custom-call | flops 1610612736 | bytes 5767168 | tf_op jit(solution)/shard_map/own_products/pallas_call | solution.py:183
  43.8 2.6 %all-to-all-done.1.refs_0_ = bf16[16,3,32,128]{3,2,1,0:T(8,128)(2,1)S(1)} async-done(((bf16[16,3,32,128]{3,2,1,0:T(8,128)(2,1)}), bf16[16,3,32,128]{3,2,1,0:T(8,128)(2,1)S(1)}, u32[]{:S(2)}, u32[]{:S(2)}) %all-to-all-start.1) | async-done | bytes 393248 | tf_op jit(solution)/shard_map/all_to_all | solution.py:564
  46.5 1.7 %collective-permute-done.7.crossed_other = bf16[16,3,32,128]{3,2,1,0:T(8,128)(2,1)S(1)} collective-permute-done((bf16[16,3,32,128]{3,2,1,0:T(8,128)(2,1)S(1)}, bf16[16,3,32,128]{3,2,1,0:T(8,128)(2,1)S(1)}, u32[]{:S(2)}, u32[]{:S(2)}) %collective-permute-start.7) | collective-permute-done | bytes 393248 | tf_op jit(solution)/shard_map/ppermute | solution.py:524
  48.2 1.5 %gradient_products.1 = (f32[128,1024]{1,0:T(8,128)S(1)}, f32[8,128]{1,0:T(8,128)S(1)}) custom-call(s32[146]{0:T(256)S(1)} %concatenate.3.index, bf16[16,3,32,128]{3,2,1,0:T(8,128)(2,1)S(1)} %after.2.crossed, bf16[16,3,32,128]{3,2,1,0:T(8,128)(2,1)S(1)} %collective-permute-done.7.crossed_other, f32[8,128]{1,0:T(8,128)S(1)} %get-tuple-element.23.refs_1_.token, ...), custom_call_target="tpu_custom_call" | custom-call | flops 150994944 | bytes 2359296 | tf_op jit(solution)/shard_map/gradient_products/pallas_call | solution.py:408
  49.7 1.9 %collective-permute-done.left = bf16[384,1024]{1,0:T(8,128)(2,1)} collective-permute-done((bf16[384,1024]{1,0:T(8,128)(2,1)S(1)}, bf16[384,1024]{1,0:T(8,128)(2,1)}, u32[]{:S(2)}, u32[]{:S(2)}) %collective-permute-start) | collective-permute-done | bytes 786464 | tf_op jit(solution)/shard_map/ppermute | solution.py:521
  51.6 1.9 %take_halves.1 = (bf16[192,1024]{1,0:T(8,128)(2,1)}, bf16[192,1024]{1,0:T(8,128)(2,1)}, bf16[384,1024]{1,0:T(8,128)(2,1)}, bf16[384,1024]{1,0:T(8,128)(2,1)}, f32[128,1024]{1,0:T(8,128)S(1)}) custom-call(bf16[384,1024]{1,0:T(8,128)(2,1)} %collective-permute-done.left, ...), custom_call_target="tpu_custom_call", output_to_operand_aliasing={{2}: (0, {}), {3}: (1, {}), {4}: (2, {})} | custom-call | bytes 3145728 | tf_op jit(solution)/shard_map/take_halves/pallas_call | solution.py:117
  53.6 0.8 copy-done.2
  54.4 0.5 collective-permute-start.11
  54.9 3.2 %collective-permute-start.9 = (bf16[192,1024]{1,0:T(8,128)(2,1)}, bf16[192,1024]{1,0:T(8,128)(2,1)S(1)}, u32[]{:S(2)}, u32[]{:S(2)}) collective-permute-start(bf16[192,1024]{1,0:T(8,128)(2,1)} %get-tuple-element.27), channel_id=1, source_target_pairs={{0,6},{1,7},{2,0},{3,1},{4,2},{5,3},{6,4},{7,5},{8,14},{9,15},{10,... | collective-permute-start | bytes 1179656 | tf_op jit(solution)/shard_map/ppermute | solution.py:521
  58.1 3.6 %all-to-all-start.2 = ((f32[16,8,1024]{2,1,0:T(8,128)}), f32[16,8,1024]{2,1,0:T(8,128)S(1)}, u32[]{:S(2)}, u32[]{:S(2)}) async-start(f32[16,8,1024]{2,1,0:T(8,128)} %bitcast.20), calls=%async_computation.2 | async-start | bytes 1048576 | tf_op jit(solution)/shard_map/all_to_all | solution.py:583
  61.7 7.6 %side_products.1 = (f32[6144,1024]{1,0:T(8,128)}, f32[8,128]{1,0:T(8,128)S(1)}) custom-call(s32[146]{0:T(256)S(1)} %concatenate.3.index, bf16[384,1024]{1,0:T(8,128)(2,1)} %get-tuple-element.28.refs_0_, bf16[384,1024]{1,0:T(8,128)(2,1)S(1)} %collective-permute-done.10.refs_1_, bf16[384,1024]{1,0:T(8,128)(2,1)} %get-tuple-element.29.refs_2_, ...), custom_call_target="tpu_custom_call" | custom-call | flops 3221225472 | bytes 11534336 | tf_op jit(solution)/shard_map/side_products/pallas_call | solution.py:183
  69.4 0.5 collective-permute-start.13
  69.9 3.2 %all-to-all-done.2.grads_in = f32[16,8,1024]{2,1,0:T(8,128)S(1)} async-done(((f32[16,8,1024]{2,1,0:T(8,128)}), f32[16,8,1024]{2,1,0:T(8,128)S(1)}, u32[]{:S(2)}, u32[]{:S(2)}) %all-to-all-start.2) | async-done | bytes 524320 | tf_op jit(solution)/shard_map/all_to_all | solution.py:583
  73.1 6.4 %last_products.1 = bf16[16,7,16,512]{3,2,1,0:T(8,128)(2,1)S(1)} custom-call(s32[146]{0:T(256)S(1)} %concatenate.3.index, bf16[192,1024]{1,0:T(8,128)(2,1)S(1)} %get-tuple-element.32.far_a, bf16[192,1024]{1,0:T(8,128)(2,1)S(1)} %get-tuple-element.33.far_b, bf16[192,1024]{1,0:T(8,128)(2,1)S(1)} %collective-permute-done.12.other_a, ...), custom_call_target="tpu_custom_call" | custom-call | flops 1610612736 | bytes 4718592 | tf_op jit(solution)/shard_map/last_products/pallas_call | solution.py:296
  79.5 31.4 %all_to_all.20.arrived.gradients = bf16[16,7,16,512]{3,2,1,0:T(8,128)(2,1)S(1)} all-to-all(bf16[16,7,16,512]{3,2,1,0:T(8,128)(2,1)S(1)} %last_products.1), channel_id=1, replica_groups=mesh['group'=16,'tp'=8] {'group'}, dimensions={0} | all-to-all | bytes 3670016 | tf_op jit(solution)/shard_map/all_to_all | solution.py:598
  110.9 1.6 %unfold.1 = (bf16[768,1024]{1,0:T(8,128)(2,1)}, f32[64,1024]{1,0:T(8,128)}, f32[64,1024]{1,0:T(8,128)}) custom-call(bf16[16,7,16,512]{3,2,1,0:T(8,128)(2,1)S(1)} %all_to_all.20.arrived.gradients, bf16[16,7,16,512]{3,2,1,0:T(8,128)(2,1)S(1)} %all_to_all.20.arrived.gradients), custom_call_target="tpu_custom_call" | custom-call | tf_op jit(solution)/shard_map/unfold/pallas_call | solution.py:466
  (54 shorter events, 1.1 us)
Async XLA Ops:
  0.6 12.3 %copy-start.9 = (s32[48]{0:T(128)S(1)}, s32[48]{0:T(128)}, u32[]{:S(2)}) copy-start(s32[48]{0:T(128)} %param.12) | copy-start | bytes 580
  0.6 12.4 %copy-start.10 = (s32[16]{0:T(128)S(1)}, s32[16]{0:T(128)}, u32[]{:S(2)}) copy-start(s32[16]{0:T(128)} %param.13) | copy-start | bytes 196
  4.7 10.0 %copy-start.8 = (f32[64,1152]{1,0:T(8,128)S(1)}, f32[64,1152]{1,0:T(8,128)}, u32[]{:S(2)}) copy-start(f32[64,1152]{1,0:T(8,128)} %get-tuple-element.22) | copy-start | bytes 884740
  4.7 22.6 %all-to-all-start = ((bf16[16,3,8,1024]{3,2,1,0:T(8,128)(2,1)}), bf16[16,3,8,1024]{3,2,1,0:T(8,128)(2,1)S(1)}, u32[]{:S(2)}, u32[]{:S(2)}) async-start(bf16[16,3,8,1024]{3,2,1,0:T(8,128)(2,1)} %bitcast.23), calls=%async_computation | async-start | bytes 1572864 | tf_op jit(solution)/shard_map/all_to_all | solution.py:529
  12.8 1.9 %collective-permute-start.2 = (f32[64,1152]{1,0:T(8,128)}, f32[64,1152]{1,0:T(8,128)S(1)}, u32[]{:S(2)}, u32[]{:S(2)}) collective-permute-start(f32[64,1152]{1,0:T(8,128)} %get-tuple-element.22), channel_id=1, source_target_pairs={{0,1},{1,0},{2,3},{3,2},{4,5},{5,4},{6,7},{7,6},{8,9},{9,8},{10,11... | collective-permute-start | bytes 884744 | tf_op jit(solution)/shard_map/ppermute | solution.py:524
  14.7 15.9 %collective-permute-start.4 = (f32[32,1152]{1,0:T(8,128)S(1)}, f32[32,1152]{1,0:T(8,128)S(1)}, u32[]{:S(2)}, u32[]{:S(2)}) collective-permute-start(f32[32,1152]{1,0:T(8,128)S(1)} %dynamic-slice_add_fusion), channel_id=1, source_target_pairs={{0,6},{1,7},{2,0},{3,1},{4,2},{5,3},{6,4},{7,5},{8,14},{9,15},{10,... | collective-permute-start | bytes 442376 | tf_op jit(solution)/shard_map/ppermute | solution.py:521
  17.8 12.8 %collective-permute-start.3 = (f32[32,1152]{1,0:T(8,128)S(1)}, f32[32,1152]{1,0:T(8,128)S(1)}, u32[]{:S(2)}, u32[]{:S(2)}) collective-permute-start(f32[32,1152]{1,0:T(8,128)S(1)} %dynamic-slice_add_fusion), channel_id=1, source_target_pairs={{0,2},{1,3},{2,4},{3,5},{4,6},{5,7},{6,0},{7,1},{8,10},{9,11},{10,... | collective-permute-start | bytes 442376 | tf_op jit(solution)/shard_map/ppermute | solution.py:521
  17.8 12.8 %collective-permute-start.5 = (f32[32,1152]{1,0:T(8,128)S(1)}, f32[32,1152]{1,0:T(8,128)S(1)}, u32[]{:S(2)}, u32[]{:S(2)}) collective-permute-start(f32[32,1152]{1,0:T(8,128)S(1)} %dynamic-slice_add_fusion), channel_id=1, source_target_pairs={{0,4},{1,5},{2,6},{3,7},{4,0},{5,1},{6,2},{7,3},{8,12},{9,13},{10,... | collective-permute-start | bytes 442376 | tf_op jit(solution)/shard_map/ppermute | solution.py:521
  27.3 9.2 %collective-permute-start.6 = (bf16[384,1024]{1,0:T(8,128)(2,1)S(1)}, bf16[384,1024]{1,0:T(8,128)(2,1)S(1)}, u32[]{:S(2)}, u32[]{:S(2)}) collective-permute-start(bf16[384,1024]{1,0:T(8,128)(2,1)S(1)} %bitcast.16), channel_id=1, source_target_pairs={{0,1},{1,0},{2,3},{3,2},{4,5},{5,4},{6,7},{7,6},{8,9},{9,8},{10,11... | collective-permute-start | bytes 2359304 | tf_op jit(solution)/shard_map/ppermute | solution.py:524
  27.5 22.2 %collective-permute-start.1 = (bf16[384,1024]{1,0:T(8,128)(2,1)S(1)}, bf16[384,1024]{1,0:T(8,128)(2,1)}, u32[]{:S(2)}, u32[]{:S(2)}) collective-permute-start(bf16[384,1024]{1,0:T(8,128)(2,1)S(1)} %bitcast.17), channel_id=1, source_target_pairs={{0,6},{1,7},{2,0},{3,1},{4,2},{5,3},{6,4},{7,5},{8,14},{9,15},{10,... | collective-permute-start | bytes 2359304 | tf_op jit(solution)/shard_map/ppermute | solution.py:521
  30.6 21.0 %collective-permute-start = (bf16[384,1024]{1,0:T(8,128)(2,1)S(1)}, bf16[384,1024]{1,0:T(8,128)(2,1)}, u32[]{:S(2)}, u32[]{:S(2)}) collective-permute-start(bf16[384,1024]{1,0:T(8,128)(2,1)S(1)} %bitcast.18), channel_id=1, source_target_pairs={{0,2},{1,3},{2,4},{3,5},{4,6},{5,7},{6,0},{7,1},{8,10},{9,11},{10,... | collective-permute-start | bytes 2359304 | tf_op jit(solution)/shard_map/ppermute | solution.py:521
  32.2 14.3 %all-to-all-start.1 = ((bf16[16,3,32,128]{3,2,1,0:T(8,128)(2,1)}), bf16[16,3,32,128]{3,2,1,0:T(8,128)(2,1)S(1)}, u32[]{:S(2)}, u32[]{:S(2)}) async-start(bf16[16,3,32,128]{3,2,1,0:T(8,128)(2,1)} %rank_sums_to_send.1.refs_3_), calls=%async_computation.1 | async-start | bytes 786432 | tf_op jit(solution)/shard_map/all_to_all | solution.py:564
  36.5 11.7 %copy-start.1 = (bf16[384,1024]{1,0:T(8,128)(2,1)S(1)}, bf16[384,1024]{1,0:T(8,128)(2,1)}, u32[]{:S(2)}) copy-start(bf16[384,1024]{1,0:T(8,128)(2,1)} %gradient.3) | copy-start | bytes 2359300
  36.5 0.9 copy-start.5
  37.4 1.1 %copy-start.6 = (bf16[384,1024]{1,0:T(8,128)(2,1)S(1)}, bf16[384,1024]{1,0:T(8,128)(2,1)}, u32[]{:S(2)}) copy-start(bf16[384,1024]{1,0:T(8,128)(2,1)} %copy-done.5) | copy-start | bytes 2359300
  38.5 9.7 %copy-start = (bf16[768,1024]{1,0:T(8,128)(2,1)S(1)}, bf16[768,1024]{1,0:T(8,128)(2,1)}, u32[]{:S(2)}) copy-start(bf16[768,1024]{1,0:T(8,128)(2,1)} %attention.3) | copy-start | bytes 4718596
  46.5 1.7 %collective-permute-start.7 = (bf16[16,3,32,128]{3,2,1,0:T(8,128)(2,1)S(1)}, bf16[16,3,32,128]{3,2,1,0:T(8,128)(2,1)S(1)}, u32[]{:S(2)}, u32[]{:S(2)}) collective-permute-start(bf16[16,3,32,128]{3,2,1,0:T(8,128)(2,1)S(1)} %after.2.crossed), channel_id=1, source_target_pairs={{0,1},{1,0},{2,3},{3,2},{4,5},{5,4},{6,7},{7,6},{8,9},{9,8},{10,11... | collective-permute-start | bytes 1179656 | tf_op jit(solution)/shard_map/ppermute | solution.py:524
  48.2 3.4 %copy-start.3 = (bf16[16,3,32,128]{3,2,1,0:T(8,128)(2,1)}, bf16[16,3,32,128]{3,2,1,0:T(8,128)(2,1)S(1)}, u32[]{:S(2)}) copy-start(bf16[16,3,32,128]{3,2,1,0:T(8,128)(2,1)S(1)} %collective-permute-done.7.crossed_other) | copy-start | bytes 1179652
  53.6 0.8 copy-start.2
  54.3 7.3 %collective-permute-start.10 = (bf16[384,1024]{1,0:T(8,128)(2,1)}, bf16[384,1024]{1,0:T(8,128)(2,1)S(1)}, u32[]{:S(2)}, u32[]{:S(2)}) collective-permute-start(bf16[384,1024]{1,0:T(8,128)(2,1)} %get-tuple-element.28.refs_0_), channel_id=1, source_target_pairs={{0,1},{1,0},{2,3},{3,2},{4,5},{5,4},{6,7},{7,6},{8,9},{9,8},{10,11... | collective-permute-start | bytes 2359304 | tf_op jit(solution)/shard_map/ppermute | solution.py:524
  54.4 7.3 %collective-permute-start.11 = (bf16[384,1024]{1,0:T(8,128)(2,1)}, bf16[384,1024]{1,0:T(8,128)(2,1)}, u32[]{:S(2)}, u32[]{:S(2)}) collective-permute-start(bf16[384,1024]{1,0:T(8,128)(2,1)} %get-tuple-element.29.refs_2_), channel_id=1, source_target_pairs={{0,1},{1,0},{2,3},{3,2},{4,5},{5,4},{6,7},{7,6},{8,9},{9,8},{10,11... | collective-permute-start | bytes 2359304 | tf_op jit(solution)/shard_map/ppermute | solution.py:524
  54.9 14.4 %collective-permute-start.8 = (bf16[192,1024]{1,0:T(8,128)(2,1)}, bf16[192,1024]{1,0:T(8,128)(2,1)S(1)}, u32[]{:S(2)}, u32[]{:S(2)}) collective-permute-start(bf16[192,1024]{1,0:T(8,128)(2,1)} %get-tuple-element.26), channel_id=1, source_target_pairs={{0,2},{1,3},{2,4},{3,5},{4,6},{5,7},{6,0},{7,1},{8,10},{9,11},{10,... | collective-permute-start | bytes 1179656 | tf_op jit(solution)/shard_map/ppermute | solution.py:521
  54.9 14.4 %collective-permute-start.9 = (bf16[192,1024]{1,0:T(8,128)(2,1)}, bf16[192,1024]{1,0:T(8,128)(2,1)S(1)}, u32[]{:S(2)}, u32[]{:S(2)}) collective-permute-start(bf16[192,1024]{1,0:T(8,128)(2,1)} %get-tuple-element.27), channel_id=1, source_target_pairs={{0,6},{1,7},{2,0},{3,1},{4,2},{5,3},{6,4},{7,5},{8,14},{9,15},{10,... | collective-permute-start | bytes 1179656 | tf_op jit(solution)/shard_map/ppermute | solution.py:521
  58.1 15.0 %all-to-all-start.2 = ((f32[16,8,1024]{2,1,0:T(8,128)}), f32[16,8,1024]{2,1,0:T(8,128)S(1)}, u32[]{:S(2)}, u32[]{:S(2)}) async-start(f32[16,8,1024]{2,1,0:T(8,128)} %bitcast.20), calls=%async_computation.2 | async-start | bytes 1048576 | tf_op jit(solution)/shard_map/all_to_all | solution.py:583
  61.7 11.4 %copy-start.4 = (bf16[16,3,32,128]{3,2,1,0:T(8,128)(2,1)S(1)}, bf16[16,3,32,128]{3,2,1,0:T(8,128)(2,1)}, u32[]{:S(2)}) copy-start(bf16[16,3,32,128]{3,2,1,0:T(8,128)(2,1)} %copy-done.3) | copy-start | bytes 1179652
  61.7 11.4 %copy-start.7 = (bf16[1024,64]{0,1:T(8,128)(2,1)S(1)}, bf16[1024,64]{0,1:T(8,128)(2,1)}, u32[]{:S(2)}) copy-start(bf16[1024,64]{0,1:T(8,128)(2,1)} %param.10) | copy-start | bytes 393220
  69.3 3.8 %collective-permute-start.12 = (bf16[192,1024]{1,0:T(8,128)(2,1)S(1)}, bf16[192,1024]{1,0:T(8,128)(2,1)S(1)}, u32[]{:S(2)}, u32[]{:S(2)}) collective-permute-start(bf16[192,1024]{1,0:T(8,128)(2,1)S(1)} %get-tuple-element.32.far_a), channel_id=1, source_target_pairs={{0,1},{1,0},{2,3},{3,2},{4,5},{5,4},{6,7},{7,6},{8,9},{9,8},{10,11... | collective-permute-start | bytes 1179656 | tf_op jit(solution)/shard_map/ppermute | solution.py:524
  69.4 3.7 %collective-permute-start.13 = (bf16[192,1024]{1,0:T(8,128)(2,1)S(1)}, bf16[192,1024]{1,0:T(8,128)(2,1)S(1)}, u32[]{:S(2)}, u32[]{:S(2)}) collective-permute-start(bf16[192,1024]{1,0:T(8,128)(2,1)S(1)} %get-tuple-element.33.far_b), channel_id=1, source_target_pairs={{0,1},{1,0},{2,3},{3,2},{4,5},{5,4},{6,7},{7,6},{8,9},{9,8},{10,11... | collective-permute-start | bytes 1179656 | tf_op jit(solution)/shard_map/ppermute | solution.py:524

commit v11 on v10

--- a/solution.py
+++ b/solution.py
@@ -96,13 +96,17 @@
 def halves_kernel(left, right, grads, token, top, bottom, *refs):
     buffer, sem = refs[3:]
     half = top.shape[0]
-    parts = ((left.at[pl.ds(0, half)], top), (right.at[pl.ds(half, half)], bottom))
-    loads = [
-        pltpu.make_async_copy(part, buffer.at[i], sem.at[i]) for i, (part, _) in enumerate(parts)
-    ]
-    stores = [
-        pltpu.make_async_copy(buffer.at[i], out, sem.at[2 + i]) for i, (_, out) in enumerate(parts)
-    ]
+    chunk = half // (buffer.shape[0] // 2)
+    loads, stores = [], []
+    for i in range(buffer.shape[0]):
+        part, start, out = (left, 0, top) if i % 2 == 0 else (right, half, bottom)
+        offset = i // 2 * chunk
+        loads.append(
+            pltpu.make_async_copy(part.at[pl.ds(start + offset, chunk)], buffer.at[i], sem.at[0, i])
+        )
+        stores.append(
+            pltpu.make_async_copy(buffer.at[i], out.at[pl.ds(offset, chunk)], sem.at[1, i])
+        )
     for load in loads:
         load.start()
     for load, store in zip(loads, stores):
@@ -122,8 +126,8 @@
         + [jax.ShapeDtypeStruct(part.shape, part.dtype) for part in (left, right, grads)],
         input_output_aliases={0: 2, 1: 3, 2: 4},
         scratch_shapes=[
-            pltpu.VMEM((2,) + half.shape, half.dtype),
-            pltpu.SemaphoreType.DMA((4,)),
+            pltpu.VMEM((8, half.shape[0] // 4, half.shape[1]), half.dtype),
+            pltpu.SemaphoreType.DMA((2, 8)),
         ],
         compiler_params=pltpu.CompilerParams(vmem_limit_bytes=SMALL_LIMIT),
         cost_estimate=pl.CostEstimate(
@@ -162,6 +166,8 @@
         if k + 3 < len(copies):
             for copy in copies[k + 3]:
                 copy.start()
+        if k == count - 1:
+            break
         value = dot_minor(x[k], w[k % 4])
         if k > 0:
             sums[...] += value
@@ -169,10 +175,24 @@
             sums[...] = value
     if not first:
         copies[count][0].wait()
-        sums[...] += sums_was[...]
-    store = pltpu.make_async_copy(sums, sums_out.at[pl.ds(0, tokens)], sem.at[1])
-    store.start()
-    store.wait()
+    tile = sums.shape[1] // 4
+    stores = []
+    for n in range(4):
+        span = slice(n * tile, (n + 1) * tile)
+        value = sums[:, span] + dot_minor(x[count - 1], w[(count - 1) % 4, span])
+        if not first:
+            value += sums_was[:, span]
+        sums[:, span] = value
+        stores.append(
+            pltpu.make_async_copy(
+                sums.at[:, pl.ds(n * tile, tile)],
+                sums_out.at[pl.ds(0, tokens), pl.ds(n * tile, tile)],
+                sem.at[1 + n],
+            )
+        )
+        stores[-1].start()
+    for store in stores:
+        store.wait()
 
 
 def block_products(index, table, blocks, weight, token, sums=None, name=""):
@@ -195,7 +215,7 @@
             pltpu.VMEM((tokens, out_width), jnp.float32),
             pltpu.SemaphoreType.DMA((count,)),
             pltpu.SemaphoreType.DMA((count,)),
-            pltpu.SemaphoreType.DMA((2,)),
+            pltpu.SemaphoreType.DMA((5,)),
         ],
         compiler_params=pltpu.CompilerParams(vmem_limit_bytes=VMEM_LIMIT),
         cost_estimate=pl.CostEstimate(

time: 113 us -> 113 us (level)
  no operation moved by 1% of the time
where the time goes in v11:
time: 113 us
  blocking collectives  31.4 us (28%)
  Pallas kernels  29.8 us (26%)
  starting transfers between devices  28.8 us (25%)
  waiting for transfers between devices  17.3 us (15%)
  local copies, waits for them, and re-layouts  3.51 us (3%)
    all_to_all x1, blocking collectives, body(): lax.all_to_all(placed, 'group', split_axis=0, concat_axis=0, tiled=True)  31.4 us
    pallas_call x2, Pallas kernels, block_products(): pl.pallas_call(functools.partial(block_kernel, table, first), in_specs=[S...  12.8 us
    ppermute x7, starting transfers between devices, move(): return lax.ppermute(value, 'tp', pairs)  11.6 us
    all_to_all x1, starting transfers between devices, body(): lax.all_to_all(pieces_out.reshape(groups, rows_here, piece, width_here),...  8.11 us
    all_to_all x1, waiting for transfers between devices, body(): lax.all_to_all(pieces_out.reshape(groups, rows_here, piece, width_here),...  6.95 us
    pallas_call x1, Pallas kernels, last_products(): pl.pallas_call(functools.partial(last_kernel, rows, scale, table, core_at...  6.4 us
    all_to_all x1, starting transfers between devices, body(): lax.all_to_all(send, 'group', split_axis=0, concat_axis=0, tiled=True)  4.28 us
    pallas_call x1, Pallas kernels, prepare(): pl.pallas_call(functools.partial(prepare_kernel, groups), in_specs=[ANY]...  4.02 us
  transfers between devices with their start and end apart: 17, of which 6 were waited for; matrix products, arithmetic and copies ran while one was open for 1% of the time, Pallas kernels for 14%

profile of v11, /device:TPU:0, one launch (start us, length us, event | category | flops | bytes accessed | tf_op | source)
XLA Modules:
  0.0 112.5 jit_solution(7974053654814788447)
XLA Ops:
  0.7 4.0 %prepare.1 = (bf16[384,1024]{1,0:T(8,128)(2,1)}, f32[64,1152]{1,0:T(8,128)}) custom-call(bf16[384,1024]{1,0:T(8,128)(2,1)} %gradient.3, bf16[768,1024]{1,0:T(8,128)(2,1)} %attention.3, bf16[64,1024]{1,0:T(8,128)(2,1)} %up.1, bf16[64,1024]{1,0:T(8,128)(2,1)} %bitcast.21), custom_call_target="tpu_custom_call" | custom-call | tf_op jit(solution)/shard_map/prepare/pallas_call | solution.py:61
  4.7 8.1 %all-to-all-start = ((bf16[16,3,8,1024]{3,2,1,0:T(8,128)(2,1)}), bf16[16,3,8,1024]{3,2,1,0:T(8,128)(2,1)S(1)}, u32[]{:S(2)}, u32[]{:S(2)}) async-start(bf16[16,3,8,1024]{3,2,1,0:T(8,128)(2,1)} %bitcast.23), calls=%async_computation | async-start | bytes 1572864 | tf_op jit(solution)/shard_map/all_to_all | solution.py:549
  13.1 0.2 select_reduce_fusion.1
  13.5 0.1 select_reduce_fusion.4
  13.7 0.1 select_reduce_fusion.3
  13.8 0.9 collective-permute-done.2
  14.7 3.1 %collective-permute-start.4 = (f32[32,1152]{1,0:T(8,128)S(1)}, f32[32,1152]{1,0:T(8,128)S(1)}, u32[]{:S(2)}, u32[]{:S(2)}) collective-permute-start(f32[32,1152]{1,0:T(8,128)S(1)} %dynamic-slice_add_fusion), channel_id=1, source_target_pairs={{0,6},{1,7},{2,0},{3,1},{4,2},{5,3},{6,4},{7,5},{8,14},{9,15},{10,... | collective-permute-start | bytes 442376 | tf_op jit(solution)/shard_map/ppermute | solution.py:541
  17.8 2.2 %collective-permute-start.5 = (f32[32,1152]{1,0:T(8,128)S(1)}, f32[32,1152]{1,0:T(8,128)S(1)}, u32[]{:S(2)}, u32[]{:S(2)}) collective-permute-start(f32[32,1152]{1,0:T(8,128)S(1)} %dynamic-slice_add_fusion), channel_id=1, source_target_pairs={{0,4},{1,5},{2,6},{3,7},{4,0},{5,1},{6,2},{7,3},{8,12},{9,13},{10,... | collective-permute-start | bytes 442376 | tf_op jit(solution)/shard_map/ppermute | solution.py:541
  20.0 0.1 copy.19
  20.4 7.0 %all-to-all-done = bf16[16,3,8,1024]{3,2,1,0:T(8,128)(2,1)S(1)} async-done(((bf16[16,3,8,1024]{3,2,1,0:T(8,128)(2,1)}), bf16[16,3,8,1024]{3,2,1,0:T(8,128)(2,1)S(1)}, u32[]{:S(2)}, u32[]{:S(2)}) %all-to-all-start) | async-done | bytes 786464 | tf_op jit(solution)/shard_map/all_to_all | solution.py:549
  27.3 0.1 select_reduce_fusion.2
  27.5 3.1 %collective-permute-start.1 = (bf16[384,1024]{1,0:T(8,128)(2,1)S(1)}, bf16[384,1024]{1,0:T(8,128)(2,1)}, u32[]{:S(2)}, u32[]{:S(2)}) collective-permute-start(bf16[384,1024]{1,0:T(8,128)(2,1)S(1)} %bitcast.17), channel_id=1, source_target_pairs={{0,6},{1,7},{2,0},{3,1},{4,2},{5,3},{6,4},{7,5},{8,14},{9,15},{10,... | collective-permute-start | bytes 2359304 | tf_op jit(solution)/shard_map/ppermute | solution.py:541
  30.7 1.5 %rank_sums_to_send.1.refs_3_ = bf16[16,3,32,128]{3,2,1,0:T(8,128)(2,1)} custom-call(s32[146]{0:T(256)S(1)} %concatenate.3.index, f32[32,1152]{1,0:T(8,128)S(1)} %add_add_fusion.share), custom_call_target="tpu_custom_call" | custom-call | flops 131072 | bytes 524288 | tf_op jit(solution)/shard_map/rank_sums_to_send/pallas_call | solution.py:366
  32.2 4.3 %all-to-all-start.1 = ((bf16[16,3,32,128]{3,2,1,0:T(8,128)(2,1)}), bf16[16,3,32,128]{3,2,1,0:T(8,128)(2,1)S(1)}, u32[]{:S(2)}, u32[]{:S(2)}) async-start(bf16[16,3,32,128]{3,2,1,0:T(8,128)(2,1)} %rank_sums_to_send.1.refs_3_), calls=%async_computation.1 | async-start | bytes 786432 | tf_op jit(solution)/shard_map/all_to_all | solution.py:584
  36.5 0.9 copy-done.5
  37.4 1.1 %copy-done.6 = bf16[384,1024]{1,0:T(8,128)(2,1)S(1)} copy-done((bf16[384,1024]{1,0:T(8,128)(2,1)S(1)}, bf16[384,1024]{1,0:T(8,128)(2,1)}, u32[]{:S(2)}) %copy-start.6) | copy-done | bytes 786456
  38.5 5.3 %own_products.1 = (f32[6144,1024]{1,0:T(8,128)}, f32[8,128]{1,0:T(8,128)S(1)}) custom-call(s32[146]{0:T(256)S(1)} %concatenate.3.index, bf16[384,1024]{1,0:T(8,128)(2,1)S(1)} %bitcast.19, bf16[384,1024]{1,0:T(8,128)(2,1)S(1)} %copy-done.6, bf16[1024,8192]{1,0:T(8,128)(2,1)} %weight.1, bf16[16,3,32,128]{3,2,1,0:T(8,128)(2,1)} %rank_sums_to_send.1.refs_3_), custom_call_target="tpu_custom_call" | custom-call | flops 1610612736 | bytes 5767168 | tf_op jit(solution)/shard_map/own_products/pallas_call | solution.py:203
  43.8 2.7 %all-to-all-done.1.refs_0_ = bf16[16,3,32,128]{3,2,1,0:T(8,128)(2,1)S(1)} async-done(((bf16[16,3,32,128]{3,2,1,0:T(8,128)(2,1)}), bf16[16,3,32,128]{3,2,1,0:T(8,128)(2,1)S(1)}, u32[]{:S(2)}, u32[]{:S(2)}) %all-to-all-start.1) | async-done | bytes 393248 | tf_op jit(solution)/shard_map/all_to_all | solution.py:584
  46.5 1.7 %collective-permute-done.7.crossed_other = bf16[16,3,32,128]{3,2,1,0:T(8,128)(2,1)S(1)} collective-permute-done((bf16[16,3,32,128]{3,2,1,0:T(8,128)(2,1)S(1)}, bf16[16,3,32,128]{3,2,1,0:T(8,128)(2,1)S(1)}, u32[]{:S(2)}, u32[]{:S(2)}) %collective-permute-start.7) | collective-permute-done | bytes 393248 | tf_op jit(solution)/shard_map/ppermute | solution.py:544
  48.2 1.5 %gradient_products.1 = (f32[128,1024]{1,0:T(8,128)S(1)}, f32[8,128]{1,0:T(8,128)S(1)}) custom-call(s32[146]{0:T(256)S(1)} %concatenate.3.index, bf16[16,3,32,128]{3,2,1,0:T(8,128)(2,1)S(1)} %after.2.crossed, bf16[16,3,32,128]{3,2,1,0:T(8,128)(2,1)S(1)} %collective-permute-done.7.crossed_other, f32[8,128]{1,0:T(8,128)S(1)} %get-tuple-element.23.refs_1_.token, ...), custom_call_target="tpu_custom_call" | custom-call | flops 150994944 | bytes 2359296 | tf_op jit(solution)/shard_map/gradient_products/pallas_call | solution.py:428
  49.7 1.9 %collective-permute-done.left = bf16[384,1024]{1,0:T(8,128)(2,1)} collective-permute-done((bf16[384,1024]{1,0:T(8,128)(2,1)S(1)}, bf16[384,1024]{1,0:T(8,128)(2,1)}, u32[]{:S(2)}, u32[]{:S(2)}) %collective-permute-start) | collective-permute-done | bytes 786464 | tf_op jit(solution)/shard_map/ppermute | solution.py:541
  51.6 2.0 %take_halves.1 = (bf16[192,1024]{1,0:T(8,128)(2,1)}, bf16[192,1024]{1,0:T(8,128)(2,1)}, bf16[384,1024]{1,0:T(8,128)(2,1)}, bf16[384,1024]{1,0:T(8,128)(2,1)}, f32[128,1024]{1,0:T(8,128)S(1)}) custom-call(bf16[384,1024]{1,0:T(8,128)(2,1)} %collective-permute-done.left, ...), custom_call_target="tpu_custom_call", output_to_operand_aliasing={{2}: (0, {}), {3}: (1, {}), {4}: (2, {})} | custom-call | bytes 3145728 | tf_op jit(solution)/shard_map/take_halves/pallas_call | solution.py:121
  53.6 0.8 copy-done.2
  54.4 0.5 collective-permute-start.11
  54.9 3.2 %collective-permute-start.9 = (bf16[192,1024]{1,0:T(8,128)(2,1)}, bf16[192,1024]{1,0:T(8,128)(2,1)S(1)}, u32[]{:S(2)}, u32[]{:S(2)}) collective-permute-start(bf16[192,1024]{1,0:T(8,128)(2,1)} %get-tuple-element.27), channel_id=1, source_target_pairs={{0,6},{1,7},{2,0},{3,1},{4,2},{5,3},{6,4},{7,5},{8,14},{9,15},{10,... | collective-permute-start | bytes 1179656 | tf_op jit(solution)/shard_map/ppermute | solution.py:541
  58.2 3.6 %all-to-all-start.2 = ((f32[16,8,1024]{2,1,0:T(8,128)}), f32[16,8,1024]{2,1,0:T(8,128)S(1)}, u32[]{:S(2)}, u32[]{:S(2)}) async-start(f32[16,8,1024]{2,1,0:T(8,128)} %bitcast.20), calls=%async_computation.2 | async-start | bytes 1048576 | tf_op jit(solution)/shard_map/all_to_all | solution.py:603
  61.8 7.5 %side_products.1 = (f32[6144,1024]{1,0:T(8,128)}, f32[8,128]{1,0:T(8,128)S(1)}) custom-call(s32[146]{0:T(256)S(1)} %concatenate.3.index, bf16[384,1024]{1,0:T(8,128)(2,1)} %get-tuple-element.28.refs_0_, bf16[384,1024]{1,0:T(8,128)(2,1)S(1)} %collective-permute-done.10.refs_1_, bf16[384,1024]{1,0:T(8,128)(2,1)} %get-tuple-element.29.refs_2_, ...), custom_call_target="tpu_custom_call" | custom-call | flops 3221225472 | bytes 11534336 | tf_op jit(solution)/shard_map/side_products/pallas_call | solution.py:203
  69.4 0.5 collective-permute-start.13
  69.9 3.2 %all-to-all-done.2.grads_in = f32[16,8,1024]{2,1,0:T(8,128)S(1)} async-done(((f32[16,8,1024]{2,1,0:T(8,128)}), f32[16,8,1024]{2,1,0:T(8,128)S(1)}, u32[]{:S(2)}, u32[]{:S(2)}) %all-to-all-start.2) | async-done | bytes 524320 | tf_op jit(solution)/shard_map/all_to_all | solution.py:603
  73.2 6.4 %last_products.1 = bf16[16,7,16,512]{3,2,1,0:T(8,128)(2,1)S(1)} custom-call(s32[146]{0:T(256)S(1)} %concatenate.3.index, bf16[192,1024]{1,0:T(8,128)(2,1)S(1)} %get-tuple-element.32.far_a, bf16[192,1024]{1,0:T(8,128)(2,1)S(1)} %get-tuple-element.33.far_b, bf16[192,1024]{1,0:T(8,128)(2,1)S(1)} %collective-permute-done.12.other_a, ...), custom_call_target="tpu_custom_call" | custom-call | flops 1610612736 | bytes 4718592 | tf_op jit(solution)/shard_map/last_products/pallas_call | solution.py:316
  79.6 31.4 %all_to_all.20.arrived.gradients = bf16[16,7,16,512]{3,2,1,0:T(8,128)(2,1)S(1)} all-to-all(bf16[16,7,16,512]{3,2,1,0:T(8,128)(2,1)S(1)} %last_products.1), channel_id=1, replica_groups=mesh['group'=16,'tp'=8] {'group'}, dimensions={0} | all-to-all | bytes 3670016 | tf_op jit(solution)/shard_map/all_to_all | solution.py:618
  110.9 1.6 %unfold.1 = (bf16[768,1024]{1,0:T(8,128)(2,1)}, f32[64,1024]{1,0:T(8,128)}, f32[64,1024]{1,0:T(8,128)}) custom-call(bf16[16,7,16,512]{3,2,1,0:T(8,128)(2,1)S(1)} %all_to_all.20.arrived.gradients, bf16[16,7,16,512]{3,2,1,0:T(8,128)(2,1)S(1)} %all_to_all.20.arrived.gradients), custom_call_target="tpu_custom_call" | custom-call | tf_op jit(solution)/shard_map/unfold/pallas_call | solution.py:486
  (54 shorter events, 1.1 us)
Async XLA Ops:
  0.6 12.3 %copy-start.9 = (s32[48]{0:T(128)S(1)}, s32[48]{0:T(128)}, u32[]{:S(2)}) copy-start(s32[48]{0:T(128)} %param.12) | copy-start | bytes 580
  0.6 12.4 %copy-start.10 = (s32[16]{0:T(128)S(1)}, s32[16]{0:T(128)}, u32[]{:S(2)}) copy-start(s32[16]{0:T(128)} %param.13) | copy-start | bytes 196
  4.7 10.0 %copy-start.8 = (f32[64,1152]{1,0:T(8,128)S(1)}, f32[64,1152]{1,0:T(8,128)}, u32[]{:S(2)}) copy-start(f32[64,1152]{1,0:T(8,128)} %get-tuple-element.22) | copy-start | bytes 884740
  4.7 22.6 %all-to-all-start = ((bf16[16,3,8,1024]{3,2,1,0:T(8,128)(2,1)}), bf16[16,3,8,1024]{3,2,1,0:T(8,128)(2,1)S(1)}, u32[]{:S(2)}, u32[]{:S(2)}) async-start(bf16[16,3,8,1024]{3,2,1,0:T(8,128)(2,1)} %bitcast.23), calls=%async_computation | async-start | bytes 1572864 | tf_op jit(solution)/shard_map/all_to_all | solution.py:549
  12.8 1.9 %collective-permute-start.2 = (f32[64,1152]{1,0:T(8,128)}, f32[64,1152]{1,0:T(8,128)S(1)}, u32[]{:S(2)}, u32[]{:S(2)}) collective-permute-start(f32[64,1152]{1,0:T(8,128)} %get-tuple-element.22), channel_id=1, source_target_pairs={{0,1},{1,0},{2,3},{3,2},{4,5},{5,4},{6,7},{7,6},{8,9},{9,8},{10,11... | collective-permute-start | bytes 884744 | tf_op jit(solution)/shard_map/ppermute | solution.py:544
  14.7 15.9 %collective-permute-start.4 = (f32[32,1152]{1,0:T(8,128)S(1)}, f32[32,1152]{1,0:T(8,128)S(1)}, u32[]{:S(2)}, u32[]{:S(2)}) collective-permute-start(f32[32,1152]{1,0:T(8,128)S(1)} %dynamic-slice_add_fusion), channel_id=1, source_target_pairs={{0,6},{1,7},{2,0},{3,1},{4,2},{5,3},{6,4},{7,5},{8,14},{9,15},{10,... | collective-permute-start | bytes 442376 | tf_op jit(solution)/shard_map/ppermute | solution.py:541
  17.8 12.8 %collective-permute-start.3 = (f32[32,1152]{1,0:T(8,128)S(1)}, f32[32,1152]{1,0:T(8,128)S(1)}, u32[]{:S(2)}, u32[]{:S(2)}) collective-permute-start(f32[32,1152]{1,0:T(8,128)S(1)} %dynamic-slice_add_fusion), channel_id=1, source_target_pairs={{0,2},{1,3},{2,4},{3,5},{4,6},{5,7},{6,0},{7,1},{8,10},{9,11},{10,... | collective-permute-start | bytes 442376 | tf_op jit(solution)/shard_map/ppermute | solution.py:541
  17.8 12.8 %collective-permute-start.5 = (f32[32,1152]{1,0:T(8,128)S(1)}, f32[32,1152]{1,0:T(8,128)S(1)}, u32[]{:S(2)}, u32[]{:S(2)}) collective-permute-start(f32[32,1152]{1,0:T(8,128)S(1)} %dynamic-slice_add_fusion), channel_id=1, source_target_pairs={{0,4},{1,5},{2,6},{3,7},{4,0},{5,1},{6,2},{7,3},{8,12},{9,13},{10,... | collective-permute-start | bytes 442376 | tf_op jit(solution)/shard_map/ppermute | solution.py:541
  27.3 9.2 %collective-permute-start.6 = (bf16[384,1024]{1,0:T(8,128)(2,1)S(1)}, bf16[384,1024]{1,0:T(8,128)(2,1)S(1)}, u32[]{:S(2)}, u32[]{:S(2)}) collective-permute-start(bf16[384,1024]{1,0:T(8,128)(2,1)S(1)} %bitcast.16), channel_id=1, source_target_pairs={{0,1},{1,0},{2,3},{3,2},{4,5},{5,4},{6,7},{7,6},{8,9},{9,8},{10,11... | collective-permute-start | bytes 2359304 | tf_op jit(solution)/shard_map/ppermute | solution.py:544
  27.5 22.2 %collective-permute-start.1 = (bf16[384,1024]{1,0:T(8,128)(2,1)S(1)}, bf16[384,1024]{1,0:T(8,128)(2,1)}, u32[]{:S(2)}, u32[]{:S(2)}) collective-permute-start(bf16[384,1024]{1,0:T(8,128)(2,1)S(1)} %bitcast.17), channel_id=1, source_target_pairs={{0,6},{1,7},{2,0},{3,1},{4,2},{5,3},{6,4},{7,5},{8,14},{9,15},{10,... | collective-permute-start | bytes 2359304 | tf_op jit(solution)/shard_map/ppermute | solution.py:541
  30.6 21.0 %collective-permute-start = (bf16[384,1024]{1,0:T(8,128)(2,1)S(1)}, bf16[384,1024]{1,0:T(8,128)(2,1)}, u32[]{:S(2)}, u32[]{:S(2)}) collective-permute-start(bf16[384,1024]{1,0:T(8,128)(2,1)S(1)} %bitcast.18), channel_id=1, source_target_pairs={{0,2},{1,3},{2,4},{3,5},{4,6},{5,7},{6,0},{7,1},{8,10},{9,11},{10,... | collective-permute-start | bytes 2359304 | tf_op jit(solution)/shard_map/ppermute | solution.py:541
  32.2 14.3 %all-to-all-start.1 = ((bf16[16,3,32,128]{3,2,1,0:T(8,128)(2,1)}), bf16[16,3,32,128]{3,2,1,0:T(8,128)(2,1)S(1)}, u32[]{:S(2)}, u32[]{:S(2)}) async-start(bf16[16,3,32,128]{3,2,1,0:T(8,128)(2,1)} %rank_sums_to_send.1.refs_3_), calls=%async_computation.1 | async-start | bytes 786432 | tf_op jit(solution)/shard_map/all_to_all | solution.py:584
  36.5 11.7 %copy-start.1 = (bf16[384,1024]{1,0:T(8,128)(2,1)S(1)}, bf16[384,1024]{1,0:T(8,128)(2,1)}, u32[]{:S(2)}) copy-start(bf16[384,1024]{1,0:T(8,128)(2,1)} %gradient.3) | copy-start | bytes 2359300
  36.5 0.9 copy-start.5
  37.4 1.1 %copy-start.6 = (bf16[384,1024]{1,0:T(8,128)(2,1)S(1)}, bf16[384,1024]{1,0:T(8,128)(2,1)}, u32[]{:S(2)}) copy-start(bf16[384,1024]{1,0:T(8,128)(2,1)} %copy-done.5) | copy-start | bytes 2359300
  38.5 9.7 %copy-start = (bf16[768,1024]{1,0:T(8,128)(2,1)S(1)}, bf16[768,1024]{1,0:T(8,128)(2,1)}, u32[]{:S(2)}) copy-start(bf16[768,1024]{1,0:T(8,128)(2,1)} %attention.3) | copy-start | bytes 4718596
  46.5 1.7 %collective-permute-start.7 = (bf16[16,3,32,128]{3,2,1,0:T(8,128)(2,1)S(1)}, bf16[16,3,32,128]{3,2,1,0:T(8,128)(2,1)S(1)}, u32[]{:S(2)}, u32[]{:S(2)}) collective-permute-start(bf16[16,3,32,128]{3,2,1,0:T(8,128)(2,1)S(1)} %after.2.crossed), channel_id=1, source_target_pairs={{0,1},{1,0},{2,3},{3,2},{4,5},{5,4},{6,7},{7,6},{8,9},{9,8},{10,11... | collective-permute-start | bytes 1179656 | tf_op jit(solution)/shard_map/ppermute | solution.py:544
  48.2 3.4 %copy-start.3 = (bf16[16,3,32,128]{3,2,1,0:T(8,128)(2,1)}, bf16[16,3,32,128]{3,2,1,0:T(8,128)(2,1)S(1)}, u32[]{:S(2)}) copy-start(bf16[16,3,32,128]{3,2,1,0:T(8,128)(2,1)S(1)} %collective-permute-done.7.crossed_other) | copy-start | bytes 1179652
  53.6 0.8 copy-start.2
  54.4 7.3 %collective-permute-start.10 = (bf16[384,1024]{1,0:T(8,128)(2,1)}, bf16[384,1024]{1,0:T(8,128)(2,1)S(1)}, u32[]{:S(2)}, u32[]{:S(2)}) collective-permute-start(bf16[384,1024]{1,0:T(8,128)(2,1)} %get-tuple-element.28.refs_0_), channel_id=1, source_target_pairs={{0,1},{1,0},{2,3},{3,2},{4,5},{5,4},{6,7},{7,6},{8,9},{9,8},{10,11... | collective-permute-start | bytes 2359304 | tf_op jit(solution)/shard_map/ppermute | solution.py:544
  54.4 7.3 %collective-permute-start.11 = (bf16[384,1024]{1,0:T(8,128)(2,1)}, bf16[384,1024]{1,0:T(8,128)(2,1)}, u32[]{:S(2)}, u32[]{:S(2)}) collective-permute-start(bf16[384,1024]{1,0:T(8,128)(2,1)} %get-tuple-element.29.refs_2_), channel_id=1, source_target_pairs={{0,1},{1,0},{2,3},{3,2},{4,5},{5,4},{6,7},{7,6},{8,9},{9,8},{10,11... | collective-permute-start | bytes 2359304 | tf_op jit(solution)/shard_map/ppermute | solution.py:544
  54.9 14.4 %collective-permute-start.8 = (bf16[192,1024]{1,0:T(8,128)(2,1)}, bf16[192,1024]{1,0:T(8,128)(2,1)S(1)}, u32[]{:S(2)}, u32[]{:S(2)}) collective-permute-start(bf16[192,1024]{1,0:T(8,128)(2,1)} %get-tuple-element.26), channel_id=1, source_target_pairs={{0,2},{1,3},{2,4},{3,5},{4,6},{5,7},{6,0},{7,1},{8,10},{9,11},{10,... | collective-permute-start | bytes 1179656 | tf_op jit(solution)/shard_map/ppermute | solution.py:541
  54.9 14.4 %collective-permute-start.9 = (bf16[192,1024]{1,0:T(8,128)(2,1)}, bf16[192,1024]{1,0:T(8,128)(2,1)S(1)}, u32[]{:S(2)}, u32[]{:S(2)}) collective-permute-start(bf16[192,1024]{1,0:T(8,128)(2,1)} %get-tuple-element.27), channel_id=1, source_target_pairs={{0,6},{1,7},{2,0},{3,1},{4,2},{5,3},{6,4},{7,5},{8,14},{9,15},{10,... | collective-permute-start | bytes 1179656 | tf_op jit(solution)/shard_map/ppermute | solution.py:541
  58.2 15.0 %all-to-all-start.2 = ((f32[16,8,1024]{2,1,0:T(8,128)}), f32[16,8,1024]{2,1,0:T(8,128)S(1)}, u32[]{:S(2)}, u32[]{:S(2)}) async-start(f32[16,8,1024]{2,1,0:T(8,128)} %bitcast.20), calls=%async_computation.2 | async-start | bytes 1048576 | tf_op jit(solution)/shard_map/all_to_all | solution.py:603
  61.8 11.4 %copy-start.4 = (bf16[16,3,32,128]{3,2,1,0:T(8,128)(2,1)S(1)}, bf16[16,3,32,128]{3,2,1,0:T(8,128)(2,1)}, u32[]{:S(2)}) copy-start(bf16[16,3,32,128]{3,2,1,0:T(8,128)(2,1)} %copy-done.3) | copy-start | bytes 1179652
  61.8 11.4 %copy-start.7 = (bf16[1024,64]{0,1:T(8,128)(2,1)S(1)}, bf16[1024,64]{0,1:T(8,128)(2,1)}, u32[]{:S(2)}) copy-start(bf16[1024,64]{0,1:T(8,128)(2,1)} %param.10) | copy-start | bytes 393220
  69.3 3.8 %collective-permute-start.12 = (bf16[192,1024]{1,0:T(8,128)(2,1)S(1)}, bf16[192,1024]{1,0:T(8,128)(2,1)S(1)}, u32[]{:S(2)}, u32[]{:S(2)}) collective-permute-start(bf16[192,1024]{1,0:T(8,128)(2,1)S(1)} %get-tuple-element.32.far_a), channel_id=1, source_target_pairs={{0,1},{1,0},{2,3},{3,2},{4,5},{5,4},{6,7},{7,6},{8,9},{9,8},{10,11... | collective-permute-start | bytes 1179656 | tf_op jit(solution)/shard_map/ppermute | solution.py:544
  69.4 3.7 %collective-permute-start.13 = (bf16[192,1024]{1,0:T(8,128)(2,1)S(1)}, bf16[192,1024]{1,0:T(8,128)(2,1)S(1)}, u32[]{:S(2)}, u32[]{:S(2)}) collective-permute-start(bf16[192,1024]{1,0:T(8,128)(2,1)S(1)} %get-tuple-element.33.far_b), channel_id=1, source_target_pairs={{0,1},{1,0},{2,3},{3,2},{4,5},{5,4},{6,7},{7,6},{8,9},{9,8},{10,11... | collective-permute-start | bytes 1179656 | tf_op jit(solution)/shard_map/ppermute | solution.py:544

commit v12 on v11

--- a/solution.py
+++ b/solution.py
@@ -51,9 +51,9 @@
         pieces[2 * pair * piece : 2 * (pair + 1) * piece, :] = jnp.concatenate(
             both, axis=0
         ).astype(pieces.dtype)
-    parts[:, :tokens] = dot_minor(up[...], rows_in[...])
+    parts[:, :tokens] = dot_minor(rows_in[...], up[...]).T
     loads[1].wait()
-    parts[:, tokens:] = dot_minor(down[...], slots_in[...])
+    parts[:, tokens:] = dot_minor(slots_in[...], down[...]).T
 
 
 def prepare(groups, gradient, attention, up, down):

time: 113 us -> 113 us (level)
  no operation moved by 1% of the time
where the time goes in v12:
time: 113 us
  blocking collectives  31.4 us (28%)
  Pallas kernels  30.1 us (27%)
  starting transfers between devices  28.8 us (25%)
  waiting for transfers between devices  17.3 us (15%)
  local copies, waits for them, and re-layouts  3.51 us (3%)
    all_to_all x1, blocking collectives, body(): lax.all_to_all(placed, 'group', split_axis=0, concat_axis=0, tiled=True)  31.4 us
    pallas_call x2, Pallas kernels, block_products(): pl.pallas_call(functools.partial(block_kernel, table, first), in_specs=[S...  12.8 us
    ppermute x7, starting transfers between devices, move(): return lax.ppermute(value, 'tp', pairs)  11.6 us
    all_to_all x1, starting transfers between devices, body(): lax.all_to_all(pieces_out.reshape(groups, rows_here, piece, width_here),...  8.1 us
    all_to_all x1, waiting for transfers between devices, body(): lax.all_to_all(pieces_out.reshape(groups, rows_here, piece, width_here),...  6.95 us
    pallas_call x1, Pallas kernels, last_products(): pl.pallas_call(functools.partial(last_kernel, rows, scale, table, core_at...  6.4 us
    all_to_all x1, starting transfers between devices, body(): lax.all_to_all(send, 'group', split_axis=0, concat_axis=0, tiled=True)  4.28 us
    pallas_call x1, Pallas kernels, prepare(): pl.pallas_call(functools.partial(prepare_kernel, groups), in_specs=[ANY]...  4.27 us
  transfers between devices with their start and end apart: 17, of which 6 were waited for; matrix products, arithmetic and copies ran while one was open for 1% of the time, Pallas kernels for 14%

profile of v12, /device:TPU:0, one launch (start us, length us, event | category | flops | bytes accessed | tf_op | source)
XLA Modules:
  0.0 112.8 jit_solution(18036000842401976323)
XLA Ops:
  0.7 4.3 %prepare.1 = (bf16[384,1024]{1,0:T(8,128)(2,1)}, f32[64,1152]{1,0:T(8,128)}) custom-call(bf16[384,1024]{1,0:T(8,128)(2,1)} %gradient.3, bf16[768,1024]{1,0:T(8,128)(2,1)} %attention.3, bf16[64,1024]{1,0:T(8,128)(2,1)} %up.1, bf16[64,1024]{1,0:T(8,128)(2,1)} %bitcast.21), custom_call_target="tpu_custom_call" | custom-call | tf_op jit(solution)/shard_map/prepare/pallas_call | solution.py:61
  4.9 8.1 %all-to-all-start = ((bf16[16,3,8,1024]{3,2,1,0:T(8,128)(2,1)}), bf16[16,3,8,1024]{3,2,1,0:T(8,128)(2,1)S(1)}, u32[]{:S(2)}, u32[]{:S(2)}) async-start(bf16[16,3,8,1024]{3,2,1,0:T(8,128)(2,1)} %bitcast.23), calls=%async_computation | async-start | bytes 1572864 | tf_op jit(solution)/shard_map/all_to_all | solution.py:549
  13.3 0.2 select_reduce_fusion.1
  13.8 0.1 select_reduce_fusion.4
  13.9 0.1 select_reduce_fusion.3
  14.1 0.9 collective-permute-done.2
  15.0 3.1 %collective-permute-start.4 = (f32[32,1152]{1,0:T(8,128)S(1)}, f32[32,1152]{1,0:T(8,128)S(1)}, u32[]{:S(2)}, u32[]{:S(2)}) collective-permute-start(f32[32,1152]{1,0:T(8,128)S(1)} %dynamic-slice_add_fusion), channel_id=1, source_target_pairs={{0,6},{1,7},{2,0},{3,1},{4,2},{5,3},{6,4},{7,5},{8,14},{9,15},{10,... | collective-permute-start | bytes 442376 | tf_op jit(solution)/shard_map/ppermute | solution.py:541
  18.0 2.2 %collective-permute-start.5 = (f32[32,1152]{1,0:T(8,128)S(1)}, f32[32,1152]{1,0:T(8,128)S(1)}, u32[]{:S(2)}, u32[]{:S(2)}) collective-permute-start(f32[32,1152]{1,0:T(8,128)S(1)} %dynamic-slice_add_fusion), channel_id=1, source_target_pairs={{0,4},{1,5},{2,6},{3,7},{4,0},{5,1},{6,2},{7,3},{8,12},{9,13},{10,... | collective-permute-start | bytes 442376 | tf_op jit(solution)/shard_map/ppermute | solution.py:541
  20.3 0.1 copy.19
  20.6 7.0 %all-to-all-done = bf16[16,3,8,1024]{3,2,1,0:T(8,128)(2,1)S(1)} async-done(((bf16[16,3,8,1024]{3,2,1,0:T(8,128)(2,1)}), bf16[16,3,8,1024]{3,2,1,0:T(8,128)(2,1)S(1)}, u32[]{:S(2)}, u32[]{:S(2)}) %all-to-all-start) | async-done | bytes 786464 | tf_op jit(solution)/shard_map/all_to_all | solution.py:549
  27.6 0.1 select_reduce_fusion.2
  27.8 3.1 %collective-permute-start.1 = (bf16[384,1024]{1,0:T(8,128)(2,1)S(1)}, bf16[384,1024]{1,0:T(8,128)(2,1)}, u32[]{:S(2)}, u32[]{:S(2)}) collective-permute-start(bf16[384,1024]{1,0:T(8,128)(2,1)S(1)} %bitcast.17), channel_id=1, source_target_pairs={{0,6},{1,7},{2,0},{3,1},{4,2},{5,3},{6,4},{7,5},{8,14},{9,15},{10,... | collective-permute-start | bytes 2359304 | tf_op jit(solution)/shard_map/ppermute | solution.py:541
  30.9 1.5 %rank_sums_to_send.1.refs_3_ = bf16[16,3,32,128]{3,2,1,0:T(8,128)(2,1)} custom-call(s32[146]{0:T(256)S(1)} %concatenate.3.index, f32[32,1152]{1,0:T(8,128)S(1)} %add_add_fusion.share), custom_call_target="tpu_custom_call" | custom-call | flops 131072 | bytes 524288 | tf_op jit(solution)/shard_map/rank_sums_to_send/pallas_call | solution.py:366
  32.4 4.3 %all-to-all-start.1 = ((bf16[16,3,32,128]{3,2,1,0:T(8,128)(2,1)}), bf16[16,3,32,128]{3,2,1,0:T(8,128)(2,1)S(1)}, u32[]{:S(2)}, u32[]{:S(2)}) async-start(bf16[16,3,32,128]{3,2,1,0:T(8,128)(2,1)} %rank_sums_to_send.1.refs_3_), calls=%async_computation.1 | async-start | bytes 786432 | tf_op jit(solution)/shard_map/all_to_all | solution.py:584
  36.8 0.9 copy-done.5
  37.6 1.1 %copy-done.6 = bf16[384,1024]{1,0:T(8,128)(2,1)S(1)} copy-done((bf16[384,1024]{1,0:T(8,128)(2,1)S(1)}, bf16[384,1024]{1,0:T(8,128)(2,1)}, u32[]{:S(2)}) %copy-start.6) | copy-done | bytes 786456
  38.8 5.3 %own_products.1 = (f32[6144,1024]{1,0:T(8,128)}, f32[8,128]{1,0:T(8,128)S(1)}) custom-call(s32[146]{0:T(256)S(1)} %concatenate.3.index, bf16[384,1024]{1,0:T(8,128)(2,1)S(1)} %bitcast.19, bf16[384,1024]{1,0:T(8,128)(2,1)S(1)} %copy-done.6, bf16[1024,8192]{1,0:T(8,128)(2,1)} %weight.1, bf16[16,3,32,128]{3,2,1,0:T(8,128)(2,1)} %rank_sums_to_send.1.refs_3_), custom_call_target="tpu_custom_call" | custom-call | flops 1610612736 | bytes 5767168 | tf_op jit(solution)/shard_map/own_products/pallas_call | solution.py:203
  44.0 2.7 %all-to-all-done.1.refs_0_ = bf16[16,3,32,128]{3,2,1,0:T(8,128)(2,1)S(1)} async-done(((bf16[16,3,32,128]{3,2,1,0:T(8,128)(2,1)}), bf16[16,3,32,128]{3,2,1,0:T(8,128)(2,1)S(1)}, u32[]{:S(2)}, u32[]{:S(2)}) %all-to-all-start.1) | async-done | bytes 393248 | tf_op jit(solution)/shard_map/all_to_all | solution.py:584
  46.7 1.7 %collective-permute-done.7.crossed_other = bf16[16,3,32,128]{3,2,1,0:T(8,128)(2,1)S(1)} collective-permute-done((bf16[16,3,32,128]{3,2,1,0:T(8,128)(2,1)S(1)}, bf16[16,3,32,128]{3,2,1,0:T(8,128)(2,1)S(1)}, u32[]{:S(2)}, u32[]{:S(2)}) %collective-permute-start.7) | collective-permute-done | bytes 393248 | tf_op jit(solution)/shard_map/ppermute | solution.py:544
  48.5 1.5 %gradient_products.1 = (f32[128,1024]{1,0:T(8,128)S(1)}, f32[8,128]{1,0:T(8,128)S(1)}) custom-call(s32[146]{0:T(256)S(1)} %concatenate.3.index, bf16[16,3,32,128]{3,2,1,0:T(8,128)(2,1)S(1)} %after.2.crossed, bf16[16,3,32,128]{3,2,1,0:T(8,128)(2,1)S(1)} %collective-permute-done.7.crossed_other, f32[8,128]{1,0:T(8,128)S(1)} %get-tuple-element.23.refs_1_.token, ...), custom_call_target="tpu_custom_call" | custom-call | flops 150994944 | bytes 2359296 | tf_op jit(solution)/shard_map/gradient_products/pallas_call | solution.py:428
  50.0 1.9 %collective-permute-done.left = bf16[384,1024]{1,0:T(8,128)(2,1)} collective-permute-done((bf16[384,1024]{1,0:T(8,128)(2,1)S(1)}, bf16[384,1024]{1,0:T(8,128)(2,1)}, u32[]{:S(2)}, u32[]{:S(2)}) %collective-permute-start) | collective-permute-done | bytes 786464 | tf_op jit(solution)/shard_map/ppermute | solution.py:541
  51.9 2.0 %take_halves.1 = (bf16[192,1024]{1,0:T(8,128)(2,1)}, bf16[192,1024]{1,0:T(8,128)(2,1)}, bf16[384,1024]{1,0:T(8,128)(2,1)}, bf16[384,1024]{1,0:T(8,128)(2,1)}, f32[128,1024]{1,0:T(8,128)S(1)}) custom-call(bf16[384,1024]{1,0:T(8,128)(2,1)} %collective-permute-done.left, ...), custom_call_target="tpu_custom_call", output_to_operand_aliasing={{2}: (0, {}), {3}: (1, {}), {4}: (2, {})} | custom-call | bytes 3145728 | tf_op jit(solution)/shard_map/take_halves/pallas_call | solution.py:121
  53.9 0.8 copy-done.2
  54.7 0.5 collective-permute-start.11
  55.2 3.2 %collective-permute-start.9 = (bf16[192,1024]{1,0:T(8,128)(2,1)}, bf16[192,1024]{1,0:T(8,128)(2,1)S(1)}, u32[]{:S(2)}, u32[]{:S(2)}) collective-permute-start(bf16[192,1024]{1,0:T(8,128)(2,1)} %get-tuple-element.27), channel_id=1, source_target_pairs={{0,6},{1,7},{2,0},{3,1},{4,2},{5,3},{6,4},{7,5},{8,14},{9,15},{10,... | collective-permute-start | bytes 1179656 | tf_op jit(solution)/shard_map/ppermute | solution.py:541
  58.4 3.6 %all-to-all-start.2 = ((f32[16,8,1024]{2,1,0:T(8,128)}), f32[16,8,1024]{2,1,0:T(8,128)S(1)}, u32[]{:S(2)}, u32[]{:S(2)}) async-start(f32[16,8,1024]{2,1,0:T(8,128)} %bitcast.20), calls=%async_computation.2 | async-start | bytes 1048576 | tf_op jit(solution)/shard_map/all_to_all | solution.py:603
  62.0 7.5 %side_products.1 = (f32[6144,1024]{1,0:T(8,128)}, f32[8,128]{1,0:T(8,128)S(1)}) custom-call(s32[146]{0:T(256)S(1)} %concatenate.3.index, bf16[384,1024]{1,0:T(8,128)(2,1)} %get-tuple-element.28.refs_0_, bf16[384,1024]{1,0:T(8,128)(2,1)S(1)} %collective-permute-done.10.refs_1_, bf16[384,1024]{1,0:T(8,128)(2,1)} %get-tuple-element.29.refs_2_, ...), custom_call_target="tpu_custom_call" | custom-call | flops 3221225472 | bytes 11534336 | tf_op jit(solution)/shard_map/side_products/pallas_call | solution.py:203
  69.7 0.5 collective-permute-start.13
  70.2 3.2 %all-to-all-done.2.grads_in = f32[16,8,1024]{2,1,0:T(8,128)S(1)} async-done(((f32[16,8,1024]{2,1,0:T(8,128)}), f32[16,8,1024]{2,1,0:T(8,128)S(1)}, u32[]{:S(2)}, u32[]{:S(2)}) %all-to-all-start.2) | async-done | bytes 524320 | tf_op jit(solution)/shard_map/all_to_all | solution.py:603
  73.4 6.4 %last_products.1 = bf16[16,7,16,512]{3,2,1,0:T(8,128)(2,1)S(1)} custom-call(s32[146]{0:T(256)S(1)} %concatenate.3.index, bf16[192,1024]{1,0:T(8,128)(2,1)S(1)} %get-tuple-element.32.far_a, bf16[192,1024]{1,0:T(8,128)(2,1)S(1)} %get-tuple-element.33.far_b, bf16[192,1024]{1,0:T(8,128)(2,1)S(1)} %collective-permute-done.12.other_a, ...), custom_call_target="tpu_custom_call" | custom-call | flops 1610612736 | bytes 4718592 | tf_op jit(solution)/shard_map/last_products/pallas_call | solution.py:316
  79.8 31.4 %all_to_all.20.arrived.gradients = bf16[16,7,16,512]{3,2,1,0:T(8,128)(2,1)S(1)} all-to-all(bf16[16,7,16,512]{3,2,1,0:T(8,128)(2,1)S(1)} %last_products.1), channel_id=1, replica_groups=mesh['group'=16,'tp'=8] {'group'}, dimensions={0} | all-to-all | bytes 3670016 | tf_op jit(solution)/shard_map/all_to_all | solution.py:618
  111.2 1.6 %unfold.1 = (bf16[768,1024]{1,0:T(8,128)(2,1)}, f32[64,1024]{1,0:T(8,128)}, f32[64,1024]{1,0:T(8,128)}) custom-call(bf16[16,7,16,512]{3,2,1,0:T(8,128)(2,1)S(1)} %all_to_all.20.arrived.gradients, bf16[16,7,16,512]{3,2,1,0:T(8,128)(2,1)S(1)} %all_to_all.20.arrived.gradients), custom_call_target="tpu_custom_call" | custom-call | tf_op jit(solution)/shard_map/unfold/pallas_call | solution.py:486
  (54 shorter events, 1.1 us)
Async XLA Ops:
  0.6 12.5 %copy-start.9 = (s32[48]{0:T(128)S(1)}, s32[48]{0:T(128)}, u32[]{:S(2)}) copy-start(s32[48]{0:T(128)} %param.12) | copy-start | bytes 580
  0.6 12.7 %copy-start.10 = (s32[16]{0:T(128)S(1)}, s32[16]{0:T(128)}, u32[]{:S(2)}) copy-start(s32[16]{0:T(128)} %param.13) | copy-start | bytes 196
  4.9 10.0 %copy-start.8 = (f32[64,1152]{1,0:T(8,128)S(1)}, f32[64,1152]{1,0:T(8,128)}, u32[]{:S(2)}) copy-start(f32[64,1152]{1,0:T(8,128)} %get-tuple-element.22) | copy-start | bytes 884740
  4.9 22.6 %all-to-all-start = ((bf16[16,3,8,1024]{3,2,1,0:T(8,128)(2,1)}), bf16[16,3,8,1024]{3,2,1,0:T(8,128)(2,1)S(1)}, u32[]{:S(2)}, u32[]{:S(2)}) async-start(bf16[16,3,8,1024]{3,2,1,0:T(8,128)(2,1)} %bitcast.23), calls=%async_computation | async-start | bytes 1572864 | tf_op jit(solution)/shard_map/all_to_all | solution.py:549
  13.1 1.9 %collective-permute-start.2 = (f32[64,1152]{1,0:T(8,128)}, f32[64,1152]{1,0:T(8,128)S(1)}, u32[]{:S(2)}, u32[]{:S(2)}) collective-permute-start(f32[64,1152]{1,0:T(8,128)} %get-tuple-element.22), channel_id=1, source_target_pairs={{0,1},{1,0},{2,3},{3,2},{4,5},{5,4},{6,7},{7,6},{8,9},{9,8},{10,11... | collective-permute-start | bytes 884744 | tf_op jit(solution)/shard_map/ppermute | solution.py:544
  15.0 15.9 %collective-permute-start.4 = (f32[32,1152]{1,0:T(8,128)S(1)}, f32[32,1152]{1,0:T(8,128)S(1)}, u32[]{:S(2)}, u32[]{:S(2)}) collective-permute-start(f32[32,1152]{1,0:T(8,128)S(1)} %dynamic-slice_add_fusion), channel_id=1, source_target_pairs={{0,6},{1,7},{2,0},{3,1},{4,2},{5,3},{6,4},{7,5},{8,14},{9,15},{10,... | collective-permute-start | bytes 442376 | tf_op jit(solution)/shard_map/ppermute | solution.py:541
  18.0 12.8 %collective-permute-start.3 = (f32[32,1152]{1,0:T(8,128)S(1)}, f32[32,1152]{1,0:T(8,128)S(1)}, u32[]{:S(2)}, u32[]{:S(2)}) collective-permute-start(f32[32,1152]{1,0:T(8,128)S(1)} %dynamic-slice_add_fusion), channel_id=1, source_target_pairs={{0,2},{1,3},{2,4},{3,5},{4,6},{5,7},{6,0},{7,1},{8,10},{9,11},{10,... | collective-permute-start | bytes 442376 | tf_op jit(solution)/shard_map/ppermute | solution.py:541
  18.0 12.8 %collective-permute-start.5 = (f32[32,1152]{1,0:T(8,128)S(1)}, f32[32,1152]{1,0:T(8,128)S(1)}, u32[]{:S(2)}, u32[]{:S(2)}) collective-permute-start(f32[32,1152]{1,0:T(8,128)S(1)} %dynamic-slice_add_fusion), channel_id=1, source_target_pairs={{0,4},{1,5},{2,6},{3,7},{4,0},{5,1},{6,2},{7,3},{8,12},{9,13},{10,... | collective-permute-start | bytes 442376 | tf_op jit(solution)/shard_map/ppermute | solution.py:541
  27.6 9.2 %collective-permute-start.6 = (bf16[384,1024]{1,0:T(8,128)(2,1)S(1)}, bf16[384,1024]{1,0:T(8,128)(2,1)S(1)}, u32[]{:S(2)}, u32[]{:S(2)}) collective-permute-start(bf16[384,1024]{1,0:T(8,128)(2,1)S(1)} %bitcast.16), channel_id=1, source_target_pairs={{0,1},{1,0},{2,3},{3,2},{4,5},{5,4},{6,7},{7,6},{8,9},{9,8},{10,11... | collective-permute-start | bytes 2359304 | tf_op jit(solution)/shard_map/ppermute | solution.py:544
  27.8 22.2 %collective-permute-start.1 = (bf16[384,1024]{1,0:T(8,128)(2,1)S(1)}, bf16[384,1024]{1,0:T(8,128)(2,1)}, u32[]{:S(2)}, u32[]{:S(2)}) collective-permute-start(bf16[384,1024]{1,0:T(8,128)(2,1)S(1)} %bitcast.17), channel_id=1, source_target_pairs={{0,6},{1,7},{2,0},{3,1},{4,2},{5,3},{6,4},{7,5},{8,14},{9,15},{10,... | collective-permute-start | bytes 2359304 | tf_op jit(solution)/shard_map/ppermute | solution.py:541
  30.9 21.0 %collective-permute-start = (bf16[384,1024]{1,0:T(8,128)(2,1)S(1)}, bf16[384,1024]{1,0:T(8,128)(2,1)}, u32[]{:S(2)}, u32[]{:S(2)}) collective-permute-start(bf16[384,1024]{1,0:T(8,128)(2,1)S(1)} %bitcast.18), channel_id=1, source_target_pairs={{0,2},{1,3},{2,4},{3,5},{4,6},{5,7},{6,0},{7,1},{8,10},{9,11},{10,... | collective-permute-start | bytes 2359304 | tf_op jit(solution)/shard_map/ppermute | solution.py:541
  32.4 14.3 %all-to-all-start.1 = ((bf16[16,3,32,128]{3,2,1,0:T(8,128)(2,1)}), bf16[16,3,32,128]{3,2,1,0:T(8,128)(2,1)S(1)}, u32[]{:S(2)}, u32[]{:S(2)}) async-start(bf16[16,3,32,128]{3,2,1,0:T(8,128)(2,1)} %rank_sums_to_send.1.refs_3_), calls=%async_computation.1 | async-start | bytes 786432 | tf_op jit(solution)/shard_map/all_to_all | solution.py:584
  36.7 11.7 %copy-start.1 = (bf16[384,1024]{1,0:T(8,128)(2,1)S(1)}, bf16[384,1024]{1,0:T(8,128)(2,1)}, u32[]{:S(2)}) copy-start(bf16[384,1024]{1,0:T(8,128)(2,1)} %gradient.3) | copy-start | bytes 2359300
  36.7 0.9 copy-start.5
  37.6 1.1 %copy-start.6 = (bf16[384,1024]{1,0:T(8,128)(2,1)S(1)}, bf16[384,1024]{1,0:T(8,128)(2,1)}, u32[]{:S(2)}) copy-start(bf16[384,1024]{1,0:T(8,128)(2,1)} %copy-done.5) | copy-start | bytes 2359300
  38.8 9.7 %copy-start = (bf16[768,1024]{1,0:T(8,128)(2,1)S(1)}, bf16[768,1024]{1,0:T(8,128)(2,1)}, u32[]{:S(2)}) copy-start(bf16[768,1024]{1,0:T(8,128)(2,1)} %attention.3) | copy-start | bytes 4718596
  46.7 1.7 %collective-permute-start.7 = (bf16[16,3,32,128]{3,2,1,0:T(8,128)(2,1)S(1)}, bf16[16,3,32,128]{3,2,1,0:T(8,128)(2,1)S(1)}, u32[]{:S(2)}, u32[]{:S(2)}) collective-permute-start(bf16[16,3,32,128]{3,2,1,0:T(8,128)(2,1)S(1)} %after.2.crossed), channel_id=1, source_target_pairs={{0,1},{1,0},{2,3},{3,2},{4,5},{5,4},{6,7},{7,6},{8,9},{9,8},{10,11... | collective-permute-start | bytes 1179656 | tf_op jit(solution)/shard_map/ppermute | solution.py:544
  48.4 3.4 %copy-start.3 = (bf16[16,3,32,128]{3,2,1,0:T(8,128)(2,1)}, bf16[16,3,32,128]{3,2,1,0:T(8,128)(2,1)S(1)}, u32[]{:S(2)}) copy-start(bf16[16,3,32,128]{3,2,1,0:T(8,128)(2,1)S(1)} %collective-permute-done.7.crossed_other) | copy-start | bytes 1179652
  53.9 0.8 copy-start.2
  54.7 7.3 %collective-permute-start.10 = (bf16[384,1024]{1,0:T(8,128)(2,1)}, bf16[384,1024]{1,0:T(8,128)(2,1)S(1)}, u32[]{:S(2)}, u32[]{:S(2)}) collective-permute-start(bf16[384,1024]{1,0:T(8,128)(2,1)} %get-tuple-element.28.refs_0_), channel_id=1, source_target_pairs={{0,1},{1,0},{2,3},{3,2},{4,5},{5,4},{6,7},{7,6},{8,9},{9,8},{10,11... | collective-permute-start | bytes 2359304 | tf_op jit(solution)/shard_map/ppermute | solution.py:544
  54.7 7.3 %collective-permute-start.11 = (bf16[384,1024]{1,0:T(8,128)(2,1)}, bf16[384,1024]{1,0:T(8,128)(2,1)}, u32[]{:S(2)}, u32[]{:S(2)}) collective-permute-start(bf16[384,1024]{1,0:T(8,128)(2,1)} %get-tuple-element.29.refs_2_), channel_id=1, source_target_pairs={{0,1},{1,0},{2,3},{3,2},{4,5},{5,4},{6,7},{7,6},{8,9},{9,8},{10,11... | collective-permute-start | bytes 2359304 | tf_op jit(solution)/shard_map/ppermute | solution.py:544
  55.2 14.4 %collective-permute-start.8 = (bf16[192,1024]{1,0:T(8,128)(2,1)}, bf16[192,1024]{1,0:T(8,128)(2,1)S(1)}, u32[]{:S(2)}, u32[]{:S(2)}) collective-permute-start(bf16[192,1024]{1,0:T(8,128)(2,1)} %get-tuple-element.26), channel_id=1, source_target_pairs={{0,2},{1,3},{2,4},{3,5},{4,6},{5,7},{6,0},{7,1},{8,10},{9,11},{10,... | collective-permute-start | bytes 1179656 | tf_op jit(solution)/shard_map/ppermute | solution.py:541
  55.2 14.4 %collective-permute-start.9 = (bf16[192,1024]{1,0:T(8,128)(2,1)}, bf16[192,1024]{1,0:T(8,128)(2,1)S(1)}, u32[]{:S(2)}, u32[]{:S(2)}) collective-permute-start(bf16[192,1024]{1,0:T(8,128)(2,1)} %get-tuple-element.27), channel_id=1, source_target_pairs={{0,6},{1,7},{2,0},{3,1},{4,2},{5,3},{6,4},{7,5},{8,14},{9,15},{10,... | collective-permute-start | bytes 1179656 | tf_op jit(solution)/shard_map/ppermute | solution.py:541
  58.4 15.0 %all-to-all-start.2 = ((f32[16,8,1024]{2,1,0:T(8,128)}), f32[16,8,1024]{2,1,0:T(8,128)S(1)}, u32[]{:S(2)}, u32[]{:S(2)}) async-start(f32[16,8,1024]{2,1,0:T(8,128)} %bitcast.20), calls=%async_computation.2 | async-start | bytes 1048576 | tf_op jit(solution)/shard_map/all_to_all | solution.py:603
  62.0 11.4 %copy-start.4 = (bf16[16,3,32,128]{3,2,1,0:T(8,128)(2,1)S(1)}, bf16[16,3,32,128]{3,2,1,0:T(8,128)(2,1)}, u32[]{:S(2)}) copy-start(bf16[16,3,32,128]{3,2,1,0:T(8,128)(2,1)} %copy-done.3) | copy-start | bytes 1179652
  62.0 11.4 %copy-start.7 = (bf16[1024,64]{0,1:T(8,128)(2,1)S(1)}, bf16[1024,64]{0,1:T(8,128)(2,1)}, u32[]{:S(2)}) copy-start(bf16[1024,64]{0,1:T(8,128)(2,1)} %param.10) | copy-start | bytes 393220
  69.6 3.8 %collective-permute-start.12 = (bf16[192,1024]{1,0:T(8,128)(2,1)S(1)}, bf16[192,1024]{1,0:T(8,128)(2,1)S(1)}, u32[]{:S(2)}, u32[]{:S(2)}) collective-permute-start(bf16[192,1024]{1,0:T(8,128)(2,1)S(1)} %get-tuple-element.32.far_a), channel_id=1, source_target_pairs={{0,1},{1,0},{2,3},{3,2},{4,5},{5,4},{6,7},{7,6},{8,9},{9,8},{10,11... | collective-permute-start | bytes 1179656 | tf_op jit(solution)/shard_map/ppermute | solution.py:544
  69.7 3.7 %collective-permute-start.13 = (bf16[192,1024]{1,0:T(8,128)(2,1)S(1)}, bf16[192,1024]{1,0:T(8,128)(2,1)S(1)}, u32[]{:S(2)}, u32[]{:S(2)}) collective-permute-start(bf16[192,1024]{1,0:T(8,128)(2,1)S(1)} %get-tuple-element.33.far_b), channel_id=1, source_target_pairs={{0,1},{1,0},{2,3},{3,2},{4,5},{5,4},{6,7},{7,6},{8,9},{9,8},{10,11... | collective-permute-start | bytes 1179656 | tf_op jit(solution)/shard_map/ppermute | solution.py:544
